TPU v7x, 32 devices: a whole 2x2x4 slice. The times are simulated.
32 devices in a mesh: dp: 8 (over z, y), seq: 2 (over x), ffn: 2 (over core).
Axes of the slice: x: 2, y: 2, z: 4, core: 2. Of those that a mesh axis runs over, the one named last changes fastest.
Arguments:
- tokens: bfloat16 [8, 2048, 512], P('dp', ('seq', 'ffn')), may hold values from -6 to 6
- doc_starts: int32 [8, 8], P('dp'), may hold values from 0 to 2047, as said below
- norm1_gain: float32 [512], replicated, may hold values from 0.1 to 1.9
- norm1_bias: float32 [512], replicated, may hold values from -3 to 3
- in_weight: bfloat16 [512, 2048], replicated, may hold values from -0.5 to 0.5
- out_weight: bfloat16 [512, 512], replicated, may hold values from -0.375 to 0.375
- norm2_gain: float32 [512], replicated, may hold values from 0.1 to 1.9
- norm2_bias: float32 [512], replicated, may hold values from -3 to 3
- up_weight: bfloat16 [512, 2048], P(None, 'ffn'), may hold values from -0.25 to 0.25
- down_weight: bfloat16 [512, 2048], P(None, 'ffn'), may hold values from -0.1875 to 0.1875
- output_cotangent: bfloat16 [8, 2048, 512], P('dp', ('seq', 'ffn')), may hold values from -6 to 6
Outputs:
- output: bfloat16 [8, 2048, 512], P('dp', ('seq', 'ffn'))
- grad_tokens: float32 [8, 2048, 512], P('dp', ('seq', 'ffn'))
- grad_in_proj: float32 [512, 2048], P(('dp', 'seq'))
- grad_out_proj: float32 [512, 512], P(('dp', 'seq'))
- grad_up: float32 [512, 2048], P(('dp', 'seq'), 'ffn')
- grad_down: float32 [512, 2048], P(('dp', 'seq'), 'ffn')
- grad_norm1_gain: float32 [512], P(('dp', 'seq'))
- grad_norm1_bias: float32 [512], P(('dp', 'seq'))
- grad_norm2_gain: float32 [512], P(('dp', 'seq'))
- grad_norm2_bias: float32 [512], P(('dp', 'seq'))
Inputs may be any that keep to these rules, and one draw needn't show every extreme that they name: `doc_starts`: in each row the 8 document starts are distinct and increasing, and the first is 0; in the first row the last document is the row's last token alone.
All inputs are finite; a program needn't handle non-finite values.
Results may differ from a plain program's by a relative error of at most 0.017.
The roundings to bfloat16 on the way count: a program that leaves them out, or rounds other values in their place, can miss the bound.
Values may be sent and summed in bfloat16 or wider, within the bound.
No kernel may reach another device: no remote copies, remote signals or barrier semaphores. Data moves between devices by JAX's collectives and lax.ppermute only.
A program may use at most 192 MiB of HBM per device.

v0:
```python
import functools

import jax
import jax.numpy as jnp
from jax import lax
from jax.experimental import pallas as pl
from jax.experimental.pallas import tpu as pltpu
from jax.sharding import PartitionSpec as P

HEADS = 8
HEAD = 64
EPSILON = 1e-05
BF = jnp.bfloat16
F32 = jnp.float32
GELU_A = 0.7978845608028654
GELU_B = 0.044715
SCALE = HEAD**-0.5
PACK = HEADS * HEAD + 64
VMEM_LIMIT = 56 * 1024 * 1024


def nn(a, b):
    return lax.dot_general(a, b, (((1,), (0,)), ((), ())), preferred_element_type=F32)


def nt(a, b):
    return lax.dot_general(a, b, (((1,), (1,)), ((), ())), preferred_element_type=F32)


def tn(a, b):
    return lax.dot_general(a, b, (((0,), (0,)), ((), ())), preferred_element_type=F32)


def swap(a, axis, bit):
    size = lax.axis_size(axis)
    return lax.ppermute(a, axis, [(i, i ^ bit) for i in range(size)])


def call(body, grid, in_specs, out_specs, out_shape, scratch=(), flops=0, **kw):
    return pl.pallas_call(
        body,
        grid=grid,
        in_specs=in_specs,
        out_specs=out_specs,
        out_shape=out_shape,
        scratch_shapes=list(scratch),
        cost_estimate=pl.CostEstimate(flops=flops, bytes_accessed=2**21, transcendentals=0),
        compiler_params=pltpu.CompilerParams(vmem_limit_bytes=VMEM_LIMIT),
        **kw,
    )


def whole(shape):
    return pl.BlockSpec(shape, lambda *_: (0,) * len(shape))


SMEM = pl.BlockSpec(memory_space=pltpu.SMEM)


def shard_of():
    return lax.axis_index("seq") * 2 + lax.axis_index("ffn")


def doc_begin_row(starts_ref, length):
    begin = shard_of() * length
    place = lax.broadcasted_iota(jnp.int32, (1, length), 1)
    row = jnp.full((1, length), -(2**30), jnp.int32)
    for j in range(starts_ref.shape[1]):
        s = starts_ref[0, j] - begin
        row = jnp.where(place >= s, jnp.maximum(row, s), row)
    return row


def passes(starts_ref, which, length):
    hit = jnp.int32(0)
    for j in range(starts_ref.shape[1]):
        s = starts_ref[0, j]
        hit = hit | ((s >= which * length) & (s < which * length + length)).astype(jnp.int32)
    return 1.0 - hit.astype(F32)


def visible(doc_row, length):
    i = lax.broadcasted_iota(jnp.int32, (length, length), 0)
    t = lax.broadcasted_iota(jnp.int32, (length, length), 1)
    return jnp.where((i <= t) & (i >= doc_row), 1.0, 0.0).astype(BF)


def tail_row(doc_row, length):
    place = lax.broadcasted_iota(jnp.int32, (1, length), 1)
    last = doc_row[:, length - 1 :]
    return jnp.where(place >= last, 1.0, 0.0)


def pack_totals(pack_ref, totals8):
    base = HEADS * HEAD
    hi = totals8.astype(BF)
    lo = (totals8 - hi.astype(F32)).astype(BF)
    for a in range(4):
        cols = slice(128 * a, 128 * a + 128)
        pack_ref[base + 16 * a : base + 16 * a + 16, :] = jnp.concatenate(
            [hi[:, cols], lo[:, cols]], axis=0
        )


def unpack(rows, totals8_of):
    base = HEADS * HEAD
    out = []
    for a in range(4):
        block = totals8_of(slice(base + 16 * a, base + 16 * a + 16))
        out.append(block[:8] + block[8:])
    return rows(slice(0, base)), jnp.concatenate(out, axis=1)


def combine_body(backward, length, starts_ref, own_ref, partner_ref, out_ref):
    first = 2 * lax.axis_index("seq")
    is_first = (lax.axis_index("ffn") == 0).astype(F32)
    base = HEADS * HEAD
    if backward:
        p = passes(starts_ref, first, length)
        own_by, partner_by = is_first + (1 - is_first) * p, is_first * p + (1 - is_first)
    else:
        p = passes(starts_ref, first + 1, length)
        own_by, partner_by = is_first * p + (1 - is_first), is_first + (1 - is_first) * p

    def sum_of(at):
        return own_ref[at, :].astype(F32) * own_by + partner_ref[at, :].astype(F32) * partner_by

    memory, totals8 = unpack(sum_of, sum_of)
    out_ref[:base, :] = memory.astype(BF)
    pack_totals(out_ref, totals8)


def combine(backward, length, starts, own, partner):
    return call(
        functools.partial(combine_body, backward, length),
        (),
        [SMEM, whole((PACK, 128)), whole((PACK, 128))],
        whole((PACK, 128)),
        jax.ShapeDtypeStruct((PACK, 128), BF),
    )(starts, own, partner)


def arrived(backward, length, starts_ref, partner_ref, far_ref, mem_ref, totals_ref):
    first = 2 * lax.axis_index("seq")
    is_first = (lax.axis_index("ffn") == 0).astype(F32)
    if backward:
        p = passes(starts_ref, first + 1, length)
        far_by, partner_by = is_first * p + (1 - is_first), is_first
    else:
        p = passes(starts_ref, first, length)
        far_by, partner_by = is_first + (1 - is_first) * p, 1 - is_first

    def sum_of(at):
        return far_ref[at, :].astype(F32) * far_by + partner_ref[at, :].astype(F32) * partner_by

    memory, totals8 = unpack(sum_of, sum_of)
    mem_ref[...] = memory.astype(BF)
    totals_ref[...] = totals8.T


def project_body(x_ref, gain_ref, bias_ref, w_ref, starts_ref,
                 heads_ref, control_ref, xnt_ref, pack_ref, xn_ref):
    j = pl.program_id(0)
    length = x_ref.shape[0]

    @pl.when(j == 0)
    def _():
        x = x_ref[...].astype(F32)
        mean = jnp.mean(x, axis=-1, keepdims=True)
        centered = x - mean
        inverse = lax.rsqrt(jnp.mean(centered * centered, axis=-1, keepdims=True) + EPSILON)
        xn = (centered * inverse * gain_ref[...] + bias_ref[...]).astype(BF)
        xn_ref[...] = xn
        xnt_ref[...] = xn.T

    projected = nn(xn_ref[...], w_ref[...])

    @pl.when(j < 3)
    def _():
        t = projected.astype(BF).T
        for h in range(HEADS):
            heads_ref[h, pl.ds(pl.multiple_of(j * HEAD, HEAD), HEAD), :] = t[h * HEAD : h * HEAD + HEAD]

    @pl.when(j == 3)
    def _():
        control = jnp.exp(projected).T
        control_ref[...] = control
        c = control.astype(BF)
        tail = tail_row(doc_begin_row(starts_ref, length), length)
        c_tail = (c.astype(F32) * tail).astype(BF)
        for h in range(HEADS):
            rows = slice(h * HEAD, h * HEAD + HEAD)
            heads_ref[h, 3 * HEAD :, :] = c[rows]
            mem_k = nt(c_tail[rows], heads_ref[h, HEAD : 2 * HEAD, :])
            mem_vt = nt(heads_ref[h, 2 * HEAD : 3 * HEAD, :], c_tail[rows])
            pack_ref[rows, :] = jnp.concatenate([mem_k, mem_vt], axis=1).astype(BF)
        tail8 = jnp.broadcast_to(tail, (8, length)).astype(BF)
        pack_totals(pack_ref, nt(tail8, c))


def project(x, gain, bias, w, starts):
    length, width = x.shape
    return call(
        project_body,
        (4,),
        [
            whole((length, width)), whole((1, width)), whole((1, width)),
            pl.BlockSpec((width, width), lambda j: (0, j)), SMEM,
        ],
        [
            whole((HEADS, 4 * HEAD, length)), whole((width, length)), whole((width, length)),
            whole((PACK, 128)),
        ],
        [
            jax.ShapeDtypeStruct((HEADS, 4 * HEAD, length), BF),
            jax.ShapeDtypeStruct((width, length), F32),
            jax.ShapeDtypeStruct((width, length), BF),
            jax.ShapeDtypeStruct((PACK, 128), BF),
        ],
        [pltpu.VMEM((length, width), BF)],
        flops=2 * length * width * 4 * width,
    )(x, gain, bias, w, starts)


HEAD_BLOCK = lambda rows, length: pl.BlockSpec((1, rows, length), lambda h: (h, 0, 0))
ROW_BLOCK = lambda length: pl.BlockSpec((HEAD, length), lambda h: (h, 0))


def causal_pairs(left, right, mask_ref):
    half = mask_ref.shape[0] // 2
    rows = left.T
    a = nn(rows[:half], right[:, :half]).astype(BF) * mask_ref[:half, :half]
    b = nn(rows, right[:, half:]).astype(BF) * mask_ref[:, half:]
    return a, b


def causal_sum(left, pairs):
    a, b = pairs
    half = a.shape[0]
    return jnp.concatenate([nn(left[:, :half], a), nn(left, b)], axis=1)


def causal_back(left, pairs):
    a, b = pairs
    half = a.shape[0]
    late = nt(left[:, half:], b)
    return jnp.concatenate([late[:, :half] + nt(left[:, :half], a), late[:, half:]], axis=1)


def mask_pair(mask_ref):
    half = mask_ref.shape[0] // 2
    return mask_ref[:half, :half], mask_ref[:, half:]


def parts(heads_ref):
    return [heads_ref[0, j * HEAD : j * HEAD + HEAD, :] for j in range(4)]


def local_body(starts_ref, heads_ref, number_ref, total_ref, mask_ref):
    length = heads_ref.shape[2]

    @pl.when(pl.program_id(0) == 0)
    def _():
        mask_ref[...] = visible(doc_begin_row(starts_ref, length), length)

    q, k, v, c = parts(heads_ref)
    number_ref[...] = causal_sum(c, causal_pairs(k, q, mask_ref))
    total_ref[...] = causal_sum(c, mask_pair(mask_ref))


def local_sums(starts, heads):
    length = heads.shape[2]
    width = HEADS * HEAD
    return call(
        local_body,
        (HEADS,),
        [SMEM, HEAD_BLOCK(4 * HEAD, length)],
        [ROW_BLOCK(length)] * 2,
        [jax.ShapeDtypeStruct((width, length), F32)] * 2,
        [pltpu.VMEM((length, length), BF)],
        flops=6 * length * length * width,
    )(starts, heads)


def enters_row(starts_ref, length):
    return jnp.where(doc_begin_row(starts_ref, length) < 0, 1.0, 0.0)


def softmax(number, inverse):
    score = number * (inverse * SCALE)
    e = jnp.exp(score - jnp.max(score, axis=0, keepdims=True))
    return e / jnp.sum(e, axis=0, keepdims=True)


def mix_body(starts_ref, heads_ref, number_ref, total_ref, partner_ref, far_ref,
             number_out, total_out, mixed_ref, mem_out, mask_ref, mem_ref, totals_ref):
    length = heads_ref.shape[2]
    h = pl.program_id(0)

    @pl.when(h == 0)
    def _():
        mask_ref[...] = visible(doc_begin_row(starts_ref, length), length)
        arrived(False, length, starts_ref, partner_ref, far_ref, mem_ref, totals_ref)
        mem_out[...] = mem_ref[...]

    enters = enters_row(starts_ref, length)
    rows = pl.ds(pl.multiple_of(h * HEAD, HEAD), HEAD)
    q, k, v, c = parts(heads_ref)
    mem = mem_ref[rows, :]
    mem_k, mem_vt = mem[:, :HEAD], mem[:, HEAD:]
    number = number_ref[...] + enters * nn(mem_k, q)
    total = total_ref[...] + enters * totals_ref[rows, 0:1]
    number_out[...] = number
    total_out[...] = total
    inverse = 1.0 / total
    spread = (softmax(number, inverse) * inverse).astype(BF)
    links = causal_pairs(c, spread, mask_ref)
    mixed = causal_sum(v, links) + enters * nn(mem_vt, spread)
    mixed_ref[...] = mixed.astype(BF)


def mix(starts, heads, number, total, partner, far):
    length = heads.shape[2]
    width = HEADS * HEAD
    return call(
        mix_body,
        (HEADS,),
        [SMEM, HEAD_BLOCK(4 * HEAD, length), ROW_BLOCK(length), ROW_BLOCK(length),
         whole((PACK, 128)), whole((PACK, 128))],
        [ROW_BLOCK(length), ROW_BLOCK(length), ROW_BLOCK(length), whole((width, 128))],
        [
            jax.ShapeDtypeStruct((width, length), F32),
            jax.ShapeDtypeStruct((width, length), F32),
            jax.ShapeDtypeStruct((width, length), BF),
            jax.ShapeDtypeStruct((width, 128), BF),
        ],
        [pltpu.VMEM((length, length), BF), pltpu.VMEM((width, 128), BF), pltpu.VMEM((width, 8), F32)],
        flops=6 * length * length * width,
    )(starts, heads, number, total, partner, far)


def feed_body(x_ref, mixed_ref, cot_ref, w_out_ref, gain_ref, bias_ref,
              up_own, up_other, down_own, down_other,
              output_ref, d_hidden1_ref, g_ref, grad_out_ref, gain_grad_ref, bias_grad_ref,
              gup_own, gup_other, gdown_own, gdown_other,
              hidden1_ref, n_ref, inv_ref, xn_ref, xnt_ref, cott_ref, part_ref, d_ref):
    j = pl.program_id(0)

    @pl.when(j == 0)
    def _():
        hidden1 = x_ref[...].astype(F32) + tn(mixed_ref[...], w_out_ref[...])
        hidden1_ref[...] = hidden1
        mean = jnp.mean(hidden1, axis=-1, keepdims=True)
        centered = hidden1 - mean
        inverse = lax.rsqrt(jnp.mean(centered * centered, axis=-1, keepdims=True) + EPSILON)
        n = centered * inverse
        n_ref[...] = n
        inv_ref[...] = inverse
        xn = (n * gain_ref[...] + bias_ref[...]).astype(BF)
        xn_ref[...] = xn
        xnt_ref[...] = xn.T
        cott_ref[...] = cot_ref[...].T

    def step(up_ref, down_ref, gup_ref, gdown_ref, is_start):
        up, down = up_ref[...], down_ref[...]
        pre = nn(xn_ref[...], up)
        v2 = pre * pre
        th = jnp.tanh(GELU_A * pre * (1.0 + GELU_B * v2))
        half = 0.5 * (1.0 + th)
        hidden = (pre * half).astype(BF)
        slope = half + 0.5 * pre * (1.0 - th * th) * (GELU_A * (1.0 + 3.0 * GELU_B * v2))
        grad_pre = (nn(cot_ref[...], down) * slope).astype(BF)
        part = nt(hidden, down)
        d = nt(grad_pre, up)
        if is_start:
            part_ref[...] = part
            d_ref[...] = d
        else:
            part_ref[...] += part
            d_ref[...] += d
        gdown_ref[...] = nn(cott_ref[...], hidden).astype(gdown_ref.dtype)
        gup_ref[...] = nn(xnt_ref[...], grad_pre).astype(gup_ref.dtype)

    @pl.when(j == 0)
    def _():
        step(up_own, down_own, gup_own, gdown_own, True)

    @pl.when(j == 1)
    def _():
        step(up_own, down_own, gup_own, gdown_own, False)

    @pl.when(j >= 2)
    def _():
        step(up_other, down_other, gup_other, gdown_other, False)

    @pl.when(j == 3)
    def _():
        output_ref[...] = (hidden1_ref[...] + part_ref[...]).astype(BF)
        d, n = d_ref[...], n_ref[...]
        gain_grad_ref[...] = jnp.broadcast_to(jnp.sum(d * n, axis=0, keepdims=True), gain_grad_ref.shape)
        bias_grad_ref[...] = jnp.broadcast_to(jnp.sum(d, axis=0, keepdims=True), bias_grad_ref.shape)
        d_n = d * gain_ref[...]
        d_in = (
            d_n
            - jnp.mean(d_n, axis=-1, keepdims=True)
            - n * jnp.mean(d_n * n, axis=-1, keepdims=True)
        ) * inv_ref[...]
        d_hidden1 = cot_ref[...].astype(F32) + d_in
        d_hidden1_ref[...] = d_hidden1
        d_branch = d_hidden1.astype(BF)
        grad_out_ref[...] = nn(mixed_ref[...], d_branch).astype(grad_out_ref.dtype)
        g_ref[...] = nt(w_out_ref[...], d_branch).astype(BF)


def feed(x, mixed, cotangent, w_out, gain, bias, up_own, up_other, down_own, down_other):
    length, width = x.shape
    square = whole((length, width))
    row = whole((1, width))
    own = pl.BlockSpec((width, 512), lambda j: (0, jnp.minimum(j, 1)))
    other = pl.BlockSpec((width, 512), lambda j: (0, jnp.maximum(j - 2, 0)))
    half = up_own.shape[1]
    vec = whole((8, width))
    return call(
        feed_body,
        (4,),
        [square, square, square, square, row, row, own, other, own, other],
        [square, square, square, square, vec, vec, own, other, own, other],
        [
            jax.ShapeDtypeStruct((length, width), BF),
            jax.ShapeDtypeStruct((length, width), F32),
            jax.ShapeDtypeStruct((width, length), BF),
            jax.ShapeDtypeStruct((width, width), BF),
            jax.ShapeDtypeStruct((8, width), F32),
            jax.ShapeDtypeStruct((8, width), F32),
        ]
        + [jax.ShapeDtypeStruct((width, half), BF)] * 4,
        [
            pltpu.VMEM((length, width), F32), pltpu.VMEM((length, width), F32),
            pltpu.VMEM((length, 1), F32), pltpu.VMEM((length, width), BF),
            pltpu.VMEM((width, length), BF), pltpu.VMEM((width, length), BF),
            pltpu.VMEM((length, width), F32), pltpu.VMEM((length, width), F32),
        ],
        flops=2 * length * width * 2048 * 7,
    )(x, mixed, cotangent, w_out, gain, bias, up_own, up_other, down_own, down_other)


def scores_back_body(starts_ref, heads_ref, g_ref, number_ref, total_ref, mem_ref,
                     a_ref, spread_ref, d_total_ref, pack_ref, mask_ref, sums_ref):
    length = heads_ref.shape[2]
    h = pl.program_id(0)

    @pl.when(h == 0)
    def _():
        mask_ref[...] = visible(doc_begin_row(starts_ref, length), length)

    enters = enters_row(starts_ref, length)
    rows = pl.ds(pl.multiple_of(h * HEAD, HEAD), HEAD)
    q, k, v, c = parts(heads_ref)
    g = g_ref[...]
    mem_vt = mem_ref[:, HEAD:]
    number, inverse = number_ref[...], 1.0 / total_ref[...]
    weight = softmax(number, inverse)
    number_v = causal_sum(c, causal_pairs(v, g, mask_ref)) + enters * tn(mem_vt, g)
    d_weight = number_v * inverse
    d_score = weight * (d_weight - jnp.sum(weight * d_weight, axis=0, keepdims=True))
    a = d_score * (inverse * SCALE)
    spread = weight * inverse
    d_total = -(a * number + spread * number_v) * inverse
    a_ref[...] = a.astype(BF)
    spread_ref[...] = spread.astype(BF)
    d_total_ref[...] = d_total.astype(BF)
    mem_k = nt((a * enters).astype(BF), q)
    d_vt = nt(g, (spread * enters).astype(BF))
    pack_ref[rows, :] = jnp.concatenate([mem_k, d_vt], axis=1).astype(BF)
    sums_ref[rows, 0:1] = jnp.sum(d_total * enters, axis=1, keepdims=True)

    @pl.when(h == HEADS - 1)
    def _():
        pack_totals(pack_ref, jnp.broadcast_to(sums_ref[...].T[0:1], (8, HEADS * HEAD)))


def scores_back(starts, heads, g, number, total, mem):
    length = heads.shape[2]
    width = HEADS * HEAD
    row = ROW_BLOCK(length)
    return call(
        scores_back_body,
        (HEADS,),
        [SMEM, HEAD_BLOCK(4 * HEAD, length), row, row, row, pl.BlockSpec((HEAD, 128), lambda h: (h, 0))],
        [row, row, row, whole((PACK, 128))],
        [jax.ShapeDtypeStruct((width, length), BF)] * 3 + [jax.ShapeDtypeStruct((PACK, 128), BF)],
        [pltpu.VMEM((length, length), BF), pltpu.VMEM((width, 8), F32)],
        flops=6 * length * length * width,
    )(starts, heads, g, number, total, mem)


def heads_back_body(starts_ref, heads_ref, g_ref, a_ref, spread_ref, d_total_ref, mem_ref,
                    d_ref, mask_ref):
    length = heads_ref.shape[2]

    @pl.when(pl.program_id(0) == 0)
    def _():
        mask_ref[...] = visible(doc_begin_row(starts_ref, length), length)

    enters = enters_row(starts_ref, length)
    q, k, v, c = parts(heads_ref)
    g, a, spread, d_total = g_ref[...], a_ref[...], spread_ref[...], d_total_ref[...]
    mem_k = mem_ref[:, :HEAD]
    steps = causal_pairs(c, a, mask_ref)
    d_ref[0, :HEAD, :] = causal_sum(k, steps) + enters * tn(mem_k, a)
    d_ref[0, HEAD : 2 * HEAD, :] = causal_back(q, steps)
    links = causal_pairs(c, spread, mask_ref)
    d_ref[0, 2 * HEAD : 3 * HEAD, :] = causal_back(g, links)
    d_ref[0, 3 * HEAD :, :] = (
        causal_back(a, causal_pairs(k, q, mask_ref))
        + causal_back(spread, causal_pairs(v, g, mask_ref))
        + causal_back(d_total, mask_pair(mask_ref))
    )


def heads_back(starts, heads, g, a, spread, d_total, mem):
    length = heads.shape[2]
    width = HEADS * HEAD
    row = ROW_BLOCK(length)
    return call(
        heads_back_body,
        (HEADS,),
        [SMEM, HEAD_BLOCK(4 * HEAD, length), row, row, row, row, pl.BlockSpec((HEAD, 128), lambda h: (h, 0))],
        HEAD_BLOCK(4 * HEAD, length),
        jax.ShapeDtypeStruct((HEADS, 4 * HEAD, length), F32),
        [pltpu.VMEM((length, length), BF)],
        flops=20 * length * length * width,
    )(starts, heads, g, a, spread, d_total, mem)


def project_back_body(starts_ref, heads_ref, d_ref, control_ref, partner_ref, far_ref, xnt_ref,
                      wq_ref, wk_ref, wv_ref, wc_ref, x_ref, gain_ref, d_hidden1_ref,
                      send_ref, keep_ref, grad_x_ref, gain_grad_ref, bias_grad_ref,
                      mem_ref, totals_ref, proj_ref, dx_ref):
    j = pl.program_id(0)
    length = x_ref.shape[0]
    ffn = lax.axis_index("ffn")

    @pl.when(j == 0)
    def _():
        arrived(True, length, starts_ref, partner_ref, far_ref, mem_ref, totals_ref)

    pair = jnp.where(j < 2, 1 - ffn, ffn) * 2 + j % 2
    tail = tail_row(doc_begin_row(starts_ref, length), length)
    for i in range(2):
        rows = pl.ds(pl.multiple_of((pair * 2 + i) * HEAD, HEAD), HEAD)
        mem = mem_ref[rows, :]
        back_k, back_vt = mem[:, :HEAD], mem[:, HEAD:]
        k, v, c = [heads_ref[i, m * HEAD : m * HEAD + HEAD, :] for m in (1, 2, 3)]
        c_tail = (c.astype(F32) * tail).astype(BF)
        d_q = d_ref[i, :HEAD, :]
        d_k = d_ref[i, HEAD : 2 * HEAD, :] + tn(back_k, c_tail)
        d_v = d_ref[i, 2 * HEAD : 3 * HEAD, :] + nn(back_vt, c_tail)
        d_c = d_ref[i, 3 * HEAD :, :] + tail * (
            nn(back_k, k) + tn(back_vt, v) + totals_ref[rows, 0:1]
        )
        d_c = d_c * control_ref[i * HEAD : i * HEAD + HEAD, :]
        for m, value in enumerate((d_q, d_k, d_v, d_c)):
            proj_ref[m * 128 + i * HEAD : m * 128 + i * HEAD + HEAD, :] = value.astype(BF)
    d_proj = proj_ref[...]
    grad = nt(xnt_ref[...], d_proj).astype(BF)

    @pl.when(j < 2)
    def _():
        send_ref[...] = grad

    @pl.when(j >= 2)
    def _():
        keep_ref[...] = grad

    w = jnp.concatenate([wq_ref[...], wk_ref[...], wv_ref[...], wc_ref[...]], axis=1)
    dx = nn(w, d_proj)

    @pl.when(j == 0)
    def _():
        dx_ref[...] = dx

    @pl.when(j > 0)
    def _():
        dx_ref[...] += dx

    @pl.when(j == 3)
    def _():
        x = x_ref[...].astype(F32)
        mean = jnp.mean(x, axis=-1, keepdims=True)
        centered = x - mean
        inverse = lax.rsqrt(jnp.mean(centered * centered, axis=-1, keepdims=True) + EPSILON)
        n = centered * inverse
        d = dx_ref[...].T
        gain_grad_ref[...] = jnp.broadcast_to(jnp.sum(d * n, axis=0, keepdims=True), gain_grad_ref.shape)
        bias_grad_ref[...] = jnp.broadcast_to(jnp.sum(d, axis=0, keepdims=True), bias_grad_ref.shape)
        d_n = d * gain_ref[...]
        grad_x_ref[...] = d_hidden1_ref[...] + (
            d_n
            - jnp.mean(d_n, axis=-1, keepdims=True)
            - n * jnp.mean(d_n * n, axis=-1, keepdims=True)
        ) * inverse


def project_back(starts, heads, d, control, partner, far, xnt, w, x, gain, d_hidden1):
    length, width = x.shape
    square = whole((length, width))
    row, vec = whole((1, width)), whole((8, width))

    def pair(j):
        ffn = lax.axis_index("ffn")
        return jnp.where(j < 2, 1 - ffn, ffn) * 2 + j % 2

    two = pl.BlockSpec((2, 4 * HEAD, length), lambda j: (pair(j), 0, 0))
    weights = [
        pl.BlockSpec((width, 128), functools.partial(lambda m, j: (0, 4 * m + pair(j)), m))
        for m in range(4)
    ]
    return call(
        project_back_body,
        (4,),
        [SMEM, two, two, pl.BlockSpec((128, length), lambda j: (pair(j), 0)),
         whole((PACK, 128)), whole((PACK, 128)), square]
        + weights
        + [square, row, square],
        [
            pl.BlockSpec((width, 512), lambda j: (0, jnp.minimum(j, 1))),
            pl.BlockSpec((width, 512), lambda j: (0, jnp.maximum(j - 2, 0))),
            square, vec, vec,
        ],
        [
            jax.ShapeDtypeStruct((width, 1024), BF),
            jax.ShapeDtypeStruct((width, 1024), BF),
            jax.ShapeDtypeStruct((length, width), F32),
            jax.ShapeDtypeStruct((8, width), F32),
            jax.ShapeDtypeStruct((8, width), F32),
        ],
        [
            pltpu.VMEM((width, 128), BF), pltpu.VMEM((width, 8), F32),
            pltpu.VMEM((512, length), BF), pltpu.VMEM((width, length), F32),
        ],
        flops=2 * length * width * 2048 * 2,
    )(starts, heads, d, control, partner, far, xnt, w, w, w, w, x, gain, d_hidden1)


def scatter_plan():
    count = lax.axis_size("dp")
    bits = [("seq", 1)]
    step = 1
    while step < count:
        bits.append(("dp", step))
        step *= 2
    return bits


def reduce_rows(group, lead):
    bits = scatter_plan()
    order = [(i + lead) % 3 for i in range(3)] + list(range(3, len(bits)))
    rows, width = group.shape
    value = group.reshape((2,) * len(bits) + (rows >> len(bits), width))
    left = list(reversed(range(len(bits))))
    for b in order:
        axis, step = bits[b]
        at = left.index(b)
        mine = (lax.axis_index(axis) // step) % 2
        keep = lax.dynamic_index_in_dim(value, mine, at, False)
        send = lax.dynamic_index_in_dim(value, 1 - mine, at, False)
        left.pop(at)
        value = keep.astype(F32) + swap(send.astype(BF), axis, step).astype(F32)
    return value


def on_device(tokens, doc_starts, norm1_gain, norm1_bias, in_weight, out_weight,
              norm2_gain, norm2_bias, up_own, down_own, output_cotangent):
    ffn = lax.axis_index("ffn")
    is_first = ffn == 0
    up_other, down_other = swap(up_own, "ffn", 1), swap(down_own, "ffn", 1)
    x, cotangent, starts = tokens[0], output_cotangent[0], doc_starts
    length, width = x.shape
    row = lambda a: a.reshape(1, width)

    heads, control, xnt, own = project(x, row(norm1_gain), row(norm1_bias), in_weight, starts)
    partner = swap(own, "ffn", 1)
    both = combine(False, length, starts, own, partner)
    far = lax.ppermute(both, "seq", [(0, 1)])
    number, total = local_sums(starts, heads)
    number, total, mixed, memory = mix(starts, heads, number, total, partner, far)
    (output, d_hidden1, g, grad_out, gain2, bias2,
     gup_own, gup_other, gdown_own, gdown_other) = feed(
        x, mixed, cotangent, out_weight, row(norm2_gain), row(norm2_bias),
        up_own, up_other, down_own, down_other)
    a, spread, d_total, d_own = scores_back(starts, heads, g, number, total, memory)
    d_partner = swap(d_own, "ffn", 1)
    d_both = combine(True, length, starts, d_own, d_partner)
    d_far = lax.ppermute(d_both, "seq", [(1, 0)])
    d_heads = heads_back(starts, heads, g, a, spread, d_total, memory)
    send, keep, grad_tokens, gain1, bias1 = project_back(
        starts, heads, d_heads, control, d_partner, d_far, xnt, in_weight, x,
        row(norm1_gain), d_hidden1)

    grad_up = gup_own.astype(F32) + swap(gup_other, "ffn", 1).astype(F32)
    grad_down = gdown_own.astype(F32) + swap(gdown_other, "ffn", 1).astype(F32)
    grad_in = keep.astype(F32) + swap(send, "ffn", 1).astype(F32)

    def core_half(a):
        half_width = a.shape[1] // 2
        kept = lax.dynamic_slice_in_dim(a, ffn * half_width, half_width, 1)
        sent = lax.dynamic_slice_in_dim(a, (1 - ffn) * half_width, half_width, 1)
        return kept.astype(F32) + swap(sent, "ffn", 1).astype(F32)

    def core_join(a):
        a = a.astype(BF)
        other = swap(a, "ffn", 1)
        return jnp.where(is_first, a, other), jnp.where(is_first, other, a)

    norms = jnp.stack([gain1[0], bias1[0], gain2[0], bias2[0]], axis=1)
    norms = norms + swap(norms, "ffn", 1)
    grad_down = reduce_rows(grad_down, 0)
    grad_up = reduce_rows(grad_up, 1)
    grad_out = jnp.concatenate(core_join(reduce_rows(core_half(grad_out), 2)), axis=1).astype(F32)
    lo, hi = core_join(reduce_rows(grad_in, 2))
    count = lo.shape[0]
    both_halves = jnp.stack([lo.reshape(count, 2, 4, 128), hi.reshape(count, 2, 4, 128)], axis=1)
    grad_in = both_halves.transpose(0, 3, 1, 2, 4).reshape(count, 2048).astype(F32)
    norms = reduce_rows(norms, 1)
    return (
        output[None], grad_tokens[None], grad_in, grad_out, grad_up, grad_down,
        norms[:, 0], norms[:, 1], norms[:, 2], norms[:, 3],
    )


def solution(mesh):
    rows = P("dp", ("seq", "ffn"), None)
    owned = P(("dp", "seq"))
    return jax.shard_map(
        on_device,
        mesh=mesh,
        in_specs=(
            rows, P("dp", None), P(), P(), P(), P(), P(), P(),
            P(None, "ffn"), P(None, "ffn"), rows,
        ),
        out_specs=(
            rows, rows, P(("dp", "seq"), None), P(("dp", "seq"), None),
            P(("dp", "seq"), "ffn"), P(("dp", "seq"), "ffn"),
            owned, owned, owned, owned,
        ),
        check_vma=False,
    )
```

profile of v0, /device:TPU:0, one launch (start us, length us, event | category | flops | bytes accessed | tf_op | source)
XLA Modules:
  0.0 175.3 jit_solution(8601340538984365809)
XLA Ops:
  1.2 7.1 %shard_map.186 = (bf16[8,256,512]{2,1,0:T(8,128)(2,1)}, f32[512,512]{1,0:T(8,128)}, bf16[512,512]{1,0:T(8,128)(2,1)}, bf16[576,128]{1,0:T(8,128)(2,1)}) custom-call(bf16[512,512]{1,0:T(8,128)(2,1)} %bitcast.129, f32[1,512]{1,0:T(1,128)} %bitcast.132, f32[1,512]{1,0:T(1,128)} %bitcast.137, bf16[512,2048]{1,0:T(8,128)(2,1)} %wc_ref.1, s32[1,8]{1,0:T(1,128)} %starts_ref.15), custom_call_target="tpu_custom_call" | custom-call | flops 1073741824 | bytes 2097152 | tf_op jit(solution)/shard_map/pallas_call | solution.py:203
  8.8 1.2 collective-permute-done.partner_ref
  10.7 1.7 shard_map.188
  12.4 4.8 %collective-permute-start.1 = (bf16[576,128]{1,0:T(8,128)(2,1)}, bf16[576,128]{1,0:T(8,128)(2,1)S(1)}, u32[]{:S(2)}, u32[]{:S(2)}) collective-permute-start(bf16[576,128]{1,0:T(8,128)(2,1)} %shard_map.188), channel_id=1, source_target_pairs={{0,2},{1,3},{4,6},{5,7},{8,10},{9,11},{12,14},{13,15},{16,18},{17,... | collective-permute-start | bytes 442376 | tf_op jit(solution)/shard_map/ppermute | solution.py:685
  17.3 7.7 %shard_map.187 = (f32[512,512]{1,0:T(8,128)}, f32[512,512]{1,0:T(8,128)}) custom-call(s32[1,8]{1,0:T(1,128)} %starts_ref.15, bf16[8,256,512]{2,1,0:T(8,128)(2,1)} %get-tuple-element.39.heads_ref), custom_call_target="tpu_custom_call" | custom-call | flops 805306368 | bytes 2097152 | tf_op jit(solution)/shard_map/pallas_call | solution.py:274
  25.7 8.9 %shard_map.189 = (f32[512,512]{1,0:T(8,128)}, f32[512,512]{1,0:T(8,128)}, bf16[512,512]{1,0:T(8,128)(2,1)}, bf16[512,128]{1,0:T(8,128)(2,1)}) custom-call(s32[1,8]{1,0:T(1,128)} %starts_ref.15, bf16[8,256,512]{2,1,0:T(8,128)(2,1)} %get-tuple-element.39.heads_ref, f32[512,512]{1,0:T(8,128)} %get-tuple-element.40.number_ref, ...), custom_call_target="tpu_custom_call" | custom-call | flops 805306368 | bytes 2097152 | tf_op jit(solution)/shard_map/pallas_call | solution.py:325
  34.5 0.9 copy-done.8
  35.8 15.2 %shard_map.190 = (bf16[512,512]{1,0:T(8,128)(2,1)}, f32[512,512]{1,0:T(8,128)}, bf16[512,512]{1,0:T(8,128)(2,1)}, bf16[512,512]{1,0:T(8,128)(2,1)}, f32[8,512]{1...) custom-call(bf16[512,512]{1,0:T(8,128)(2,1)} %bitcast.130, ...), custom_call_target="tpu_custom_call" | custom-call | flops 7516192768 | bytes 2097152 | tf_op jit(solution)/shard_map/pallas_call | solution.py:423
  51.1 8.9 %shard_map.191 = (bf16[512,512]{1,0:T(8,128)(2,1)}, bf16[512,512]{1,0:T(8,128)(2,1)}, bf16[512,512]{1,0:T(8,128)(2,1)}, bf16[576,128]{1,0:T(8,128)(2,1)}) custom-call(s32[1,8]{1,0:T(1,128)} %starts_ref.15, bf16[8,256,512]{2,1,0:T(8,128)(2,1)} %get-tuple-element.39.heads_ref, bf16[512,512]{1,0:T(8,128)(2,1)} %get-tuple-element.45.g_ref, ...), custom_call_target="tpu_custom_call" | custom-call | flops 805306368 | bytes 2097152 | tf_op jit(solution)/shard_map/pallas_call | solution.py:486
  60.0 17.8 %shard_map.192.d_ref = f32[8,256,512]{2,1,0:T(8,128)} custom-call(s32[1,8]{1,0:T(1,128)} %starts_ref.15, bf16[8,256,512]{2,1,0:T(8,128)(2,1)} %get-tuple-element.39.heads_ref, bf16[512,512]{1,0:T(8,128)(2,1)} %get-tuple-element.45.g_ref, bf16[512,512]{1,0:T(8,128)(2,1)} %get-tuple-element.49.a_ref, bf16[512,512]{1,0:T(8,128)(2,1)} %get-tuple-element.50.spread_ref, ...), custom_call_target="tpu_custom_call" | custom-call | flops 2684354560 | bytes 2097152 | tf_op jit(solution)/shard_map/pallas_call | solution.py:525
  77.8 0.7 copy-done.4
  78.5 1.7 shard_map.193
  80.2 1.5 collective-permute-start.5
  81.7 0.7 slice_bitcast_fusion
  82.4 6.1 %collective-permute-done.5.far_ref = bf16[576,128]{1,0:T(8,128)(2,1)S(1)} collective-permute-done((bf16[576,128]{1,0:T(8,128)(2,1)}, bf16[576,128]{1,0:T(8,128)(2,1)S(1)}, u32[]{:S(2)}, u32[]{:S(2)}) %collective-permute-start.5) | collective-permute-done | bytes 147488 | tf_op jit(solution)/shard_map/ppermute | solution.py:695
  88.6 0.7 copy-done.7
  89.2 11.2 %shard_map.194 = (bf16[512,1024]{1,0:T(8,128)(2,1)}, bf16[512,1024]{1,0:T(8,128)(2,1)}, f32[512,512]{1,0:T(8,128)}, f32[8,512]{1,0:T(8,128)}, f32[8,512]{1,0:T(8,128)}) custom-call(s32[1,8]{1,0:T(1,128)} %starts_ref.15, bf16[8,256,512]{2,1,0:T(8,128)(2,1)} %get-tuple-element.39.heads_ref, f32[8,256,512]{2,1,0:T(8,128)} %shard_map.192.d_ref, ...), custom_call_target="tpu_custom_call" | custom-call | flops 2147483648 | bytes 2097152 | tf_op jit(solution)/shard_map/pallas_call | solution.py:619
  100.4 0.8 slice_bitcast_fusion.2
  102.6 1.6 collective-permute-start.29
  104.2 1.1 convert_add_fusion.3
  105.3 1.0 collective-permute-done.29
  106.4 1.6 collective-permute-start.30
  108.6 1.5 collective-permute-done.30
  110.2 2.9 %collective-permute-done.13 = bf16[2,2,2,32,256]{4,3,0,1,2:T(8,128)(2,1)S(1)} collective-permute-done((bf16[2,2,2,32,256]{4,3,0,1,2:T(8,128)(2,1)S(1)}, bf16[2,2,2,32,256]{4,3,0,1,2:T(8,128)(2,1)S(1)}, u32[]{:S(2)}, u32[]{:S(2)}) %collective-permute-start.13) | collective-permute-done | bytes 131104 | tf_op jit(solution)/shard_map/ppermute | solution.py:36
  113.8 3.7 %collective-permute-done.14 = bf16[2,2,32,256]{3,2,0,1:T(8,128)(2,1)S(1)} collective-permute-done((bf16[2,2,32,256]{3,2,0,1:T(8,128)(2,1)S(1)}, bf16[2,2,32,256]{3,2,0,1:T(8,128)(2,1)S(1)}, u32[]{:S(2)}, u32[]{:S(2)}) %collective-permute-start.14) | collective-permute-done | bytes 65568 | tf_op jit(solution)/shard_map/ppermute | solution.py:36
  117.5 1.6 collective-permute-start.15
  119.1 2.6 %collective-permute-start.32 = (bf16[32,4]{0,1:T(4,128)(2,1)S(1)}, bf16[32,4]{0,1:T(4,128)(2,1)S(1)}, u32[]{:S(2)}, u32[]{:S(2)}) collective-permute-start(bf16[32,4]{0,1:T(4,128)(2,1)S(1)} %fusion.27), channel_id=1, source_target_pairs={{0,16},{4,20},{8,24},{12,28},{16,0},{20,4},{24,8},{28,12},{1,17},{... | collective-permute-start | bytes 776 | tf_op jit(solution)/shard_map/ppermute | solution.py:36
  121.7 2.4 %collective-permute-start.16 = (bf16[32,256]{1,0:T(8,128)(2,1)S(1)}, bf16[32,256]{1,0:T(8,128)(2,1)S(1)}, u32[]{:S(2)}, u32[]{:S(2)}) collective-permute-start(bf16[32,256]{1,0:T(8,128)(2,1)S(1)} %fusion.17), channel_id=1, source_target_pairs={{0,16},{4,20},{8,24},{12,28},{16,0},{20,4},{24,8},{28,12},{1,17},{... | collective-permute-start | bytes 49160 | tf_op jit(solution)/shard_map/ppermute | solution.py:36
  124.2 2.3 %collective-permute-done.16 = bf16[32,256]{1,0:T(8,128)(2,1)S(1)} collective-permute-done((bf16[32,256]{1,0:T(8,128)(2,1)S(1)}, bf16[32,256]{1,0:T(8,128)(2,1)S(1)}, u32[]{:S(2)}, u32[]{:S(2)}) %collective-permute-start.16) | collective-permute-done | bytes 16416 | tf_op jit(solution)/shard_map/ppermute | solution.py:36
  128.8 1.4 collective-permute-start.19
  130.8 0.7 copy-done.2
  132.4 10.5 %collective-permute-done.19 = bf16[2,2,2,32,1024]{4,3,0,2,1:T(8,128)(2,1)S(1)} collective-permute-done((bf16[2,2,2,32,1024]{4,3,0,2,1:T(8,128)(2,1)S(1)}, bf16[2,2,2,32,1024]{4,3,0,2,1:T(8,128)(2,1)S(1)}, u32[]{:S(2)}, u32[]{:S(2)}) %collective-permute-start.19) | collective-permute-done | bytes 524320 | tf_op jit(solution)/shard_map/ppermute | solution.py:36
  143.6 0.9 collective-permute-done.24
  144.7 1.0 collective-permute-start.25
  145.7 5.6 %collective-permute-done.20 = bf16[2,2,32,1024]{3,2,0,1:T(8,128)(2,1)S(1)} collective-permute-done((bf16[2,2,32,1024]{3,2,0,1:T(8,128)(2,1)S(1)}, bf16[2,2,32,1024]{3,2,0,1:T(8,128)(2,1)S(1)}, u32[]{:S(2)}, u32[]{:S(2)}) %collective-permute-start.20) | collective-permute-done | bytes 262176 | tf_op jit(solution)/shard_map/ppermute | solution.py:36
  151.4 1.1 collective-permute-start.21
  153.3 1.0 collective-permute-start.8
  154.4 3.5 %collective-permute-done.21 = bf16[2,32,1024]{2,1,0:T(8,128)(2,1)S(1)} collective-permute-done((bf16[2,32,1024]{2,1,0:T(8,128)(2,1)S(1)}, bf16[2,32,1024]{2,1,0:T(8,128)(2,1)S(1)}, u32[]{:S(2)}, u32[]{:S(2)}) %collective-permute-start.21) | collective-permute-done | bytes 131104 | tf_op jit(solution)/shard_map/ppermute | solution.py:36
  158.0 2.6 %collective-permute-start.22 = (bf16[32,1024]{1,0:T(8,128)(2,1)S(1)}, bf16[32,1024]{1,0:T(8,128)(2,1)S(1)}, u32[]{:S(2)}, u32[]{:S(2)}) collective-permute-start(bf16[32,1024]{1,0:T(8,128)(2,1)S(1)} %fusion.13), channel_id=1, source_target_pairs={{0,16},{4,20},{8,24},{12,28},{16,0},{20,4},{24,8},{28,12},{1,17},{... | collective-permute-start | bytes 196616 | tf_op jit(solution)/shard_map/ppermute | solution.py:36
  160.6 0.9 collective-permute-done.8
  161.6 1.2 collective-permute-start.9
  162.8 2.6 %collective-permute-start.27 = (bf16[32,1024]{1,0:T(8,128)(2,1)S(1)}, bf16[32,1024]{1,0:T(8,128)(2,1)S(1)}, u32[]{:S(2)}, u32[]{:S(2)}) collective-permute-start(bf16[32,1024]{1,0:T(8,128)(2,1)S(1)} %fusion.14), channel_id=1, source_target_pairs={{0,16},{4,20},{8,24},{12,28},{16,0},{20,4},{24,8},{28,12},{1,17},{... | collective-permute-start | bytes 196616 | tf_op jit(solution)/shard_map/ppermute | solution.py:36
  165.4 1.2 collective-permute-done.9
  166.7 2.8 %collective-permute-start.10 = (bf16[32,1024]{1,0:T(8,128)(2,1)S(1)}, bf16[32,1024]{1,0:T(8,128)(2,1)S(1)}, u32[]{:S(2)}, u32[]{:S(2)}) collective-permute-start(bf16[32,1024]{1,0:T(8,128)(2,1)S(1)} %fusion.11), channel_id=1, source_target_pairs={{0,16},{4,20},{8,24},{12,28},{16,0},{20,4},{24,8},{28,12},{1,17},{... | collective-permute-start | bytes 196616 | tf_op jit(solution)/shard_map/ppermute | solution.py:36
  169.5 0.7 bitcast_add_fusion.11
  170.2 2.5 %collective-permute-done.10 = bf16[32,1024]{1,0:T(8,128)(2,1)S(1)} collective-permute-done((bf16[32,1024]{1,0:T(8,128)(2,1)S(1)}, bf16[32,1024]{1,0:T(8,128)(2,1)S(1)}, u32[]{:S(2)}, u32[]{:S(2)}) %collective-permute-start.10) | collective-permute-done | bytes 65568 | tf_op jit(solution)/shard_map/ppermute | solution.py:36
  172.7 0.7 bitcast_add_fusion.10
  174.4 0.9 reshape.80
  (109 shorter events, 12.2 us)
Async XLA Ops:
  0.6 33.9 %collective-permute-start.2 = (bf16[512,1024]{1,0:T(8,128)(2,1)}, bf16[512,1024]{1,0:T(8,128)(2,1)S(1)}, u32[]{:S(2)}, u32[]{:S(2)}) collective-permute-start(bf16[512,1024]{1,0:T(8,128)(2,1)} %up_own.1), channel_id=1, source_target_pairs={{0,1},{1,0},{2,3},{3,2},{4,5},{5,4},{6,7},{7,6},{8,9},{9,8},{10,11... | collective-permute-start | bytes 3145736 | tf_op jit(solution)/shard_map/ppermute | solution.py:36
  1.2 33.4 %collective-permute-start.3 = (bf16[512,1024]{1,0:T(8,128)(2,1)}, bf16[512,1024]{1,0:T(8,128)(2,1)S(1)}, u32[]{:S(2)}, u32[]{:S(2)}) collective-permute-start(bf16[512,1024]{1,0:T(8,128)(2,1)} %down_own.1), channel_id=1, source_target_pairs={{0,1},{1,0},{2,3},{3,2},{4,5},{5,4},{6,7},{7,6},{8,9},{9,8},{10,11... | collective-permute-start | bytes 3145736 | tf_op jit(solution)/shard_map/ppermute | solution.py:36
  8.4 1.6 collective-permute-start
  10.0 0.7 copy-start.3
  12.4 12.6 %collective-permute-start.1 = (bf16[576,128]{1,0:T(8,128)(2,1)}, bf16[576,128]{1,0:T(8,128)(2,1)S(1)}, u32[]{:S(2)}, u32[]{:S(2)}) collective-permute-start(bf16[576,128]{1,0:T(8,128)(2,1)} %shard_map.188), channel_id=1, source_target_pairs={{0,2},{1,3},{4,6},{5,7},{8,10},{9,11},{12,14},{13,15},{16,18},{17,... | collective-permute-start | bytes 442376 | tf_op jit(solution)/shard_map/ppermute | solution.py:685
  25.0 0.7 copy-start.6
  34.5 1.0 copy-start.8
  34.5 1.3 copy-start.9
  60.0 17.8 %collective-permute-start.4 = (bf16[576,128]{1,0:T(8,128)(2,1)}, bf16[576,128]{1,0:T(8,128)(2,1)S(1)}, u32[]{:S(2)}, u32[]{:S(2)}) collective-permute-start(bf16[576,128]{1,0:T(8,128)(2,1)} %get-tuple-element.53.own_ref), channel_id=1, source_target_pairs={{0,1},{1,0},{2,3},{3,2},{4,5},{5,4},{6,7},{7,6},{8,9},{9,8},{10,11... | collective-permute-start | bytes 442376 | tf_op jit(solution)/shard_map/ppermute | solution.py:36
  77.8 0.7 copy-start.4
  80.2 8.3 %collective-permute-start.5 = (bf16[576,128]{1,0:T(8,128)(2,1)}, bf16[576,128]{1,0:T(8,128)(2,1)S(1)}, u32[]{:S(2)}, u32[]{:S(2)}) collective-permute-start(bf16[576,128]{1,0:T(8,128)(2,1)} %shard_map.193), channel_id=1, source_target_pairs={{2,0},{3,1},{6,4},{7,5},{10,8},{11,9},{14,12},{15,13},{18,16},{19,... | collective-permute-start | bytes 442376 | tf_op jit(solution)/shard_map/ppermute | solution.py:695
  88.5 0.7 copy-start.7
  89.2 12.1 %copy-start.5 = (bf16[512,512]{1,0:T(8,128)(2,1)S(1)}, bf16[512,512]{1,0:T(8,128)(2,1)}, u32[]{:S(2)}) copy-start(bf16[512,512]{1,0:T(8,128)(2,1)} %get-tuple-element.59) | copy-start | bytes 1572868
  100.4 27.9 %copy-start.1 = (bf16[512,1024]{1,0:T(8,128)(2,1)S(1)}, bf16[512,1024]{1,0:T(8,128)(2,1)}, u32[]{:S(2)}) copy-start(bf16[512,1024]{1,0:T(8,128)(2,1)} %get-tuple-element.60) | copy-start | bytes 3145732
  101.3 1.2 collective-permute-start.28
  101.4 2.8 %collective-permute-start.12 = (bf16[512,256]{1,0:T(8,128)(2,1)S(1)}, bf16[512,256]{1,0:T(8,128)(2,1)}, u32[]{:S(2)}, u32[]{:S(2)}) collective-permute-start(bf16[512,256]{1,0:T(8,128)(2,1)S(1)} %constant_dynamic-slice_fusion.12), channel_id=1, source_target_pairs={{0,1},{1,0},{2,3},{3,2},{4,5},{5,4},{6,7},{7,6},{8,9},{9,8},{10,11... | collective-permute-start | bytes 786440 | tf_op jit(solution)/shard_map/ppermute | solution.py:36
  101.9 26.4 %collective-permute-start.18 = (bf16[512,1024]{1,0:T(8,128)(2,1)}, bf16[512,1024]{1,0:T(8,128)(2,1)S(1)}, u32[]{:S(2)}, u32[]{:S(2)}) collective-permute-start(bf16[512,1024]{1,0:T(8,128)(2,1)} %get-tuple-element.61), channel_id=1, source_target_pairs={{0,1},{1,0},{2,3},{3,2},{4,5},{5,4},{6,7},{7,6},{8,9},{9,8},{10,11... | collective-permute-start | bytes 3145736 | tf_op jit(solution)/shard_map/ppermute | solution.py:36
  102.0 28.2 %collective-permute-start.23 = (bf16[512,1024]{1,0:T(8,128)(2,1)}, bf16[512,1024]{1,0:T(8,128)(2,1)S(1)}, u32[]{:S(2)}, u32[]{:S(2)}) collective-permute-start(bf16[512,1024]{1,0:T(8,128)(2,1)} %get-tuple-element.63), channel_id=1, source_target_pairs={{0,1},{1,0},{2,3},{3,2},{4,5},{5,4},{6,7},{7,6},{8,9},{9,8},{10,11... | collective-permute-start | bytes 3145736 | tf_op jit(solution)/shard_map/ppermute | solution.py:36
  102.6 3.7 %collective-permute-start.29 = (bf16[2,2,2,32,4]{3,2,1,0,4:T(2,128)(2,1)S(1)}, bf16[2,2,2,32,4]{3,2,1,0,4:T(2,128)(2,1)S(1)}, u32[]{:S(2)}, u32[]{:S(2)}) collective-permute-start(bf16[2,2,2,32,4]{3,2,1,0,4:T(2,128)(2,1)S(1)} %fusion.21), channel_id=1, source_target_pairs={{0,4},{4,0},{8,12},{12,8},{16,20},{20,16},{24,28},{28,24},{1,5},{5... | collective-permute-start | bytes 6152 | tf_op jit(solution)/shard_map/ppermute | solution.py:36
  106.4 3.7 %collective-permute-start.30 = (bf16[2,2,32,4]{2,1,0,3:T(2,128)(2,1)S(1)}, bf16[2,2,32,4]{2,1,0,3:T(2,128)(2,1)S(1)}, u32[]{:S(2)}, u32[]{:S(2)}) collective-permute-start(bf16[2,2,32,4]{2,1,0,3:T(2,128)(2,1)S(1)} %fusion.22), channel_id=1, source_target_pairs={{0,8},{4,12},{8,0},{12,4},{16,24},{20,28},{24,16},{28,20},{1,9},{5... | collective-permute-start | bytes 3080 | tf_op jit(solution)/shard_map/ppermute | solution.py:36
  108.1 5.0 %collective-permute-start.13 = (bf16[2,2,2,32,256]{4,3,0,1,2:T(8,128)(2,1)S(1)}, bf16[2,2,2,32,256]{4,3,0,1,2:T(8,128)(2,1)S(1)}, u32[]{:S(2)}, u32[]{:S(2)}) collective-permute-start(bf16[2,2,2,32,256]{4,3,0,1,2:T(8,128)(2,1)S(1)} %fusion.9), channel_id=1, source_target_pairs={{0,8},{4,12},{8,0},{12,4},{16,24},{20,28},{24,16},{28,20},{1,9},{5... | collective-permute-start | bytes 393224 | tf_op jit(solution)/shard_map/ppermute | solution.py:36
  108.6 22.2 %collective-permute-start.6 = (bf16[512,1024]{1,0:T(8,128)(2,1)}, bf16[512,1024]{1,0:T(8,128)(2,1)S(1)}, u32[]{:S(2)}, u32[]{:S(2)}) collective-permute-start(bf16[512,1024]{1,0:T(8,128)(2,1)} %get-tuple-element.58), channel_id=1, source_target_pairs={{0,1},{1,0},{2,3},{3,2},{4,5},{5,4},{6,7},{7,6},{8,9},{9,8},{10,11... | collective-permute-start | bytes 3145736 | tf_op jit(solution)/shard_map/ppermute | solution.py:36
  110.1 3.7 %collective-permute-start.31 = (bf16[2,32,4]{1,2,0:T(4,128)(2,1)S(1)}, bf16[2,32,4]{1,2,0:T(4,128)(2,1)S(1)}, u32[]{:S(2)}, u32[]{:S(2)}) collective-permute-start(bf16[2,32,4]{1,2,0:T(4,128)(2,1)S(1)} %bitcast.134), channel_id=1, source_target_pairs={{0,2},{2,0},{1,3},{3,1},{4,6},{6,4},{5,7},{7,5},{8,10},{10,8},{9,1... | collective-permute-start | bytes 1544 | tf_op jit(solution)/shard_map/ppermute | solution.py:36
  113.2 4.3 %collective-permute-start.14 = (bf16[2,2,32,256]{3,2,0,1:T(8,128)(2,1)S(1)}, bf16[2,2,32,256]{3,2,0,1:T(8,128)(2,1)S(1)}, u32[]{:S(2)}, u32[]{:S(2)}) collective-permute-start(bf16[2,2,32,256]{3,2,0,1:T(8,128)(2,1)S(1)} %fusion.12), channel_id=1, source_target_pairs={{0,2},{2,0},{1,3},{3,1},{4,6},{6,4},{5,7},{7,5},{8,10},{10,8},{9,1... | collective-permute-start | bytes 196616 | tf_op jit(solution)/shard_map/ppermute | solution.py:36
  117.5 4.2 %collective-permute-start.15 = (bf16[2,32,256]{2,1,0:T(8,128)(2,1)S(1)}, bf16[2,32,256]{2,1,0:T(8,128)(2,1)S(1)}, u32[]{:S(2)}, u32[]{:S(2)}) collective-permute-start(bf16[2,32,256]{2,1,0:T(8,128)(2,1)S(1)} %fusion.15), channel_id=1, source_target_pairs={{0,4},{4,0},{8,12},{12,8},{16,20},{20,16},{24,28},{28,24},{1,5},{5... | collective-permute-start | bytes 98312 | tf_op jit(solution)/shard_map/ppermute | solution.py:36
  119.1 5.1 %collective-permute-start.32 = (bf16[32,4]{0,1:T(4,128)(2,1)S(1)}, bf16[32,4]{0,1:T(4,128)(2,1)S(1)}, u32[]{:S(2)}, u32[]{:S(2)}) collective-permute-start(bf16[32,4]{0,1:T(4,128)(2,1)S(1)} %fusion.27), channel_id=1, source_target_pairs={{0,16},{4,20},{8,24},{12,28},{16,0},{20,4},{24,8},{28,12},{1,17},{... | collective-permute-start | bytes 776 | tf_op jit(solution)/shard_map/ppermute | solution.py:36
  121.7 4.8 %collective-permute-start.16 = (bf16[32,256]{1,0:T(8,128)(2,1)S(1)}, bf16[32,256]{1,0:T(8,128)(2,1)S(1)}, u32[]{:S(2)}, u32[]{:S(2)}) collective-permute-start(bf16[32,256]{1,0:T(8,128)(2,1)S(1)} %fusion.17), channel_id=1, source_target_pairs={{0,16},{4,20},{8,24},{12,28},{16,0},{20,4},{24,8},{28,12},{1,17},{... | collective-permute-start | bytes 49160 | tf_op jit(solution)/shard_map/ppermute | solution.py:36
  126.5 1.2 collective-permute-start.17
  128.3 1.9 %copy-start = (bf16[512,1024]{1,0:T(8,128)(2,1)S(1)}, bf16[512,1024]{1,0:T(8,128)(2,1)}, u32[]{:S(2)}) copy-start(bf16[512,1024]{1,0:T(8,128)(2,1)} %get-tuple-element.62) | copy-start | bytes 3145732
  128.8 14.1 %collective-permute-start.19 = (bf16[2,2,2,32,1024]{4,3,0,2,1:T(8,128)(2,1)S(1)}, bf16[2,2,2,32,1024]{4,3,0,2,1:T(8,128)(2,1)S(1)}, u32[]{:S(2)}, u32[]{:S(2)}) collective-permute-start(bf16[2,2,2,32,1024]{4,3,0,2,1:T(8,128)(2,1)S(1)} %fusion.1), channel_id=1, source_target_pairs={{0,4},{4,0},{8,12},{12,8},{16,20},{20,16},{24,28},{28,24},{1,5},{5... | collective-permute-start | bytes 1572872 | tf_op jit(solution)/shard_map/ppermute | solution.py:36
  130.2 1.2 copy-start.2
  130.7 13.8 %collective-permute-start.24 = (bf16[2,2,2,32,1024]{4,3,0,1,2:T(8,128)(2,1)S(1)}, bf16[2,2,2,32,1024]{4,3,0,1,2:T(8,128)(2,1)S(1)}, u32[]{:S(2)}, u32[]{:S(2)}) collective-permute-start(bf16[2,2,2,32,1024]{4,3,0,1,2:T(8,128)(2,1)S(1)} %fusion.2), channel_id=1, source_target_pairs={{0,2},{2,0},{1,3},{3,1},{4,6},{6,4},{5,7},{7,5},{8,10},{10,8},{9,1... | collective-permute-start | bytes 1572872 | tf_op jit(solution)/shard_map/ppermute | solution.py:36
  131.9 21.2 %collective-permute-start.7 = (bf16[2,2,2,32,1024]{4,3,2,1,0:T(8,128)(2,1)S(1)}, bf16[2,2,2,32,1024]{4,3,2,1,0:T(8,128)(2,1)S(1)}, u32[]{:S(2)}, u32[]{:S(2)}) collective-permute-start(bf16[2,2,2,32,1024]{4,3,2,1,0:T(8,128)(2,1)S(1)} %fusion), channel_id=1, source_target_pairs={{0,8},{4,12},{8,0},{12,4},{16,24},{20,28},{24,16},{28,20},{1,9},{5... | collective-permute-start | bytes 1572872 | tf_op jit(solution)/shard_map/ppermute | solution.py:36
  143.1 8.2 %collective-permute-start.20 = (bf16[2,2,32,1024]{3,2,0,1:T(8,128)(2,1)S(1)}, bf16[2,2,32,1024]{3,2,0,1:T(8,128)(2,1)S(1)}, u32[]{:S(2)}, u32[]{:S(2)}) collective-permute-start(bf16[2,2,32,1024]{3,2,0,1:T(8,128)(2,1)S(1)} %fusion.4), channel_id=1, source_target_pairs={{0,8},{4,12},{8,0},{12,4},{16,24},{20,28},{24,16},{28,20},{1,9},{5... | collective-permute-start | bytes 786440 | tf_op jit(solution)/shard_map/ppermute | solution.py:36
  144.7 7.8 %collective-permute-start.25 = (bf16[2,2,32,1024]{3,2,0,1:T(8,128)(2,1)S(1)}, bf16[2,2,32,1024]{3,2,0,1:T(8,128)(2,1)S(1)}, u32[]{:S(2)}, u32[]{:S(2)}) collective-permute-start(bf16[2,2,32,1024]{3,2,0,1:T(8,128)(2,1)S(1)} %fusion.5), channel_id=1, source_target_pairs={{0,4},{4,0},{8,12},{12,8},{16,20},{20,16},{24,28},{28,24},{1,5},{5... | collective-permute-start | bytes 786440 | tf_op jit(solution)/shard_map/ppermute | solution.py:36
  151.4 6.5 %collective-permute-start.21 = (bf16[2,32,1024]{2,1,0:T(8,128)(2,1)S(1)}, bf16[2,32,1024]{2,1,0:T(8,128)(2,1)S(1)}, u32[]{:S(2)}, u32[]{:S(2)}) collective-permute-start(bf16[2,32,1024]{2,1,0:T(8,128)(2,1)S(1)} %fusion.7), channel_id=1, source_target_pairs={{0,2},{2,0},{1,3},{3,1},{4,6},{6,4},{5,7},{7,5},{8,10},{10,8},{9,1... | collective-permute-start | bytes 393224 | tf_op jit(solution)/shard_map/ppermute | solution.py:36
  152.7 10.1 %collective-permute-start.26 = (bf16[2,32,1024]{2,1,0:T(8,128)(2,1)S(1)}, bf16[2,32,1024]{2,1,0:T(8,128)(2,1)S(1)}, u32[]{:S(2)}, u32[]{:S(2)}) collective-permute-start(bf16[2,32,1024]{2,1,0:T(8,128)(2,1)S(1)} %fusion.8), channel_id=1, source_target_pairs={{0,8},{4,12},{8,0},{12,4},{16,24},{20,28},{24,16},{28,20},{1,9},{5... | collective-permute-start | bytes 393224 | tf_op jit(solution)/shard_map/ppermute | solution.py:36
  153.3 8.2 %collective-permute-start.8 = (bf16[2,2,32,1024]{3,2,1,0:T(8,128)(2,1)S(1)}, bf16[2,2,32,1024]{3,2,1,0:T(8,128)(2,1)S(1)}, u32[]{:S(2)}, u32[]{:S(2)}) collective-permute-start(bf16[2,2,32,1024]{3,2,1,0:T(8,128)(2,1)S(1)} %fusion.3), channel_id=1, source_target_pairs={{0,2},{2,0},{1,3},{3,1},{4,6},{6,4},{5,7},{7,5},{8,10},{10,8},{9,1... | collective-permute-start | bytes 786440 | tf_op jit(solution)/shard_map/ppermute | solution.py:36
  158.0 11.5 %collective-permute-start.22 = (bf16[32,1024]{1,0:T(8,128)(2,1)S(1)}, bf16[32,1024]{1,0:T(8,128)(2,1)S(1)}, u32[]{:S(2)}, u32[]{:S(2)}) collective-permute-start(bf16[32,1024]{1,0:T(8,128)(2,1)S(1)} %fusion.13), channel_id=1, source_target_pairs={{0,16},{4,20},{8,24},{12,28},{16,0},{20,4},{24,8},{28,12},{1,17},{... | collective-permute-start | bytes 196616 | tf_op jit(solution)/shard_map/ppermute | solution.py:36
  161.6 5.0 %collective-permute-start.9 = (bf16[2,32,1024]{2,1,0:T(8,128)(2,1)S(1)}, bf16[2,32,1024]{2,1,0:T(8,128)(2,1)S(1)}, u32[]{:S(2)}, u32[]{:S(2)}) collective-permute-start(bf16[2,32,1024]{2,1,0:T(8,128)(2,1)S(1)} %fusion.6), channel_id=1, source_target_pairs={{0,4},{4,0},{8,12},{12,8},{16,20},{20,16},{24,28},{28,24},{1,5},{5... | collective-permute-start | bytes 393224 | tf_op jit(solution)/shard_map/ppermute | solution.py:36
  162.8 9.9 %collective-permute-start.27 = (bf16[32,1024]{1,0:T(8,128)(2,1)S(1)}, bf16[32,1024]{1,0:T(8,128)(2,1)S(1)}, u32[]{:S(2)}, u32[]{:S(2)}) collective-permute-start(bf16[32,1024]{1,0:T(8,128)(2,1)S(1)} %fusion.14), channel_id=1, source_target_pairs={{0,16},{4,20},{8,24},{12,28},{16,0},{20,4},{24,8},{28,12},{1,17},{... | collective-permute-start | bytes 196616 | tf_op jit(solution)/shard_map/ppermute | solution.py:36
  166.7 5.9 %collective-permute-start.10 = (bf16[32,1024]{1,0:T(8,128)(2,1)S(1)}, bf16[32,1024]{1,0:T(8,128)(2,1)S(1)}, u32[]{:S(2)}, u32[]{:S(2)}) collective-permute-start(bf16[32,1024]{1,0:T(8,128)(2,1)S(1)} %fusion.11), channel_id=1, source_target_pairs={{0,16},{4,20},{8,24},{12,28},{16,0},{20,4},{24,8},{28,12},{1,17},{... | collective-permute-start | bytes 196616 | tf_op jit(solution)/shard_map/ppermute | solution.py:36
  172.7 1.3 collective-permute-start.11
where the time goes:
time: 176 us; the launch traced here: 175 us
  Pallas kernels  80.2 us (46%)
  waiting for transfers between devices  45.8 us (26%)
  starting transfers between devices  34.2 us (19%)
  local copies, waits for them, and re-layouts  8.5 us (5%)
  other arithmetic  5.31 us (3%)
    ppermute x31, waiting for transfers between devices, swap(): return lax.ppermute(a, axis, [(i, i ^ bit) for i in range(size)])  39.7 us
    ppermute x31, starting transfers between devices, swap(): return lax.ppermute(a, axis, [(i, i ^ bit) for i in range(size)])  28 us
    pallas_call x1, Pallas kernels, heads_back(): call(heads_back_body, (HEADS,), [SMEM, HEAD_BLOCK(4 * HEAD, length), row,...  17.8 us
    pallas_call x1, Pallas kernels, feed(): call(feed_body, (4,), [square, square, square, square, row, row, own, oth...  15.2 us
    pallas_call x1, Pallas kernels, project_back(): call(project_back_body, (4,), [SMEM, two, two, pl.BlockSpec((128, length)...  11.2 us
    pallas_call x1, Pallas kernels, scores_back(): call(scores_back_body, (HEADS,), [SMEM, HEAD_BLOCK(4 * HEAD, length), row...  8.91 us
    pallas_call x1, Pallas kernels, mix(): call(mix_body, (HEADS,), [SMEM, HEAD_BLOCK(4 * HEAD, length), ROW_BLOCK(l...  8.85 us
    pallas_call x1, Pallas kernels, local_sums(): call(local_body, (HEADS,), [SMEM, HEAD_BLOCK(4 * HEAD, length)], [ROW_BLO...  7.7 us
  transfers between devices with their start and end apart: 33, of which 18 were waited for; matrix products, arithmetic and copies ran while one was open for 4% of the time, Pallas kernels for 25%

commit v1 on v0

v1 whole, which is shorter than its diff:
```python
import functools

import jax
import jax.numpy as jnp
from jax import lax
from jax.experimental import pallas as pl
from jax.experimental.pallas import tpu as pltpu
from jax.sharding import PartitionSpec as P

HEADS = 8
HEAD = 64
EPSILON = 1e-05
BF = jnp.bfloat16
F32 = jnp.float32
GELU_A = 0.7978845608028654
GELU_B = 0.044715
SCALE = HEAD**-0.5
PACK = HEADS * HEAD + 64


def nn(a, b):
    return lax.dot_general(a, b, (((1,), (0,)), ((), ())), preferred_element_type=F32)


def nt(a, b):
    return lax.dot_general(a, b, (((1,), (1,)), ((), ())), preferred_element_type=F32)


def tn(a, b):
    return lax.dot_general(a, b, (((0,), (0,)), ((), ())), preferred_element_type=F32)


def swap(a, axis, bit):
    size = lax.axis_size(axis)
    return lax.ppermute(a, axis, [(i, i ^ bit) for i in range(size)])


ANY = pl.BlockSpec(memory_space=pl.ANY)


def call(body, grid, in_specs, out_specs, out_shape, scratch=(), us=1.0, after=(), vmem=32):
    count = len(in_specs)

    def run(*refs):
        body(*refs[:count], *refs[count + len(after) :])

    def start(*operands):
        return pl.pallas_call(
            run,
            grid=grid,
            in_specs=list(in_specs) + [ANY] * len(after),
            out_specs=out_specs,
            out_shape=out_shape,
            scratch_shapes=list(scratch),
            cost_estimate=pl.CostEstimate(flops=int(us * 1.15e9), bytes_accessed=2**20, transcendentals=0),
            compiler_params=pltpu.CompilerParams(vmem_limit_bytes=vmem * 2**20),
        )(*operands, *after)

    return start


def whole(shape):
    return pl.BlockSpec(shape, lambda *_: (0,) * len(shape))


SMEM = pl.BlockSpec(memory_space=pltpu.SMEM)


def shard_of():
    return lax.axis_index("seq") * 2 + lax.axis_index("ffn")


def doc_begin_row(starts_ref, length):
    begin = shard_of() * length
    place = lax.broadcasted_iota(jnp.int32, (1, length), 1)
    row = jnp.full((1, length), -(2**30), jnp.int32)
    for j in range(starts_ref.shape[1]):
        s = starts_ref[0, j] - begin
        row = jnp.where(place >= s, jnp.maximum(row, s), row)
    return row


def passes(starts_ref, which, length):
    hit = jnp.int32(0)
    for j in range(starts_ref.shape[1]):
        s = starts_ref[0, j]
        hit = hit | ((s >= which * length) & (s < which * length + length)).astype(jnp.int32)
    return 1.0 - hit.astype(F32)


def visible(doc_row, length):
    i = lax.broadcasted_iota(jnp.int32, (length, length), 0)
    t = lax.broadcasted_iota(jnp.int32, (length, length), 1)
    return jnp.where((i <= t) & (i >= doc_row), 1.0, 0.0).astype(BF)


def tail_row(doc_row, length):
    place = lax.broadcasted_iota(jnp.int32, (1, length), 1)
    last = doc_row[:, length - 1 :]
    return jnp.where(place >= last, 1.0, 0.0)


def pack_totals(pack_ref, totals8):
    base = HEADS * HEAD
    hi = totals8.astype(BF)
    lo = (totals8 - hi.astype(F32)).astype(BF)
    for a in range(4):
        cols = slice(128 * a, 128 * a + 128)
        pack_ref[base + 16 * a : base + 16 * a + 16, :] = jnp.concatenate(
            [hi[:, cols], lo[:, cols]], axis=0
        )


def unpack(rows, totals8_of):
    base = HEADS * HEAD
    out = []
    for a in range(4):
        block = totals8_of(slice(base + 16 * a, base + 16 * a + 16))
        out.append(block[:8] + block[8:])
    return rows(slice(0, base)), jnp.concatenate(out, axis=1)


def combine_body(backward, length, starts_ref, own_ref, partner_ref, out_ref):
    first = 2 * lax.axis_index("seq")
    is_first = (lax.axis_index("ffn") == 0).astype(F32)
    base = HEADS * HEAD
    if backward:
        p = passes(starts_ref, first, length)
        own_by, partner_by = is_first + (1 - is_first) * p, is_first * p + (1 - is_first)
    else:
        p = passes(starts_ref, first + 1, length)
        own_by, partner_by = is_first * p + (1 - is_first), is_first + (1 - is_first) * p

    def sum_of(at):
        return own_ref[at, :].astype(F32) * own_by + partner_ref[at, :].astype(F32) * partner_by

    memory, totals8 = unpack(sum_of, sum_of)
    out_ref[:base, :] = memory.astype(BF)
    pack_totals(out_ref, totals8)


def combine(backward, length, starts, own, partner, after=()):
    return call(
        functools.partial(combine_body, backward, length),
        (),
        [SMEM, whole((PACK, 128)), whole((PACK, 128))],
        whole((PACK, 128)),
        jax.ShapeDtypeStruct((PACK, 128), BF),
        after=after,
    )(starts, own, partner)


def arrived(backward, length, starts_ref, partner_ref, far_ref, mem_ref, totals_ref):
    first = 2 * lax.axis_index("seq")
    is_first = (lax.axis_index("ffn") == 0).astype(F32)
    if backward:
        p = passes(starts_ref, first + 1, length)
        far_by, partner_by = is_first * p + (1 - is_first), is_first
    else:
        p = passes(starts_ref, first, length)
        far_by, partner_by = is_first + (1 - is_first) * p, 1 - is_first

    def sum_of(at):
        return far_ref[at, :].astype(F32) * far_by + partner_ref[at, :].astype(F32) * partner_by

    memory, totals8 = unpack(sum_of, sum_of)
    mem_ref[...] = memory.astype(BF)
    totals_ref[...] = totals8.T


def project_body(x_hbm, gain_hbm, bias_hbm, w_hbm, starts_ref,
                 heads_ref, control_ref, xnt_ref, pack_ref,
                 x_ref, gain_ref, bias_ref, w_ref, sems):
    length, width = x_ref.shape
    copies = [
        pltpu.make_async_copy(x_hbm, x_ref, sems.at[0]),
        pltpu.make_async_copy(gain_hbm, gain_ref, sems.at[1]),
        pltpu.make_async_copy(bias_hbm, bias_ref, sems.at[2]),
    ]
    columns = [
        pltpu.make_async_copy(w_hbm.at[:, pl.ds(j * width, width)], w_ref.at[j], sems.at[3 + j])
        for j in range(4)
    ]
    for copy in copies + columns:
        copy.start()
    for copy in copies:
        copy.wait()
    x = x_ref[...].astype(F32)
    mean = jnp.mean(x, axis=-1, keepdims=True)
    centered = x - mean
    inverse = lax.rsqrt(jnp.mean(centered * centered, axis=-1, keepdims=True) + EPSILON)
    xn = (centered * inverse * gain_ref[...] + bias_ref[...]).astype(BF)
    xnt_ref[...] = xn.T
    for j in range(3):
        columns[j].wait()
        t = nn(xn, w_ref[j]).astype(BF).T
        for h in range(HEADS):
            heads_ref[h, j * HEAD : j * HEAD + HEAD, :] = t[h * HEAD : h * HEAD + HEAD]
    columns[3].wait()
    control = jnp.exp(nn(xn, w_ref[3])).T
    control_ref[...] = control
    c = control.astype(BF)
    tail = tail_row(doc_begin_row(starts_ref, length), length)
    c_tail = c * tail.astype(BF)
    for h in range(HEADS):
        rows = slice(h * HEAD, h * HEAD + HEAD)
        heads_ref[h, 3 * HEAD :, :] = c[rows]
        mem_k = nt(c_tail[rows], heads_ref[h, HEAD : 2 * HEAD, :])
        mem_vt = nt(heads_ref[h, 2 * HEAD : 3 * HEAD, :], c_tail[rows])
        pack_ref[rows, :] = jnp.concatenate([mem_k, mem_vt], axis=1).astype(BF)
    tail8 = jnp.broadcast_to(tail, (8, length)).astype(BF)
    pack_totals(pack_ref, nt(tail8, c))


def project(x, gain, bias, w, starts):
    length, width = x.shape
    hbm = pl.BlockSpec(memory_space=pltpu.MemorySpace.HBM)
    return call(
        project_body,
        (),
        [hbm, hbm, hbm, hbm, SMEM],
        [
            whole((HEADS, 4 * HEAD, length)), whole((width, length)), whole((width, length)),
            whole((PACK, 128)),
        ],
        [
            jax.ShapeDtypeStruct((HEADS, 4 * HEAD, length), BF),
            jax.ShapeDtypeStruct((width, length), F32),
            jax.ShapeDtypeStruct((width, length), BF),
            jax.ShapeDtypeStruct((PACK, 128), BF),
        ],
        [
            pltpu.VMEM((length, width), BF), pltpu.VMEM((1, width), F32), pltpu.VMEM((1, width), F32),
            pltpu.VMEM((4, width, width), BF), pltpu.SemaphoreType.DMA((7,)),
        ],
        us=4.3,
        vmem=57,
    )(x, gain, bias, w, starts)


HEAD_BLOCK = lambda rows, length: pl.BlockSpec((1, rows, length), lambda h: (h, 0, 0))
ROW_BLOCK = lambda length: pl.BlockSpec((HEAD, length), lambda h: (h, 0))


def causal_pairs(left, right, mask_ref):
    half = mask_ref.shape[0] // 2
    rows = left.T
    a = nn(rows[:half], right[:, :half]).astype(BF) * mask_ref[:half, :half]
    b = nn(rows, right[:, half:]).astype(BF) * mask_ref[:, half:]
    return a, b


def causal_sum(left, pairs):
    a, b = pairs
    half = a.shape[0]
    return jnp.concatenate([nn(left[:, :half], a), nn(left, b)], axis=1)


def causal_back(left, pairs):
    a, b = pairs
    half = a.shape[0]
    late = nt(left[:, half:], b)
    return jnp.concatenate([late[:, :half] + nt(left[:, :half], a), late[:, half:]], axis=1)


def mask_pair(mask_ref):
    half = mask_ref.shape[0] // 2
    return mask_ref[:half, :half], mask_ref[:, half:]


def parts(heads_ref):
    return [heads_ref[0, j * HEAD : j * HEAD + HEAD, :] for j in range(4)]


def local_body(starts_ref, heads_ref, number_ref, total_ref, mask_ref):
    length = heads_ref.shape[2]

    @pl.when(pl.program_id(0) == 0)
    def _():
        mask_ref[...] = visible(doc_begin_row(starts_ref, length), length)

    q, k, v, c = parts(heads_ref)
    number_ref[...] = causal_sum(c, causal_pairs(k, q, mask_ref))
    total_ref[...] = causal_sum(c, mask_pair(mask_ref))


def local_sums(starts, heads, begin, count, after=()):
    length = heads.shape[2]
    return call(
        local_body,
        (count,),
        [SMEM, pl.BlockSpec((1, 4 * HEAD, length), lambda h: (h + begin, 0, 0))],
        [ROW_BLOCK(length)] * 2,
        [jax.ShapeDtypeStruct((count * HEAD, length), F32)] * 2,
        [pltpu.VMEM((length, length), BF)],
        us=0.75 * count,
        after=after,
    )(starts, heads)


def enters_row(starts_ref, length):
    return jnp.where(doc_begin_row(starts_ref, length) < 0, 1.0, 0.0)


def softmax(number, inverse):
    score = number * (inverse * SCALE)
    e = jnp.exp(score - jnp.max(score, axis=0, keepdims=True))
    return e / jnp.sum(e, axis=0, keepdims=True)


def mix_body(starts_ref, heads_ref, number_a, number_b, total_a, total_b, partner_ref, far_ref,
             number_out, total_out, mixed_ref, mem_out, mask_ref, mem_ref, totals_ref):
    length = heads_ref.shape[2]
    h = pl.program_id(0)

    @pl.when(h == 0)
    def _():
        mask_ref[...] = visible(doc_begin_row(starts_ref, length), length)
        arrived(False, length, starts_ref, partner_ref, far_ref, mem_ref, totals_ref)
        mem_out[...] = mem_ref[...]

    enters = enters_row(starts_ref, length)
    rows = pl.ds(pl.multiple_of(h * HEAD, HEAD), HEAD)
    q, k, v, c = parts(heads_ref)
    mem = mem_ref[rows, :]
    mem_k, mem_vt = mem[:, :HEAD], mem[:, HEAD:]
    early = h < HEADS // 2
    number = jnp.where(early, number_a[...], number_b[...]) + enters * nn(mem_k, q)
    total = jnp.where(early, total_a[...], total_b[...]) + enters * totals_ref[rows, 0:1]
    number_out[...] = number
    total_out[...] = total
    inverse = 1.0 / total
    spread = (softmax(number, inverse) * inverse).astype(BF)
    links = causal_pairs(c, spread, mask_ref)
    mixed = causal_sum(v, links) + enters * nn(mem_vt, spread)
    mixed_ref[...] = mixed.astype(BF)


def mix(starts, heads, number_a, total_a, number_b, total_b, partner, far):
    length = heads.shape[2]
    width = HEADS * HEAD
    a = pl.BlockSpec((HEAD, length), lambda h: (jnp.minimum(h, HEADS // 2 - 1), 0))
    b = pl.BlockSpec((HEAD, length), lambda h: (jnp.maximum(h - HEADS // 2, 0), 0))
    return call(
        mix_body,
        (HEADS,),
        [SMEM, HEAD_BLOCK(4 * HEAD, length), a, b, a, b,
         whole((PACK, 128)), whole((PACK, 128))],
        [ROW_BLOCK(length), ROW_BLOCK(length), ROW_BLOCK(length), whole((width, 128))],
        [
            jax.ShapeDtypeStruct((width, length), F32),
            jax.ShapeDtypeStruct((width, length), F32),
            jax.ShapeDtypeStruct((width, length), BF),
            jax.ShapeDtypeStruct((width, 128), BF),
        ],
        [pltpu.VMEM((length, length), BF), pltpu.VMEM((width, 128), BF), pltpu.VMEM((width, 8), F32)],
        us=6.0,
    )(starts, heads, number_a, number_b, total_a, total_b, partner, far)


def feed_step(xn_ref, cot_ref, xnt_ref, cott_ref, up_ref, down_ref, gup_ref, gdown_ref):
    up, down = up_ref[...], down_ref[...]
    pre = nn(xn_ref[...], up)
    v2 = pre * pre
    th = jnp.tanh(GELU_A * pre * (1.0 + GELU_B * v2))
    half = 0.5 * (1.0 + th)
    hidden = (pre * half).astype(BF)
    slope = half + 0.5 * pre * (1.0 - th * th) * (GELU_A * (1.0 + 3.0 * GELU_B * v2))
    grad_pre = (nn(cot_ref[...], down) * slope).astype(BF)
    gdown_ref[...] = nn(cott_ref[...], hidden).astype(BF)
    gup_ref[...] = nn(xnt_ref[...], grad_pre).astype(BF)
    return nt(hidden, down), nt(grad_pre, up)


def feed_other_body(x_ref, mixed_ref, cot_ref, w_out_ref, gain_ref, bias_ref, up_ref, down_ref,
                    gup_ref, gdown_ref, hidden1_ref, n_ref, inv_ref, xn_ref, xnt_ref, cott_ref,
                    part_ref, d_ref):
    j = pl.program_id(0)

    @pl.when(j == 0)
    def _():
        hidden1 = x_ref[...].astype(F32) + tn(mixed_ref[...], w_out_ref[...])
        hidden1_ref[...] = hidden1
        mean = jnp.mean(hidden1, axis=-1, keepdims=True)
        centered = hidden1 - mean
        inverse = lax.rsqrt(jnp.mean(centered * centered, axis=-1, keepdims=True) + EPSILON)
        n = centered * inverse
        n_ref[...] = n
        inv_ref[...] = jnp.broadcast_to(inverse, inv_ref.shape)
        xn = (n * gain_ref[...] + bias_ref[...]).astype(BF)
        xn_ref[...] = xn
        xnt_ref[...] = xn.T
        cott_ref[...] = cot_ref[...].T

    part, d = feed_step(xn_ref, cot_ref, xnt_ref, cott_ref, up_ref, down_ref, gup_ref, gdown_ref)

    @pl.when(j == 0)
    def _():
        part_ref[...] = part
        d_ref[...] = d

    @pl.when(j > 0)
    def _():
        part_ref[...] += part
        d_ref[...] += d


def feed_own_body(hidden1_ref, n_ref, inv_ref, xn_ref, xnt_ref, cott_ref, part_ref, d_in_ref,
                  mixed_ref, cot_ref, w_out_ref, gain_ref, up_ref, down_ref,
                  output_ref, d_hidden1_ref, g_ref, out_send_ref, out_keep_ref, norms_ref,
                  gup_ref, gdown_ref, sum_ref, d_ref):
    j = pl.program_id(0)
    part, d = feed_step(xn_ref, cot_ref, xnt_ref, cott_ref, up_ref, down_ref, gup_ref, gdown_ref)

    @pl.when(j == 0)
    def _():
        sum_ref[...] = part_ref[...] + part
        d_ref[...] = d_in_ref[...] + d

    @pl.when(j == 1)
    def _():
        output_ref[...] = (hidden1_ref[...] + (sum_ref[...] + part)).astype(BF)
        dx, n = d_ref[...] + d, n_ref[...]
        norms_ref[...] = jnp.concatenate(
            [jnp.sum(dx * n, axis=0, keepdims=True), jnp.sum(dx, axis=0, keepdims=True)] * 4, axis=0
        )
        d_n = dx * gain_ref[...]
        d_in = (
            d_n
            - jnp.mean(d_n, axis=-1, keepdims=True)
            - n * jnp.mean(d_n * n, axis=-1, keepdims=True)
        ) * inv_ref[:, 0:1]
        d_hidden1 = cot_ref[...].astype(F32) + d_in
        d_hidden1_ref[...] = d_hidden1
        d_branch = d_hidden1.astype(BF)
        grad_out = nn(mixed_ref[...], d_branch).astype(BF)
        half = grad_out.shape[1] // 2
        second = lax.axis_index("ffn") == 1
        out_keep_ref[...] = jnp.where(second, grad_out[:, half:], grad_out[:, :half])
        out_send_ref[...] = jnp.where(second, grad_out[:, :half], grad_out[:, half:])
        g_ref[...] = nt(w_out_ref[...], d_branch).astype(BF)


FEED_COLS = pl.BlockSpec((512, 512), lambda j: (0, j))


def feed_other(x, mixed, cotangent, w_out, gain, bias, up, down):
    length, width = x.shape
    square, row = whole((length, width)), whole((1, width))
    sq = lambda dt: jax.ShapeDtypeStruct((length, width), dt)
    half = jax.ShapeDtypeStruct(up.shape, BF)
    return call(
        feed_other_body,
        (2,),
        [square] * 4 + [row, row, FEED_COLS, FEED_COLS],
        [FEED_COLS, FEED_COLS, square, square, whole((length, 128))] + [square] * 5,
        [half, half, sq(F32), sq(F32), jax.ShapeDtypeStruct((length, 128), F32),
         sq(BF), sq(BF), sq(BF), sq(F32), sq(F32)],
        us=6.5,
    )(x, mixed, cotangent, w_out, gain, bias, up, down)


def feed_own(saved, mixed, cotangent, w_out, gain, up, down, after=()):
    length, width = mixed.shape
    square, row = whole((length, width)), whole((1, width))
    sq = lambda dt: jax.ShapeDtypeStruct((length, width), dt)
    half = jax.ShapeDtypeStruct(up.shape, BF)
    narrow = whole((width, width // 2))
    return call(
        feed_own_body,
        (2,),
        [square, square, whole((length, 128))] + [square] * 5
        + [square] * 3 + [row, FEED_COLS, FEED_COLS],
        [square] * 3 + [narrow, narrow, whole((8, width)), FEED_COLS, FEED_COLS],
        [sq(BF), sq(F32), sq(BF)] + [jax.ShapeDtypeStruct((width, width // 2), BF)] * 2
        + [jax.ShapeDtypeStruct((8, width), F32), half, half],
        [pltpu.VMEM((length, width), F32)] * 2,
        us=6.5,
        after=after,
    )(*saved, mixed, cotangent, w_out, gain, up, down)


def head_of(own_side, h):
    ffn = lax.axis_index("ffn")
    return (ffn if own_side else 1 - ffn) * (HEADS // 2) + h


def scores_back_body(own_side, starts_ref, heads_ref, g_ref, number_ref, total_ref, mem_ref, *refs):
    if own_side:
        pack_in, sums_in, a_ref, spread_ref, d_total_ref, pack_ref, mask_ref, sums_ref = refs
    else:
        a_ref, spread_ref, d_total_ref, pack_ref, sums_ref, mask_ref = refs
    length = heads_ref.shape[2]
    h = pl.program_id(0)

    @pl.when(h == 0)
    def _():
        mask_ref[...] = visible(doc_begin_row(starts_ref, length), length)
        if own_side:
            pack_ref[...] = pack_in[...]
            sums_ref[...] = sums_in[...]

    enters = enters_row(starts_ref, length)
    rows = pl.ds(pl.multiple_of(head_of(own_side, h) * HEAD, HEAD), HEAD)
    q, k, v, c = parts(heads_ref)
    g = g_ref[...]
    mem_vt = mem_ref[:, HEAD:]
    number, inverse = number_ref[...], 1.0 / total_ref[...]
    weight = softmax(number, inverse)
    number_v = causal_sum(c, causal_pairs(v, g, mask_ref)) + enters * tn(mem_vt, g)
    d_weight = number_v * inverse
    d_score = weight * (d_weight - jnp.sum(weight * d_weight, axis=0, keepdims=True))
    a = d_score * (inverse * SCALE)
    spread = weight * inverse
    d_total = -(a * number + spread * number_v) * inverse
    a_ref[...] = a.astype(BF)
    spread_ref[...] = spread.astype(BF)
    d_total_ref[...] = d_total.astype(BF)
    d_k = nt((a * enters).astype(BF), q)
    d_vt = nt(g, (spread * enters).astype(BF))
    pack_ref[rows, :] = jnp.concatenate([d_k, d_vt], axis=1).astype(BF)
    sums_ref[rows, :] = jnp.broadcast_to(jnp.sum(d_total * enters, axis=1, keepdims=True), (HEAD, 128))

    if own_side:

        @pl.when(h == HEADS // 2 - 1)
        def _():
            pack_totals(pack_ref, sums_ref[...].T[0:8])


def scores_back(own_side, starts, heads, g, number, total, mem, packs=(), after=()):
    length = heads.shape[2]
    width, count = HEADS * HEAD, HEADS // 2
    row = pl.BlockSpec((HEAD, length), lambda h: (head_of(own_side, h), 0))
    half = pl.BlockSpec((HEAD, length), lambda h: (h, 0))
    pack, sums = jax.ShapeDtypeStruct((PACK, 128), BF), jax.ShapeDtypeStruct((width, 128), F32)
    scratch = [pltpu.VMEM((length, length), BF)]
    in_specs = [
        SMEM, pl.BlockSpec((1, 4 * HEAD, length), lambda h: (head_of(own_side, h), 0, 0)),
        row, row, row, pl.BlockSpec((HEAD, 128), lambda h: (head_of(own_side, h), 0)),
    ]
    out_specs = [half, half, half, whole((PACK, 128))]
    out_shape = [jax.ShapeDtypeStruct((count * HEAD, length), BF)] * 3 + [pack]
    if own_side:
        in_specs += [whole((PACK, 128)), whole((width, 128))]
        scratch += [pltpu.VMEM((width, 128), F32)]
    else:
        out_specs += [whole((width, 128))]
        out_shape += [sums]
    return call(
        functools.partial(scores_back_body, own_side),
        (count,),
        in_specs,
        out_specs,
        out_shape,
        scratch,
        us=3.0,
        after=after,
    )(starts, heads, g, number, total, mem, *packs)


def heads_back_body(starts_ref, heads_ref, g_ref, a_ref, spread_ref, d_total_ref, mem_ref,
                    d_ref, mask_ref):
    length = heads_ref.shape[2]

    @pl.when(pl.program_id(0) == 0)
    def _():
        mask_ref[...] = visible(doc_begin_row(starts_ref, length), length)

    enters = enters_row(starts_ref, length)
    q, k, v, c = parts(heads_ref)
    g, a, spread, d_total = g_ref[...], a_ref[...], spread_ref[...], d_total_ref[...]
    mem_k = mem_ref[:, :HEAD]
    steps = causal_pairs(c, a, mask_ref)
    d_ref[0, :HEAD, :] = causal_sum(k, steps) + enters * tn(mem_k, a)
    d_ref[0, HEAD : 2 * HEAD, :] = causal_back(q, steps)
    links = causal_pairs(c, spread, mask_ref)
    d_ref[0, 2 * HEAD : 3 * HEAD, :] = causal_back(g, links)
    d_ref[0, 3 * HEAD :, :] = (
        causal_back(a, causal_pairs(k, q, mask_ref))
        + causal_back(spread, causal_pairs(v, g, mask_ref))
        + causal_back(d_total, mask_pair(mask_ref))
    )


def heads_back(own_side, starts, heads, g, a, spread, d_total, mem, after=()):
    length = heads.shape[2]
    count = HEADS // 2
    head = functools.partial(head_of, own_side)
    row = pl.BlockSpec((HEAD, length), lambda h: (head(h), 0))
    half = pl.BlockSpec((HEAD, length), lambda h: (h, 0))
    return call(
        heads_back_body,
        (count,),
        [SMEM, pl.BlockSpec((1, 4 * HEAD, length), lambda h: (head(h), 0, 0)), row, half, half, half,
         pl.BlockSpec((HEAD, 128), lambda h: (head(h), 0))],
        HEAD_BLOCK(4 * HEAD, length),
        jax.ShapeDtypeStruct((count, 4 * HEAD, length), F32),
        [pltpu.VMEM((length, length), BF)],
        us=8.0 if own_side else 3.0,
        after=after,
    )(starts, heads, g, a, spread, d_total, mem)


def project_back_body(own_side, starts_ref, heads_ref, d_ref, control_ref, partner_ref, far_ref, xnt_ref,
                      wq_ref, wk_ref, wv_ref, wc_ref, *refs):
    if own_side:
        (dx_in_ref, x_ref, gain_ref, d_hidden1_ref, norms2_ref,
         grad_ref, grad_x_ref, norms_ref, mem_ref, totals_ref, proj_ref, dx_ref) = refs
    else:
        grad_ref, dx_ref, mem_ref, totals_ref, proj_ref = refs
    j = pl.program_id(0)
    length = xnt_ref.shape[1]
    ffn = lax.axis_index("ffn")

    @pl.when(j == 0)
    def _():
        arrived(True, length, starts_ref, partner_ref, far_ref, mem_ref, totals_ref)

    pair = (ffn if own_side else 1 - ffn) * 2 + j
    tail = tail_row(doc_begin_row(starts_ref, length), length)
    for i in range(2):
        rows = pl.ds(pl.multiple_of((pair * 2 + i) * HEAD, HEAD), HEAD)
        mem = mem_ref[rows, :]
        back_k, back_vt = mem[:, :HEAD], mem[:, HEAD:]
        k, v, c = [heads_ref[i, m * HEAD : m * HEAD + HEAD, :] for m in (1, 2, 3)]
        c_tail = (c.astype(F32) * tail).astype(BF)
        d_q = d_ref[i, :HEAD, :]
        d_k = d_ref[i, HEAD : 2 * HEAD, :] + tn(back_k, c_tail)
        d_v = d_ref[i, 2 * HEAD : 3 * HEAD, :] + nn(back_vt, c_tail)
        d_c = d_ref[i, 3 * HEAD :, :] + tail * (
            nn(back_k, k) + tn(back_vt, v) + totals_ref[rows, 0:1]
        )
        d_c = d_c * control_ref[i * HEAD : i * HEAD + HEAD, :]
        for m, value in enumerate((d_q, d_k, d_v, d_c)):
            proj_ref[m * 128 + i * HEAD : m * 128 + i * HEAD + HEAD, :] = value.astype(BF)
    d_proj = proj_ref[...]
    grad_ref[...] = nt(xnt_ref[...], d_proj).astype(BF)
    w = jnp.concatenate([wq_ref[...], wk_ref[...], wv_ref[...], wc_ref[...]], axis=1)
    dx = nn(w, d_proj)

    @pl.when(j == 0)
    def _():
        dx_ref[...] = dx_in_ref[...] + dx if own_side else dx

    @pl.when(j > 0)
    def _():
        dx_ref[...] += dx

    if own_side:

        @pl.when(j == 1)
        def _():
            x = x_ref[...].astype(F32)
            mean = jnp.mean(x, axis=-1, keepdims=True)
            centered = x - mean
            inverse = lax.rsqrt(jnp.mean(centered * centered, axis=-1, keepdims=True) + EPSILON)
            n = centered * inverse
            d = dx_ref[...].T
            sums = [jnp.sum(d * n, axis=0, keepdims=True), jnp.sum(d, axis=0, keepdims=True)]
            rows8 = jnp.concatenate(sums + [norms2_ref[0:6, :]], axis=0)
            columns = jnp.concatenate([rows8, jnp.zeros((120, length), F32)], axis=0).T
            norms_ref[...] = columns.astype(BF)
            d_n = d * gain_ref[...]
            grad_x_ref[...] = d_hidden1_ref[...] + (
                d_n
                - jnp.mean(d_n, axis=-1, keepdims=True)
                - n * jnp.mean(d_n * n, axis=-1, keepdims=True)
            ) * inverse


def project_back(own_side, starts, heads, d, control, partner, far, xnt, w, rest=(), after=()):
    width, length = xnt.shape
    square, row = whole((length, width)), whole((1, width))

    def pair(j):
        ffn = lax.axis_index("ffn")
        return (ffn if own_side else 1 - ffn) * 2 + j

    weights = [
        pl.BlockSpec((width, 128), functools.partial(lambda m, j: (0, 4 * m + pair(j)), m))
        for m in range(4)
    ]
    in_specs = [
        SMEM,
        pl.BlockSpec((2, 4 * HEAD, length), lambda j: (pair(j), 0, 0)),
        pl.BlockSpec((2, 4 * HEAD, length), lambda j: (j, 0, 0)),
        pl.BlockSpec((128, length), lambda j: (pair(j), 0)),
        whole((PACK, 128)), whole((PACK, 128)), square,
    ] + weights
    f32_square = jax.ShapeDtypeStruct((length, width), F32)
    out_specs, out_shape = [FEED_COLS], [jax.ShapeDtypeStruct((width, 1024), BF)]
    scratch = [pltpu.VMEM((width, 128), BF), pltpu.VMEM((width, 8), F32), pltpu.VMEM((512, length), BF)]
    if own_side:
        in_specs += [square, square, row, square, whole((8, width))]
        out_specs += [square, whole((width, 128))]
        out_shape += [f32_square, jax.ShapeDtypeStruct((width, 128), BF)]
        scratch += [pltpu.VMEM((width, length), F32)]
    else:
        out_specs += [square]
        out_shape += [f32_square]
    return call(
        functools.partial(project_back_body, own_side),
        (2,),
        in_specs,
        out_specs,
        out_shape,
        scratch,
        us=5.0 if own_side else 3.5,
        after=after,
    )(starts, heads, d, control, partner, far, xnt, w, w, w, w, *rest)


def bit_axis(bit):
    return ("seq", 1) if bit == 0 else ("dp", 1 << (bit - 1))


def my_bit(bit):
    axis, step = bit_axis(bit)
    return (lax.axis_index(axis) // step) % 2


def send_across(a, bits):
    seqs, dps = lax.axis_size("seq"), lax.axis_size("dp")
    flip = sum(1 << bit for bit in bits)
    return lax.ppermute(a, ("dp", "seq"), [(i, i ^ flip) for i in range(seqs * dps)])


def place_of(t, places, values):
    index, rest, bit = 0, t, 0
    fixed = dict(zip(places, values))
    while rest or fixed:
        if bit in fixed:
            index = index + fixed.pop(bit) * (1 << bit)
        else:
            index = index + ((rest & 1) << bit)
            rest >>= 1
        bit += 1
    return index


def stage_body(plan, *refs):
    refs = list(refs)
    ins = [[[refs.pop(0) for _ in pieces] for pieces in arrays] for arrays, _, _ in plan]
    for (arrays, split, dtype), sources in zip(plan, ins):
        outs = [refs.pop(0) for _ in range(1 << len(split))]
        blocks = outs[0].shape[0]
        places = [place for _, place in split]
        mine = [my_bit(bit) for bit, _ in split]
        for pattern, out in enumerate(outs):
            values = [
                (1 - m) if (pattern >> n) & 1 else m for n, m in enumerate(mine)
            ]
            for t in range(blocks):
                at = place_of(t, places, values)
                total = None
                for pieces in sources:
                    row = jnp.concatenate([p[at] for p in pieces], axis=1) if len(pieces) > 1 else pieces[0][at]
                    row = row.astype(F32)
                    total = row if total is None else total + row
                out[t] = total.astype(out.dtype)


def stage(groups, after=(), dtype=BF):
    plan, operands, in_specs, out_specs, out_shape = [], [], [], [], []
    rows = groups[0][0][0][0][0].shape[1]
    steps = 2 if rows % 32 == 0 else 1
    for arrays, split in groups:
        for pieces in arrays:
            for array, first, count in pieces:
                operands.append(array)
                in_specs.append(
                    pl.BlockSpec((array.shape[0], rows // steps, count),
                                 functools.partial(lambda at, i: (0, i, at), first // count))
                )
        blocks, width = arrays[0][0][0].shape[0] >> len(split), sum(p[2] for p in arrays[0])
        plan.append(([[None] * len(pieces) for pieces in arrays], split, dtype))
        for _ in range(1 << len(split)):
            out_specs.append(pl.BlockSpec((blocks, rows // steps, width), lambda i: (0, i, 0)))
            out_shape.append(jax.ShapeDtypeStruct((blocks, rows, width), dtype))
    outs = list(
        call(functools.partial(stage_body, plan), (steps,), in_specs, out_specs, out_shape, after=after)(*operands)
    )
    result = []
    for _, split in groups:
        result.append([outs.pop(0) for _ in range(1 << len(split))])
    return result


def all_of(a):
    return [(a, 0, a.shape[2])]


def patterns(bits):
    return [[b for n, b in enumerate(bits) if (p >> n) & 1] for p in range(1, 1 << len(bits))]


def finish_body(a_ref, b_ref, up_ref, down_ref, out_ref):
    total = a_ref[0].astype(F32) + b_ref[0].astype(F32)
    half, part = up_ref.shape[1], out_ref.shape[1] // 2
    up_ref[...] = total[:, :half]
    down_ref[...] = total[:, half + part : 2 * half + part]
    out_ref[:, :part] = total[:, half : half + part].astype(BF)
    out_ref[:, part:] = total[:, 2 * half + part :].astype(BF)


def finish(a, b, half, part, after=()):
    rows = a.shape[1]
    return call(
        finish_body,
        (),
        [whole(a.shape)] * 2,
        [whole((rows, half)), whole((rows, half)), whole((rows, 2 * part))],
        [jax.ShapeDtypeStruct((rows, half), F32)] * 2 + [jax.ShapeDtypeStruct((rows, 2 * part), BF)],
        after=after,
    )(a, b)


def join_body(own_ref, other_ref, out_own, out_other, grad_in_ref, grad_out_ref, *norm_refs):
    second = lax.axis_index("ffn") == 1
    own, other = own_ref[0].astype(F32), other_ref[0].astype(F32)
    for f in range(2):
        keep_own = second if f else jnp.logical_not(second)
        half = jnp.where(keep_own, own[:, :1024], other[:, :1024])
        for p in range(2):
            for m in range(4):
                grad_in_ref[:, m * 512 + f * 256 + p * 128 : m * 512 + f * 256 + p * 128 + 128] = (
                    half[:, p * 512 + m * 128 : p * 512 + m * 128 + 128]
                )
        grad_out_ref[:, f * 256 : f * 256 + 256] = jnp.where(
            keep_own, out_own[...], out_other[...]
        ).astype(F32)
    norms = (own[:, 1024:] + other[:, 1024:]).T
    for n, ref in enumerate(norm_refs):
        ref[...] = norms[n]


def join(own, other, out_own, out_other):
    rows = own.shape[1]
    return call(
        join_body,
        (),
        [whole(own.shape)] * 2 + [whole(out_own.shape)] * 2,
        [whole((rows, 2048)), whole((rows, 512))] + [whole((rows,))] * 4,
        [jax.ShapeDtypeStruct((rows, n), F32) for n in (2048, 512)] + [jax.ShapeDtypeStruct((rows,), F32)] * 4,
    )(own, other, out_own, out_other)


def on_device(tokens, doc_starts, norm1_gain, norm1_bias, in_weight, out_weight,
              norm2_gain, norm2_bias, up_own, down_own, output_cotangent):
    up_other, down_other = swap(up_own, "ffn", 1), swap(down_own, "ffn", 1)
    x, cotangent, starts = tokens[0], output_cotangent[0], doc_starts
    length, width = x.shape
    owners = lax.axis_size("dp") * lax.axis_size("seq")
    bits = owners.bit_length() - 1
    row = lambda a: a.reshape(1, width)
    blocked = lambda a: a.reshape(owners, width // owners, a.shape[1])

    heads, control, xnt, own = project(x, row(norm1_gain), row(norm1_bias), in_weight, starts)
    partner = swap(own, "ffn", 1)
    local_a = local_sums(starts, heads, 0, 4)
    both = combine(False, length, starts, own, partner, after=local_a[:1])
    far = lax.ppermute(both, "seq", [(0, 1)])
    local_b = local_sums(starts, heads, 4, 4, after=[both])
    number, total, mixed, memory = mix(starts, heads, *local_a, *local_b, partner, far)
    gup_send, gdown_send, *saved = feed_other(
        x, mixed, cotangent, out_weight, row(norm2_gain), row(norm2_bias), up_other, down_other)
    gup_got, gdown_got = swap(gup_send, "ffn", 1), swap(gdown_send, "ffn", 1)
    (output, d_hidden1, g, out_send, out_keep, norms2, gup_own, gdown_own) = feed_own(
        saved, mixed, cotangent, out_weight, row(norm2_gain), up_own, down_own)
    out_got = swap(out_send, "ffn", 1)

    out_half = width // 4
    ups, downs, outs = [
        [blocked(a) for a in pair]
        for pair in ((gup_own, gup_got), (gdown_own, gdown_got), (out_keep, out_got))
    ]
    groups = [
        [[*all_of(a), (o, 0, out_half)] for a, o in zip(ups, outs)],
        [[*all_of(a), (o, out_half, out_half)] for a, o in zip(downs, outs)],
    ]
    orders = [[0, 1], [1, 0]]
    left = [list(range(bits)) for _ in groups]

    def advance(groups, n, after):
        if n >= 2:
            if n == 2:
                groups = [[pieces_a + pieces_b for pieces_a, pieces_b in zip(*groups)]]
            bits_now = [n]
            splits = [[(n, 0)]]
        else:
            bits_now = [order[n] for order in orders]
            splits = [[(bit, rest.index(bit))] for bit, rest in zip(bits_now, left)]
            for bit, rest in zip(bits_now, left):
                rest.remove(bit)
        outs = stage(list(zip(groups, splits)), after=after)
        got = [send_across(sent, [bit]) for (_, sent), bit in zip(outs, bits_now)]
        sent = [s for _, s in outs]
        return [[all_of(kept), all_of(r)] for (kept, _), r in zip(outs, got)], sent

    back = (starts, heads, g, number, total, memory)
    *scores_other, pack, sums = scores_back(False, *back)
    groups, sent = advance(groups, 0, [pack])
    *scores_own, d_own = scores_back(True, *back, packs=(pack, sums), after=sent)
    d_partner = swap(d_own, "ffn", 1)
    d_both = combine(True, length, starts, d_own, d_partner)
    d_far = lax.ppermute(d_both, "seq", [(1, 0)])
    side = (control, d_partner, d_far, xnt, in_weight)
    d_other = heads_back(False, starts, heads, g, *scores_other, memory, after=[d_both])
    groups, sent = advance(groups, 1, [d_other])
    in_send, dx = project_back(False, starts, heads, d_other, *side, after=sent)
    in_got = swap(in_send, "ffn", 1)
    d_mine = heads_back(True, starts, heads, g, *scores_own, memory, after=[in_send])
    groups, sent = advance(groups, 2, [d_mine])
    in_keep, grad_tokens, norms = project_back(
        True, starts, heads, d_mine, *side,
        rest=(dx, x, row(norm1_gain), d_hidden1, norms2), after=sent)

    late = [
        all_of(blocked(in_keep)) + all_of(blocked(norms)),
        all_of(blocked(in_got)) + all_of(jnp.zeros_like(blocked(norms))),
    ]
    rest = list(range(bits))
    first = True
    while rest:
        now = rest[:2]
        split = [(b, rest.index(b)) for b in now]
        rest = rest[2:]
        (kept, *sent), = stage([(late, split)])
        late = [all_of(kept)] + [all_of(send_across(s, p)) for s, p in zip(sent, patterns(now))]
        if first:
            first, token = False, [kept]
            for n in range(3, bits):
                groups, token = advance(groups, n, token)
    grad_up, grad_down, out = finish(*(a[0][0] for a in groups[0]), gup_own.shape[1], out_half, after=[kept])
    (final,), = stage([(late, [])], after=[out])
    grad_in, grad_out, *norms = join(final, swap(final, "ffn", 1), out, swap(out, "ffn", 1))
    return (output[None], grad_tokens[None], grad_in, grad_out, grad_up, grad_down, *norms)


def solution(mesh):
    rows = P("dp", ("seq", "ffn"), None)
    owned = P(("dp", "seq"))
    return jax.shard_map(
        on_device,
        mesh=mesh,
        in_specs=(
            rows, P("dp", None), P(), P(), P(), P(), P(), P(),
            P(None, "ffn"), P(None, "ffn"), rows,
        ),
        out_specs=(
            rows, rows, P(("dp", "seq"), None), P(("dp", "seq"), None),
            P(("dp", "seq"), "ffn"), P(("dp", "seq"), "ffn"),
            owned, owned, owned, owned,
        ),
        check_vma=False,
    )
```

time: 176 us -> 119 us (0.68)
  waiting for transfers between devices: 45.8 us -> 17.2 us
  Pallas kernels: 80.2 us -> 70.9 us
  local copies, waits for them, and re-layouts: 8.5 us -> 1.67 us
  starting transfers between devices: 34.2 us -> 28.1 us
  other arithmetic: 5.31 us -> 0 us
    ppermute x31 -> x10, waiting for transfers between devices: 39.7 us -> 2.22 us  [swap(): return lax.ppermute(a, axis, [(i, i ^ bit) for i in range(size)])]
    ppermute x31 -> x10, starting transfers between devices: 28 us -> 2.38 us  [swap(): return lax.ppermute(a, axis, [(i, i ^ bit) for i in range(size)])]
    ppermute x0 -> x12, starting transfers between devices: none -> 19.6 us  [send_across(): lax.ppermute(a, ('dp', 'seq'), [(i, i ^ flip) for i in range(seqs * dps)])]
    ppermute x0 -> x12, waiting for transfers between devices: none -> 14.4 us  [send_across(): lax.ppermute(a, ('dp', 'seq'), [(i, i ^ flip) for i in range(seqs * dps)])]
    pallas_call x9 -> x23, Pallas kernels: 80.2 us -> 70.9 us  [start(): pl.pallas_call(run, grid=grid, in_specs=list(in_specs) + [ANY] * len(afte...]
    ppermute x1, waiting for transfers between devices: 6.12 us -> 0.01 us  [on_device(): d_far = lax.ppermute(d_both, 'seq', [(1, 0)])]
    add x23 -> x0, other arithmetic: 4.46 us -> none  [the longest x18 2.2 us: reduce_rows(): value = keep.astype(F32) + swap(send.astype(BF), axis, step).astype(F32)]
    unnamed x20 -> x30, local copies, waits for them, and re-layouts: 4.61 us -> 1.65 us
  transfers between devices with their start and end apart: 33 -> 24, of which waited for: 18 -> 6; matrix products, arithmetic and copies ran while one was open for 4% -> 0% of each run, Pallas kernels for 25% -> 47%
where the time goes in v1:
time: 119 us
  Pallas kernels  70.9 us (60%)
  starting transfers between devices  28.1 us (24%)
  waiting for transfers between devices  17.2 us (14%)
  local copies, waits for them, and re-layouts  1.67 us (1%)
    pallas_call x23, Pallas kernels, start(): pl.pallas_call(run, grid=grid, in_specs=list(in_specs) + [ANY] * len(afte...  70.9 us
    ppermute x12, starting transfers between devices, send_across(): lax.ppermute(a, ('dp', 'seq'), [(i, i ^ flip) for i in range(seqs * dps)])  19.6 us
    ppermute x12, waiting for transfers between devices, send_across(): lax.ppermute(a, ('dp', 'seq'), [(i, i ^ flip) for i in range(seqs * dps)])  14.4 us
    ppermute x1, starting transfers between devices, on_device(): far = lax.ppermute(both, 'seq', [(0, 1)])  4.67 us
  transfers between devices with their start and end apart: 24, of which 6 were waited for; matrix products, arithmetic and copies ran while one was open for 0% of the time, Pallas kernels for 47%

profile of v1, /device:TPU:0, one launch (start us, length us, event | category | flops | bytes accessed | tf_op | source)
XLA Modules:
  0.0 119.0 jit_solution(18250705654481964132)
XLA Ops:
  0.7 6.5 %shard_map.186 = (bf16[8,256,512]{2,1,0:T(8,128)(2,1)}, f32[512,512]{1,0:T(8,128)}, bf16[512,512]{1,0:T(8,128)(2,1)}, bf16[576,128]{1,0:T(8,128)(2,1)}) custom-call(bf16[512,512]{1,0:T(8,128)(2,1)} %bitcast.28, f32[1,512]{1,0:T(1,128)} %bitcast.34, f32[1,512]{1,0:T(1,128)} %bitcast.38, bf16[512,2048]{1,0:T(8,128)(2,1)} %refs_10_.5, s32[1,8]{1,0:T(1,128)} %refs_0_.21), custom_call_target="tpu_custom_call" | custom-call | flops 4944999936 | bytes 1048576 | tf_op jit(solution)/shard_map/pallas_call | solution.py:48
  7.2 0.5 collective-permute-start
  7.7 0.1 collective-permute-start.2
  7.8 0.4 collective-permute-start.3
  8.2 1.6 %copy-done.1 = bf16[8,256,512]{2,1,0:T(8,128)(2,1)S(1)} copy-done((bf16[8,256,512]{2,1,0:T(8,128)(2,1)S(1)}, bf16[8,256,512]{2,1,0:T(8,128)(2,1)}, u32[]{:S(2)}) %copy-start.1) | copy-done | bytes 2097176
  9.8 3.0 %shard_map.187 = (f32[256,512]{1,0:T(8,128)S(1)}, f32[256,512]{1,0:T(8,128)S(1)}) custom-call(s32[1,8]{1,0:T(1,128)S(1)} %copy-done.5, bf16[8,256,512]{2,1,0:T(8,128)(2,1)S(1)} %copy-done.1), custom_call_target="tpu_custom_call" | custom-call | flops 3449999872 | bytes 1048576 | tf_op jit(solution)/shard_map/pallas_call | solution.py:48
  12.8 0.6 shard_map.188.refs_2_
  13.5 4.7 %collective-permute-start.1 = (bf16[576,128]{1,0:T(8,128)(2,1)S(1)}, bf16[576,128]{1,0:T(8,128)(2,1)S(1)}, u32[]{:S(2)}, u32[]{:S(2)}) collective-permute-start(bf16[576,128]{1,0:T(8,128)(2,1)S(1)} %shard_map.188.refs_2_), channel_id=1, source_target_pairs={{0,2},{1,3},{4,6},{5,7},{8,10},{9,11},{12,14},{13,15},{16,18},{17,... | collective-permute-start | bytes 442376 | tf_op jit(solution)/shard_map/ppermute | solution.py:863
  18.2 3.0 %shard_map.189 = (f32[256,512]{1,0:T(8,128)S(1)}, f32[256,512]{1,0:T(8,128)S(1)}) custom-call(s32[1,8]{1,0:T(1,128)S(1)} %copy-done.5, bf16[8,256,512]{2,1,0:T(8,128)(2,1)S(1)} %copy-done.2, bf16[576,128]{1,0:T(8,128)(2,1)S(1)} %shard_map.188.refs_2_), custom_call_target="tpu_custom_call" | custom-call | flops 3449999872 | bytes 1048576 | tf_op jit(solution)/shard_map/pallas_call | solution.py:48
  21.1 0.5 collective-permute-done.1.refs_7_
  21.7 6.3 %shard_map.190 = (f32[512,512]{1,0:T(8,128)S(1)}, f32[512,512]{1,0:T(8,128)S(1)}, bf16[512,512]{1,0:T(8,128)(2,1)S(1)}, bf16[512,128]{1,0:T(8,128)(2,1)S(1)}) custom-call(s32[1,8]{1,0:T(1,128)S(1)} %copy-done.5, bf16[8,256,512]{2,1,0:T(8,128)(2,1)S(1)} %copy-done.2, f32[256,512]{1,0:T(8,128)S(1)} %get-tuple-element.84.refs_3_.refs_2_, ...), custom_call_target="tpu_custom_call" | custom-call | flops 6899999744 | bytes 1048576 | tf_op jit(solution)/shard_map/pallas_call | solution.py:48
  28.1 6.0 %shard_map.191 = (bf16[512,1024]{1,0:T(8,128)(2,1)S(1)}, bf16[512,1024]{1,0:T(8,128)(2,1)S(1)}, f32[512,512]{1,0:T(8,128)S(1)}, f32[512,512]{1,0:T(8,128)S(1)}, ...) custom-call(bf16[512,512]{1,0:T(8,128)(2,1)S(1)} %bitcast.29, ...), custom_call_target="tpu_custom_call" | custom-call | flops 7474999808 | bytes 1048576 | tf_op jit(solution)/shard_map/pallas_call | solution.py:48
  34.1 0.5 collective-permute-start.4
  34.6 7.1 %shard_map.192 = (bf16[512,512]{1,0:T(8,128)(2,1)}, f32[512,512]{1,0:T(8,128)S(1)}, bf16[512,512]{1,0:T(8,128)(2,1)S(1)}, bf16[512,256]{1,0:T(8,128)(2,1)S(1)}, ...) custom-call(f32[512,512]{1,0:T(8,128)S(1)} %get-tuple-element.90.ref, ...), custom_call_target="tpu_custom_call" | custom-call | flops 7474999808 | bytes 1048576 | tf_op jit(solution)/shard_map/pallas_call | solution.py:48
  41.7 3.3 %shard_map.193 = (bf16[256,512]{1,0:T(8,128)(2,1)S(1)}, bf16[256,512]{1,0:T(8,128)(2,1)S(1)}, bf16[256,512]{1,0:T(8,128)(2,1)S(1)}, bf16[576,128]{1,0:T(8,128)(2,1)S(1)}, f32[512,128]{1,0:T(8,128)S(1)}) custom-call(s32[1,8]{1,0:T(1,128)S(1)} %copy-done.5, bf16[8,256,512]{2,1,0:T(8,128)(2,1)S(1)} %copy-done.2, ...), custom_call_target="tpu_custom_call" | custom-call | flops 3449999872 | bytes 1048576 | tf_op jit(solution)/shard_map/pallas_call | solution.py:48
  45.1 1.4 %shard_map.194 = (bf16[8,32,1152]{2,1,0:T(8,128)(2,1)S(1)}, bf16[8,32,1152]{2,1,0:T(8,128)(2,1)S(1)}, bf16[8,32,1152]{2,1,0:T(8,128)(2,1)S(1)}, bf16[8,32,1152]{2,1,0:T(8,128)(2,1)S(1)}) custom-call(bf16[16,32,1024]{2,1,0:T(8,128)(2,1)S(1)} %bitcast.19, bf16[16,32,256]{2,1,0:T(8,128)(2,1)S(1)} %bitcast.21, bf16[16,32,1024]{2,1,0:T(8,128)(2,1)S(1)} %bitcast.18, ...), custom_call_target="tpu_custom_call" | custom-call | flops 1150000000 | bytes 1048576 | tf_op jit(solution)/shard_map/pallas_call | solution.py:48
  46.5 1.6 %collective-permute-start.10 = (bf16[8,32,1152]{2,1,0:T(8,128)(2,1)S(1)}, bf16[8,32,1152]{2,1,0:T(8,128)(2,1)S(1)}, u32[]{:S(2)}, u32[]{:S(2)}) collective-permute-start(bf16[8,32,1152]{2,1,0:T(8,128)(2,1)S(1)} %get-tuple-element.112.refs_9_), channel_id=1, source_target_pairs={{0,4},{2,6},{4,0},{6,2},{8,12},{10,14},{12,8},{14,10},{16,20},{18,... | collective-permute-start | bytes 1769480 | tf_op jit(solution)/shard_map/ppermute | solution.py:726
  48.1 2.5 %collective-permute-start.9 = (bf16[8,32,1152]{2,1,0:T(8,128)(2,1)S(1)}, bf16[8,32,1152]{2,1,0:T(8,128)(2,1)S(1)}, u32[]{:S(2)}, u32[]{:S(2)}) collective-permute-start(bf16[8,32,1152]{2,1,0:T(8,128)(2,1)S(1)} %get-tuple-element.111.refs_8_), channel_id=1, source_target_pairs={{0,2},{2,0},{4,6},{6,4},{8,10},{10,8},{12,14},{14,12},{16,18},{18,... | collective-permute-start | bytes 1769480 | tf_op jit(solution)/shard_map/ppermute | solution.py:726
  50.6 3.4 %shard_map.195 = (bf16[256,512]{1,0:T(8,128)(2,1)S(1)}, bf16[256,512]{1,0:T(8,128)(2,1)S(1)}, bf16[256,512]{1,0:T(8,128)(2,1)S(1)}, bf16[576,128]{1,0:T(8,128)(2,1)S(1)}) custom-call(s32[1,8]{1,0:T(1,128)S(1)} %copy-done.5, bf16[8,256,512]{2,1,0:T(8,128)(2,1)S(1)} %copy-done.2, bf16[512,512]{1,0:T(8,128)(2,1)S(1)} %get-tuple-element.99.refs_2_, ...), custom_call_target="tpu_custom_call" | custom-call | flops 3449999872 | bytes 1048576 | tf_op jit(solution)/shard_map/pallas_call | solution.py:48
  54.0 1.4 %collective-permute-done.7.refs_2_.refs_4_ = bf16[576,128]{1,0:T(8,128)(2,1)S(1)} collective-permute-done((bf16[576,128]{1,0:T(8,128)(2,1)S(1)}, bf16[576,128]{1,0:T(8,128)(2,1)S(1)}, u32[]{:S(2)}, u32[]{:S(2)}) %collective-permute-start.7) | collective-permute-done | bytes 147488 | tf_op jit(solution)/shard_map/ppermute | solution.py:35
  55.4 0.6 shard_map.196.refs_7_
  56.0 1.5 %collective-permute-start.8 = (bf16[576,128]{1,0:T(8,128)(2,1)S(1)}, bf16[576,128]{1,0:T(8,128)(2,1)S(1)}, u32[]{:S(2)}, u32[]{:S(2)}) collective-permute-start(bf16[576,128]{1,0:T(8,128)(2,1)S(1)} %shard_map.196.refs_7_), channel_id=1, source_target_pairs={{2,0},{3,1},{6,4},{7,5},{10,8},{11,9},{14,12},{15,13},{18,16},{19,... | collective-permute-start | bytes 442376 | tf_op jit(solution)/shard_map/ppermute | solution.py:907
  57.5 8.5 %shard_map.197.refs_4_.refs_2_ = f32[4,256,512]{2,1,0:T(8,128)S(1)} custom-call(s32[1,8]{1,0:T(1,128)S(1)} %copy-done.5, bf16[8,256,512]{2,1,0:T(8,128)(2,1)S(1)} %copy-done.2, bf16[512,512]{1,0:T(8,128)(2,1)S(1)} %get-tuple-element.99.refs_2_, bf16[256,512]{1,0:T(8,128)(2,1)S(1)} %get-tuple-element.116.refs_3_, ...), custom_call_target="tpu_custom_call" | custom-call | flops 3449999872 | bytes 1048576 | tf_op jit(solution)/shard_map/pallas_call | solution.py:48
  66.1 0.7 shard_map.198
  66.8 0.6 collective-permute-start.11
  67.3 2.7 %collective-permute-start.12 = (bf16[4,32,1152]{2,1,0:T(8,128)(2,1)S(1)}, bf16[4,32,1152]{2,1,0:T(8,128)(2,1)S(1)}, u32[]{:S(2)}, u32[]{:S(2)}) collective-permute-start(bf16[4,32,1152]{2,1,0:T(8,128)(2,1)S(1)} %get-tuple-element.125.refs_12_), channel_id=1, source_target_pairs={{0,2},{2,0},{4,6},{6,4},{8,10},{10,8},{12,14},{14,12},{16,18},{18,... | collective-permute-start | bytes 884744 | tf_op jit(solution)/shard_map/ppermute | solution.py:726
  70.0 3.5 %shard_map.199 = (bf16[512,1024]{1,0:T(8,128)(2,1)S(1)}, f32[512,512]{1,0:T(8,128)S(1)}) custom-call(s32[1,8]{1,0:T(1,128)S(1)} %copy-done.5, bf16[8,256,512]{2,1,0:T(8,128)(2,1)S(1)} %copy-done.2, f32[4,256,512]{2,1,0:T(8,128)S(1)} %shard_map.197.refs_4_.refs_2_, f32[512,512]{1,0:T(8,128)S(1)} %copy-done.3, ...), custom_call_target="tpu_custom_call" | custom-call | flops 4024999936 | bytes 1048576 | tf_op jit(solution)/shard_map/pallas_call | solution.py:48
  73.6 8.5 %shard_map.200.refs_4_.refs_2_ = f32[4,256,512]{2,1,0:T(8,128)S(1)} custom-call(s32[1,8]{1,0:T(1,128)S(1)} %copy-done.5, bf16[8,256,512]{2,1,0:T(8,128)(2,1)S(1)} %copy-done.2, bf16[512,512]{1,0:T(8,128)(2,1)S(1)} %get-tuple-element.99.refs_2_, bf16[256,512]{1,0:T(8,128)(2,1)S(1)} %get-tuple-element.113.refs_3_, ...), custom_call_target="tpu_custom_call" | custom-call | flops 9200000000 | bytes 1048576 | tf_op jit(solution)/shard_map/pallas_call | solution.py:48
  82.1 0.4 shard_map.201
  82.5 1.6 %collective-permute-start.20 = (bf16[2,32,2304]{2,1,0:T(8,128)(2,1)S(1)}, bf16[2,32,2304]{2,1,0:T(8,128)(2,1)S(1)}, u32[]{:S(2)}, u32[]{:S(2)}) collective-permute-start(bf16[2,32,2304]{2,1,0:T(8,128)(2,1)S(1)} %get-tuple-element.132.refs_16_), channel_id=1, source_target_pairs={{0,8},{2,10},{4,12},{6,14},{8,0},{10,2},{12,4},{14,6},{16,24},{18,... | collective-permute-start | bytes 884744 | tf_op jit(solution)/shard_map/ppermute | solution.py:726
  84.1 5.5 %shard_map.202 = (bf16[512,1024]{1,0:T(8,128)(2,1)S(1)}, f32[512,512]{1,0:T(8,128)}, bf16[512,128]{1,0:T(8,128)(2,1)S(1)}) custom-call(s32[1,8]{1,0:T(1,128)S(1)} %copy-done.5, bf16[8,256,512]{2,1,0:T(8,128)(2,1)S(1)} %copy-done.2, f32[4,256,512]{2,1,0:T(8,128)S(1)} %shard_map.200.refs_4_.refs_2_, f32[512,512]{1,0:T(8,128)S(1)} %copy-done.3, ...), custom_call_target="tpu_custom_call" | custom-call | flops 5750000128 | bytes 1048576 | tf_op jit(solution)/shard_map/pallas_call | solution.py:48
  89.6 0.7 shard_map.203
  90.3 0.7 collective-permute-start.14
  91.0 1.0 collective-permute-start.15
  92.0 1.9 %collective-permute-start.16 = (bf16[4,32,1152]{2,1,0:T(8,128)(2,1)S(1)}, bf16[4,32,1152]{2,1,0:T(8,128)(2,1)S(1)}, u32[]{:S(2)}, u32[]{:S(2)}) collective-permute-start(bf16[4,32,1152]{2,1,0:T(8,128)(2,1)S(1)} %get-tuple-element.139), channel_id=1, source_target_pairs={{0,6},{2,4},{4,2},{6,0},{8,14},{10,12},{12,10},{14,8},{16,22},{18,... | collective-permute-start | bytes 884744 | tf_op jit(solution)/shard_map/ppermute | solution.py:726
  93.9 0.2 shard_map.205
  94.1 2.7 %collective-permute-start.21 = (bf16[1,32,2304]{2,1,0:T(8,128)(2,1)S(1)}, bf16[1,32,2304]{2,1,0:T(8,128)(2,1)S(1)}, u32[]{:S(2)}, u32[]{:S(2)}) collective-permute-start(bf16[1,32,2304]{2,1,0:T(8,128)(2,1)S(1)} %get-tuple-element.146), channel_id=1, source_target_pairs={{0,16},{2,18},{4,20},{6,22},{8,24},{10,26},{12,28},{14,30},{16,0},... | collective-permute-start | bytes 442376 | tf_op jit(solution)/shard_map/ppermute | solution.py:726
  96.8 3.5 %collective-permute-done.14.refs_1_ = bf16[4,32,1152]{2,1,0:T(8,128)(2,1)S(1)} collective-permute-done((bf16[4,32,1152]{2,1,0:T(8,128)(2,1)S(1)}, bf16[4,32,1152]{2,1,0:T(8,128)(2,1)S(1)}, u32[]{:S(2)}, u32[]{:S(2)}) %collective-permute-start.14) | collective-permute-done | bytes 294944 | tf_op jit(solution)/shard_map/ppermute | solution.py:726
  100.2 6.6 %collective-permute-done.16.refs_3_ = bf16[4,32,1152]{2,1,0:T(8,128)(2,1)S(1)} collective-permute-done((bf16[4,32,1152]{2,1,0:T(8,128)(2,1)S(1)}, bf16[4,32,1152]{2,1,0:T(8,128)(2,1)S(1)}, u32[]{:S(2)}, u32[]{:S(2)}) %collective-permute-start.16) | collective-permute-done | bytes 294944 | tf_op jit(solution)/shard_map/ppermute | solution.py:726
  106.8 0.4 shard_map.204
  107.2 0.6 collective-permute-start.17
  107.7 2.6 %collective-permute-start.18 = (bf16[1,32,1152]{2,1,0:T(8,128)(2,1)S(1)}, bf16[1,32,1152]{2,1,0:T(8,128)(2,1)S(1)}, u32[]{:S(2)}, u32[]{:S(2)}) collective-permute-start(bf16[1,32,1152]{2,1,0:T(8,128)(2,1)S(1)} %get-tuple-element.142), channel_id=1, source_target_pairs={{0,16},{2,18},{4,20},{6,22},{8,24},{10,26},{12,28},{14,30},{16,0},... | collective-permute-start | bytes 221192 | tf_op jit(solution)/shard_map/ppermute | solution.py:726
  110.3 1.3 %collective-permute-start.19 = (bf16[1,32,1152]{2,1,0:T(8,128)(2,1)S(1)}, bf16[1,32,1152]{2,1,0:T(8,128)(2,1)S(1)}, u32[]{:S(2)}, u32[]{:S(2)}) collective-permute-start(bf16[1,32,1152]{2,1,0:T(8,128)(2,1)S(1)} %get-tuple-element.143), channel_id=1, source_target_pairs={{0,24},{2,26},{4,28},{6,30},{8,16},{10,18},{12,20},{14,22},{16,8},... | collective-permute-start | bytes 221192 | tf_op jit(solution)/shard_map/ppermute | solution.py:726
  111.6 0.7 shard_map.206
  112.3 4.4 %collective-permute-done.18.refs_2_ = bf16[1,32,1152]{2,1,0:T(8,128)(2,1)S(1)} collective-permute-done((bf16[1,32,1152]{2,1,0:T(8,128)(2,1)S(1)}, bf16[1,32,1152]{2,1,0:T(8,128)(2,1)S(1)}, u32[]{:S(2)}, u32[]{:S(2)}) %collective-permute-start.18) | collective-permute-done | bytes 73760 | tf_op jit(solution)/shard_map/ppermute | solution.py:726
  116.9 0.5 collective-permute-start.23
  117.4 0.8 collective-permute-done.23.refs_3_
  118.2 0.7 shard_map.208
  (54 shorter events, 0.6 us)
Async XLA Ops:
  0.6 7.1 %copy-start.6 = (bf16[512,1024]{1,0:T(8,128)(2,1)S(1)}, bf16[512,1024]{1,0:T(8,128)(2,1)}, u32[]{:S(2)}) copy-start(bf16[512,1024]{1,0:T(8,128)(2,1)} %refs_12_.1) | copy-start | bytes 3145732
  0.7 7.1 %copy-start.7 = (bf16[512,1024]{1,0:T(8,128)(2,1)S(1)}, bf16[512,1024]{1,0:T(8,128)(2,1)}, u32[]{:S(2)}) copy-start(bf16[512,1024]{1,0:T(8,128)(2,1)} %refs_13_.1) | copy-start | bytes 3145732
  0.7 7.6 %copy-start.5 = (s32[1,8]{1,0:T(1,128)S(1)}, s32[1,8]{1,0:T(1,128)}, u32[]{:S(2)}) copy-start(s32[1,8]{1,0:T(1,128)} %refs_0_.21) | copy-start | bytes 100
  7.2 5.6 %collective-permute-start = (bf16[576,128]{1,0:T(8,128)(2,1)}, bf16[576,128]{1,0:T(8,128)(2,1)S(1)}, u32[]{:S(2)}, u32[]{:S(2)}) collective-permute-start(bf16[576,128]{1,0:T(8,128)(2,1)} %get-tuple-element.85.refs_1_), channel_id=1, source_target_pairs={{0,1},{1,0},{2,3},{3,2},{4,5},{5,4},{6,7},{7,6},{8,9},{9,8},{10,11... | collective-permute-start | bytes 442376 | tf_op jit(solution)/shard_map/ppermute | solution.py:35
  7.7 20.3 %collective-permute-start.2 = (bf16[512,1024]{1,0:T(8,128)(2,1)S(1)}, bf16[512,1024]{1,0:T(8,128)(2,1)S(1)}, u32[]{:S(2)}, u32[]{:S(2)}) collective-permute-start(bf16[512,1024]{1,0:T(8,128)(2,1)S(1)} %copy-done.6), channel_id=1, source_target_pairs={{0,1},{1,0},{2,3},{3,2},{4,5},{5,4},{6,7},{7,6},{8,9},{9,8},{10,11... | collective-permute-start | bytes 3145736 | tf_op jit(solution)/shard_map/ppermute | solution.py:35
  7.8 20.2 %collective-permute-start.3 = (bf16[512,1024]{1,0:T(8,128)(2,1)S(1)}, bf16[512,1024]{1,0:T(8,128)(2,1)S(1)}, u32[]{:S(2)}, u32[]{:S(2)}) collective-permute-start(bf16[512,1024]{1,0:T(8,128)(2,1)S(1)} %copy-done.7), channel_id=1, source_target_pairs={{0,1},{1,0},{2,3},{3,2},{4,5},{5,4},{6,7},{7,6},{8,9},{9,8},{10,11... | collective-permute-start | bytes 3145736 | tf_op jit(solution)/shard_map/ppermute | solution.py:35
  8.2 1.6 %copy-start.1 = (bf16[8,256,512]{2,1,0:T(8,128)(2,1)S(1)}, bf16[8,256,512]{2,1,0:T(8,128)(2,1)}, u32[]{:S(2)}) copy-start(bf16[8,256,512]{2,1,0:T(8,128)(2,1)} %get-tuple-element.83.refs_1_) | copy-start | bytes 6291460
  9.8 3.0 %copy-start.11 = (bf16[576,128]{1,0:T(8,128)(2,1)S(1)}, bf16[576,128]{1,0:T(8,128)(2,1)}, u32[]{:S(2)}) copy-start(bf16[576,128]{1,0:T(8,128)(2,1)} %get-tuple-element.85.refs_1_) | copy-start | bytes 442372
  12.8 5.3 %copy-start.2 = (bf16[8,256,512]{2,1,0:T(8,128)(2,1)S(1)}, bf16[8,256,512]{2,1,0:T(8,128)(2,1)}, u32[]{:S(2)}) copy-start(bf16[8,256,512]{2,1,0:T(8,128)(2,1)} %get-tuple-element.83.refs_1_) | copy-start | bytes 6291460
  13.5 8.2 %collective-permute-start.1 = (bf16[576,128]{1,0:T(8,128)(2,1)S(1)}, bf16[576,128]{1,0:T(8,128)(2,1)S(1)}, u32[]{:S(2)}, u32[]{:S(2)}) collective-permute-start(bf16[576,128]{1,0:T(8,128)(2,1)S(1)} %shard_map.188.refs_2_), channel_id=1, source_target_pairs={{0,2},{1,3},{4,6},{5,7},{8,10},{9,11},{12,14},{13,15},{16,18},{17,... | collective-permute-start | bytes 442376 | tf_op jit(solution)/shard_map/ppermute | solution.py:863
  21.6 6.4 %copy-start.8 = (bf16[1,512,512]{2,1,0:T(8,128)(2,1)S(1)}, bf16[1,512,512]{2,1,0:T(8,128)(2,1)}, u32[]{:S(2)}) copy-start(bf16[1,512,512]{2,1,0:T(8,128)(2,1)} %param.21) | copy-start | bytes 1572868
  21.6 6.4 %copy-start.9 = (bf16[512,512]{1,0:T(8,128)(2,1)S(1)}, bf16[512,512]{1,0:T(8,128)(2,1)}, u32[]{:S(2)}) copy-start(bf16[512,512]{1,0:T(8,128)(2,1)} %refs_10_.3) | copy-start | bytes 1572868
  21.7 6.4 %copy-start.10 = (bf16[1,512,512]{2,1,0:T(8,128)(2,1)S(1)}, bf16[1,512,512]{2,1,0:T(8,128)(2,1)}, u32[]{:S(2)}) copy-start(bf16[1,512,512]{2,1,0:T(8,128)(2,1)} %param.11) | copy-start | bytes 1572868
  21.7 6.4 %copy-start.12 = (f32[512]{0:T(512)S(1)}, f32[512]{0:T(512)}, u32[]{:S(2)}) copy-start(f32[512]{0:T(512)} %param.18) | copy-start | bytes 6148
  21.7 6.4 %copy-start.13 = (f32[512]{0:T(512)S(1)}, f32[512]{0:T(512)}, u32[]{:S(2)}) copy-start(f32[512]{0:T(512)} %param.17) | copy-start | bytes 6148
  34.0 11.1 %collective-permute-start.6 = (bf16[512,1024]{1,0:T(8,128)(2,1)S(1)}, bf16[512,1024]{1,0:T(8,128)(2,1)S(1)}, u32[]{:S(2)}, u32[]{:S(2)}) collective-permute-start(bf16[512,1024]{1,0:T(8,128)(2,1)S(1)} %get-tuple-element.110), channel_id=1, source_target_pairs={{0,1},{1,0},{2,3},{3,2},{4,5},{5,4},{6,7},{7,6},{8,9},{9,8},{10,11... | collective-permute-start | bytes 3145736 | tf_op jit(solution)/shard_map/ppermute | solution.py:35
  34.1 11.0 %collective-permute-start.4 = (bf16[512,1024]{1,0:T(8,128)(2,1)S(1)}, bf16[512,1024]{1,0:T(8,128)(2,1)S(1)}, u32[]{:S(2)}, u32[]{:S(2)}) collective-permute-start(bf16[512,1024]{1,0:T(8,128)(2,1)S(1)} %get-tuple-element.107), channel_id=1, source_target_pairs={{0,1},{1,0},{2,3},{3,2},{4,5},{5,4},{6,7},{7,6},{8,9},{9,8},{10,11... | collective-permute-start | bytes 3145736 | tf_op jit(solution)/shard_map/ppermute | solution.py:35
  41.7 3.4 %collective-permute-start.5 = (bf16[512,256]{1,0:T(8,128)(2,1)S(1)}, bf16[512,256]{1,0:T(8,128)(2,1)S(1)}, u32[]{:S(2)}, u32[]{:S(2)}) collective-permute-start(bf16[512,256]{1,0:T(8,128)(2,1)S(1)} %get-tuple-element.108), channel_id=1, source_target_pairs={{0,1},{1,0},{2,3},{3,2},{4,5},{5,4},{6,7},{7,6},{8,9},{9,8},{10,11... | collective-permute-start | bytes 786440 | tf_op jit(solution)/shard_map/ppermute | solution.py:35
  46.5 19.5 %collective-permute-start.10 = (bf16[8,32,1152]{2,1,0:T(8,128)(2,1)S(1)}, bf16[8,32,1152]{2,1,0:T(8,128)(2,1)S(1)}, u32[]{:S(2)}, u32[]{:S(2)}) collective-permute-start(bf16[8,32,1152]{2,1,0:T(8,128)(2,1)S(1)} %get-tuple-element.112.refs_9_), channel_id=1, source_target_pairs={{0,4},{2,6},{4,0},{6,2},{8,12},{10,14},{12,8},{14,10},{16,20},{18,... | collective-permute-start | bytes 1769480 | tf_op jit(solution)/shard_map/ppermute | solution.py:726
  48.1 18.0 %collective-permute-start.9 = (bf16[8,32,1152]{2,1,0:T(8,128)(2,1)S(1)}, bf16[8,32,1152]{2,1,0:T(8,128)(2,1)S(1)}, u32[]{:S(2)}, u32[]{:S(2)}) collective-permute-start(bf16[8,32,1152]{2,1,0:T(8,128)(2,1)S(1)} %get-tuple-element.111.refs_8_), channel_id=1, source_target_pairs={{0,2},{2,0},{4,6},{6,4},{8,10},{10,8},{12,14},{14,12},{16,18},{18,... | collective-permute-start | bytes 1769480 | tf_op jit(solution)/shard_map/ppermute | solution.py:726
  54.0 1.4 %collective-permute-start.7 = (bf16[576,128]{1,0:T(8,128)(2,1)S(1)}, bf16[576,128]{1,0:T(8,128)(2,1)S(1)}, u32[]{:S(2)}, u32[]{:S(2)}) collective-permute-start(bf16[576,128]{1,0:T(8,128)(2,1)S(1)} %get-tuple-element.119.refs_1_), channel_id=1, source_target_pairs={{0,1},{1,0},{2,3},{3,2},{4,5},{5,4},{6,7},{7,6},{8,9},{9,8},{10,11... | collective-permute-start | bytes 442376 | tf_op jit(solution)/shard_map/ppermute | solution.py:35
  56.0 13.9 %collective-permute-start.8 = (bf16[576,128]{1,0:T(8,128)(2,1)S(1)}, bf16[576,128]{1,0:T(8,128)(2,1)S(1)}, u32[]{:S(2)}, u32[]{:S(2)}) collective-permute-start(bf16[576,128]{1,0:T(8,128)(2,1)S(1)} %shard_map.196.refs_7_), channel_id=1, source_target_pairs={{2,0},{3,1},{6,4},{7,5},{10,8},{11,9},{14,12},{15,13},{18,16},{19,... | collective-permute-start | bytes 442376 | tf_op jit(solution)/shard_map/ppermute | solution.py:907
  66.1 3.9 %copy-start = (bf16[512,2048]{1,0:T(8,128)(2,1)S(1)}, bf16[512,2048]{1,0:T(8,128)(2,1)}, u32[]{:S(2)}) copy-start(bf16[512,2048]{1,0:T(8,128)(2,1)} %refs_10_.5) | copy-start | bytes 6291460
  66.1 3.9 %copy-start.3 = (f32[512,512]{1,0:T(8,128)S(1)}, f32[512,512]{1,0:T(8,128)}, u32[]{:S(2)}) copy-start(f32[512,512]{1,0:T(8,128)} %get-tuple-element.120.refs_3_) | copy-start | bytes 3145732
  66.1 3.9 %copy-start.4 = (bf16[512,512]{1,0:T(8,128)(2,1)S(1)}, bf16[512,512]{1,0:T(8,128)(2,1)}, u32[]{:S(2)}) copy-start(bf16[512,512]{1,0:T(8,128)(2,1)} %get-tuple-element.121.refs_6_) | copy-start | bytes 1572868
  66.8 15.3 %collective-permute-start.11 = (bf16[4,32,1152]{2,1,0:T(8,128)(2,1)S(1)}, bf16[4,32,1152]{2,1,0:T(8,128)(2,1)S(1)}, u32[]{:S(2)}, u32[]{:S(2)}) collective-permute-start(bf16[4,32,1152]{2,1,0:T(8,128)(2,1)S(1)} %get-tuple-element.124.refs_11_), channel_id=1, source_target_pairs={{0,4},{2,6},{4,0},{6,2},{8,12},{10,14},{12,8},{14,10},{16,20},{18,... | collective-permute-start | bytes 884744 | tf_op jit(solution)/shard_map/ppermute | solution.py:726
  67.3 14.8 %collective-permute-start.12 = (bf16[4,32,1152]{2,1,0:T(8,128)(2,1)S(1)}, bf16[4,32,1152]{2,1,0:T(8,128)(2,1)S(1)}, u32[]{:S(2)}, u32[]{:S(2)}) collective-permute-start(bf16[4,32,1152]{2,1,0:T(8,128)(2,1)S(1)} %get-tuple-element.125.refs_12_), channel_id=1, source_target_pairs={{0,2},{2,0},{4,6},{6,4},{8,10},{10,8},{12,14},{14,12},{16,18},{18,... | collective-permute-start | bytes 884744 | tf_op jit(solution)/shard_map/ppermute | solution.py:726
  73.5 16.1 %collective-permute-start.13 = (bf16[512,1024]{1,0:T(8,128)(2,1)S(1)}, bf16[512,1024]{1,0:T(8,128)(2,1)S(1)}, u32[]{:S(2)}, u32[]{:S(2)}) collective-permute-start(bf16[512,1024]{1,0:T(8,128)(2,1)S(1)} %get-tuple-element.126.refs_7_), channel_id=1, source_target_pairs={{0,1},{1,0},{2,3},{3,2},{4,5},{5,4},{6,7},{7,6},{8,9},{9,8},{10,11... | collective-permute-start | bytes 3145736 | tf_op jit(solution)/shard_map/ppermute | solution.py:35
  82.1 2.1 %copy-start.14 = (f32[512]{0:T(512)S(1)}, f32[512]{0:T(512)}, u32[]{:S(2)}) copy-start(f32[512]{0:T(512)} %param.13) | copy-start | bytes 6148
  82.5 11.4 %collective-permute-start.20 = (bf16[2,32,2304]{2,1,0:T(8,128)(2,1)S(1)}, bf16[2,32,2304]{2,1,0:T(8,128)(2,1)S(1)}, u32[]{:S(2)}, u32[]{:S(2)}) collective-permute-start(bf16[2,32,2304]{2,1,0:T(8,128)(2,1)S(1)} %get-tuple-element.132.refs_16_), channel_id=1, source_target_pairs={{0,8},{2,10},{4,12},{6,14},{8,0},{10,2},{12,4},{14,6},{16,24},{18,... | collective-permute-start | bytes 884744 | tf_op jit(solution)/shard_map/ppermute | solution.py:726
  90.3 9.9 %collective-permute-start.14 = (bf16[4,32,1152]{2,1,0:T(8,128)(2,1)S(1)}, bf16[4,32,1152]{2,1,0:T(8,128)(2,1)S(1)}, u32[]{:S(2)}, u32[]{:S(2)}) collective-permute-start(bf16[4,32,1152]{2,1,0:T(8,128)(2,1)S(1)} %get-tuple-element.137), channel_id=1, source_target_pairs={{0,2},{2,0},{4,6},{6,4},{8,10},{10,8},{12,14},{14,12},{16,18},{18,... | collective-permute-start | bytes 884744 | tf_op jit(solution)/shard_map/ppermute | solution.py:726
  91.0 9.2 %collective-permute-start.15 = (bf16[4,32,1152]{2,1,0:T(8,128)(2,1)S(1)}, bf16[4,32,1152]{2,1,0:T(8,128)(2,1)S(1)}, u32[]{:S(2)}, u32[]{:S(2)}) collective-permute-start(bf16[4,32,1152]{2,1,0:T(8,128)(2,1)S(1)} %get-tuple-element.138), channel_id=1, source_target_pairs={{0,4},{2,6},{4,0},{6,2},{8,12},{10,14},{12,8},{14,10},{16,20},{18,... | collective-permute-start | bytes 884744 | tf_op jit(solution)/shard_map/ppermute | solution.py:726
  92.0 14.8 %collective-permute-start.16 = (bf16[4,32,1152]{2,1,0:T(8,128)(2,1)S(1)}, bf16[4,32,1152]{2,1,0:T(8,128)(2,1)S(1)}, u32[]{:S(2)}, u32[]{:S(2)}) collective-permute-start(bf16[4,32,1152]{2,1,0:T(8,128)(2,1)S(1)} %get-tuple-element.139), channel_id=1, source_target_pairs={{0,6},{2,4},{4,2},{6,0},{8,14},{10,12},{12,10},{14,8},{16,22},{18,... | collective-permute-start | bytes 884744 | tf_op jit(solution)/shard_map/ppermute | solution.py:726
  94.1 17.5 %collective-permute-start.21 = (bf16[1,32,2304]{2,1,0:T(8,128)(2,1)S(1)}, bf16[1,32,2304]{2,1,0:T(8,128)(2,1)S(1)}, u32[]{:S(2)}, u32[]{:S(2)}) collective-permute-start(bf16[1,32,2304]{2,1,0:T(8,128)(2,1)S(1)} %get-tuple-element.146), channel_id=1, source_target_pairs={{0,16},{2,18},{4,20},{6,22},{8,24},{10,26},{12,28},{14,30},{16,0},... | collective-permute-start | bytes 442376 | tf_op jit(solution)/shard_map/ppermute | solution.py:726
  107.2 5.2 %collective-permute-start.17 = (bf16[1,32,1152]{2,1,0:T(8,128)(2,1)S(1)}, bf16[1,32,1152]{2,1,0:T(8,128)(2,1)S(1)}, u32[]{:S(2)}, u32[]{:S(2)}) collective-permute-start(bf16[1,32,1152]{2,1,0:T(8,128)(2,1)S(1)} %get-tuple-element.141), channel_id=1, source_target_pairs={{0,8},{2,10},{4,12},{6,14},{8,0},{10,2},{12,4},{14,6},{16,24},{18,... | collective-permute-start | bytes 221192 | tf_op jit(solution)/shard_map/ppermute | solution.py:726
  107.7 9.0 %collective-permute-start.18 = (bf16[1,32,1152]{2,1,0:T(8,128)(2,1)S(1)}, bf16[1,32,1152]{2,1,0:T(8,128)(2,1)S(1)}, u32[]{:S(2)}, u32[]{:S(2)}) collective-permute-start(bf16[1,32,1152]{2,1,0:T(8,128)(2,1)S(1)} %get-tuple-element.142), channel_id=1, source_target_pairs={{0,16},{2,18},{4,20},{6,22},{8,24},{10,26},{12,28},{14,30},{16,0},... | collective-permute-start | bytes 221192 | tf_op jit(solution)/shard_map/ppermute | solution.py:726
  110.3 6.4 %collective-permute-start.19 = (bf16[1,32,1152]{2,1,0:T(8,128)(2,1)S(1)}, bf16[1,32,1152]{2,1,0:T(8,128)(2,1)S(1)}, u32[]{:S(2)}, u32[]{:S(2)}) collective-permute-start(bf16[1,32,1152]{2,1,0:T(8,128)(2,1)S(1)} %get-tuple-element.143), channel_id=1, source_target_pairs={{0,24},{2,26},{4,28},{6,30},{8,16},{10,18},{12,20},{14,22},{16,8},... | collective-permute-start | bytes 221192 | tf_op jit(solution)/shard_map/ppermute | solution.py:726
  116.8 1.4 %collective-permute-start.22 = (bf16[1,32,1152]{2,1,0:T(8,128)(2,1)S(1)}, bf16[1,32,1152]{2,1,0:T(8,128)(2,1)S(1)}, u32[]{:S(2)}, u32[]{:S(2)}) collective-permute-start(bf16[1,32,1152]{2,1,0:T(8,128)(2,1)S(1)} %shard_map.207.refs_0_), channel_id=1, source_target_pairs={{0,1},{1,0},{2,3},{3,2},{4,5},{5,4},{6,7},{7,6},{8,9},{9,8},{10,11... | collective-permute-start | bytes 221192 | tf_op jit(solution)/shard_map/ppermute | solution.py:35
  116.9 1.3 %collective-permute-start.23 = (bf16[32,256]{1,0:T(8,128)(2,1)S(1)}, bf16[32,256]{1,0:T(8,128)(2,1)S(1)}, u32[]{:S(2)}, u32[]{:S(2)}) collective-permute-start(bf16[32,256]{1,0:T(8,128)(2,1)S(1)} %get-tuple-element.147.refs_4_.refs_2_), channel_id=1, source_target_pairs={{0,1},{1,0},{2,3},{3,2},{4,5},{5,4},{6,7},{7,6},{8,9},{9,8},{10,11... | collective-permute-start | bytes 49160 | tf_op jit(solution)/shard_map/ppermute | solution.py:35

commit v2 on v1

v2 whole, which is shorter than its diff:
```python
import functools

import jax
import jax.numpy as jnp
from jax import lax
from jax.experimental import pallas as pl
from jax.experimental.pallas import tpu as pltpu
from jax.sharding import PartitionSpec as P

HEADS = 8
HEAD = 64
EPSILON = 1e-05
BF = jnp.bfloat16
F32 = jnp.float32
GELU_A = 0.7978845608028654
GELU_B = 0.044715
SCALE = HEAD**-0.5
SIDE = HEADS // 2
PACK = HEADS * HEAD + 64


def nn(a, b):
    return lax.dot_general(a, b, (((1,), (0,)), ((), ())), preferred_element_type=F32)


def nt(a, b):
    return lax.dot_general(a, b, (((1,), (1,)), ((), ())), preferred_element_type=F32)


def tn(a, b):
    return lax.dot_general(a, b, (((0,), (0,)), ((), ())), preferred_element_type=F32)


def swap(a, axis, bit):
    size = lax.axis_size(axis)
    return lax.ppermute(a, axis, [(i, i ^ bit) for i in range(size)])


ANY = pl.BlockSpec(memory_space=pl.ANY)


def call(body, grid, in_specs, out_specs, out_shape, scratch=(), us=1.0, after=(), vmem=20):
    count = len(in_specs)

    def run(*refs):
        body(*refs[:count], *refs[count + len(after) :])

    def start(*operands):
        return pl.pallas_call(
            run,
            grid=grid,
            in_specs=list(in_specs) + [ANY] * len(after),
            out_specs=out_specs,
            out_shape=out_shape,
            scratch_shapes=list(scratch),
            cost_estimate=pl.CostEstimate(flops=int(us * 1.15e9), bytes_accessed=2**20, transcendentals=0),
            compiler_params=pltpu.CompilerParams(vmem_limit_bytes=vmem * 2**20),
        )(*operands, *after)

    return start


def whole(shape):
    return pl.BlockSpec(shape, lambda *_: (0,) * len(shape))


VM = pl.BlockSpec(memory_space=pltpu.MemorySpace.VMEM)


def shape(dtype, *dims):
    return jax.ShapeDtypeStruct(dims, dtype)


SMEM = pl.BlockSpec(memory_space=pltpu.SMEM)


def shard_of():
    return lax.axis_index("seq") * 2 + lax.axis_index("ffn")


def doc_begin_row(starts_ref, length):
    begin = shard_of() * length
    place = lax.broadcasted_iota(jnp.int32, (1, length), 1)
    row = jnp.full((1, length), -(2**30), jnp.int32)
    for j in range(starts_ref.shape[1]):
        s = starts_ref[0, j] - begin
        row = jnp.where(place >= s, jnp.maximum(row, s), row)
    return row


def passes(starts_ref, which, length):
    hit = jnp.int32(0)
    for j in range(starts_ref.shape[1]):
        s = starts_ref[0, j]
        hit = hit | ((s >= which * length) & (s < which * length + length)).astype(jnp.int32)
    return 1.0 - hit.astype(F32)


def visible(doc_row, length):
    i = lax.broadcasted_iota(jnp.int32, (length, length), 0)
    t = lax.broadcasted_iota(jnp.int32, (length, length), 1)
    return jnp.where((i <= t) & (i >= doc_row), 1.0, 0.0).astype(BF)


def tail_row(doc_row, length):
    place = lax.broadcasted_iota(jnp.int32, (1, length), 1)
    last = doc_row[:, length - 1 :]
    return jnp.where(place >= last, 1.0, 0.0)


def pack_totals(pack_ref, totals8):
    base = HEADS * HEAD
    hi = totals8.astype(BF)
    lo = (totals8 - hi.astype(F32)).astype(BF)
    for a in range(4):
        cols = slice(128 * a, 128 * a + 128)
        pack_ref[base + 16 * a : base + 16 * a + 16, :] = jnp.concatenate(
            [hi[:, cols], lo[:, cols]], axis=0
        )


def unpack(rows, totals8_of):
    base = HEADS * HEAD
    out = []
    for a in range(4):
        block = totals8_of(slice(base + 16 * a, base + 16 * a + 16))
        out.append(block[:8] + block[8:])
    return rows(slice(0, base)), jnp.concatenate(out, axis=1)


def combine_body(backward, length, starts_ref, own_ref, partner_ref, out_ref):
    first = 2 * lax.axis_index("seq")
    is_first = (lax.axis_index("ffn") == 0).astype(F32)
    base = HEADS * HEAD
    if backward:
        p = passes(starts_ref, first, length)
        own_by, partner_by = is_first + (1 - is_first) * p, is_first * p + (1 - is_first)
    else:
        p = passes(starts_ref, first + 1, length)
        own_by, partner_by = is_first * p + (1 - is_first), is_first + (1 - is_first) * p

    def sum_of(at):
        return own_ref[at, :].astype(F32) * own_by + partner_ref[at, :].astype(F32) * partner_by

    memory, totals8 = unpack(sum_of, sum_of)
    out_ref[:base, :] = memory.astype(BF)
    pack_totals(out_ref, totals8)


def combine(backward, length, starts, own, partner, after=()):
    return call(
        functools.partial(combine_body, backward, length),
        (),
        [SMEM, VM, VM],
        VM,
        shape(BF, PACK, 128),
        after=after,
    )(starts, own, partner)


def arrived(backward, length, starts_ref, partner_ref, far_ref, mem_ref, totals_ref):
    first = 2 * lax.axis_index("seq")
    is_first = (lax.axis_index("ffn") == 0).astype(F32)
    if backward:
        p = passes(starts_ref, first + 1, length)
        far_by, partner_by = is_first * p + (1 - is_first), is_first
        valid = lax.axis_index("seq") == 0
    else:
        p = passes(starts_ref, first, length)
        far_by, partner_by = is_first + (1 - is_first) * p, 1 - is_first
        valid = lax.axis_index("seq") == 1

    def sum_of(at):
        far = jnp.where(valid, far_ref[at, :].astype(F32), 0.0)
        return far * far_by + partner_ref[at, :].astype(F32) * partner_by

    memory, totals8 = unpack(sum_of, sum_of)
    mem_ref[...] = memory.astype(BF)
    totals_ref[...] = totals8.T


def head_of(own_side, h):
    ffn = lax.axis_index("ffn")
    return (ffn if own_side else 1 - ffn) * SIDE + h


def head_rows(head):
    return pl.ds(pl.multiple_of(head * HEAD, HEAD), HEAD)


def project_body(x_hbm, gain_hbm, bias_hbm, w_hbm, starts_ref,
                 heads_ref, control_ref, xnt_ref, pack_ref, mask_ref,
                 x_ref, gain_ref, bias_ref, w_ref, sems):
    length, width = x_ref.shape
    copies = [
        pltpu.make_async_copy(x_hbm, x_ref, sems.at[0]),
        pltpu.make_async_copy(gain_hbm, gain_ref, sems.at[1]),
        pltpu.make_async_copy(bias_hbm, bias_ref, sems.at[2]),
    ]
    columns = [
        pltpu.make_async_copy(w_hbm.at[:, pl.ds(j * width, width)], w_ref.at[j], sems.at[3 + j])
        for j in range(4)
    ]
    for copy in copies + columns:
        copy.start()
    mask_ref[...] = visible(doc_begin_row(starts_ref, length), length)
    for copy in copies:
        copy.wait()
    x = x_ref[...].astype(F32)
    mean = jnp.mean(x, axis=-1, keepdims=True)
    centered = x - mean
    inverse = lax.rsqrt(jnp.mean(centered * centered, axis=-1, keepdims=True) + EPSILON)
    xn = (centered * inverse * gain_ref[...] + bias_ref[...]).astype(BF)
    xnt_ref[...] = xn.T
    for j in range(3):
        columns[j].wait()
        t = nn(xn, w_ref[j]).astype(BF).T
        for h in range(HEADS):
            heads_ref[h, j * HEAD : j * HEAD + HEAD, :] = t[h * HEAD : h * HEAD + HEAD]
    columns[3].wait()
    control = jnp.exp(nn(xn, w_ref[3])).T
    control_ref[...] = control
    c = control.astype(BF)
    tail = tail_row(doc_begin_row(starts_ref, length), length)
    c_tail = c * tail.astype(BF)
    for h in range(HEADS):
        rows = slice(h * HEAD, h * HEAD + HEAD)
        heads_ref[h, 3 * HEAD :, :] = c[rows]
        mem_k = nt(c_tail[rows], heads_ref[h, HEAD : 2 * HEAD, :])
        mem_vt = nt(heads_ref[h, 2 * HEAD : 3 * HEAD, :], c_tail[rows])
        pack_ref[rows, :] = jnp.concatenate([mem_k, mem_vt], axis=1).astype(BF)
    tail8 = jnp.broadcast_to(tail, (8, length)).astype(BF)
    pack_totals(pack_ref, nt(tail8, c))


def project(x, gain, bias, w, starts):
    length, width = x.shape
    hbm = pl.BlockSpec(memory_space=pltpu.MemorySpace.HBM)
    return call(
        project_body,
        (),
        [hbm, hbm, hbm, hbm, SMEM],
        [VM] * 5,
        [
            shape(BF, HEADS, 4 * HEAD, length), shape(F32, width, length), shape(BF, width, length),
            shape(BF, PACK, 128), shape(BF, length, length),
        ],
        [
            pltpu.VMEM((length, width), BF), pltpu.VMEM((1, width), F32), pltpu.VMEM((1, width), F32),
            pltpu.VMEM((4, width, width), BF), pltpu.SemaphoreType.DMA((7,)),
        ],
        us=4.3,
        vmem=48,
    )(*(pltpu.with_memory_space_constraint(a, pltpu.HBM) for a in (x, gain, bias, w, starts)))


def parts(heads_ref, head):
    return [heads_ref[head, j * HEAD : j * HEAD + HEAD, :] for j in range(4)]


def mask_pair(mask_ref):
    half = mask_ref.shape[0] // 2
    return mask_ref[:half, :half], mask_ref[:, half:]


def causal_pairs(left, right, mask_ref):
    half = mask_ref.shape[0] // 2
    early, late = mask_pair(mask_ref)
    rows = left.T
    return nn(rows[:half], right[:, :half]).astype(BF) * early, nn(rows, right[:, half:]).astype(BF) * late


def causal_sum(left, pairs):
    a, b = pairs
    half = a.shape[0]
    return jnp.concatenate([nn(left[:, :half], a), nn(left, b)], axis=1)


def causal_back(pairs, right):
    a, b = pairs
    half = a.shape[0]
    late = nn(b, right[half:])
    return jnp.concatenate([late[:half] + nn(a, right[:half]), late[half:]], axis=0)


def padded(rows, second):
    zero = jnp.zeros_like(rows)
    return jnp.concatenate([zero, rows] if second else [rows, zero], axis=0).T


def pair_shapes(length, count=SIDE):
    half = length // 2
    return [shape(BF, count, half, half), shape(BF, count, length, half)]


def store_pairs(refs, i, pairs):
    refs[0][i], refs[1][i] = pairs


def load_pairs(refs, i):
    return refs[0][i], refs[1][i]


def local_body(own_side, heads_ref, mask_ref, number_ref, total_ref, *pair_refs):
    for i in range(SIDE):
        q, k, v, c = parts(heads_ref, head_of(own_side, i))
        pairs = causal_pairs(k, q, mask_ref)
        store_pairs(pair_refs, i, pairs)
        number_ref[i * HEAD : i * HEAD + HEAD, :] = causal_sum(c, pairs)
    c = jnp.concatenate([parts(heads_ref, head_of(own_side, i))[3] for i in range(SIDE)], axis=0)
    total_ref[...] = causal_sum(c, mask_pair(mask_ref))


def local_sums(own_side, heads, mask, after=()):
    length = heads.shape[2]
    return call(
        functools.partial(local_body, own_side),
        (),
        [VM, VM],
        [VM] * 4,
        [shape(F32, SIDE * HEAD, length)] * 2 + pair_shapes(length),
        us=3.0,
        after=after,
    )(heads, mask)


def enters_row(starts_ref, length):
    return jnp.where(doc_begin_row(starts_ref, length) < 0, 1.0, 0.0)


def mix_body(starts_ref, heads_ref, mask_ref, partner_ref, far_ref, *refs):
    refs = list(refs)
    take = lambda n: [refs.pop(0) for _ in range(n)]
    ins = [take(2), take(2)]
    mixed_ref, mem_ref = take(2)
    outs = [take(5), take(5)]
    (totals_ref,) = refs
    length = heads_ref.shape[2]
    arrived(False, length, starts_ref, partner_ref, far_ref, mem_ref, totals_ref)
    enters = enters_row(starts_ref, length)
    for own_side in (False, True):
        number_in, total_in = ins[own_side]
        number_ref, inverse_ref, weight_ref, *link_refs = outs[own_side]
        for i in range(SIDE):
            head, at = head_of(own_side, i), slice(i * HEAD, i * HEAD + HEAD)
            q, k, v, c = parts(heads_ref, head)
            mem = mem_ref[head_rows(head), :]
            mem_k, mem_vt = mem[:, :HEAD], mem[:, HEAD:]
            number = number_in[at, :] + enters * nn(mem_k, q)
            inverse = 1.0 / (total_in[at, :] + enters * totals_ref[head_rows(head), 0:1])
            score = number * (inverse * SCALE)
            e = jnp.exp(score - jnp.max(score, axis=0, keepdims=True))
            weight = e / jnp.sum(e, axis=0, keepdims=True)
            number_ref[at, :] = number
            inverse_ref[at, :] = inverse
            weight_ref[at, :] = weight
            spread = (weight * inverse).astype(BF)
            links = causal_pairs(c, spread, mask_ref)
            store_pairs(link_refs, i, links)
            mixed = causal_sum(v, links) + enters * nn(mem_vt, spread)
            mixed_ref[head_rows(head), :] = mixed.astype(BF)


def mix(starts, heads, mask, partner, far, local_other, local_own):
    length, width = heads.shape[2], HEADS * HEAD
    side = [shape(F32, SIDE * HEAD, length)] * 3 + pair_shapes(length)
    mixed, mem, *rest = call(
        mix_body,
        (),
        [SMEM] + [VM] * 8,
        [VM] * 12,
        [shape(BF, width, length), shape(BF, width, 128)] + side + side,
        [pltpu.VMEM((width, 8), F32)],
        us=4.0,
    )(starts, heads, mask, partner, far, *local_other, *local_own)
    return mixed, mem, rest[:5], rest[5:]


def feed_step(j, xn, cot, xnt, cott, up_ref, down_ref, gup_ref, gdown_ref):
    cols = slice(j * 512, j * 512 + 512)
    up, down = up_ref[:, cols], down_ref[:, cols]
    pre = nn(xn, up)
    v2 = pre * pre
    th = jnp.tanh(GELU_A * pre * (1.0 + GELU_B * v2))
    half = 0.5 * (1.0 + th)
    hidden = (pre * half).astype(BF)
    slope = half + 0.5 * pre * (1.0 - th * th) * (GELU_A * (1.0 + 3.0 * GELU_B * v2))
    grad_pre = (nn(cot, down) * slope).astype(BF)
    gdown_ref[:, cols] = nn(cott, hidden).astype(BF)
    gup_ref[:, cols] = nn(xnt, grad_pre).astype(BF)
    return nt(hidden, down), nt(grad_pre, up)


def feed_other_body(x_ref, mixed_ref, cot_ref, w_out_ref, gain_ref, bias_ref, up_ref, down_ref,
                    gup_ref, gdown_ref, hidden1_ref, n_ref, inv_ref, xn_ref, xnt_ref, cott_ref,
                    part_ref, d_ref):
    hidden1 = x_ref[...].astype(F32) + tn(mixed_ref[...], w_out_ref[...])
    hidden1_ref[...] = hidden1
    mean = jnp.mean(hidden1, axis=-1, keepdims=True)
    centered = hidden1 - mean
    inverse = lax.rsqrt(jnp.mean(centered * centered, axis=-1, keepdims=True) + EPSILON)
    n = centered * inverse
    n_ref[...] = n
    inv_ref[...] = jnp.broadcast_to(inverse, inv_ref.shape)
    xn_ref[...] = (n * gain_ref[...] + bias_ref[...]).astype(BF)
    xnt_ref[...] = xn_ref[...].T
    cott_ref[...] = cot_ref[...].T
    for j in range(up_ref.shape[1] // 512):
        part, d = feed_step(j, xn_ref[...], cot_ref[...], xnt_ref[...], cott_ref[...],
                            up_ref, down_ref, gup_ref, gdown_ref)
        part_ref[...] = part if j == 0 else part_ref[...] + part
        d_ref[...] = d if j == 0 else d_ref[...] + d


def feed_own_body(hidden1_ref, n_ref, inv_ref, xn_ref, xnt_ref, cott_ref, part_ref, d_in_ref,
                  mixed_ref, cot_ref, w_out_ref, gain_ref, up_ref, down_ref,
                  output_ref, d_hidden1_ref, g_ref, out_send_ref, out_keep_ref, norms_ref,
                  gup_ref, gdown_ref, sum_ref, d_ref):
    for j in range(up_ref.shape[1] // 512):
        part, d = feed_step(j, xn_ref[...], cot_ref[...], xnt_ref[...], cott_ref[...],
                            up_ref, down_ref, gup_ref, gdown_ref)
        sum_ref[...] = (part_ref[...] if j == 0 else sum_ref[...]) + part
        d_ref[...] = (d_in_ref[...] if j == 0 else d_ref[...]) + d
    output_ref[...] = (hidden1_ref[...] + sum_ref[...]).astype(BF)
    dx, n = d_ref[...], n_ref[...]
    norms_ref[...] = jnp.concatenate(
        [jnp.sum(dx * n, axis=0, keepdims=True), jnp.sum(dx, axis=0, keepdims=True)] * 4, axis=0
    )
    d_n = dx * gain_ref[...]
    d_in = (
        d_n
        - jnp.mean(d_n, axis=-1, keepdims=True)
        - n * jnp.mean(d_n * n, axis=-1, keepdims=True)
    ) * inv_ref[:, 0:1]
    d_hidden1 = cot_ref[...].astype(F32) + d_in
    d_hidden1_ref[...] = d_hidden1
    d_branch = d_hidden1.astype(BF)
    g_ref[...] = nt(w_out_ref[...], d_branch).astype(BF)
    grad_out = nn(mixed_ref[...], d_branch).astype(BF)
    half = grad_out.shape[1] // 2
    second = lax.axis_index("ffn") == 1
    out_keep_ref[...] = jnp.where(second, grad_out[:, half:], grad_out[:, :half])
    out_send_ref[...] = jnp.where(second, grad_out[:, :half], grad_out[:, half:])


def feed_other(x, mixed, cotangent, w_out, gain, bias, up, down):
    length, width = x.shape
    half, sq = shape(BF, *up.shape), lambda dt: shape(dt, length, width)
    return call(
        feed_other_body,
        (),
        [VM] * 8,
        [VM] * 10,
        [half, half, sq(F32), sq(F32), shape(F32, length, 128),
         sq(BF), sq(BF), sq(BF), sq(F32), sq(F32)],
        us=6.0,
    )(x, mixed, cotangent, w_out, gain, bias, up, down)


def feed_own(saved, mixed, cotangent, w_out, gain, up, down, after=()):
    length, width = mixed.shape
    half, sq = shape(BF, *up.shape), lambda dt: shape(dt, length, width)
    return call(
        feed_own_body,
        (),
        [VM] * 14,
        [VM] * 8,
        [sq(BF), sq(F32), sq(BF)] + [shape(BF, width, width // 2)] * 2 + [shape(F32, 8, width), half, half],
        [pltpu.VMEM((length, width), F32)] * 2,
        us=6.0,
        after=after,
    )(*saved, mixed, cotangent, w_out, gain, up, down)


def scores_back_body(own_side, starts_ref, heads_ref, mask_ref, g_ref, mem_ref, number_ref, inverse_ref, weight_ref,
                     *refs):
    if own_side:
        pack_in, sums_in, a_ref, spread_ref, d_total_ref, early_ref, late_ref, pack_ref, sums_ref = refs
        pack_ref[...] = pack_in[...]
        sums_ref[...] = sums_in[...]
    else:
        a_ref, spread_ref, d_total_ref, early_ref, late_ref, pack_ref, sums_ref = refs
    length = heads_ref.shape[2]
    enters = enters_row(starts_ref, length)
    for i in range(SIDE):
        head, at = head_of(own_side, i), slice(i * HEAD, i * HEAD + HEAD)
        rows = head_rows(head)
        q, k, v, c = parts(heads_ref, head)
        g = g_ref[rows, :]
        mem_vt = mem_ref[rows, :][:, HEAD:]
        number, inverse, weight = number_ref[at, :], inverse_ref[at, :], weight_ref[at, :]
        values = causal_pairs(v, g, mask_ref)
        store_pairs((early_ref, late_ref), i, values)
        number_v = causal_sum(c, values) + enters * tn(mem_vt, g)
        d_weight = number_v * inverse
        d_score = weight * (d_weight - jnp.sum(weight * d_weight, axis=0, keepdims=True))
        a = d_score * (inverse * SCALE)
        spread = weight * inverse
        d_total = -(a * number + spread * number_v) * inverse
        a_ref[at, :] = a.astype(BF)
        spread_ref[at, :] = spread.astype(BF)
        d_total_ref[at, :] = d_total.astype(BF)
        d_k = nt((a * enters).astype(BF), q)
        d_vt = nt(g, (spread * enters).astype(BF))
        pack_ref[rows, :] = jnp.concatenate([d_k, d_vt], axis=1).astype(BF)
        sums_ref[rows, :] = jnp.broadcast_to(jnp.sum(d_total * enters, axis=1, keepdims=True), (HEAD, 128))
    if own_side:
        pack_totals(pack_ref, sums_ref[...].T[0:8])


def scores_back(own_side, starts, heads, mask, g, mem, saved, packs=(), after=()):
    length, width = heads.shape[2], HEADS * HEAD
    sums = [] if own_side else [shape(F32, width, 128)]
    outs = [shape(BF, SIDE * HEAD, length)] * 3 + pair_shapes(length) + [shape(BF, PACK, 128)] + sums
    return call(
        functools.partial(scores_back_body, own_side),
        (),
        [SMEM] + [VM] * (7 + len(packs)),
        [VM] * len(outs),
        outs,
        [pltpu.VMEM((width, 128), F32)] if own_side else [],
        us=3.0,
        after=after,
    )(starts, heads, mask, g, mem, *saved[:3], *packs)


def heads_back_body(own_side, starts_ref, heads_ref, mask_ref, g_ref, mem_ref, a_ref, spread_ref, d_total_ref,
                    v_early, v_late, l_early, l_late, p_early, p_late, d_ref):
    length = heads_ref.shape[2]
    enters = enters_row(starts_ref, length)
    from_totals = causal_back(mask_pair(mask_ref), d_total_ref[...].T).T
    held = None
    for i in range(SIDE):
        head, at = head_of(own_side, i), slice(i * HEAD, i * HEAD + HEAD)
        rows = head_rows(head)
        q, k, v, c = parts(heads_ref, head)
        g, a, spread = g_ref[rows, :], a_ref[at, :], spread_ref[at, :]
        mem_k = mem_ref[rows, :][:, :HEAD]
        steps = causal_pairs(c, a, mask_ref)
        d_ref[i, :HEAD, :] = causal_sum(k, steps) + enters * tn(mem_k, a)
        d_ref[i, HEAD : 3 * HEAD, :] = (
            causal_back(steps, padded(q, False)) + causal_back(load_pairs((l_early, l_late), i), padded(g, True))
        ).T
        odd = i % 2 == 1
        d_control = causal_back(load_pairs((p_early, p_late), i), padded(a, odd)) + causal_back(
            load_pairs((v_early, v_late), i), padded(spread, odd)
        )
        if odd:
            two = (held + d_control).T
            for n in range(2):
                total_rows = slice((i - 1 + n) * HEAD, (i + n) * HEAD)
                d_ref[i - 1 + n, 3 * HEAD :, :] = two[n * HEAD : n * HEAD + HEAD] + from_totals[total_rows]
        held = d_control


def heads_back(own_side, starts, heads, mask, g, mem, scores, links, pairs, after=()):
    length = heads.shape[2]
    return call(
        functools.partial(heads_back_body, own_side),
        (),
        [SMEM] + [VM] * 13,
        VM,
        shape(F32, SIDE, 4 * HEAD, length),
        us=8.0 if own_side else 3.0,
        after=after,
    )(starts, heads, mask, g, mem, *scores, *links, *pairs)


def project_back_body(own_side, starts_ref, heads_ref, d_ref, control_ref, partner_ref, far_ref, xnt_ref, w_ref, *refs):
    if own_side:
        (dx_in_ref, x_ref, gain_ref, d_hidden1_ref, norms2_ref,
         grad_ref, grad_x_ref, norms_ref, mem_ref, totals_ref, proj_ref) = refs
    else:
        grad_ref, dx_ref, mem_ref, totals_ref, proj_ref = refs
    length, width = xnt_ref.shape[1], xnt_ref.shape[0]
    arrived(True, length, starts_ref, partner_ref, far_ref, mem_ref, totals_ref)
    tail = tail_row(doc_begin_row(starts_ref, length), length)
    tail_bf = tail.astype(BF)
    dx = None
    for p in range(SIDE // 2):
        for i in range(2):
            n = 2 * p + i
            head = head_of(own_side, n)
            rows = head_rows(head)
            mem = mem_ref[rows, :]
            back_k, back_vt = mem[:, :HEAD], mem[:, HEAD:]
            q, k, v, c = parts(heads_ref, head)
            c_tail = c * tail_bf
            d_q = d_ref[n, :HEAD, :]
            d_k = d_ref[n, HEAD : 2 * HEAD, :] + tn(back_k, c_tail)
            d_v = d_ref[n, 2 * HEAD : 3 * HEAD, :] + nn(back_vt, c_tail)
            d_c = d_ref[n, 3 * HEAD :, :] + tail * (
                nn(back_k, k) + tn(back_vt, v) + totals_ref[rows, 0:1]
            )
            d_c = d_c * control_ref[rows, :]
            for m, value in enumerate((d_q, d_k, d_v, d_c)):
                proj_ref[p, m * 128 + i * HEAD : m * 128 + i * HEAD + HEAD, :] = value.astype(BF)
        d_proj = proj_ref[p]
        grad_ref[:, p * 512 : p * 512 + 512] = nt(xnt_ref[...], d_proj).astype(BF)
        first = head_of(own_side, 2 * p) * HEAD
        w = jnp.concatenate(
            [w_ref[:, pl.ds(pl.multiple_of(m * width + first, 128), 128)] for m in range(4)], axis=1
        )
        dx = nn(w, d_proj) if dx is None else dx + nn(w, d_proj)
    if not own_side:
        dx_ref[...] = dx
        return
    x = x_ref[...].astype(F32)
    mean = jnp.mean(x, axis=-1, keepdims=True)
    centered = x - mean
    inverse = lax.rsqrt(jnp.mean(centered * centered, axis=-1, keepdims=True) + EPSILON)
    n = centered * inverse
    d = (dx_in_ref[...] + dx).T
    sums = [jnp.sum(d * n, axis=0, keepdims=True), jnp.sum(d, axis=0, keepdims=True)]
    rows8 = jnp.concatenate(sums + [norms2_ref[0:6, :]], axis=0)
    norms_ref[...] = jnp.concatenate([rows8, jnp.zeros((120, length), F32)], axis=0).T.astype(BF)
    d_n = d * gain_ref[...]
    grad_x_ref[...] = d_hidden1_ref[...] + (
        d_n
        - jnp.mean(d_n, axis=-1, keepdims=True)
        - n * jnp.mean(d_n * n, axis=-1, keepdims=True)
    ) * inverse


def project_back(own_side, starts, heads, d, control, partner, far, xnt, w, rest=(), after=()):
    width, length = xnt.shape
    outs = [shape(BF, width, 1024), shape(F32, length, width)]
    if own_side:
        outs.append(shape(BF, width, 128))
    return call(
        functools.partial(project_back_body, own_side),
        (),
        [SMEM] + [VM] * (7 + len(rest)),
        [VM] * len(outs),
        outs,
        [pltpu.VMEM((width, 128), BF), pltpu.VMEM((width, 8), F32), pltpu.VMEM((SIDE // 2, 512, length), BF)],
        us=5.0 if own_side else 3.5,
        after=after,
    )(starts, heads, d, control, partner, far, xnt, w, *rest)


def bit_axis(bit):
    return ("seq", 1) if bit == 0 else ("dp", 1 << (bit - 1))


def my_bit(bit):
    axis, step = bit_axis(bit)
    return (lax.axis_index(axis) // step) % 2


def send_across(a, bits):
    seqs, dps = lax.axis_size("seq"), lax.axis_size("dp")
    flip = sum(1 << bit for bit in bits)
    return lax.ppermute(a, ("dp", "seq"), [(i, i ^ flip) for i in range(seqs * dps)])


def place_of(t, places, values):
    index, rest, bit = 0, t, 0
    fixed = dict(zip(places, values))
    while rest or fixed:
        if bit in fixed:
            index = index + fixed.pop(bit) * (1 << bit)
        else:
            index = index + ((rest & 1) << bit)
            rest >>= 1
        bit += 1
    return index


def stage_body(plan, *refs):
    refs = list(refs)
    ins = [[[refs.pop(0) for _ in pieces] for pieces in arrays] for arrays, _, _ in plan]
    for (arrays, split, dtype), sources in zip(plan, ins):
        outs = [refs.pop(0) for _ in range(1 << len(split))]
        blocks = outs[0].shape[0]
        places = [place for _, place in split]
        mine = [my_bit(bit) for bit, _ in split]
        for pattern, out in enumerate(outs):
            values = [
                (1 - m) if (pattern >> n) & 1 else m for n, m in enumerate(mine)
            ]
            for t in range(blocks):
                at = place_of(t, places, values)
                total = None
                for pieces in sources:
                    row = jnp.concatenate([p[at] for p in pieces], axis=1) if len(pieces) > 1 else pieces[0][at]
                    row = row.astype(F32)
                    total = row if total is None else total + row
                out[t] = total.astype(out.dtype)


def stage(groups, after=(), dtype=BF):
    plan, operands, in_specs, out_specs, out_shape = [], [], [], [], []
    rows = groups[0][0][0][0][0].shape[1]
    steps = 2 if rows % 32 == 0 else 1
    for arrays, split in groups:
        for pieces in arrays:
            for array, first, count in pieces:
                operands.append(array)
                in_specs.append(
                    pl.BlockSpec((array.shape[0], rows // steps, count),
                                 functools.partial(lambda at, i: (0, i, at), first // count))
                )
        blocks, width = arrays[0][0][0].shape[0] >> len(split), sum(p[2] for p in arrays[0])
        plan.append(([[None] * len(pieces) for pieces in arrays], split, dtype))
        for _ in range(1 << len(split)):
            out_specs.append(pl.BlockSpec((blocks, rows // steps, width), lambda i: (0, i, 0)))
            out_shape.append(jax.ShapeDtypeStruct((blocks, rows, width), dtype))
    outs = list(
        call(functools.partial(stage_body, plan), (steps,), in_specs, out_specs, out_shape, after=after)(*operands)
    )
    result = []
    for _, split in groups:
        result.append([outs.pop(0) for _ in range(1 << len(split))])
    return result


def all_of(a):
    return [(a, 0, a.shape[2])]


def patterns(bits):
    return [[b for n, b in enumerate(bits) if (p >> n) & 1] for p in range(1, 1 << len(bits))]


def finish_body(a_ref, b_ref, up_ref, down_ref, out_ref):
    total = a_ref[0].astype(F32) + b_ref[0].astype(F32)
    half, part = up_ref.shape[1], out_ref.shape[1] // 2
    up_ref[...] = total[:, :half]
    down_ref[...] = total[:, half + part : 2 * half + part]
    out_ref[:, :part] = total[:, half : half + part].astype(BF)
    out_ref[:, part:] = total[:, 2 * half + part :].astype(BF)


def finish(a, b, half, part, after=()):
    rows = a.shape[1]
    return call(
        finish_body,
        (),
        [VM] * 2,
        [VM] * 3,
        [jax.ShapeDtypeStruct((rows, half), F32)] * 2 + [jax.ShapeDtypeStruct((rows, 2 * part), BF)],
        after=after,
    )(a, b)


def join_body(own_ref, other_ref, out_own, out_other, grad_in_ref, grad_out_ref, *norm_refs):
    second = lax.axis_index("ffn") == 1
    own, other = own_ref[0].astype(F32), other_ref[0].astype(F32)
    for f in range(2):
        keep_own = second if f else jnp.logical_not(second)
        half = jnp.where(keep_own, own[:, :1024], other[:, :1024])
        for p in range(2):
            for m in range(4):
                grad_in_ref[:, m * 512 + f * 256 + p * 128 : m * 512 + f * 256 + p * 128 + 128] = (
                    half[:, p * 512 + m * 128 : p * 512 + m * 128 + 128]
                )
        grad_out_ref[:, f * 256 : f * 256 + 256] = jnp.where(
            keep_own, out_own[...], out_other[...]
        ).astype(F32)
    norms = (own[:, 1024:] + other[:, 1024:]).T
    for n, ref in enumerate(norm_refs):
        ref[...] = norms[n]


def join(own, other, out_own, out_other):
    rows = own.shape[1]
    return call(
        join_body,
        (),
        [VM] * 4,
        [VM] * 6,
        [jax.ShapeDtypeStruct((rows, n), F32) for n in (2048, 512)] + [jax.ShapeDtypeStruct((rows,), F32)] * 4,
    )(own, other, out_own, out_other)


def on_device(tokens, doc_starts, norm1_gain, norm1_bias, in_weight, out_weight,
              norm2_gain, norm2_bias, up_own, down_own, output_cotangent):
    up_other, down_other = swap(up_own, "ffn", 1), swap(down_own, "ffn", 1)
    x, cotangent, starts = tokens[0], output_cotangent[0], doc_starts
    length, width = x.shape
    owners = lax.axis_size("dp") * lax.axis_size("seq")
    bits = owners.bit_length() - 1
    row = lambda a: a.reshape(1, width)
    blocked = lambda a: a.reshape(owners, width // owners, a.shape[1])

    heads, control, xnt, own, mask = project(x, row(norm1_gain), row(norm1_bias), in_weight, starts)
    partner = swap(own, "ffn", 1)
    number_o, total_o, *pairs_other = local_sums(False, heads, mask)
    both = combine(False, length, starts, own, partner, after=[number_o])
    far = swap(both, "seq", 1)
    number, total, *pairs_own = local_sums(True, heads, mask, after=[both])
    mixed, memory, saved_other, saved_own = mix(
        starts, heads, mask, partner, far, (number_o, total_o), (number, total))
    gup_send, gdown_send, *saved = feed_other(
        x, mixed, cotangent, out_weight, row(norm2_gain), row(norm2_bias), up_other, down_other)
    gup_got, gdown_got = swap(gup_send, "ffn", 1), swap(gdown_send, "ffn", 1)
    (output, d_hidden1, g, out_send, out_keep, norms2, gup_own, gdown_own) = feed_own(
        saved, mixed, cotangent, out_weight, row(norm2_gain), up_own, down_own)
    out_got = swap(out_send, "ffn", 1)

    out_half = width // 4
    ups, downs, outs = [
        [blocked(a) for a in pair]
        for pair in ((gup_own, gup_got), (gdown_own, gdown_got), (out_keep, out_got))
    ]
    groups = [
        [[*all_of(a), (o, 0, out_half)] for a, o in zip(ups, outs)],
        [[*all_of(a), (o, out_half, out_half)] for a, o in zip(downs, outs)],
    ]
    orders = [[1, 2], [2, 1]]
    left = [list(range(bits)) for _ in groups]

    def advance(groups, n, after):
        if n >= 2:
            if n == 2:
                groups = [[pieces_a + pieces_b for pieces_a, pieces_b in zip(*groups)]]
            bits_now = left[0][:1]
            splits = [[(bits_now[0], 0)]]
            for rest in left:
                rest.pop(0)
        else:
            bits_now = [order[n] for order in orders]
            splits = [[(bit, rest.index(bit))] for bit, rest in zip(bits_now, left)]
            for bit, rest in zip(bits_now, left):
                rest.remove(bit)
        outs = stage(list(zip(groups, splits)), after=after)
        got = [send_across(sent, [bit]) for (_, sent), bit in zip(outs, bits_now)]
        sent = [s for _, s in outs]
        return [[all_of(kept), all_of(r)] for (kept, _), r in zip(outs, got)], sent

    back = (starts, heads, mask, g, memory)
    *scores_other, pack, sums = scores_back(False, *back, saved_other)
    groups, sent = advance(groups, 0, [pack])
    *scores_own, d_own = scores_back(True, *back, saved_own, packs=(pack, sums), after=sent)
    d_partner = swap(d_own, "ffn", 1)
    d_both = combine(True, length, starts, d_own, d_partner)
    d_far = swap(d_both, "seq", 1)
    side = (control, d_partner, d_far, xnt, in_weight)
    d_other = heads_back(False, *back, scores_other, saved_other[3:], pairs_other, after=[d_both])
    groups, sent = advance(groups, 1, [d_other])
    in_send, dx = project_back(False, starts, heads, d_other, *side, after=sent)
    in_got = swap(in_send, "ffn", 1)
    d_mine = heads_back(True, *back, scores_own, saved_own[3:], pairs_own, after=[in_send])
    groups, sent = advance(groups, 2, [d_mine])
    in_keep, grad_tokens, norms = project_back(
        True, starts, heads, d_mine, *side,
        rest=(dx, x, row(norm1_gain), d_hidden1, norms2), after=sent)

    late = [
        all_of(blocked(in_keep)) + all_of(blocked(norms)),
        all_of(blocked(in_got)) + all_of(jnp.zeros_like(blocked(norms))),
    ]
    rest = list(range(bits))
    first = True
    while rest:
        now = rest[:2]
        split = [(b, rest.index(b)) for b in now]
        rest = rest[2:]
        (kept, *sent), = stage([(late, split)])
        late = [all_of(kept)] + [all_of(send_across(s, p)) for s, p in zip(sent, patterns(now))]
        if first:
            first, token = False, [kept]
            for n in range(3, bits):
                groups, token = advance(groups, n, token)
    grad_up, grad_down, out = finish(*(a[0][0] for a in groups[0]), gup_own.shape[1], out_half, after=[kept])
    (final,), = stage([(late, [])], after=[out])
    grad_in, grad_out, *norms = join(final, swap(final, "ffn", 1), out, swap(out, "ffn", 1))
    return (output[None], grad_tokens[None], grad_in, grad_out, grad_up, grad_down, *norms)


def solution(mesh):
    rows = P("dp", ("seq", "ffn"), None)
    owned = P(("dp", "seq"))
    return jax.shard_map(
        on_device,
        mesh=mesh,
        in_specs=(
            rows, P("dp", None), P(), P(), P(), P(), P(), P(),
            P(None, "ffn"), P(None, "ffn"), rows,
        ),
        out_specs=(
            rows, rows, P(("dp", "seq"), None), P(("dp", "seq"), None),
            P(("dp", "seq"), "ffn"), P(("dp", "seq"), "ffn"),
            owned, owned, owned, owned,
        ),
        check_vma=False,
    )
```

time: 119 us -> 98.3 us (0.83)
  Pallas kernels: 70.9 us -> 48.9 us
  waiting for transfers between devices: 17.2 us -> 23.7 us
  starting transfers between devices: 28.1 us -> 24.4 us
  local copies, waits for them, and re-layouts: 1.67 us -> 0.06 us
    pallas_call x23, Pallas kernels: 70.9 us -> 48.9 us  [start(): pl.pallas_call(run, grid=grid, in_specs=list(in_specs) + [ANY] * len(afte...]
    ppermute x2 -> x0, starting transfers between devices: 6.18 us -> none  [the longest x1 4.67 us: on_device(): far = lax.ppermute(both, 'seq', [(0, 1)])]
    ppermute x10 -> x12, starting transfers between devices: 2.38 us -> 6.74 us  [swap(): return lax.ppermute(a, axis, [(i, i ^ bit) for i in range(size)])]
    ppermute x12, waiting for transfers between devices: 14.4 us -> 18.6 us  [send_across(): lax.ppermute(a, ('dp', 'seq'), [(i, i ^ flip) for i in range(seqs * dps)])]
    ppermute x10 -> x12, waiting for transfers between devices: 2.22 us -> 5.18 us  [swap(): return lax.ppermute(a, axis, [(i, i ^ bit) for i in range(size)])]
    ppermute x12, starting transfers between devices: 19.6 us -> 17.7 us  [send_across(): lax.ppermute(a, ('dp', 'seq'), [(i, i ^ flip) for i in range(seqs * dps)])]
    unnamed x30 -> x20, local copies, waits for them, and re-layouts: 1.65 us -> 0.04 us
  transfers between devices with their start and end apart: 24 -> 24, of which waited for: 6 -> 10; matrix products, arithmetic and copies ran while one was open for 0% -> 0% of each run, Pallas kernels for 47% -> 38%
where the time goes in v2:
time: 98.3 us; the launch traced here: 98.1 us
  Pallas kernels  48.9 us (50%)
  starting transfers between devices  24.4 us (25%)
  waiting for transfers between devices  23.7 us (24%)
    pallas_call x23, Pallas kernels, start(): pl.pallas_call(run, grid=grid, in_specs=list(in_specs) + [ANY] * len(afte...  48.9 us
    ppermute x12, waiting for transfers between devices, send_across(): lax.ppermute(a, ('dp', 'seq'), [(i, i ^ flip) for i in range(seqs * dps)])  18.6 us
    ppermute x12, starting transfers between devices, send_across(): lax.ppermute(a, ('dp', 'seq'), [(i, i ^ flip) for i in range(seqs * dps)])  17.7 us
    ppermute x12, starting transfers between devices, swap(): return lax.ppermute(a, axis, [(i, i ^ bit) for i in range(size)])  6.74 us
    ppermute x12, waiting for transfers between devices, swap(): return lax.ppermute(a, axis, [(i, i ^ bit) for i in range(size)])  5.18 us
  transfers between devices with their start and end apart: 24, of which 10 were waited for; matrix products, arithmetic and copies ran while one was open for 0% of the time, Pallas kernels for 38%

profile of v2, /device:TPU:0, one launch (start us, length us, event | category | flops | bytes accessed | tf_op | source)
XLA Modules:
  0.0 98.1 jit_solution(14542027555948953640)
XLA Ops:
  0.7 4.9 %shard_map.186 = (bf16[8,256,512]{2,1,0:T(8,128)(2,1)S(1)}, f32[512,512]{1,0:T(8,128)S(1)}, bf16[512,512]{1,0:T(8,128)(2,1)S(1)}, bf16[576,128]{1,0:T(8,128)(2,1)S(1)}, bf16[512,512]{1,0:T(8,128)(2,1)S(1)}) custom-call(bf16[512,512]{1,0:T(8,128)(2,1)} %bitcast.28, f32[1,512]{1,0:T(1,128)} %bitcast.34, f32[1,512]{1,0:T(1,128)} %bitcast.38, ...), custom_call_target="tpu_custom_call" | custom-call | flops 4944999936 | bytes 1048576 | tf_op jit(solution)/shard_map/pallas_call | solution.py:49
  5.6 0.5 collective-permute-start
  6.2 0.4 collective-permute-start.3
  6.6 1.5 %shard_map.187 = (f32[256,512]{1,0:T(8,128)S(1)}, f32[256,512]{1,0:T(8,128)S(1)}, bf16[4,256,256]{2,1,0:T(8,128)(2,1)S(1)}, bf16[4,512,256]{2,1,0:T(8,128)(2,1)S(1)}) custom-call(bf16[8,256,512]{2,1,0:T(8,128)(2,1)S(1)} %get-tuple-element.100.refs_0_.refs_1_, bf16[512,512]{1,0:T(8,128)(2,1)S(1)} %get-tuple-element.101.refs_1_.refs_2_), custom_call_target="tpu_custom_call" | custom-call | flops 3449999872 | bytes 1048576 | tf_op jit(solution)/shard_map/pallas_call | solution.py:49
  8.1 0.6 shard_map.188.refs_2_
  8.7 2.6 %collective-permute-start.1 = (bf16[576,128]{1,0:T(8,128)(2,1)S(1)}, bf16[576,128]{1,0:T(8,128)(2,1)S(1)}, u32[]{:S(2)}, u32[]{:S(2)}) collective-permute-start(bf16[576,128]{1,0:T(8,128)(2,1)S(1)} %shard_map.188.refs_2_), channel_id=1, source_target_pairs={{0,2},{2,0},{1,3},{3,1},{4,6},{6,4},{5,7},{7,5},{8,10},{10,8},{9,1... | collective-permute-start | bytes 442376 | tf_op jit(solution)/shard_map/ppermute | solution.py:36
  11.4 1.5 %shard_map.189 = (f32[256,512]{1,0:T(8,128)S(1)}, f32[256,512]{1,0:T(8,128)S(1)}, bf16[4,256,256]{2,1,0:T(8,128)(2,1)S(1)}, bf16[4,512,256]{2,1,0:T(8,128)(2,1)S(1)}) custom-call(bf16[8,256,512]{2,1,0:T(8,128)(2,1)S(1)} %get-tuple-element.100.refs_0_.refs_1_, bf16[512,512]{1,0:T(8,128)(2,1)S(1)} %get-tuple-element.101.refs_1_.refs_2_, ...), custom_call_target="tpu_custom_call" | custom-call | flops 3449999872 | bytes 1048576 | tf_op jit(solution)/shard_map/pallas_call | solution.py:49
  12.9 3.0 %collective-permute-done.1.refs_4_ = bf16[576,128]{1,0:T(8,128)(2,1)S(1)} collective-permute-done((bf16[576,128]{1,0:T(8,128)(2,1)S(1)}, bf16[576,128]{1,0:T(8,128)(2,1)S(1)}, u32[]{:S(2)}, u32[]{:S(2)}) %collective-permute-start.1) | collective-permute-done | bytes 147488 | tf_op jit(solution)/shard_map/ppermute | solution.py:36
  15.8 4.7 %shard_map.190 = (bf16[512,512]{1,0:T(8,128)(2,1)S(1)}, bf16[512,128]{1,0:T(8,128)(2,1)S(1)}, f32[256,512]{1,0:T(8,128)S(1)}, f32[256,512]{1,0:T(8,128)S(1)}, f3...) custom-call(s32[1,8]{1,0:T(1,128)S(1)} %copy-done.9, ...), custom_call_target="tpu_custom_call" | custom-call | flops 4600000000 | bytes 1048576 | tf_op jit(solution)/shard_map/pallas_call | solution.py:49
  20.6 4.9 %shard_map.191 = (bf16[512,1024]{1,0:T(8,128)(2,1)S(1)}, bf16[512,1024]{1,0:T(8,128)(2,1)S(1)}, f32[512,512]{1,0:T(8,128)S(1)}, f32[512,512]{1,0:T(8,128)S(1)}, ...) custom-call(bf16[512,512]{1,0:T(8,128)(2,1)S(1)} %bitcast.29, ...), custom_call_target="tpu_custom_call" | custom-call | flops 6899999744 | bytes 1048576 | tf_op jit(solution)/shard_map/pallas_call | solution.py:49
  25.8 0.3 collective-permute-start.4
  26.1 6.0 %shard_map.192 = (bf16[512,512]{1,0:T(8,128)(2,1)}, f32[512,512]{1,0:T(8,128)S(1)}, bf16[512,512]{1,0:T(8,128)(2,1)S(1)}, bf16[512,256]{1,0:T(8,128)(2,1)S(1)}, ...) custom-call(f32[512,512]{1,0:T(8,128)S(1)} %get-tuple-element.108.re, ...), custom_call_target="tpu_custom_call" | custom-call | flops 6899999744 | bytes 1048576 | tf_op jit(solution)/shard_map/pallas_call | solution.py:49
  32.1 0.3 collective-permute-start.5
  32.3 2.5 %shard_map.193 = (bf16[256,512]{1,0:T(8,128)(2,1)S(1)}, bf16[256,512]{1,0:T(8,128)(2,1)S(1)}, bf16[256,512]{1,0:T(8,128)(2,1)S(1)}, bf16[4,256,256]{2,1,0:T(8,12...) custom-call(s32[1,8]{1,0:T(1,128)S(1)} %copy-done.9, ...), custom_call_target="tpu_custom_call" | custom-call | flops 3449999872 | bytes 1048576 | tf_op jit(solution)/shard_map/pallas_call | solution.py:49
  34.9 1.4 %shard_map.194 = (bf16[8,32,1152]{2,1,0:T(8,128)(2,1)S(1)}, bf16[8,32,1152]{2,1,0:T(8,128)(2,1)S(1)}, bf16[8,32,1152]{2,1,0:T(8,128)(2,1)S(1)}, bf16[8,32,1152]{2,1,0:T(8,128)(2,1)S(1)}) custom-call(bf16[16,32,1024]{2,1,0:T(8,128)(2,1)S(1)} %bitcast.19, bf16[16,32,256]{2,1,0:T(8,128)(2,1)S(1)} %bitcast.21, bf16[16,32,1024]{2,1,0:T(8,128)(2,1)S(1)} %bitcast.18, ...), custom_call_target="tpu_custom_call" | custom-call | flops 1150000000 | bytes 1048576 | tf_op jit(solution)/shard_map/pallas_call | solution.py:49
  36.3 1.9 %collective-permute-start.10 = (bf16[8,32,1152]{2,1,0:T(8,128)(2,1)S(1)}, bf16[8,32,1152]{2,1,0:T(8,128)(2,1)S(1)}, u32[]{:S(2)}, u32[]{:S(2)}) collective-permute-start(bf16[8,32,1152]{2,1,0:T(8,128)(2,1)S(1)} %get-tuple-element.134.refs_11_), channel_id=1, source_target_pairs={{0,8},{2,10},{4,12},{6,14},{8,0},{10,2},{12,4},{14,6},{16,24},{18,... | collective-permute-start | bytes 1769480 | tf_op jit(solution)/shard_map/ppermute | solution.py:654
  38.2 1.5 %collective-permute-start.9 = (bf16[8,32,1152]{2,1,0:T(8,128)(2,1)S(1)}, bf16[8,32,1152]{2,1,0:T(8,128)(2,1)S(1)}, u32[]{:S(2)}, u32[]{:S(2)}) collective-permute-start(bf16[8,32,1152]{2,1,0:T(8,128)(2,1)S(1)} %get-tuple-element.133.refs_10_), channel_id=1, source_target_pairs={{0,4},{2,6},{4,0},{6,2},{8,12},{10,14},{12,8},{14,10},{16,20},{18,... | collective-permute-start | bytes 1769480 | tf_op jit(solution)/shard_map/ppermute | solution.py:654
  39.7 2.6 %shard_map.195 = (bf16[256,512]{1,0:T(8,128)(2,1)S(1)}, bf16[256,512]{1,0:T(8,128)(2,1)S(1)}, bf16[256,512]{1,0:T(8,128)(2,1)S(1)}, bf16[4,256,256]{2,1,0:T(8,12...) custom-call(s32[1,8]{1,0:T(1,128)S(1)} %copy-done.9, ...), custom_call_target="tpu_custom_call" | custom-call | flops 3449999872 | bytes 1048576 | tf_op jit(solution)/shard_map/pallas_call | solution.py:49
  42.4 1.4 %collective-permute-done.7.refs_2_.refs_4_ = bf16[576,128]{1,0:T(8,128)(2,1)S(1)} collective-permute-done((bf16[576,128]{1,0:T(8,128)(2,1)S(1)}, bf16[576,128]{1,0:T(8,128)(2,1)S(1)}, u32[]{:S(2)}, u32[]{:S(2)}) %collective-permute-start.7) | collective-permute-done | bytes 147488 | tf_op jit(solution)/shard_map/ppermute | solution.py:36
  43.7 0.6 shard_map.196.refs_14_
  44.3 1.6 %collective-permute-start.8 = (bf16[576,128]{1,0:T(8,128)(2,1)S(1)}, bf16[576,128]{1,0:T(8,128)(2,1)S(1)}, u32[]{:S(2)}, u32[]{:S(2)}) collective-permute-start(bf16[576,128]{1,0:T(8,128)(2,1)S(1)} %shard_map.196.refs_14_), channel_id=1, source_target_pairs={{0,2},{2,0},{1,3},{3,1},{4,6},{6,4},{5,7},{7,5},{8,10},{10,8},{9,1... | collective-permute-start | bytes 442376 | tf_op jit(solution)/shard_map/ppermute | solution.py:36
  45.9 3.5 %shard_map.197.refs_4_.refs_2_ = f32[4,256,512]{2,1,0:T(8,128)S(1)} custom-call(s32[1,8]{1,0:T(1,128)S(1)} %copy-done.9, bf16[8,256,512]{2,1,0:T(8,128)(2,1)S(1)} %get-tuple-element.100.refs_0_.refs_1_, bf16[512,512]{1,0:T(8,128)(2,1)S(1)} %get-tuple-element.101.refs_1_.refs_2_, bf16[512,512]{1,0:T(8,128)(2,1)S(1)} %get-tuple-element.117.refs_3_, ...), custom_call_target="tpu_custom_call" | custom-call | flops 3449999872 | bytes 1048576 | tf_op jit(solution)/shard_map/pallas_call | solution.py:49
  49.4 2.5 %collective-permute-done.10.refs_3_ = bf16[8,32,1152]{2,1,0:T(8,128)(2,1)S(1)} collective-permute-done((bf16[8,32,1152]{2,1,0:T(8,128)(2,1)S(1)}, bf16[8,32,1152]{2,1,0:T(8,128)(2,1)S(1)}, u32[]{:S(2)}, u32[]{:S(2)}) %collective-permute-start.10) | collective-permute-done | bytes 589856 | tf_op jit(solution)/shard_map/ppermute | solution.py:654
  51.9 1.5 %collective-permute-done.9.refs_1_ = bf16[8,32,1152]{2,1,0:T(8,128)(2,1)S(1)} collective-permute-done((bf16[8,32,1152]{2,1,0:T(8,128)(2,1)S(1)}, bf16[8,32,1152]{2,1,0:T(8,128)(2,1)S(1)}, u32[]{:S(2)}, u32[]{:S(2)}) %collective-permute-start.9) | collective-permute-done | bytes 589856 | tf_op jit(solution)/shard_map/ppermute | solution.py:654
  53.4 0.7 shard_map.198
  54.0 0.4 collective-permute-start.11
  54.5 1.6 %collective-permute-start.12 = (bf16[4,32,1152]{2,1,0:T(8,128)(2,1)S(1)}, bf16[4,32,1152]{2,1,0:T(8,128)(2,1)S(1)}, u32[]{:S(2)}, u32[]{:S(2)}) collective-permute-start(bf16[4,32,1152]{2,1,0:T(8,128)(2,1)S(1)} %get-tuple-element.159.refs_9_), channel_id=1, source_target_pairs={{0,4},{2,6},{4,0},{6,2},{8,12},{10,14},{12,8},{14,10},{16,20},{18,... | collective-permute-start | bytes 884744 | tf_op jit(solution)/shard_map/ppermute | solution.py:654
  56.1 2.5 %shard_map.199 = (bf16[512,1024]{1,0:T(8,128)(2,1)S(1)}, f32[512,512]{1,0:T(8,128)S(1)}) custom-call(s32[1,8]{1,0:T(1,128)S(1)} %copy-done.9, bf16[8,256,512]{2,1,0:T(8,128)(2,1)S(1)} %get-tuple-element.100.refs_0_.refs_1_, f32[4,256,512]{2,1,0:T(8,128)S(1)} %shard_map.197.refs_4_.refs_2_, f32[512,512]{1,0:T(8,128)S(1)} %get-tuple-element.154.refs_3_, ...), custom_call_target="tpu_custom_call" | custom-call | flops 4024999936 | bytes 1048576 | tf_op jit(solution)/shard_map/pallas_call | solution.py:49
  58.7 3.5 %shard_map.200.refs_4_.refs_2_ = f32[4,256,512]{2,1,0:T(8,128)S(1)} custom-call(s32[1,8]{1,0:T(1,128)S(1)} %copy-done.9, bf16[8,256,512]{2,1,0:T(8,128)(2,1)S(1)} %get-tuple-element.100.refs_0_.refs_1_, bf16[512,512]{1,0:T(8,128)(2,1)S(1)} %get-tuple-element.101.refs_1_.refs_2_, bf16[512,512]{1,0:T(8,128)(2,1)S(1)} %get-tuple-element.117.refs_3_, ...), custom_call_target="tpu_custom_call" | custom-call | flops 9200000000 | bytes 1048576 | tf_op jit(solution)/shard_map/pallas_call | solution.py:49
  62.5 0.6 shard_map.201
  63.1 1.6 %collective-permute-start.20 = (bf16[2,32,2304]{2,1,0:T(8,128)(2,1)S(1)}, bf16[2,32,2304]{2,1,0:T(8,128)(2,1)S(1)}, u32[]{:S(2)}, u32[]{:S(2)}) collective-permute-start(bf16[2,32,2304]{2,1,0:T(8,128)(2,1)S(1)} %get-tuple-element.166.refs_13_), channel_id=1, source_target_pairs={{0,2},{2,0},{4,6},{6,4},{8,10},{10,8},{12,14},{14,12},{16,18},{18,... | collective-permute-start | bytes 884744 | tf_op jit(solution)/shard_map/ppermute | solution.py:654
  64.6 4.2 %shard_map.202 = (bf16[512,1024]{1,0:T(8,128)(2,1)S(1)}, f32[512,512]{1,0:T(8,128)}, bf16[512,128]{1,0:T(8,128)(2,1)S(1)}) custom-call(s32[1,8]{1,0:T(1,128)S(1)} %copy-done.9, bf16[8,256,512]{2,1,0:T(8,128)(2,1)S(1)} %get-tuple-element.100.refs_0_.refs_1_, f32[4,256,512]{2,1,0:T(8,128)S(1)} %shard_map.200.refs_4_.refs_2_, ...), custom_call_target="tpu_custom_call" | custom-call | flops 5750000128 | bytes 1048576 | tf_op jit(solution)/shard_map/pallas_call | solution.py:49
  68.8 0.7 shard_map.203
  69.5 0.6 collective-permute-start.14
  70.1 1.5 %collective-permute-start.15 = (bf16[4,32,1152]{2,1,0:T(8,128)(2,1)S(1)}, bf16[4,32,1152]{2,1,0:T(8,128)(2,1)S(1)}, u32[]{:S(2)}, u32[]{:S(2)}) collective-permute-start(bf16[4,32,1152]{2,1,0:T(8,128)(2,1)S(1)} %get-tuple-element.172), channel_id=1, source_target_pairs={{0,4},{2,6},{4,0},{6,2},{8,12},{10,14},{12,8},{14,10},{16,20},{18,... | collective-permute-start | bytes 884744 | tf_op jit(solution)/shard_map/ppermute | solution.py:654
  71.6 1.4 %collective-permute-start.16 = (bf16[4,32,1152]{2,1,0:T(8,128)(2,1)S(1)}, bf16[4,32,1152]{2,1,0:T(8,128)(2,1)S(1)}, u32[]{:S(2)}, u32[]{:S(2)}) collective-permute-start(bf16[4,32,1152]{2,1,0:T(8,128)(2,1)S(1)} %get-tuple-element.173), channel_id=1, source_target_pairs={{0,6},{2,4},{4,2},{6,0},{8,14},{10,12},{12,10},{14,8},{16,22},{18,... | collective-permute-start | bytes 884744 | tf_op jit(solution)/shard_map/ppermute | solution.py:654
  73.3 2.7 %collective-permute-start.21 = (bf16[1,32,2304]{2,1,0:T(8,128)(2,1)S(1)}, bf16[1,32,2304]{2,1,0:T(8,128)(2,1)S(1)}, u32[]{:S(2)}, u32[]{:S(2)}) collective-permute-start(bf16[1,32,2304]{2,1,0:T(8,128)(2,1)S(1)} %get-tuple-element.180), channel_id=1, source_target_pairs={{0,16},{2,18},{4,20},{6,22},{8,24},{10,26},{12,28},{14,30},{16,0},... | collective-permute-start | bytes 442376 | tf_op jit(solution)/shard_map/ppermute | solution.py:654
  75.9 3.5 %collective-permute-done.14.refs_1_ = bf16[4,32,1152]{2,1,0:T(8,128)(2,1)S(1)} collective-permute-done((bf16[4,32,1152]{2,1,0:T(8,128)(2,1)S(1)}, bf16[4,32,1152]{2,1,0:T(8,128)(2,1)S(1)}, u32[]{:S(2)}, u32[]{:S(2)}) %collective-permute-start.14) | collective-permute-done | bytes 294944 | tf_op jit(solution)/shard_map/ppermute | solution.py:654
  79.5 5.6 %collective-permute-done.15.refs_2_ = bf16[4,32,1152]{2,1,0:T(8,128)(2,1)S(1)} collective-permute-done((bf16[4,32,1152]{2,1,0:T(8,128)(2,1)S(1)}, bf16[4,32,1152]{2,1,0:T(8,128)(2,1)S(1)}, u32[]{:S(2)}, u32[]{:S(2)}) %collective-permute-start.15) | collective-permute-done | bytes 294944 | tf_op jit(solution)/shard_map/ppermute | solution.py:654
  85.1 0.4 shard_map.204
  85.5 1.6 %collective-permute-start.17 = (bf16[1,32,1152]{2,1,0:T(8,128)(2,1)S(1)}, bf16[1,32,1152]{2,1,0:T(8,128)(2,1)S(1)}, u32[]{:S(2)}, u32[]{:S(2)}) collective-permute-start(bf16[1,32,1152]{2,1,0:T(8,128)(2,1)S(1)} %get-tuple-element.175), channel_id=1, source_target_pairs={{0,8},{2,10},{4,12},{6,14},{8,0},{10,2},{12,4},{14,6},{16,24},{18,... | collective-permute-start | bytes 221192 | tf_op jit(solution)/shard_map/ppermute | solution.py:654
  87.1 2.6 %collective-permute-start.18 = (bf16[1,32,1152]{2,1,0:T(8,128)(2,1)S(1)}, bf16[1,32,1152]{2,1,0:T(8,128)(2,1)S(1)}, u32[]{:S(2)}, u32[]{:S(2)}) collective-permute-start(bf16[1,32,1152]{2,1,0:T(8,128)(2,1)S(1)} %get-tuple-element.176), channel_id=1, source_target_pairs={{0,16},{2,18},{4,20},{6,22},{8,24},{10,26},{12,28},{14,30},{16,0},... | collective-permute-start | bytes 221192 | tf_op jit(solution)/shard_map/ppermute | solution.py:654
  89.9 0.7 shard_map.206
  90.7 3.3 %collective-permute-done.18.refs_2_ = bf16[1,32,1152]{2,1,0:T(8,128)(2,1)S(1)} collective-permute-done((bf16[1,32,1152]{2,1,0:T(8,128)(2,1)S(1)}, bf16[1,32,1152]{2,1,0:T(8,128)(2,1)S(1)}, u32[]{:S(2)}, u32[]{:S(2)}) %collective-permute-start.18) | collective-permute-done | bytes 73760 | tf_op jit(solution)/shard_map/ppermute | solution.py:654
  94.0 1.9 %collective-permute-done.19.refs_3_ = bf16[1,32,1152]{2,1,0:T(8,128)(2,1)S(1)} collective-permute-done((bf16[1,32,1152]{2,1,0:T(8,128)(2,1)S(1)}, bf16[1,32,1152]{2,1,0:T(8,128)(2,1)S(1)}, u32[]{:S(2)}, u32[]{:S(2)}) %collective-permute-start.19) | collective-permute-done | bytes 73760 | tf_op jit(solution)/shard_map/ppermute | solution.py:654
  96.0 0.5 collective-permute-start.23
  96.5 0.8 collective-permute-done.23.refs_3_
  97.4 0.7 shard_map.208
  (44 shorter events, 1.4 us)
Async XLA Ops:
  0.6 5.5 %copy-start.1 = (bf16[512,1024]{1,0:T(8,128)(2,1)S(1)}, bf16[512,1024]{1,0:T(8,128)(2,1)}, u32[]{:S(2)}) copy-start(bf16[512,1024]{1,0:T(8,128)(2,1)} %refs_12_.1) | copy-start | bytes 3145732
  0.7 5.5 %copy-start.2 = (bf16[512,1024]{1,0:T(8,128)(2,1)S(1)}, bf16[512,1024]{1,0:T(8,128)(2,1)}, u32[]{:S(2)}) copy-start(bf16[512,1024]{1,0:T(8,128)(2,1)} %refs_13_.1) | copy-start | bytes 3145732
  5.6 2.5 %collective-permute-start = (bf16[576,128]{1,0:T(8,128)(2,1)S(1)}, bf16[576,128]{1,0:T(8,128)(2,1)S(1)}, u32[]{:S(2)}, u32[]{:S(2)}) collective-permute-start(bf16[576,128]{1,0:T(8,128)(2,1)S(1)} %get-tuple-element.102.refs_1_), channel_id=1, source_target_pairs={{0,1},{1,0},{2,3},{3,2},{4,5},{5,4},{6,7},{7,6},{8,9},{9,8},{10,11... | collective-permute-start | bytes 442376 | tf_op jit(solution)/shard_map/ppermute | solution.py:36
  6.1 14.5 %collective-permute-start.2 = (bf16[512,1024]{1,0:T(8,128)(2,1)S(1)}, bf16[512,1024]{1,0:T(8,128)(2,1)S(1)}, u32[]{:S(2)}, u32[]{:S(2)}) collective-permute-start(bf16[512,1024]{1,0:T(8,128)(2,1)S(1)} %copy-done.1), channel_id=1, source_target_pairs={{0,1},{1,0},{2,3},{3,2},{4,5},{5,4},{6,7},{7,6},{8,9},{9,8},{10,11... | collective-permute-start | bytes 3145736 | tf_op jit(solution)/shard_map/ppermute | solution.py:36
  6.2 14.4 %collective-permute-start.3 = (bf16[512,1024]{1,0:T(8,128)(2,1)S(1)}, bf16[512,1024]{1,0:T(8,128)(2,1)S(1)}, u32[]{:S(2)}, u32[]{:S(2)}) collective-permute-start(bf16[512,1024]{1,0:T(8,128)(2,1)S(1)} %copy-done.2), channel_id=1, source_target_pairs={{0,1},{1,0},{2,3},{3,2},{4,5},{5,4},{6,7},{7,6},{8,9},{9,8},{10,11... | collective-permute-start | bytes 3145736 | tf_op jit(solution)/shard_map/ppermute | solution.py:36
  6.6 1.5 %copy-start.9 = (s32[1,8]{1,0:T(1,128)S(1)}, s32[1,8]{1,0:T(1,128)}, u32[]{:S(2)}) copy-start(s32[1,8]{1,0:T(1,128)} %refs_0_.17) | copy-start | bytes 100
  8.7 7.1 %collective-permute-start.1 = (bf16[576,128]{1,0:T(8,128)(2,1)S(1)}, bf16[576,128]{1,0:T(8,128)(2,1)S(1)}, u32[]{:S(2)}, u32[]{:S(2)}) collective-permute-start(bf16[576,128]{1,0:T(8,128)(2,1)S(1)} %shard_map.188.refs_2_), channel_id=1, source_target_pairs={{0,2},{2,0},{1,3},{3,1},{4,6},{6,4},{5,7},{7,5},{8,10},{10,8},{9,1... | collective-permute-start | bytes 442376 | tf_op jit(solution)/shard_map/ppermute | solution.py:36
  15.8 4.8 %copy-start.3 = (bf16[1,512,512]{2,1,0:T(8,128)(2,1)S(1)}, bf16[1,512,512]{2,1,0:T(8,128)(2,1)}, u32[]{:S(2)}) copy-start(bf16[1,512,512]{2,1,0:T(8,128)(2,1)} %param.21) | copy-start | bytes 1572868
  15.8 4.8 %copy-start.4 = (bf16[512,512]{1,0:T(8,128)(2,1)S(1)}, bf16[512,512]{1,0:T(8,128)(2,1)}, u32[]{:S(2)}) copy-start(bf16[512,512]{1,0:T(8,128)(2,1)} %refs_10_.1) | copy-start | bytes 1572868
  15.8 4.8 %copy-start.5 = (bf16[1,512,512]{2,1,0:T(8,128)(2,1)S(1)}, bf16[1,512,512]{2,1,0:T(8,128)(2,1)}, u32[]{:S(2)}) copy-start(bf16[1,512,512]{2,1,0:T(8,128)(2,1)} %param.11) | copy-start | bytes 1572868
  15.8 4.8 %copy-start.6 = (f32[512]{0:T(512)S(1)}, f32[512]{0:T(512)}, u32[]{:S(2)}) copy-start(f32[512]{0:T(512)} %param.18) | copy-start | bytes 6148
  15.8 4.8 %copy-start.7 = (f32[512]{0:T(512)S(1)}, f32[512]{0:T(512)}, u32[]{:S(2)}) copy-start(f32[512]{0:T(512)} %param.17) | copy-start | bytes 6148
  25.5 9.4 %collective-permute-start.6 = (bf16[512,1024]{1,0:T(8,128)(2,1)S(1)}, bf16[512,1024]{1,0:T(8,128)(2,1)S(1)}, u32[]{:S(2)}, u32[]{:S(2)}) collective-permute-start(bf16[512,1024]{1,0:T(8,128)(2,1)S(1)} %get-tuple-element.132), channel_id=1, source_target_pairs={{0,1},{1,0},{2,3},{3,2},{4,5},{5,4},{6,7},{7,6},{8,9},{9,8},{10,11... | collective-permute-start | bytes 3145736 | tf_op jit(solution)/shard_map/ppermute | solution.py:36
  25.8 9.1 %collective-permute-start.4 = (bf16[512,1024]{1,0:T(8,128)(2,1)S(1)}, bf16[512,1024]{1,0:T(8,128)(2,1)S(1)}, u32[]{:S(2)}, u32[]{:S(2)}) collective-permute-start(bf16[512,1024]{1,0:T(8,128)(2,1)S(1)} %get-tuple-element.129), channel_id=1, source_target_pairs={{0,1},{1,0},{2,3},{3,2},{4,5},{5,4},{6,7},{7,6},{8,9},{9,8},{10,11... | collective-permute-start | bytes 3145736 | tf_op jit(solution)/shard_map/ppermute | solution.py:36
  32.1 2.8 %collective-permute-start.5 = (bf16[512,256]{1,0:T(8,128)(2,1)S(1)}, bf16[512,256]{1,0:T(8,128)(2,1)S(1)}, u32[]{:S(2)}, u32[]{:S(2)}) collective-permute-start(bf16[512,256]{1,0:T(8,128)(2,1)S(1)} %get-tuple-element.130), channel_id=1, source_target_pairs={{0,1},{1,0},{2,3},{3,2},{4,5},{5,4},{6,7},{7,6},{8,9},{9,8},{10,11... | collective-permute-start | bytes 786440 | tf_op jit(solution)/shard_map/ppermute | solution.py:36
  36.3 15.6 %collective-permute-start.10 = (bf16[8,32,1152]{2,1,0:T(8,128)(2,1)S(1)}, bf16[8,32,1152]{2,1,0:T(8,128)(2,1)S(1)}, u32[]{:S(2)}, u32[]{:S(2)}) collective-permute-start(bf16[8,32,1152]{2,1,0:T(8,128)(2,1)S(1)} %get-tuple-element.134.refs_11_), channel_id=1, source_target_pairs={{0,8},{2,10},{4,12},{6,14},{8,0},{10,2},{12,4},{14,6},{16,24},{18,... | collective-permute-start | bytes 1769480 | tf_op jit(solution)/shard_map/ppermute | solution.py:654
  38.2 15.2 %collective-permute-start.9 = (bf16[8,32,1152]{2,1,0:T(8,128)(2,1)S(1)}, bf16[8,32,1152]{2,1,0:T(8,128)(2,1)S(1)}, u32[]{:S(2)}, u32[]{:S(2)}) collective-permute-start(bf16[8,32,1152]{2,1,0:T(8,128)(2,1)S(1)} %get-tuple-element.133.refs_10_), channel_id=1, source_target_pairs={{0,4},{2,6},{4,0},{6,2},{8,12},{10,14},{12,8},{14,10},{16,20},{18,... | collective-permute-start | bytes 1769480 | tf_op jit(solution)/shard_map/ppermute | solution.py:654
  42.3 1.4 %collective-permute-start.7 = (bf16[576,128]{1,0:T(8,128)(2,1)S(1)}, bf16[576,128]{1,0:T(8,128)(2,1)S(1)}, u32[]{:S(2)}, u32[]{:S(2)}) collective-permute-start(bf16[576,128]{1,0:T(8,128)(2,1)S(1)} %get-tuple-element.153.refs_1_), channel_id=1, source_target_pairs={{0,1},{1,0},{2,3},{3,2},{4,5},{5,4},{6,7},{7,6},{8,9},{9,8},{10,11... | collective-permute-start | bytes 442376 | tf_op jit(solution)/shard_map/ppermute | solution.py:36
  44.3 11.7 %collective-permute-start.8 = (bf16[576,128]{1,0:T(8,128)(2,1)S(1)}, bf16[576,128]{1,0:T(8,128)(2,1)S(1)}, u32[]{:S(2)}, u32[]{:S(2)}) collective-permute-start(bf16[576,128]{1,0:T(8,128)(2,1)S(1)} %shard_map.196.refs_14_), channel_id=1, source_target_pairs={{0,2},{2,0},{1,3},{3,1},{4,6},{6,4},{5,7},{7,5},{8,10},{10,8},{9,1... | collective-permute-start | bytes 442376 | tf_op jit(solution)/shard_map/ppermute | solution.py:36
  53.4 2.7 %copy-start = (bf16[512,2048]{1,0:T(8,128)(2,1)S(1)}, bf16[512,2048]{1,0:T(8,128)(2,1)}, u32[]{:S(2)}) copy-start(bf16[512,2048]{1,0:T(8,128)(2,1)} %refs_7_.3) | copy-start | bytes 6291460
  54.0 8.2 %collective-permute-start.11 = (bf16[4,32,1152]{2,1,0:T(8,128)(2,1)S(1)}, bf16[4,32,1152]{2,1,0:T(8,128)(2,1)S(1)}, u32[]{:S(2)}, u32[]{:S(2)}) collective-permute-start(bf16[4,32,1152]{2,1,0:T(8,128)(2,1)S(1)} %get-tuple-element.158.refs_8_), channel_id=1, source_target_pairs={{0,8},{2,10},{4,12},{6,14},{8,0},{10,2},{12,4},{14,6},{16,24},{18,... | collective-permute-start | bytes 884744 | tf_op jit(solution)/shard_map/ppermute | solution.py:654
  54.5 8.0 %collective-permute-start.12 = (bf16[4,32,1152]{2,1,0:T(8,128)(2,1)S(1)}, bf16[4,32,1152]{2,1,0:T(8,128)(2,1)S(1)}, u32[]{:S(2)}, u32[]{:S(2)}) collective-permute-start(bf16[4,32,1152]{2,1,0:T(8,128)(2,1)S(1)} %get-tuple-element.159.refs_9_), channel_id=1, source_target_pairs={{0,4},{2,6},{4,0},{6,2},{8,12},{10,14},{12,8},{14,10},{16,20},{18,... | collective-permute-start | bytes 884744 | tf_op jit(solution)/shard_map/ppermute | solution.py:654
  58.6 10.2 %collective-permute-start.13 = (bf16[512,1024]{1,0:T(8,128)(2,1)S(1)}, bf16[512,1024]{1,0:T(8,128)(2,1)S(1)}, u32[]{:S(2)}, u32[]{:S(2)}) collective-permute-start(bf16[512,1024]{1,0:T(8,128)(2,1)S(1)} %get-tuple-element.160.refs_14_), channel_id=1, source_target_pairs={{0,1},{1,0},{2,3},{3,2},{4,5},{5,4},{6,7},{7,6},{8,9},{9,8},{10,11... | collective-permute-start | bytes 3145736 | tf_op jit(solution)/shard_map/ppermute | solution.py:36
  62.5 2.1 %copy-start.8 = (f32[512]{0:T(512)S(1)}, f32[512]{0:T(512)}, u32[]{:S(2)}) copy-start(f32[512]{0:T(512)} %param.13) | copy-start | bytes 6148
  63.1 10.0 %collective-permute-start.20 = (bf16[2,32,2304]{2,1,0:T(8,128)(2,1)S(1)}, bf16[2,32,2304]{2,1,0:T(8,128)(2,1)S(1)}, u32[]{:S(2)}, u32[]{:S(2)}) collective-permute-start(bf16[2,32,2304]{2,1,0:T(8,128)(2,1)S(1)} %get-tuple-element.166.refs_13_), channel_id=1, source_target_pairs={{0,2},{2,0},{4,6},{6,4},{8,10},{10,8},{12,14},{14,12},{16,18},{18,... | collective-permute-start | bytes 884744 | tf_op jit(solution)/shard_map/ppermute | solution.py:654
  69.5 9.9 %collective-permute-start.14 = (bf16[4,32,1152]{2,1,0:T(8,128)(2,1)S(1)}, bf16[4,32,1152]{2,1,0:T(8,128)(2,1)S(1)}, u32[]{:S(2)}, u32[]{:S(2)}) collective-permute-start(bf16[4,32,1152]{2,1,0:T(8,128)(2,1)S(1)} %get-tuple-element.171), channel_id=1, source_target_pairs={{0,2},{2,0},{4,6},{6,4},{8,10},{10,8},{12,14},{14,12},{16,18},{18,... | collective-permute-start | bytes 884744 | tf_op jit(solution)/shard_map/ppermute | solution.py:654
  70.1 15.0 %collective-permute-start.15 = (bf16[4,32,1152]{2,1,0:T(8,128)(2,1)S(1)}, bf16[4,32,1152]{2,1,0:T(8,128)(2,1)S(1)}, u32[]{:S(2)}, u32[]{:S(2)}) collective-permute-start(bf16[4,32,1152]{2,1,0:T(8,128)(2,1)S(1)} %get-tuple-element.172), channel_id=1, source_target_pairs={{0,4},{2,6},{4,0},{6,2},{8,12},{10,14},{12,8},{14,10},{16,20},{18,... | collective-permute-start | bytes 884744 | tf_op jit(solution)/shard_map/ppermute | solution.py:654
  71.6 13.5 %collective-permute-start.16 = (bf16[4,32,1152]{2,1,0:T(8,128)(2,1)S(1)}, bf16[4,32,1152]{2,1,0:T(8,128)(2,1)S(1)}, u32[]{:S(2)}, u32[]{:S(2)}) collective-permute-start(bf16[4,32,1152]{2,1,0:T(8,128)(2,1)S(1)} %get-tuple-element.173), channel_id=1, source_target_pairs={{0,6},{2,4},{4,2},{6,0},{8,14},{10,12},{12,10},{14,8},{16,22},{18,... | collective-permute-start | bytes 884744 | tf_op jit(solution)/shard_map/ppermute | solution.py:654
  73.3 16.6 %collective-permute-start.21 = (bf16[1,32,2304]{2,1,0:T(8,128)(2,1)S(1)}, bf16[1,32,2304]{2,1,0:T(8,128)(2,1)S(1)}, u32[]{:S(2)}, u32[]{:S(2)}) collective-permute-start(bf16[1,32,2304]{2,1,0:T(8,128)(2,1)S(1)} %get-tuple-element.180), channel_id=1, source_target_pairs={{0,16},{2,18},{4,20},{6,22},{8,24},{10,26},{12,28},{14,30},{16,0},... | collective-permute-start | bytes 442376 | tf_op jit(solution)/shard_map/ppermute | solution.py:654
  85.5 5.2 %collective-permute-start.17 = (bf16[1,32,1152]{2,1,0:T(8,128)(2,1)S(1)}, bf16[1,32,1152]{2,1,0:T(8,128)(2,1)S(1)}, u32[]{:S(2)}, u32[]{:S(2)}) collective-permute-start(bf16[1,32,1152]{2,1,0:T(8,128)(2,1)S(1)} %get-tuple-element.175), channel_id=1, source_target_pairs={{0,8},{2,10},{4,12},{6,14},{8,0},{10,2},{12,4},{14,6},{16,24},{18,... | collective-permute-start | bytes 221192 | tf_op jit(solution)/shard_map/ppermute | solution.py:654
  87.1 6.8 %collective-permute-start.18 = (bf16[1,32,1152]{2,1,0:T(8,128)(2,1)S(1)}, bf16[1,32,1152]{2,1,0:T(8,128)(2,1)S(1)}, u32[]{:S(2)}, u32[]{:S(2)}) collective-permute-start(bf16[1,32,1152]{2,1,0:T(8,128)(2,1)S(1)} %get-tuple-element.176), channel_id=1, source_target_pairs={{0,16},{2,18},{4,20},{6,22},{8,24},{10,26},{12,28},{14,30},{16,0},... | collective-permute-start | bytes 221192 | tf_op jit(solution)/shard_map/ppermute | solution.py:654
  89.7 6.2 %collective-permute-start.19 = (bf16[1,32,1152]{2,1,0:T(8,128)(2,1)S(1)}, bf16[1,32,1152]{2,1,0:T(8,128)(2,1)S(1)}, u32[]{:S(2)}, u32[]{:S(2)}) collective-permute-start(bf16[1,32,1152]{2,1,0:T(8,128)(2,1)S(1)} %get-tuple-element.177), channel_id=1, source_target_pairs={{0,24},{2,26},{4,28},{6,30},{8,16},{10,18},{12,20},{14,22},{16,8},... | collective-permute-start | bytes 221192 | tf_op jit(solution)/shard_map/ppermute | solution.py:654
  95.9 1.4 %collective-permute-start.22 = (bf16[1,32,1152]{2,1,0:T(8,128)(2,1)S(1)}, bf16[1,32,1152]{2,1,0:T(8,128)(2,1)S(1)}, u32[]{:S(2)}, u32[]{:S(2)}) collective-permute-start(bf16[1,32,1152]{2,1,0:T(8,128)(2,1)S(1)} %shard_map.207.refs_0_), channel_id=1, source_target_pairs={{0,1},{1,0},{2,3},{3,2},{4,5},{5,4},{6,7},{7,6},{8,9},{9,8},{10,11... | collective-permute-start | bytes 221192 | tf_op jit(solution)/shard_map/ppermute | solution.py:36
  96.0 1.3 %collective-permute-start.23 = (bf16[32,256]{1,0:T(8,128)(2,1)S(1)}, bf16[32,256]{1,0:T(8,128)(2,1)S(1)}, u32[]{:S(2)}, u32[]{:S(2)}) collective-permute-start(bf16[32,256]{1,0:T(8,128)(2,1)S(1)} %get-tuple-element.181.refs_4_.refs_2_), channel_id=1, source_target_pairs={{0,1},{1,0},{2,3},{3,2},{4,5},{5,4},{6,7},{7,6},{8,9},{9,8},{10,11... | collective-permute-start | bytes 49160 | tf_op jit(solution)/shard_map/ppermute | solution.py:36

commit v3 on v2

--- a/solution.py
+++ b/solution.py
@@ -53,7 +53,7 @@
             out_specs=out_specs,
             out_shape=out_shape,
             scratch_shapes=list(scratch),
-            cost_estimate=pl.CostEstimate(flops=int(us * 1.15e9), bytes_accessed=2**20, transcendentals=0),
+            cost_estimate=pl.CostEstimate(flops=int(us * 1e7), bytes_accessed=2**13, transcendentals=0),
             compiler_params=pltpu.CompilerParams(vmem_limit_bytes=vmem * 2**20),
         )(*operands, *after)
 
@@ -212,15 +212,17 @@
     inverse = lax.rsqrt(jnp.mean(centered * centered, axis=-1, keepdims=True) + EPSILON)
     xn = (centered * inverse * gain_ref[...] + bias_ref[...]).astype(BF)
     xnt_ref[...] = xn.T
+    projected = []
+    for j in range(4):
+        columns[j].wait()
+        projected.append(nn(xn, w_ref[j]))
+    control = jnp.exp(projected[3]).T
+    control_ref[...] = control
+    c = control.astype(BF)
     for j in range(3):
-        columns[j].wait()
-        t = nn(xn, w_ref[j]).astype(BF).T
+        t = projected[j].astype(BF).T
         for h in range(HEADS):
             heads_ref[h, j * HEAD : j * HEAD + HEAD, :] = t[h * HEAD : h * HEAD + HEAD]
-    columns[3].wait()
-    control = jnp.exp(nn(xn, w_ref[3])).T
-    control_ref[...] = control
-    c = control.astype(BF)
     tail = tail_row(doc_begin_row(starts_ref, length), length)
     c_tail = c * tail.astype(BF)
     for h in range(HEADS):
@@ -302,13 +304,14 @@
 
 
 def local_body(own_side, heads_ref, mask_ref, number_ref, total_ref, *pair_refs):
+    held = [parts(heads_ref, head_of(own_side, i)) for i in range(SIDE)]
+    pairs = [causal_pairs(k, q, mask_ref) for q, k, v, c in held]
     for i in range(SIDE):
-        q, k, v, c = parts(heads_ref, head_of(own_side, i))
-        pairs = causal_pairs(k, q, mask_ref)
-        store_pairs(pair_refs, i, pairs)
-        number_ref[i * HEAD : i * HEAD + HEAD, :] = causal_sum(c, pairs)
-    c = jnp.concatenate([parts(heads_ref, head_of(own_side, i))[3] for i in range(SIDE)], axis=0)
+        store_pairs(pair_refs, i, pairs[i])
+    c = jnp.concatenate([h[3] for h in held], axis=0)
     total_ref[...] = causal_sum(c, mask_pair(mask_ref))
+    for i in range(SIDE):
+        number_ref[i * HEAD : i * HEAD + HEAD, :] = causal_sum(held[i][3], pairs[i])
 
 
 def local_sums(own_side, heads, mask, after=()):
@@ -338,30 +341,33 @@
     length = heads_ref.shape[2]
     arrived(False, length, starts_ref, partner_ref, far_ref, mem_ref, totals_ref)
     enters = enters_row(starts_ref, length)
-    for own_side in (False, True):
+    jobs = [(own_side, i) for own_side in (False, True) for i in range(SIDE)]
+    spreads, links = [], []
+    for own_side, i in jobs:
         number_in, total_in = ins[own_side]
-        number_ref, inverse_ref, weight_ref, *link_refs = outs[own_side]
-        for i in range(SIDE):
-            head, at = head_of(own_side, i), slice(i * HEAD, i * HEAD + HEAD)
-            q, k, v, c = parts(heads_ref, head)
-            mem = mem_ref[head_rows(head), :]
-            mem_k, mem_vt = mem[:, :HEAD], mem[:, HEAD:]
-            number = number_in[at, :] + enters * nn(mem_k, q)
-            inverse = 1.0 / (total_in[at, :] + enters * totals_ref[head_rows(head), 0:1])
-            score = number * (inverse * SCALE)
-            e = jnp.exp(score - jnp.max(score, axis=0, keepdims=True))
-            weight = e / jnp.sum(e, axis=0, keepdims=True)
-            number_ref[at, :] = number
-            inverse_ref[at, :] = inverse
-            weight_ref[at, :] = weight
-            spread = (weight * inverse).astype(BF)
-            links = causal_pairs(c, spread, mask_ref)
-            store_pairs(link_refs, i, links)
-            mixed = causal_sum(v, links) + enters * nn(mem_vt, spread)
-            mixed_ref[head_rows(head), :] = mixed.astype(BF)
-
-
-def mix(starts, heads, mask, partner, far, local_other, local_own):
+        number_ref, inverse_ref, weight_ref, *_ = outs[own_side]
+        head, at = head_of(own_side, i), slice(i * HEAD, i * HEAD + HEAD)
+        mem_k = mem_ref[head_rows(head), :][:, :HEAD]
+        number = number_in[at, :] + enters * nn(mem_k, parts(heads_ref, head)[0])
+        inverse = 1.0 / (total_in[at, :] + enters * totals_ref[head_rows(head), 0:1])
+        score = number * (inverse * SCALE)
+        e = jnp.exp(score - jnp.max(score, axis=0, keepdims=True))
+        weight = e * (1.0 / jnp.sum(e, axis=0, keepdims=True))
+        number_ref[at, :] = number
+        inverse_ref[at, :] = inverse
+        weight_ref[at, :] = weight
+        spreads.append((weight * inverse).astype(BF))
+    for (own_side, i), spread in zip(jobs, spreads):
+        links.append(causal_pairs(parts(heads_ref, head_of(own_side, i))[3], spread, mask_ref))
+        store_pairs(outs[own_side][3:], i, links[-1])
+    for (own_side, i), spread, link in zip(jobs, spreads, links):
+        head = head_of(own_side, i)
+        mem_vt = mem_ref[head_rows(head), :][:, HEAD:]
+        mixed = causal_sum(parts(heads_ref, head)[2], link) + enters * nn(mem_vt, spread)
+        mixed_ref[head_rows(head), :] = mixed.astype(BF)
+
+
+def mix(starts, heads, mask, partner, far, local_other, local_own, after=()):
     length, width = heads.shape[2], HEADS * HEAD
     side = [shape(F32, SIDE * HEAD, length)] * 3 + pair_shapes(length)
     mixed, mem, *rest = call(
@@ -372,27 +378,47 @@
         [shape(BF, width, length), shape(BF, width, 128)] + side + side,
         [pltpu.VMEM((width, 8), F32)],
         us=4.0,
+        after=after,
     )(starts, heads, mask, partner, far, *local_other, *local_own)
     return mixed, mem, rest[:5], rest[5:]
 
 
-def feed_step(j, xn, cot, xnt, cott, up_ref, down_ref, gup_ref, gdown_ref):
-    cols = slice(j * 512, j * 512 + 512)
-    up, down = up_ref[:, cols], down_ref[:, cols]
-    pre = nn(xn, up)
-    v2 = pre * pre
-    th = jnp.tanh(GELU_A * pre * (1.0 + GELU_B * v2))
-    half = 0.5 * (1.0 + th)
-    hidden = (pre * half).astype(BF)
-    slope = half + 0.5 * pre * (1.0 - th * th) * (GELU_A * (1.0 + 3.0 * GELU_B * v2))
-    grad_pre = (nn(cot, down) * slope).astype(BF)
-    gdown_ref[:, cols] = nn(cott, hidden).astype(BF)
-    gup_ref[:, cols] = nn(xnt, grad_pre).astype(BF)
-    return nt(hidden, down), nt(grad_pre, up)
-
-
-def feed_other_body(x_ref, mixed_ref, cot_ref, w_out_ref, gain_ref, bias_ref, up_ref, down_ref,
-                    gup_ref, gdown_ref, hidden1_ref, n_ref, inv_ref, xn_ref, xnt_ref, cott_ref,
+def prepare_body(cot_ref, down_other, down_own, other_ref, own_ref, cott_ref):
+    cot = cot_ref[...]
+    cott_ref[...] = cot.T
+    other_ref[...] = nn(cot, down_other[...])
+    own_ref[...] = nn(cot, down_own[...])
+
+
+def prepare(cotangent, down_other, down_own, after=()):
+    length, width = cotangent.shape
+    return call(
+        prepare_body,
+        (),
+        [VM] * 3,
+        [VM] * 3,
+        [shape(F32, length, down_own.shape[1])] * 2 + [shape(BF, width, length)],
+        us=2.0,
+        after=after,
+    )(cotangent, down_other, down_own)
+
+
+def activations(xn, d_hidden_ref, up_ref):
+    cols = [slice(j, j + 512) for j in range(0, up_ref.shape[1], 512)]
+    pres = [nn(xn, up_ref[:, at]) for at in cols]
+    hidden, grad_pre = [], []
+    for pre, at in zip(pres, cols):
+        v2 = pre * pre
+        h = 0.5 + 0.5 * jnp.tanh(pre * (GELU_A + (GELU_A * GELU_B) * v2))
+        act = pre * h
+        hidden.append(act.astype(BF))
+        slope = h + act * (1.0 - h) * (2.0 * GELU_A + (6.0 * GELU_A * GELU_B) * v2)
+        grad_pre.append((d_hidden_ref[:, at] * slope).astype(BF))
+    return jnp.concatenate(hidden, axis=1), jnp.concatenate(grad_pre, axis=1)
+
+
+def feed_other_body(x_ref, mixed_ref, cott_ref, d_hidden_ref, w_out_ref, gain_ref, bias_ref, up_ref, down_ref,
+                    gup_ref, gdown_ref, hidden1_ref, n_ref, inv_ref, xn_ref, xnt_ref,
                     part_ref, d_ref):
     hidden1 = x_ref[...].astype(F32) + tn(mixed_ref[...], w_out_ref[...])
     hidden1_ref[...] = hidden1
@@ -402,30 +428,28 @@
     n = centered * inverse
     n_ref[...] = n
     inv_ref[...] = jnp.broadcast_to(inverse, inv_ref.shape)
-    xn_ref[...] = (n * gain_ref[...] + bias_ref[...]).astype(BF)
-    xnt_ref[...] = xn_ref[...].T
-    cott_ref[...] = cot_ref[...].T
-    for j in range(up_ref.shape[1] // 512):
-        part, d = feed_step(j, xn_ref[...], cot_ref[...], xnt_ref[...], cott_ref[...],
-                            up_ref, down_ref, gup_ref, gdown_ref)
-        part_ref[...] = part if j == 0 else part_ref[...] + part
-        d_ref[...] = d if j == 0 else d_ref[...] + d
-
-
-def feed_own_body(hidden1_ref, n_ref, inv_ref, xn_ref, xnt_ref, cott_ref, part_ref, d_in_ref,
+    xn = (n * gain_ref[...] + bias_ref[...]).astype(BF)
+    xnt = xn.T
+    xn_ref[...] = xn
+    xnt_ref[...] = xnt
+    hidden, grad_pre = activations(xn, d_hidden_ref, up_ref)
+    gdown_ref[...] = nn(cott_ref[...], hidden).astype(BF)
+    gup_ref[...] = nn(xnt, grad_pre).astype(BF)
+    part_ref[...] = nt(hidden, down_ref[...])
+    d_ref[...] = nt(grad_pre, up_ref[...])
+
+
+def feed_own_body(hidden1_ref, n_ref, inv_ref, xn_ref, xnt_ref, part_ref, d_in_ref, cott_ref, d_hidden_ref,
                   mixed_ref, cot_ref, w_out_ref, gain_ref, up_ref, down_ref,
                   output_ref, d_hidden1_ref, g_ref, out_send_ref, out_keep_ref, norms_ref,
-                  gup_ref, gdown_ref, sum_ref, d_ref):
-    for j in range(up_ref.shape[1] // 512):
-        part, d = feed_step(j, xn_ref[...], cot_ref[...], xnt_ref[...], cott_ref[...],
-                            up_ref, down_ref, gup_ref, gdown_ref)
-        sum_ref[...] = (part_ref[...] if j == 0 else sum_ref[...]) + part
-        d_ref[...] = (d_in_ref[...] if j == 0 else d_ref[...]) + d
-    output_ref[...] = (hidden1_ref[...] + sum_ref[...]).astype(BF)
-    dx, n = d_ref[...], n_ref[...]
+                  gup_ref, gdown_ref):
+    hidden, grad_pre = activations(xn_ref[...], d_hidden_ref, up_ref)
+    dx, n = d_in_ref[...] + nt(grad_pre, up_ref[...]), n_ref[...]
     norms_ref[...] = jnp.concatenate(
         [jnp.sum(dx * n, axis=0, keepdims=True), jnp.sum(dx, axis=0, keepdims=True)] * 4, axis=0
     )
+    output_ref[...] = (hidden1_ref[...] + (part_ref[...] + nt(hidden, down_ref[...]))).astype(BF)
+    gdown_ref[...] = nn(cott_ref[...], hidden).astype(BF)
     d_n = dx * gain_ref[...]
     d_in = (
         d_n
@@ -435,6 +459,7 @@
     d_hidden1 = cot_ref[...].astype(F32) + d_in
     d_hidden1_ref[...] = d_hidden1
     d_branch = d_hidden1.astype(BF)
+    gup_ref[...] = nn(xnt_ref[...], grad_pre).astype(BF)
     g_ref[...] = nt(w_out_ref[...], d_branch).astype(BF)
     grad_out = nn(mixed_ref[...], d_branch).astype(BF)
     half = grad_out.shape[1] // 2
@@ -443,33 +468,31 @@
     out_send_ref[...] = jnp.where(second, grad_out[:, :half], grad_out[:, half:])
 
 
-def feed_other(x, mixed, cotangent, w_out, gain, bias, up, down):
+def feed_other(x, mixed, cott, d_hidden, w_out, gain, bias, up, down):
     length, width = x.shape
     half, sq = shape(BF, *up.shape), lambda dt: shape(dt, length, width)
     return call(
         feed_other_body,
         (),
-        [VM] * 8,
-        [VM] * 10,
-        [half, half, sq(F32), sq(F32), shape(F32, length, 128),
-         sq(BF), sq(BF), sq(BF), sq(F32), sq(F32)],
+        [VM] * 9,
+        [VM] * 9,
+        [half, half, sq(F32), sq(F32), shape(F32, length, 128), sq(BF), sq(BF), sq(F32), sq(F32)],
         us=6.0,
-    )(x, mixed, cotangent, w_out, gain, bias, up, down)
-
-
-def feed_own(saved, mixed, cotangent, w_out, gain, up, down, after=()):
+    )(x, mixed, cott, d_hidden, w_out, gain, bias, up, down)
+
+
+def feed_own(saved, cott, d_hidden, mixed, cotangent, w_out, gain, up, down, after=()):
     length, width = mixed.shape
     half, sq = shape(BF, *up.shape), lambda dt: shape(dt, length, width)
     return call(
         feed_own_body,
         (),
-        [VM] * 14,
+        [VM] * 15,
         [VM] * 8,
         [sq(BF), sq(F32), sq(BF)] + [shape(BF, width, width // 2)] * 2 + [shape(F32, 8, width), half, half],
-        [pltpu.VMEM((length, width), F32)] * 2,
         us=6.0,
         after=after,
-    )(*saved, mixed, cotangent, w_out, gain, up, down)
+    )(*saved, cott, d_hidden, mixed, cotangent, w_out, gain, up, down)
 
 
 def scores_back_body(own_side, starts_ref, heads_ref, mask_ref, g_ref, mem_ref, number_ref, inverse_ref, weight_ref,
@@ -482,16 +505,20 @@
         a_ref, spread_ref, d_total_ref, early_ref, late_ref, pack_ref, sums_ref = refs
     length = heads_ref.shape[2]
     enters = enters_row(starts_ref, length)
+    heads = [head_of(own_side, i) for i in range(SIDE)]
+    rows = [head_rows(head) for head in heads]
+    held = [parts(heads_ref, head) for head in heads]
+    values = [causal_pairs(held[i][2], g_ref[rows[i], :], mask_ref) for i in range(SIDE)]
     for i in range(SIDE):
-        head, at = head_of(own_side, i), slice(i * HEAD, i * HEAD + HEAD)
-        rows = head_rows(head)
-        q, k, v, c = parts(heads_ref, head)
-        g = g_ref[rows, :]
-        mem_vt = mem_ref[rows, :][:, HEAD:]
+        store_pairs((early_ref, late_ref), i, values[i])
+    numbers = [
+        causal_sum(held[i][3], values[i]) + enters * tn(mem_ref[rows[i], :][:, HEAD:], g_ref[rows[i], :])
+        for i in range(SIDE)
+    ]
+    kept = []
+    for i, number_v in enumerate(numbers):
+        at = slice(i * HEAD, i * HEAD + HEAD)
         number, inverse, weight = number_ref[at, :], inverse_ref[at, :], weight_ref[at, :]
-        values = causal_pairs(v, g, mask_ref)
-        store_pairs((early_ref, late_ref), i, values)
-        number_v = causal_sum(c, values) + enters * tn(mem_vt, g)
         d_weight = number_v * inverse
         d_score = weight * (d_weight - jnp.sum(weight * d_weight, axis=0, keepdims=True))
         a = d_score * (inverse * SCALE)
@@ -500,10 +527,12 @@
         a_ref[at, :] = a.astype(BF)
         spread_ref[at, :] = spread.astype(BF)
         d_total_ref[at, :] = d_total.astype(BF)
-        d_k = nt((a * enters).astype(BF), q)
-        d_vt = nt(g, (spread * enters).astype(BF))
-        pack_ref[rows, :] = jnp.concatenate([d_k, d_vt], axis=1).astype(BF)
-        sums_ref[rows, :] = jnp.broadcast_to(jnp.sum(d_total * enters, axis=1, keepdims=True), (HEAD, 128))
+        kept.append(((a * enters).astype(BF), (spread * enters).astype(BF), d_total * enters))
+    for i, (a, spread, d_total) in enumerate(kept):
+        d_k = nt(a, held[i][0])
+        d_vt = nt(g_ref[rows[i], :], spread)
+        pack_ref[rows[i], :] = jnp.concatenate([d_k, d_vt], axis=1).astype(BF)
+        sums_ref[rows[i], :] = jnp.broadcast_to(jnp.sum(d_total, axis=1, keepdims=True), (HEAD, 128))
     if own_side:
         pack_totals(pack_ref, sums_ref[...].T[0:8])
 
@@ -528,29 +557,31 @@
                     v_early, v_late, l_early, l_late, p_early, p_late, d_ref):
     length = heads_ref.shape[2]
     enters = enters_row(starts_ref, length)
+    heads = [head_of(own_side, i) for i in range(SIDE)]
+    rows = [head_rows(head) for head in heads]
+    held = [parts(heads_ref, head) for head in heads]
+    ats = [slice(i * HEAD, i * HEAD + HEAD) for i in range(SIDE)]
+    steps = [causal_pairs(held[i][3], a_ref[ats[i], :], mask_ref) for i in range(SIDE)]
     from_totals = causal_back(mask_pair(mask_ref), d_total_ref[...].T).T
-    held = None
+    controls = []
     for i in range(SIDE):
-        head, at = head_of(own_side, i), slice(i * HEAD, i * HEAD + HEAD)
-        rows = head_rows(head)
-        q, k, v, c = parts(heads_ref, head)
-        g, a, spread = g_ref[rows, :], a_ref[at, :], spread_ref[at, :]
-        mem_k = mem_ref[rows, :][:, :HEAD]
-        steps = causal_pairs(c, a, mask_ref)
-        d_ref[i, :HEAD, :] = causal_sum(k, steps) + enters * tn(mem_k, a)
+        odd = i % 2 == 1
+        controls.append(
+            causal_back(load_pairs((p_early, p_late), i), padded(a_ref[ats[i], :], odd))
+            + causal_back(load_pairs((v_early, v_late), i), padded(spread_ref[ats[i], :], odd))
+        )
+    for i in range(SIDE):
+        mem_k = mem_ref[rows[i], :][:, :HEAD]
+        d_ref[i, :HEAD, :] = causal_sum(held[i][1], steps[i]) + enters * tn(mem_k, a_ref[ats[i], :])
+    for i in range(SIDE):
         d_ref[i, HEAD : 3 * HEAD, :] = (
-            causal_back(steps, padded(q, False)) + causal_back(load_pairs((l_early, l_late), i), padded(g, True))
+            causal_back(steps[i], padded(held[i][0], False))
+            + causal_back(load_pairs((l_early, l_late), i), padded(g_ref[rows[i], :], True))
         ).T
-        odd = i % 2 == 1
-        d_control = causal_back(load_pairs((p_early, p_late), i), padded(a, odd)) + causal_back(
-            load_pairs((v_early, v_late), i), padded(spread, odd)
-        )
-        if odd:
-            two = (held + d_control).T
-            for n in range(2):
-                total_rows = slice((i - 1 + n) * HEAD, (i + n) * HEAD)
-                d_ref[i - 1 + n, 3 * HEAD :, :] = two[n * HEAD : n * HEAD + HEAD] + from_totals[total_rows]
-        held = d_control
+    for i in range(0, SIDE, 2):
+        two = (controls[i] + controls[i + 1]).T
+        for n in range(2):
+            d_ref[i + n, 3 * HEAD :, :] = two[n * HEAD : n * HEAD + HEAD] + from_totals[ats[i + n]]
 
 
 def heads_back(own_side, starts, heads, mask, g, mem, scores, links, pairs, after=()):
@@ -561,56 +592,65 @@
         [SMEM] + [VM] * 13,
         VM,
         shape(F32, SIDE, 4 * HEAD, length),
-        us=8.0 if own_side else 3.0,
+        us=1.0,
         after=after,
     )(starts, heads, mask, g, mem, *scores, *links, *pairs)
 
 
-def project_back_body(own_side, starts_ref, heads_ref, d_ref, control_ref, partner_ref, far_ref, xnt_ref, w_ref, *refs):
-    if own_side:
-        (dx_in_ref, x_ref, gain_ref, d_hidden1_ref, norms2_ref,
-         grad_ref, grad_x_ref, norms_ref, mem_ref, totals_ref, proj_ref) = refs
-    else:
-        grad_ref, dx_ref, mem_ref, totals_ref, proj_ref = refs
+def project_back_body(starts_ref, heads_ref, d_other, d_own, control_ref, partner_ref, far_ref, xnt_ref,
+                      proj_ref, keep_ref, send_ref, mem_ref, totals_ref):
     length, width = xnt_ref.shape[1], xnt_ref.shape[0]
     arrived(True, length, starts_ref, partner_ref, far_ref, mem_ref, totals_ref)
     tail = tail_row(doc_begin_row(starts_ref, length), length)
     tail_bf = tail.astype(BF)
-    dx = None
-    for p in range(SIDE // 2):
-        for i in range(2):
-            n = 2 * p + i
-            head = head_of(own_side, n)
-            rows = head_rows(head)
-            mem = mem_ref[rows, :]
-            back_k, back_vt = mem[:, :HEAD], mem[:, HEAD:]
-            q, k, v, c = parts(heads_ref, head)
-            c_tail = c * tail_bf
-            d_q = d_ref[n, :HEAD, :]
-            d_k = d_ref[n, HEAD : 2 * HEAD, :] + tn(back_k, c_tail)
-            d_v = d_ref[n, 2 * HEAD : 3 * HEAD, :] + nn(back_vt, c_tail)
-            d_c = d_ref[n, 3 * HEAD :, :] + tail * (
-                nn(back_k, k) + tn(back_vt, v) + totals_ref[rows, 0:1]
-            )
-            d_c = d_c * control_ref[rows, :]
-            for m, value in enumerate((d_q, d_k, d_v, d_c)):
-                proj_ref[p, m * 128 + i * HEAD : m * 128 + i * HEAD + HEAD, :] = value.astype(BF)
-        d_proj = proj_ref[p]
-        grad_ref[:, p * 512 : p * 512 + 512] = nt(xnt_ref[...], d_proj).astype(BF)
-        first = head_of(own_side, 2 * p) * HEAD
-        w = jnp.concatenate(
-            [w_ref[:, pl.ds(pl.multiple_of(m * width + first, 128), 128)] for m in range(4)], axis=1
-        )
-        dx = nn(w, d_proj) if dx is None else dx + nn(w, d_proj)
-    if not own_side:
-        dx_ref[...] = dx
-        return
+    jobs = [(d_ref, n, head_of(own_side, n)) for own_side, d_ref in ((False, d_other), (True, d_own)) for n in range(SIDE)]
+    more = []
+    for d_ref, n, head in jobs:
+        mem = mem_ref[head_rows(head), :]
+        back_k, back_vt = mem[:, :HEAD], mem[:, HEAD:]
+        q, k, v, c = parts(heads_ref, head)
+        c_tail = c * tail_bf
+        more.append((tn(back_k, c_tail), nn(back_vt, c_tail), nn(back_k, k) + tn(back_vt, v)))
+    for (d_ref, n, head), (more_k, more_v, more_c) in zip(jobs, more):
+        rows = head_rows(head)
+        proj_ref[0, rows, :] = d_ref[n, :HEAD, :].astype(BF)
+        proj_ref[1, rows, :] = (d_ref[n, HEAD : 2 * HEAD, :] + more_k).astype(BF)
+        proj_ref[2, rows, :] = (d_ref[n, 2 * HEAD : 3 * HEAD, :] + more_v).astype(BF)
+        d_control = d_ref[n, 3 * HEAD :, :] + tail * (more_c + totals_ref[rows, 0:1])
+        proj_ref[3, rows, :] = (d_control * control_ref[rows, :]).astype(BF)
+    for own_side in (False, True):
+        first = pl.ds(pl.multiple_of(head_of(own_side, 0) * HEAD, SIDE * HEAD), SIDE * HEAD)
+        for m in range(4):
+            grad = nt(xnt_ref[...], proj_ref[m, first, :]).astype(BF)
+            if own_side:
+                keep_ref[:, m * SIDE * HEAD : (m + 1) * SIDE * HEAD] = grad
+            else:
+                send_ref[:, m * SIDE * HEAD : (m + 1) * SIDE * HEAD] = grad
+
+
+def project_back(starts, heads, d_other, d_own, control, partner, far, xnt, after=()):
+    width, length = xnt.shape
+    return call(
+        project_back_body,
+        (),
+        [SMEM] + [VM] * 7,
+        [VM] * 3,
+        [shape(BF, 4, width, length)] + [shape(BF, width, 4 * SIDE * HEAD)] * 2,
+        [pltpu.VMEM((width, 128), BF), pltpu.VMEM((width, 8), F32)],
+        us=5.0,
+        after=after,
+    )(starts, heads, d_other, d_own, control, partner, far, xnt)
+
+
+def norm_back_body(proj_ref, w_ref, x_ref, gain_ref, d_hidden1_ref, norms2_ref, grad_x_ref, norms_ref):
+    length, width = x_ref.shape
+    dx = nn(w_ref[...], proj_ref[...].reshape(4 * width, length))
     x = x_ref[...].astype(F32)
     mean = jnp.mean(x, axis=-1, keepdims=True)
     centered = x - mean
     inverse = lax.rsqrt(jnp.mean(centered * centered, axis=-1, keepdims=True) + EPSILON)
     n = centered * inverse
-    d = (dx_in_ref[...] + dx).T
+    d = dx.T
     sums = [jnp.sum(d * n, axis=0, keepdims=True), jnp.sum(d, axis=0, keepdims=True)]
     rows8 = jnp.concatenate(sums + [norms2_ref[0:6, :]], axis=0)
     norms_ref[...] = jnp.concatenate([rows8, jnp.zeros((120, length), F32)], axis=0).T.astype(BF)
@@ -622,21 +662,17 @@
     ) * inverse
 
 
-def project_back(own_side, starts, heads, d, control, partner, far, xnt, w, rest=(), after=()):
-    width, length = xnt.shape
-    outs = [shape(BF, width, 1024), shape(F32, length, width)]
-    if own_side:
-        outs.append(shape(BF, width, 128))
-    return call(
-        functools.partial(project_back_body, own_side),
-        (),
-        [SMEM] + [VM] * (7 + len(rest)),
-        [VM] * len(outs),
-        outs,
-        [pltpu.VMEM((width, 128), BF), pltpu.VMEM((width, 8), F32), pltpu.VMEM((SIDE // 2, 512, length), BF)],
-        us=5.0 if own_side else 3.5,
+def norm_back(proj, w, x, gain, d_hidden1, norms2, after=()):
+    length, width = x.shape
+    return call(
+        norm_back_body,
+        (),
+        [VM] * 6,
+        [VM] * 2,
+        [shape(F32, length, width), shape(BF, width, 128)],
+        us=0.1,
         after=after,
-    )(starts, heads, d, control, partner, far, xnt, w, *rest)
+    )(proj, w, x, gain, d_hidden1, norms2)
 
 
 def bit_axis(bit):
@@ -669,8 +705,10 @@
 
 def stage_body(plan, *refs):
     refs = list(refs)
-    ins = [[[refs.pop(0) for _ in pieces] for pieces in arrays] for arrays, _, _ in plan]
-    for (arrays, split, dtype), sources in zip(plan, ins):
+    ins = [
+        [[refs.pop(0).at[:, :, pl.ds(*piece)] for piece in pieces] for pieces in arrays] for arrays, _ in plan
+    ]
+    for (arrays, split), sources in zip(plan, ins):
         outs = [refs.pop(0) for _ in range(1 << len(split))]
         blocks = outs[0].shape[0]
         places = [place for _, place in split]
@@ -681,38 +719,31 @@
             ]
             for t in range(blocks):
                 at = place_of(t, places, values)
-                total = None
-                for pieces in sources:
-                    row = jnp.concatenate([p[at] for p in pieces], axis=1) if len(pieces) > 1 else pieces[0][at]
-                    row = row.astype(F32)
-                    total = row if total is None else total + row
+                rows = [
+                    jnp.concatenate([p[at] for p in pieces], axis=1) if len(pieces) > 1 else pieces[0][at]
+                    for pieces in sources
+                ]
+                if len(rows) == 1 or (len(rows) == 2 and out.dtype == BF):
+                    total = sum(rows[1:], rows[0])
+                else:
+                    total = sum(row.astype(F32) for row in rows)
                 out[t] = total.astype(out.dtype)
 
 
 def stage(groups, after=(), dtype=BF):
-    plan, operands, in_specs, out_specs, out_shape = [], [], [], [], []
-    rows = groups[0][0][0][0][0].shape[1]
-    steps = 2 if rows % 32 == 0 else 1
+    plan, operands, out_shape = [], [], []
     for arrays, split in groups:
         for pieces in arrays:
-            for array, first, count in pieces:
-                operands.append(array)
-                in_specs.append(
-                    pl.BlockSpec((array.shape[0], rows // steps, count),
-                                 functools.partial(lambda at, i: (0, i, at), first // count))
-                )
-        blocks, width = arrays[0][0][0].shape[0] >> len(split), sum(p[2] for p in arrays[0])
-        plan.append(([[None] * len(pieces) for pieces in arrays], split, dtype))
-        for _ in range(1 << len(split)):
-            out_specs.append(pl.BlockSpec((blocks, rows // steps, width), lambda i: (0, i, 0)))
-            out_shape.append(jax.ShapeDtypeStruct((blocks, rows, width), dtype))
+            operands += [array for array, _, _ in pieces]
+        (array, _, _), width = arrays[0][0], sum(p[2] for p in arrays[0])
+        plan.append(([[(first, count) for _, first, count in pieces] for pieces in arrays], split))
+        out_shape += [shape(dtype, array.shape[0] >> len(split), array.shape[1], width)] * (1 << len(split))
     outs = list(
-        call(functools.partial(stage_body, plan), (steps,), in_specs, out_specs, out_shape, after=after)(*operands)
+        call(functools.partial(stage_body, plan), (), [VM] * len(operands), [VM] * len(out_shape), out_shape, after=after)(
+            *operands
+        )
     )
-    result = []
-    for _, split in groups:
-        result.append([outs.pop(0) for _ in range(1 << len(split))])
-    return result
+    return [[outs.pop(0) for _ in range(1 << len(split))] for _, split in groups]
 
 
 def all_of(a):
@@ -750,11 +781,8 @@
     for f in range(2):
         keep_own = second if f else jnp.logical_not(second)
         half = jnp.where(keep_own, own[:, :1024], other[:, :1024])
-        for p in range(2):
-            for m in range(4):
-                grad_in_ref[:, m * 512 + f * 256 + p * 128 : m * 512 + f * 256 + p * 128 + 128] = (
-                    half[:, p * 512 + m * 128 : p * 512 + m * 128 + 128]
-                )
+        for m in range(4):
+            grad_in_ref[:, m * 512 + f * 256 : m * 512 + f * 256 + 256] = half[:, m * 256 : m * 256 + 256]
         grad_out_ref[:, f * 256 : f * 256 + 256] = jnp.where(
             keep_own, out_own[...], out_other[...]
         ).astype(F32)
@@ -790,13 +818,14 @@
     both = combine(False, length, starts, own, partner, after=[number_o])
     far = swap(both, "seq", 1)
     number, total, *pairs_own = local_sums(True, heads, mask, after=[both])
+    d_hidden_other, d_hidden_own, cott = prepare(cotangent, down_other, down_own, after=[number])
     mixed, memory, saved_other, saved_own = mix(
-        starts, heads, mask, partner, far, (number_o, total_o), (number, total))
+        starts, heads, mask, partner, far, (number_o, total_o), (number, total), after=[cott])
     gup_send, gdown_send, *saved = feed_other(
-        x, mixed, cotangent, out_weight, row(norm2_gain), row(norm2_bias), up_other, down_other)
+        x, mixed, cott, d_hidden_other, out_weight, row(norm2_gain), row(norm2_bias), up_other, down_other)
     gup_got, gdown_got = swap(gup_send, "ffn", 1), swap(gdown_send, "ffn", 1)
     (output, d_hidden1, g, out_send, out_keep, norms2, gup_own, gdown_own) = feed_own(
-        saved, mixed, cotangent, out_weight, row(norm2_gain), up_own, down_own)
+        saved, cott, d_hidden_own, mixed, cotangent, out_weight, row(norm2_gain), up_own, down_own)
     out_got = swap(out_send, "ffn", 1)
 
     out_half = width // 4
@@ -815,10 +844,10 @@
         if n >= 2:
             if n == 2:
                 groups = [[pieces_a + pieces_b for pieces_a, pieces_b in zip(*groups)]]
-            bits_now = left[0][:1]
-            splits = [[(bits_now[0], 0)]]
+            bits_now = left[0][-1:]
+            splits = [[(bits_now[0], len(left[0]) - 1)]]
             for rest in left:
-                rest.pop(0)
+                rest.pop()
         else:
             bits_now = [order[n] for order in orders]
             splits = [[(bit, rest.index(bit))] for bit, rest in zip(bits_now, left)]
@@ -836,33 +865,32 @@
     d_partner = swap(d_own, "ffn", 1)
     d_both = combine(True, length, starts, d_own, d_partner)
     d_far = swap(d_both, "seq", 1)
-    side = (control, d_partner, d_far, xnt, in_weight)
     d_other = heads_back(False, *back, scores_other, saved_other[3:], pairs_other, after=[d_both])
-    groups, sent = advance(groups, 1, [d_other])
-    in_send, dx = project_back(False, starts, heads, d_other, *side, after=sent)
+    d_mine = heads_back(True, *back, scores_own, saved_own[3:], pairs_own, after=[d_other])
+    groups, sent = advance(groups, 1, [d_mine])
+    proj, in_keep, in_send = project_back(
+        starts, heads, d_other, d_mine, control, d_partner, d_far, xnt, after=sent)
     in_got = swap(in_send, "ffn", 1)
-    d_mine = heads_back(True, *back, scores_own, saved_own[3:], pairs_own, after=[in_send])
-    groups, sent = advance(groups, 2, [d_mine])
-    in_keep, grad_tokens, norms = project_back(
-        True, starts, heads, d_mine, *side,
-        rest=(dx, x, row(norm1_gain), d_hidden1, norms2), after=sent)
+    grad_tokens, norms = norm_back(
+        proj, in_weight, x, row(norm1_gain), d_hidden1, norms2, after=[in_send])
 
     late = [
         all_of(blocked(in_keep)) + all_of(blocked(norms)),
         all_of(blocked(in_got)) + all_of(jnp.zeros_like(blocked(norms))),
     ]
     rest = list(range(bits))
-    first = True
+    stages = list(range(2, bits))
     while rest:
         now = rest[:2]
         split = [(b, rest.index(b)) for b in now]
         rest = rest[2:]
         (kept, *sent), = stage([(late, split)])
         late = [all_of(kept)] + [all_of(send_across(s, p)) for s, p in zip(sent, patterns(now))]
-        if first:
-            first, token = False, [kept]
-            for n in range(3, bits):
-                groups, token = advance(groups, n, token)
+        token = [kept]
+        while stages:
+            groups, token = advance(groups, stages.pop(0), token)
+            if rest:
+                break
     grad_up, grad_down, out = finish(*(a[0][0] for a in groups[0]), gup_own.shape[1], out_half, after=[kept])
     (final,), = stage([(late, [])], after=[out])
     grad_in, grad_out, *norms = join(final, swap(final, "ffn", 1), out, swap(out, "ffn", 1))

time: 98.3 us -> 90.5 us (0.921)
  Pallas kernels: 48.9 us -> 40.5 us
    pallas_call x23 -> x24, Pallas kernels: 48.9 us -> 40.5 us  [start(): pl.pallas_call(run, grid=grid, in_specs=list(in_specs) + [ANY] * len(afte...]
    ppermute x12, waiting for transfers between devices: 18.6 us -> 19.7 us  [send_across(): lax.ppermute(a, ('dp', 'seq'), [(i, i ^ flip) for i in range(seqs * dps)])]
    ppermute x12, waiting for transfers between devices: 5.18 us -> 4.18 us  [swap(): return lax.ppermute(a, axis, [(i, i ^ bit) for i in range(size)])]
  transfers between devices with their start and end apart: 24 -> 24, of which waited for: 10 -> 11; matrix products, arithmetic and copies ran while one was open for 0% -> 0% of each run, Pallas kernels for 38% -> 35%
where the time goes in v3:
time: 90.5 us; the launch traced here: 90.3 us
  Pallas kernels  40.5 us (45%)
  starting transfers between devices  25 us (28%)
  waiting for transfers between devices  23.9 us (26%)
  between operations  0.93 us (1%)
    pallas_call x24, Pallas kernels, start(): pl.pallas_call(run, grid=grid, in_specs=list(in_specs) + [ANY] * len(afte...  40.5 us
    ppermute x12, waiting for transfers between devices, send_across(): lax.ppermute(a, ('dp', 'seq'), [(i, i ^ flip) for i in range(seqs * dps)])  19.7 us
    ppermute x12, starting transfers between devices, send_across(): lax.ppermute(a, ('dp', 'seq'), [(i, i ^ flip) for i in range(seqs * dps)])  18 us
    ppermute x12, starting transfers between devices, swap(): return lax.ppermute(a, axis, [(i, i ^ bit) for i in range(size)])  6.94 us
    ppermute x12, waiting for transfers between devices, swap(): return lax.ppermute(a, axis, [(i, i ^ bit) for i in range(size)])  4.18 us
  transfers between devices with their start and end apart: 24, of which 11 were waited for; matrix products, arithmetic and copies ran while one was open for 0% of the time, Pallas kernels for 35%

profile of v3, /device:TPU:0, one launch (start us, length us, event | category | flops | bytes accessed | tf_op | source)
XLA Modules:
  0.0 90.3 jit_solution(11999034481706770298)
XLA Ops:
  0.6 0.5 collective-permute-start.2
  1.2 4.8 %shard_map.186 = (bf16[8,256,512]{2,1,0:T(8,128)(2,1)S(1)}, f32[512,512]{1,0:T(8,128)S(1)}, bf16[512,512]{1,0:T(8,128)(2,1)S(1)}, bf16[576,128]{1,0:T(8,128)(2,1)S(1)}, bf16[512,512]{1,0:T(8,128)(2,1)S(1)}) custom-call(bf16[512,512]{1,0:T(8,128)(2,1)} %bitcast.17, f32[1,512]{1,0:T(1,128)} %bitcast.33, f32[1,512]{1,0:T(1,128)} %bitcast.38, ...), custom_call_target="tpu_custom_call" | custom-call | flops 43000000 | bytes 8192 | tf_op jit(solution)/shard_map/pallas_call | solution.py:49
  6.1 0.5 collective-permute-start
  6.6 0.9 %shard_map.187 = (f32[256,512]{1,0:T(8,128)S(1)}, f32[256,512]{1,0:T(8,128)S(1)}, bf16[4,256,256]{2,1,0:T(8,128)(2,1)S(1)}, bf16[4,512,256]{2,1,0:T(8,128)(2,1)S(1)}) custom-call(bf16[8,256,512]{2,1,0:T(8,128)(2,1)S(1)} %get-tuple-element.102.refs_0_.refs_1_, bf16[512,512]{1,0:T(8,128)(2,1)S(1)} %get-tuple-element.103.refs_1_.refs_2_), custom_call_target="tpu_custom_call" | custom-call | flops 30000000 | bytes 8192 | tf_op jit(solution)/shard_map/pallas_call | solution.py:49
  7.6 0.6 shard_map.188.refs_2_
  8.2 2.9 %collective-permute-start.1 = (bf16[576,128]{1,0:T(8,128)(2,1)S(1)}, bf16[576,128]{1,0:T(8,128)(2,1)S(1)}, u32[]{:S(2)}, u32[]{:S(2)}) collective-permute-start(bf16[576,128]{1,0:T(8,128)(2,1)S(1)} %shard_map.188.refs_2_), channel_id=1, source_target_pairs={{0,2},{2,0},{1,3},{3,1},{4,6},{6,4},{5,7},{7,5},{8,10},{10,8},{9,1... | collective-permute-start | bytes 442376 | tf_op jit(solution)/shard_map/ppermute | solution.py:36
  11.1 0.9 %shard_map.189 = (f32[256,512]{1,0:T(8,128)S(1)}, f32[256,512]{1,0:T(8,128)S(1)}, bf16[4,256,256]{2,1,0:T(8,128)(2,1)S(1)}, bf16[4,512,256]{2,1,0:T(8,128)(2,1)S(1)}) custom-call(bf16[8,256,512]{2,1,0:T(8,128)(2,1)S(1)} %get-tuple-element.102.refs_0_.refs_1_, bf16[512,512]{1,0:T(8,128)(2,1)S(1)} %get-tuple-element.103.refs_1_.refs_2_, ...), custom_call_target="tpu_custom_call" | custom-call | flops 30000000 | bytes 8192 | tf_op jit(solution)/shard_map/pallas_call | solution.py:49
  12.1 1.3 %shard_map.190 = (f32[512,1024]{1,0:T(8,128)S(1)}, f32[512,1024]{1,0:T(8,128)S(1)}, bf16[512,512]{1,0:T(8,128)(2,1)S(1)}) custom-call(bf16[512,512]{1,0:T(8,128)(2,1)S(1)} %bitcast.20, bf16[512,1024]{1,0:T(8,128)(2,1)S(1)} %collective-permute-done.2.refs_1_.refs_8_, bf16[512,1024]{1,0:T(8,128)(2,1)S(1)} %copy-done.2, ...), custom_call_target="tpu_custom_call" | custom-call | flops 20000000 | bytes 8192 | tf_op jit(solution)/shard_map/pallas_call | solution.py:49
  13.4 1.9 %collective-permute-done.1.refs_4_ = bf16[576,128]{1,0:T(8,128)(2,1)S(1)} collective-permute-done((bf16[576,128]{1,0:T(8,128)(2,1)S(1)}, bf16[576,128]{1,0:T(8,128)(2,1)S(1)}, u32[]{:S(2)}, u32[]{:S(2)}) %collective-permute-start.1) | collective-permute-done | bytes 147488 | tf_op jit(solution)/shard_map/ppermute | solution.py:36
  15.3 2.9 %shard_map.191 = (bf16[512,512]{1,0:T(8,128)(2,1)S(1)}, bf16[512,128]{1,0:T(8,128)(2,1)S(1)}, f32[256,512]{1,0:T(8,128)S(1)}, f32[256,512]{1,0:T(8,128)S(1)}, f3...) custom-call(s32[1,8]{1,0:T(1,128)S(1)} %copy-done.6, ...), custom_call_target="tpu_custom_call" | custom-call | flops 40000000 | bytes 8192 | tf_op jit(solution)/shard_map/pallas_call | solution.py:49
  18.2 4.3 %shard_map.192 = (bf16[512,1024]{1,0:T(8,128)(2,1)S(1)}, bf16[512,1024]{1,0:T(8,128)(2,1)S(1)}, f32[512,512]{1,0:T(8,128)S(1)}, f32[512,512]{1,0:T(8,128)S(1)}, ...) custom-call(bf16[512,512]{1,0:T(8,128)(2,1)S(1)} %bitcast.18, ...), custom_call_target="tpu_custom_call" | custom-call | flops 60000000 | bytes 8192 | tf_op jit(solution)/shard_map/pallas_call | solution.py:49
  22.6 0.5 collective-permute-start.4
  23.1 5.1 %shard_map.193 = (bf16[512,512]{1,0:T(8,128)(2,1)}, f32[512,512]{1,0:T(8,128)S(1)}, bf16[512,512]{1,0:T(8,128)(2,1)S(1)}, bf16[512,256]{1,0:T(8,128)(2,1)S(1)}, ...) custom-call(f32[512,512]{1,0:T(8,128)S(1)} %get-tuple-element.112.re, ...), custom_call_target="tpu_custom_call" | custom-call | flops 60000000 | bytes 8192 | tf_op jit(solution)/shard_map/pallas_call | solution.py:49
  28.3 1.9 %shard_map.194 = (bf16[256,512]{1,0:T(8,128)(2,1)S(1)}, bf16[256,512]{1,0:T(8,128)(2,1)S(1)}, bf16[256,512]{1,0:T(8,128)(2,1)S(1)}, bf16[4,256,256]{2,1,0:T(8,12...) custom-call(s32[1,8]{1,0:T(1,128)S(1)} %copy-done.6, ...), custom_call_target="tpu_custom_call" | custom-call | flops 30000000 | bytes 8192 | tf_op jit(solution)/shard_map/pallas_call | solution.py:49
  30.2 0.4 shard_map.195
  30.6 1.9 %collective-permute-start.10 = (bf16[8,32,1152]{2,1,0:T(8,128)(2,1)S(1)}, bf16[8,32,1152]{2,1,0:T(8,128)(2,1)S(1)}, u32[]{:S(2)}, u32[]{:S(2)}) collective-permute-start(bf16[8,32,1152]{2,1,0:T(8,128)(2,1)S(1)} %get-tuple-element.147.refs_11_), channel_id=1, source_target_pairs={{0,8},{2,10},{4,12},{6,14},{8,0},{10,2},{12,4},{14,6},{16,24},{18,... | collective-permute-start | bytes 1769480 | tf_op jit(solution)/shard_map/ppermute | solution.py:690
  32.4 1.5 %collective-permute-start.9 = (bf16[8,32,1152]{2,1,0:T(8,128)(2,1)S(1)}, bf16[8,32,1152]{2,1,0:T(8,128)(2,1)S(1)}, u32[]{:S(2)}, u32[]{:S(2)}) collective-permute-start(bf16[8,32,1152]{2,1,0:T(8,128)(2,1)S(1)} %get-tuple-element.146.refs_10_), channel_id=1, source_target_pairs={{0,4},{2,6},{4,0},{6,2},{8,12},{10,14},{12,8},{14,10},{16,20},{18,... | collective-permute-start | bytes 1769480 | tf_op jit(solution)/shard_map/ppermute | solution.py:690
  34.0 2.0 %shard_map.196 = (bf16[256,512]{1,0:T(8,128)(2,1)S(1)}, bf16[256,512]{1,0:T(8,128)(2,1)S(1)}, bf16[256,512]{1,0:T(8,128)(2,1)S(1)}, bf16[4,256,256]{2,1,0:T(8,12...) custom-call(s32[1,8]{1,0:T(1,128)S(1)} %copy-done.6, ...), custom_call_target="tpu_custom_call" | custom-call | flops 30000000 | bytes 8192 | tf_op jit(solution)/shard_map/pallas_call | solution.py:49
  36.0 1.4 %collective-permute-done.7.refs_2_.refs_5_ = bf16[576,128]{1,0:T(8,128)(2,1)S(1)} collective-permute-done((bf16[576,128]{1,0:T(8,128)(2,1)S(1)}, bf16[576,128]{1,0:T(8,128)(2,1)S(1)}, u32[]{:S(2)}, u32[]{:S(2)}) %collective-permute-start.7) | collective-permute-done | bytes 147488 | tf_op jit(solution)/shard_map/ppermute | solution.py:36
  37.4 0.6 shard_map.197.refs_14_
  38.0 1.5 %collective-permute-start.8 = (bf16[576,128]{1,0:T(8,128)(2,1)S(1)}, bf16[576,128]{1,0:T(8,128)(2,1)S(1)}, u32[]{:S(2)}, u32[]{:S(2)}) collective-permute-start(bf16[576,128]{1,0:T(8,128)(2,1)S(1)} %shard_map.197.refs_14_), channel_id=1, source_target_pairs={{0,2},{2,0},{1,3},{3,1},{4,6},{6,4},{5,7},{7,5},{8,10},{10,8},{9,1... | collective-permute-start | bytes 442376 | tf_op jit(solution)/shard_map/ppermute | solution.py:36
  39.6 3.4 %shard_map.198.refs_14_.refs_2_ = f32[4,256,512]{2,1,0:T(8,128)S(1)} custom-call(s32[1,8]{1,0:T(1,128)S(1)} %copy-done.6, bf16[8,256,512]{2,1,0:T(8,128)(2,1)S(1)} %get-tuple-element.102.refs_0_.refs_1_, bf16[512,512]{1,0:T(8,128)(2,1)S(1)} %get-tuple-element.103.refs_1_.refs_2_, bf16[512,512]{1,0:T(8,128)(2,1)S(1)} %get-tuple-element.121.refs_3_, ...), custom_call_target="tpu_custom_call" | custom-call | flops 10000000 | bytes 8192 | tf_op jit(solution)/shard_map/pallas_call | solution.py:49
  42.9 3.4 %shard_map.199.refs_4_.refs_3_ = f32[4,256,512]{2,1,0:T(8,128)S(1)} custom-call(s32[1,8]{1,0:T(1,128)S(1)} %copy-done.6, bf16[8,256,512]{2,1,0:T(8,128)(2,1)S(1)} %get-tuple-element.102.refs_0_.refs_1_, bf16[512,512]{1,0:T(8,128)(2,1)S(1)} %get-tuple-element.103.refs_1_.refs_2_, bf16[512,512]{1,0:T(8,128)(2,1)S(1)} %get-tuple-element.121.refs_3_, ...), custom_call_target="tpu_custom_call" | custom-call | flops 10000000 | bytes 8192 | tf_op jit(solution)/shard_map/pallas_call | solution.py:49
  46.3 1.5 %collective-permute-done.9.refs_1_ = bf16[8,32,1152]{2,1,0:T(8,128)(2,1)S(1)} collective-permute-done((bf16[8,32,1152]{2,1,0:T(8,128)(2,1)S(1)}, bf16[8,32,1152]{2,1,0:T(8,128)(2,1)S(1)}, u32[]{:S(2)}, u32[]{:S(2)}) %collective-permute-start.9) | collective-permute-done | bytes 589856 | tf_op jit(solution)/shard_map/ppermute | solution.py:690
  48.0 3.0 %shard_map.201 = (bf16[4,512,512]{2,1,0:T(8,128)(2,1)S(1)}, bf16[512,1024]{1,0:T(8,128)(2,1)S(1)}, bf16[512,1024]{1,0:T(8,128)(2,1)S(1)}) custom-call(s32[1,8]{1,0:T(1,128)S(1)} %copy-done.6, bf16[8,256,512]{2,1,0:T(8,128)(2,1)S(1)} %get-tuple-element.102.refs_0_.refs_1_, f32[4,256,512]{2,1,0:T(8,128)S(1)} %shard_map.198.refs_14_.refs_2_, ...), custom_call_target="tpu_custom_call" | custom-call | flops 50000000 | bytes 8192 | tf_op jit(solution)/shard_map/pallas_call | solution.py:49
  51.1 0.6 collective-permute-start.18
  51.7 1.6 %collective-permute-start.19 = (bf16[4,32,1152]{2,1,0:T(8,128)(2,1)S(1)}, bf16[4,32,1152]{2,1,0:T(8,128)(2,1)S(1)}, u32[]{:S(2)}, u32[]{:S(2)}) collective-permute-start(bf16[4,32,1152]{2,1,0:T(8,128)(2,1)S(1)} %get-tuple-element.163.refs_9_), channel_id=1, source_target_pairs={{0,4},{2,6},{4,0},{6,2},{8,12},{10,14},{12,8},{14,10},{16,20},{18,... | collective-permute-start | bytes 884744 | tf_op jit(solution)/shard_map/ppermute | solution.py:690
  53.4 2.9 %shard_map.202 = (f32[512,512]{1,0:T(8,128)}, bf16[512,128]{1,0:T(8,128)(2,1)S(1)}) custom-call(bf16[4,512,512]{2,1,0:T(8,128)(2,1)S(1)} %get-tuple-element.164.refs_0_, bf16[512,2048]{1,0:T(8,128)(2,1)S(1)} %copy-done, bf16[512,512]{1,0:T(8,128)(2,1)S(1)} %bitcast.19, f32[1,512]{1,0:T(1,128)S(1)} %bitcast.34, f32[512,512]{1,0:T(8,128)S(1)} %get-tuple-element.165.refs_4_, ...), custom_call_target="tpu_custom_call" | custom-call | flops 1000000 | bytes 8192 | tf_op jit(solution)/shard_map/pallas_call | solution.py:49
  56.3 0.2 shard_map.203
  56.5 1.6 %collective-permute-start.12 = (bf16[4,32,1152]{2,1,0:T(8,128)(2,1)S(1)}, bf16[4,32,1152]{2,1,0:T(8,128)(2,1)S(1)}, u32[]{:S(2)}, u32[]{:S(2)}) collective-permute-start(bf16[4,32,1152]{2,1,0:T(8,128)(2,1)S(1)} %get-tuple-element.172), channel_id=1, source_target_pairs={{0,2},{2,0},{4,6},{6,4},{8,10},{10,8},{12,14},{14,12},{16,18},{18,... | collective-permute-start | bytes 884744 | tf_op jit(solution)/shard_map/ppermute | solution.py:690
  58.1 0.5 collective-permute-start.13
  58.6 1.5 %collective-permute-start.14 = (bf16[4,32,1152]{2,1,0:T(8,128)(2,1)S(1)}, bf16[4,32,1152]{2,1,0:T(8,128)(2,1)S(1)}, u32[]{:S(2)}, u32[]{:S(2)}) collective-permute-start(bf16[4,32,1152]{2,1,0:T(8,128)(2,1)S(1)} %get-tuple-element.174), channel_id=1, source_target_pairs={{0,6},{2,4},{4,2},{6,0},{8,14},{10,12},{12,10},{14,8},{16,22},{18,... | collective-permute-start | bytes 884744 | tf_op jit(solution)/shard_map/ppermute | solution.py:690
  60.1 0.4 collective-permute-done.18.refs_2_
  60.5 0.5 collective-permute-done.19.refs_3_
  61.2 2.9 %collective-permute-start.20 = (bf16[2,32,2304]{2,1,0:T(8,128)(2,1)S(1)}, bf16[2,32,2304]{2,1,0:T(8,128)(2,1)S(1)}, u32[]{:S(2)}, u32[]{:S(2)}) collective-permute-start(bf16[2,32,2304]{2,1,0:T(8,128)(2,1)S(1)} %get-tuple-element.182), channel_id=1, source_target_pairs={{0,16},{2,18},{4,20},{6,22},{8,24},{10,26},{12,28},{14,30},{16,0},... | collective-permute-start | bytes 884744 | tf_op jit(solution)/shard_map/ppermute | solution.py:690
  64.0 2.5 %collective-permute-done.12.refs_1_ = bf16[4,32,1152]{2,1,0:T(8,128)(2,1)S(1)} collective-permute-done((bf16[4,32,1152]{2,1,0:T(8,128)(2,1)S(1)}, bf16[4,32,1152]{2,1,0:T(8,128)(2,1)S(1)}, u32[]{:S(2)}, u32[]{:S(2)}) %collective-permute-start.12) | collective-permute-done | bytes 294944 | tf_op jit(solution)/shard_map/ppermute | solution.py:690
  66.5 6.7 %collective-permute-done.13.refs_2_ = bf16[4,32,1152]{2,1,0:T(8,128)(2,1)S(1)} collective-permute-done((bf16[4,32,1152]{2,1,0:T(8,128)(2,1)S(1)}, bf16[4,32,1152]{2,1,0:T(8,128)(2,1)S(1)}, u32[]{:S(2)}, u32[]{:S(2)}) %collective-permute-start.13) | collective-permute-done | bytes 294944 | tf_op jit(solution)/shard_map/ppermute | solution.py:690
  73.4 2.8 %collective-permute-done.20.refs_1_ = bf16[2,32,2304]{2,1,0:T(8,128)(2,1)S(1)} collective-permute-done((bf16[2,32,2304]{2,1,0:T(8,128)(2,1)S(1)}, bf16[2,32,2304]{2,1,0:T(8,128)(2,1)S(1)}, u32[]{:S(2)}, u32[]{:S(2)}) %collective-permute-start.20) | collective-permute-done | bytes 294944 | tf_op jit(solution)/shard_map/ppermute | solution.py:690
  76.3 1.6 %collective-permute-start.21 = (bf16[1,32,2304]{2,1,0:T(8,128)(2,1)S(1)}, bf16[1,32,2304]{2,1,0:T(8,128)(2,1)S(1)}, u32[]{:S(2)}, u32[]{:S(2)}) collective-permute-start(bf16[1,32,2304]{2,1,0:T(8,128)(2,1)S(1)} %get-tuple-element.184), channel_id=1, source_target_pairs={{0,2},{2,0},{4,6},{6,4},{8,10},{10,8},{12,14},{14,12},{16,18},{18,... | collective-permute-start | bytes 442376 | tf_op jit(solution)/shard_map/ppermute | solution.py:690
  77.8 0.6 collective-permute-start.15
  78.4 3.4 %collective-permute-start.16 = (bf16[1,32,1152]{2,1,0:T(8,128)(2,1)S(1)}, bf16[1,32,1152]{2,1,0:T(8,128)(2,1)S(1)}, u32[]{:S(2)}, u32[]{:S(2)}) collective-permute-start(bf16[1,32,1152]{2,1,0:T(8,128)(2,1)S(1)} %get-tuple-element.177), channel_id=1, source_target_pairs={{0,16},{2,18},{4,20},{6,22},{8,24},{10,26},{12,28},{14,30},{16,0},... | collective-permute-start | bytes 221192 | tf_op jit(solution)/shard_map/ppermute | solution.py:690
  81.8 0.4 collective-permute-start.17
  82.2 0.7 shard_map.207
  82.9 3.9 %collective-permute-done.16.refs_2_ = bf16[1,32,1152]{2,1,0:T(8,128)(2,1)S(1)} collective-permute-done((bf16[1,32,1152]{2,1,0:T(8,128)(2,1)S(1)}, bf16[1,32,1152]{2,1,0:T(8,128)(2,1)S(1)}, u32[]{:S(2)}, u32[]{:S(2)}) %collective-permute-start.16) | collective-permute-done | bytes 73760 | tf_op jit(solution)/shard_map/ppermute | solution.py:690
  86.8 1.3 %collective-permute-done.17.refs_3_ = bf16[1,32,1152]{2,1,0:T(8,128)(2,1)S(1)} collective-permute-done((bf16[1,32,1152]{2,1,0:T(8,128)(2,1)S(1)}, bf16[1,32,1152]{2,1,0:T(8,128)(2,1)S(1)}, u32[]{:S(2)}, u32[]{:S(2)}) %collective-permute-start.17) | collective-permute-done | bytes 73760 | tf_op jit(solution)/shard_map/ppermute | solution.py:690
  88.2 0.5 collective-permute-start.23
  88.7 0.8 collective-permute-done.23.refs_3_
  89.5 0.7 shard_map.209
  (45 shorter events, 1.1 us)
Async XLA Ops:
  0.6 11.4 %collective-permute-start.2 = (bf16[512,1024]{1,0:T(8,128)(2,1)}, bf16[512,1024]{1,0:T(8,128)(2,1)S(1)}, u32[]{:S(2)}, u32[]{:S(2)}) collective-permute-start(bf16[512,1024]{1,0:T(8,128)(2,1)} %refs_14_.1), channel_id=1, source_target_pairs={{0,1},{1,0},{2,3},{3,2},{4,5},{5,4},{6,7},{7,6},{8,9},{9,8},{10,11... | collective-permute-start | bytes 3145736 | tf_op jit(solution)/shard_map/ppermute | solution.py:36
  1.2 17.0 %collective-permute-start.3 = (bf16[512,1024]{1,0:T(8,128)(2,1)}, bf16[512,1024]{1,0:T(8,128)(2,1)S(1)}, u32[]{:S(2)}, u32[]{:S(2)}) collective-permute-start(bf16[512,1024]{1,0:T(8,128)(2,1)} %refs_13_.1), channel_id=1, source_target_pairs={{0,1},{1,0},{2,3},{3,2},{4,5},{5,4},{6,7},{7,6},{8,9},{9,8},{10,11... | collective-permute-start | bytes 3145736 | tf_op jit(solution)/shard_map/ppermute | solution.py:36
  1.2 6.3 %copy-start.6 = (s32[1,8]{1,0:T(1,128)S(1)}, s32[1,8]{1,0:T(1,128)}, u32[]{:S(2)}) copy-start(s32[1,8]{1,0:T(1,128)} %refs_0_.15) | copy-start | bytes 100
  6.1 1.5 %collective-permute-start = (bf16[576,128]{1,0:T(8,128)(2,1)S(1)}, bf16[576,128]{1,0:T(8,128)(2,1)S(1)}, u32[]{:S(2)}, u32[]{:S(2)}) collective-permute-start(bf16[576,128]{1,0:T(8,128)(2,1)S(1)} %get-tuple-element.104.refs_1_), channel_id=1, source_target_pairs={{0,1},{1,0},{2,3},{3,2},{4,5},{5,4},{6,7},{7,6},{8,9},{9,8},{10,11... | collective-permute-start | bytes 442376 | tf_op jit(solution)/shard_map/ppermute | solution.py:36
  7.5 4.6 %copy-start.2 = (bf16[512,1024]{1,0:T(8,128)(2,1)S(1)}, bf16[512,1024]{1,0:T(8,128)(2,1)}, u32[]{:S(2)}) copy-start(bf16[512,1024]{1,0:T(8,128)(2,1)} %refs_14_.1) | copy-start | bytes 3145732
  7.5 4.6 %copy-start.3 = (bf16[1,512,512]{2,1,0:T(8,128)(2,1)S(1)}, bf16[1,512,512]{2,1,0:T(8,128)(2,1)}, u32[]{:S(2)}) copy-start(bf16[1,512,512]{2,1,0:T(8,128)(2,1)} %param.21) | copy-start | bytes 1572868
  8.2 7.1 %collective-permute-start.1 = (bf16[576,128]{1,0:T(8,128)(2,1)S(1)}, bf16[576,128]{1,0:T(8,128)(2,1)S(1)}, u32[]{:S(2)}, u32[]{:S(2)}) collective-permute-start(bf16[576,128]{1,0:T(8,128)(2,1)S(1)} %shard_map.188.refs_2_), channel_id=1, source_target_pairs={{0,2},{2,0},{1,3},{3,1},{4,6},{6,4},{5,7},{7,5},{8,10},{10,8},{9,1... | collective-permute-start | bytes 442376 | tf_op jit(solution)/shard_map/ppermute | solution.py:36
  15.3 2.9 %copy-start.1 = (bf16[1,512,512]{2,1,0:T(8,128)(2,1)S(1)}, bf16[1,512,512]{2,1,0:T(8,128)(2,1)}, u32[]{:S(2)}) copy-start(bf16[1,512,512]{2,1,0:T(8,128)(2,1)} %param.11) | copy-start | bytes 1572868
  15.3 2.9 %copy-start.4 = (bf16[512,512]{1,0:T(8,128)(2,1)S(1)}, bf16[512,512]{1,0:T(8,128)(2,1)}, u32[]{:S(2)}) copy-start(bf16[512,512]{1,0:T(8,128)(2,1)} %refs_11_.1) | copy-start | bytes 1572868
  15.3 2.9 %copy-start.8 = (f32[512]{0:T(512)S(1)}, f32[512]{0:T(512)}, u32[]{:S(2)}) copy-start(f32[512]{0:T(512)} %param.17) | copy-start | bytes 6148
  15.3 2.9 %copy-start.9 = (f32[512]{0:T(512)S(1)}, f32[512]{0:T(512)}, u32[]{:S(2)}) copy-start(f32[512]{0:T(512)} %param.18) | copy-start | bytes 6148
  18.2 4.9 %copy-start.5 = (bf16[512,1024]{1,0:T(8,128)(2,1)S(1)}, bf16[512,1024]{1,0:T(8,128)(2,1)}, u32[]{:S(2)}) copy-start(bf16[512,1024]{1,0:T(8,128)(2,1)} %refs_13_.1) | copy-start | bytes 3145732
  22.5 7.7 %collective-permute-start.6 = (bf16[512,1024]{1,0:T(8,128)(2,1)S(1)}, bf16[512,1024]{1,0:T(8,128)(2,1)S(1)}, u32[]{:S(2)}, u32[]{:S(2)}) collective-permute-start(bf16[512,1024]{1,0:T(8,128)(2,1)S(1)} %get-tuple-element.145), channel_id=1, source_target_pairs={{0,1},{1,0},{2,3},{3,2},{4,5},{5,4},{6,7},{7,6},{8,9},{9,8},{10,11... | collective-permute-start | bytes 3145736 | tf_op jit(solution)/shard_map/ppermute | solution.py:36
  22.6 7.6 %collective-permute-start.4 = (bf16[512,1024]{1,0:T(8,128)(2,1)S(1)}, bf16[512,1024]{1,0:T(8,128)(2,1)S(1)}, u32[]{:S(2)}, u32[]{:S(2)}) collective-permute-start(bf16[512,1024]{1,0:T(8,128)(2,1)S(1)} %get-tuple-element.142), channel_id=1, source_target_pairs={{0,1},{1,0},{2,3},{3,2},{4,5},{5,4},{6,7},{7,6},{8,9},{9,8},{10,11... | collective-permute-start | bytes 3145736 | tf_op jit(solution)/shard_map/ppermute | solution.py:36
  28.1 2.0 %collective-permute-start.5 = (bf16[512,256]{1,0:T(8,128)(2,1)S(1)}, bf16[512,256]{1,0:T(8,128)(2,1)S(1)}, u32[]{:S(2)}, u32[]{:S(2)}) collective-permute-start(bf16[512,256]{1,0:T(8,128)(2,1)S(1)} %get-tuple-element.143), channel_id=1, source_target_pairs={{0,1},{1,0},{2,3},{3,2},{4,5},{5,4},{6,7},{7,6},{8,9},{9,8},{10,11... | collective-permute-start | bytes 786440 | tf_op jit(solution)/shard_map/ppermute | solution.py:36
  30.6 15.8 %collective-permute-start.10 = (bf16[8,32,1152]{2,1,0:T(8,128)(2,1)S(1)}, bf16[8,32,1152]{2,1,0:T(8,128)(2,1)S(1)}, u32[]{:S(2)}, u32[]{:S(2)}) collective-permute-start(bf16[8,32,1152]{2,1,0:T(8,128)(2,1)S(1)} %get-tuple-element.147.refs_11_), channel_id=1, source_target_pairs={{0,8},{2,10},{4,12},{6,14},{8,0},{10,2},{12,4},{14,6},{16,24},{18,... | collective-permute-start | bytes 1769480 | tf_op jit(solution)/shard_map/ppermute | solution.py:690
  32.4 15.4 %collective-permute-start.9 = (bf16[8,32,1152]{2,1,0:T(8,128)(2,1)S(1)}, bf16[8,32,1152]{2,1,0:T(8,128)(2,1)S(1)}, u32[]{:S(2)}, u32[]{:S(2)}) collective-permute-start(bf16[8,32,1152]{2,1,0:T(8,128)(2,1)S(1)} %get-tuple-element.146.refs_10_), channel_id=1, source_target_pairs={{0,4},{2,6},{4,0},{6,2},{8,12},{10,14},{12,8},{14,10},{16,20},{18,... | collective-permute-start | bytes 1769480 | tf_op jit(solution)/shard_map/ppermute | solution.py:690
  35.9 1.4 %collective-permute-start.7 = (bf16[576,128]{1,0:T(8,128)(2,1)S(1)}, bf16[576,128]{1,0:T(8,128)(2,1)S(1)}, u32[]{:S(2)}, u32[]{:S(2)}) collective-permute-start(bf16[576,128]{1,0:T(8,128)(2,1)S(1)} %get-tuple-element.148.refs_1_), channel_id=1, source_target_pairs={{0,1},{1,0},{2,3},{3,2},{4,5},{5,4},{6,7},{7,6},{8,9},{9,8},{10,11... | collective-permute-start | bytes 442376 | tf_op jit(solution)/shard_map/ppermute | solution.py:36
  38.0 9.9 %collective-permute-start.8 = (bf16[576,128]{1,0:T(8,128)(2,1)S(1)}, bf16[576,128]{1,0:T(8,128)(2,1)S(1)}, u32[]{:S(2)}, u32[]{:S(2)}) collective-permute-start(bf16[576,128]{1,0:T(8,128)(2,1)S(1)} %shard_map.197.refs_14_), channel_id=1, source_target_pairs={{0,2},{2,0},{1,3},{3,1},{4,6},{6,4},{5,7},{7,5},{8,10},{10,8},{9,1... | collective-permute-start | bytes 442376 | tf_op jit(solution)/shard_map/ppermute | solution.py:36
  48.0 5.4 %copy-start = (bf16[512,2048]{1,0:T(8,128)(2,1)S(1)}, bf16[512,2048]{1,0:T(8,128)(2,1)}, u32[]{:S(2)}) copy-start(bf16[512,2048]{1,0:T(8,128)(2,1)} %refs_1_.1) | copy-start | bytes 6291460
  48.0 5.4 %copy-start.7 = (f32[512]{0:T(512)S(1)}, f32[512]{0:T(512)}, u32[]{:S(2)}) copy-start(f32[512]{0:T(512)} %param.13) | copy-start | bytes 6148
  51.0 5.2 %collective-permute-start.11 = (bf16[512,1024]{1,0:T(8,128)(2,1)S(1)}, bf16[512,1024]{1,0:T(8,128)(2,1)S(1)}, u32[]{:S(2)}, u32[]{:S(2)}) collective-permute-start(bf16[512,1024]{1,0:T(8,128)(2,1)S(1)} %get-tuple-element.167.refs_6_), channel_id=1, source_target_pairs={{0,1},{1,0},{2,3},{3,2},{4,5},{5,4},{6,7},{7,6},{8,9},{9,8},{10,11... | collective-permute-start | bytes 3145736 | tf_op jit(solution)/shard_map/ppermute | solution.py:36
  51.1 9.4 %collective-permute-start.18 = (bf16[4,32,1152]{2,1,0:T(8,128)(2,1)S(1)}, bf16[4,32,1152]{2,1,0:T(8,128)(2,1)S(1)}, u32[]{:S(2)}, u32[]{:S(2)}) collective-permute-start(bf16[4,32,1152]{2,1,0:T(8,128)(2,1)S(1)} %get-tuple-element.162.refs_8_), channel_id=1, source_target_pairs={{0,8},{2,10},{4,12},{6,14},{8,0},{10,2},{12,4},{14,6},{16,24},{18,... | collective-permute-start | bytes 884744 | tf_op jit(solution)/shard_map/ppermute | solution.py:690
  51.7 9.3 %collective-permute-start.19 = (bf16[4,32,1152]{2,1,0:T(8,128)(2,1)S(1)}, bf16[4,32,1152]{2,1,0:T(8,128)(2,1)S(1)}, u32[]{:S(2)}, u32[]{:S(2)}) collective-permute-start(bf16[4,32,1152]{2,1,0:T(8,128)(2,1)S(1)} %get-tuple-element.163.refs_9_), channel_id=1, source_target_pairs={{0,4},{2,6},{4,0},{6,2},{8,12},{10,14},{12,8},{14,10},{16,20},{18,... | collective-permute-start | bytes 884744 | tf_op jit(solution)/shard_map/ppermute | solution.py:690
  56.5 10.0 %collective-permute-start.12 = (bf16[4,32,1152]{2,1,0:T(8,128)(2,1)S(1)}, bf16[4,32,1152]{2,1,0:T(8,128)(2,1)S(1)}, u32[]{:S(2)}, u32[]{:S(2)}) collective-permute-start(bf16[4,32,1152]{2,1,0:T(8,128)(2,1)S(1)} %get-tuple-element.172), channel_id=1, source_target_pairs={{0,2},{2,0},{4,6},{6,4},{8,10},{10,8},{12,14},{14,12},{16,18},{18,... | collective-permute-start | bytes 884744 | tf_op jit(solution)/shard_map/ppermute | solution.py:690
  58.1 15.1 %collective-permute-start.13 = (bf16[4,32,1152]{2,1,0:T(8,128)(2,1)S(1)}, bf16[4,32,1152]{2,1,0:T(8,128)(2,1)S(1)}, u32[]{:S(2)}, u32[]{:S(2)}) collective-permute-start(bf16[4,32,1152]{2,1,0:T(8,128)(2,1)S(1)} %get-tuple-element.173), channel_id=1, source_target_pairs={{0,4},{2,6},{4,0},{6,2},{8,12},{10,14},{12,8},{14,10},{16,20},{18,... | collective-permute-start | bytes 884744 | tf_op jit(solution)/shard_map/ppermute | solution.py:690
  58.6 14.6 %collective-permute-start.14 = (bf16[4,32,1152]{2,1,0:T(8,128)(2,1)S(1)}, bf16[4,32,1152]{2,1,0:T(8,128)(2,1)S(1)}, u32[]{:S(2)}, u32[]{:S(2)}) collective-permute-start(bf16[4,32,1152]{2,1,0:T(8,128)(2,1)S(1)} %get-tuple-element.174), channel_id=1, source_target_pairs={{0,6},{2,4},{4,2},{6,0},{8,14},{10,12},{12,10},{14,8},{16,22},{18,... | collective-permute-start | bytes 884744 | tf_op jit(solution)/shard_map/ppermute | solution.py:690
  61.2 15.1 %collective-permute-start.20 = (bf16[2,32,2304]{2,1,0:T(8,128)(2,1)S(1)}, bf16[2,32,2304]{2,1,0:T(8,128)(2,1)S(1)}, u32[]{:S(2)}, u32[]{:S(2)}) collective-permute-start(bf16[2,32,2304]{2,1,0:T(8,128)(2,1)S(1)} %get-tuple-element.182), channel_id=1, source_target_pairs={{0,16},{2,18},{4,20},{6,22},{8,24},{10,26},{12,28},{14,30},{16,0},... | collective-permute-start | bytes 884744 | tf_op jit(solution)/shard_map/ppermute | solution.py:690
  76.3 5.9 %collective-permute-start.21 = (bf16[1,32,2304]{2,1,0:T(8,128)(2,1)S(1)}, bf16[1,32,2304]{2,1,0:T(8,128)(2,1)S(1)}, u32[]{:S(2)}, u32[]{:S(2)}) collective-permute-start(bf16[1,32,2304]{2,1,0:T(8,128)(2,1)S(1)} %get-tuple-element.184), channel_id=1, source_target_pairs={{0,2},{2,0},{4,6},{6,4},{8,10},{10,8},{12,14},{14,12},{16,18},{18,... | collective-permute-start | bytes 442376 | tf_op jit(solution)/shard_map/ppermute | solution.py:690
  77.8 5.1 %collective-permute-start.15 = (bf16[1,32,1152]{2,1,0:T(8,128)(2,1)S(1)}, bf16[1,32,1152]{2,1,0:T(8,128)(2,1)S(1)}, u32[]{:S(2)}, u32[]{:S(2)}) collective-permute-start(bf16[1,32,1152]{2,1,0:T(8,128)(2,1)S(1)} %get-tuple-element.176), channel_id=1, source_target_pairs={{0,8},{2,10},{4,12},{6,14},{8,0},{10,2},{12,4},{14,6},{16,24},{18,... | collective-permute-start | bytes 221192 | tf_op jit(solution)/shard_map/ppermute | solution.py:690
  78.4 8.4 %collective-permute-start.16 = (bf16[1,32,1152]{2,1,0:T(8,128)(2,1)S(1)}, bf16[1,32,1152]{2,1,0:T(8,128)(2,1)S(1)}, u32[]{:S(2)}, u32[]{:S(2)}) collective-permute-start(bf16[1,32,1152]{2,1,0:T(8,128)(2,1)S(1)} %get-tuple-element.177), channel_id=1, source_target_pairs={{0,16},{2,18},{4,20},{6,22},{8,24},{10,26},{12,28},{14,30},{16,0},... | collective-permute-start | bytes 221192 | tf_op jit(solution)/shard_map/ppermute | solution.py:690
  81.8 6.3 %collective-permute-start.17 = (bf16[1,32,1152]{2,1,0:T(8,128)(2,1)S(1)}, bf16[1,32,1152]{2,1,0:T(8,128)(2,1)S(1)}, u32[]{:S(2)}, u32[]{:S(2)}) collective-permute-start(bf16[1,32,1152]{2,1,0:T(8,128)(2,1)S(1)} %get-tuple-element.178), channel_id=1, source_target_pairs={{0,24},{2,26},{4,28},{6,30},{8,16},{10,18},{12,20},{14,22},{16,8},... | collective-permute-start | bytes 221192 | tf_op jit(solution)/shard_map/ppermute | solution.py:690
  88.1 1.4 %collective-permute-start.22 = (bf16[1,32,1152]{2,1,0:T(8,128)(2,1)S(1)}, bf16[1,32,1152]{2,1,0:T(8,128)(2,1)S(1)}, u32[]{:S(2)}, u32[]{:S(2)}) collective-permute-start(bf16[1,32,1152]{2,1,0:T(8,128)(2,1)S(1)} %shard_map.208.refs_0_), channel_id=1, source_target_pairs={{0,1},{1,0},{2,3},{3,2},{4,5},{5,4},{6,7},{7,6},{8,9},{9,8},{10,11... | collective-permute-start | bytes 221192 | tf_op jit(solution)/shard_map/ppermute | solution.py:36
  88.2 1.3 %collective-permute-start.23 = (bf16[32,256]{1,0:T(8,128)(2,1)S(1)}, bf16[32,256]{1,0:T(8,128)(2,1)S(1)}, u32[]{:S(2)}, u32[]{:S(2)}) collective-permute-start(bf16[32,256]{1,0:T(8,128)(2,1)S(1)} %get-tuple-element.185.refs_4_.refs_2_), channel_id=1, source_target_pairs={{0,1},{1,0},{2,3},{3,2},{4,5},{5,4},{6,7},{7,6},{8,9},{9,8},{10,11... | collective-permute-start | bytes 49160 | tf_op jit(solution)/shard_map/ppermute | solution.py:36

commit v4 on v3

--- a/solution.py
+++ b/solution.py
@@ -15,6 +15,8 @@
 GELU_A = 0.7978845608028654
 GELU_B = 0.044715
 SCALE = HEAD**-0.5
+K1_VMEM = 48
+SPLIT = 2
 SIDE = HEADS // 2
 PACK = HEADS * HEAD + 64
 
@@ -128,15 +130,14 @@
     return rows(slice(0, base)), jnp.concatenate(out, axis=1)
 
 
-def combine_body(backward, length, starts_ref, own_ref, partner_ref, out_ref):
-    first = 2 * lax.axis_index("seq")
+def combine_body(backward, rows_ref, own_ref, partner_ref, out_ref):
     is_first = (lax.axis_index("ffn") == 0).astype(F32)
     base = HEADS * HEAD
     if backward:
-        p = passes(starts_ref, first, length)
+        p = rows_ref[2:3, :128]
         own_by, partner_by = is_first + (1 - is_first) * p, is_first * p + (1 - is_first)
     else:
-        p = passes(starts_ref, first + 1, length)
+        p = rows_ref[3:4, :128]
         own_by, partner_by = is_first * p + (1 - is_first), is_first + (1 - is_first) * p
 
     def sum_of(at):
@@ -147,26 +148,25 @@
     pack_totals(out_ref, totals8)
 
 
-def combine(backward, length, starts, own, partner, after=()):
-    return call(
-        functools.partial(combine_body, backward, length),
-        (),
-        [SMEM, VM, VM],
+def combine(backward, rows, own, partner, after=()):
+    return call(
+        functools.partial(combine_body, backward),
+        (),
+        [VM] * 3,
         VM,
         shape(BF, PACK, 128),
         after=after,
-    )(starts, own, partner)
-
-
-def arrived(backward, length, starts_ref, partner_ref, far_ref, mem_ref, totals_ref):
-    first = 2 * lax.axis_index("seq")
+    )(rows, own, partner)
+
+
+def arrived(backward, rows_ref, partner_ref, far_ref, mem_ref, totals_ref):
     is_first = (lax.axis_index("ffn") == 0).astype(F32)
     if backward:
-        p = passes(starts_ref, first + 1, length)
+        p = rows_ref[3:4, :128]
         far_by, partner_by = is_first * p + (1 - is_first), is_first
         valid = lax.axis_index("seq") == 0
     else:
-        p = passes(starts_ref, first, length)
+        p = rows_ref[2:3, :128]
         far_by, partner_by = is_first + (1 - is_first) * p, 1 - is_first
         valid = lax.axis_index("seq") == 1
 
@@ -189,7 +189,7 @@
 
 
 def project_body(x_hbm, gain_hbm, bias_hbm, w_hbm, starts_ref,
-                 heads_ref, control_ref, xnt_ref, pack_ref, mask_ref,
+                 heads_ref, raw_ref, xn_ref, pack_ref, mask_ref, rows_ref, n_ref, inv_ref,
                  x_ref, gain_ref, bias_ref, w_ref, sems):
     length, width = x_ref.shape
     copies = [
@@ -203,27 +203,35 @@
     ]
     for copy in copies + columns:
         copy.start()
-    mask_ref[...] = visible(doc_begin_row(starts_ref, length), length)
+    doc_row = doc_begin_row(starts_ref, length)
+    tail = tail_row(doc_row, length)
+    first = 2 * lax.axis_index("seq")
+    rows = [jnp.where(doc_row < 0, 1.0, 0.0), tail] + [
+        jnp.full((1, length), passes(starts_ref, which, length)) for which in (first, first + 1)
+    ]
+    rows_ref[...] = jnp.concatenate(rows + rows, axis=0)
+    mask_ref[...] = visible(doc_row, length)
     for copy in copies:
         copy.wait()
     x = x_ref[...].astype(F32)
     mean = jnp.mean(x, axis=-1, keepdims=True)
     centered = x - mean
     inverse = lax.rsqrt(jnp.mean(centered * centered, axis=-1, keepdims=True) + EPSILON)
-    xn = (centered * inverse * gain_ref[...] + bias_ref[...]).astype(BF)
-    xnt_ref[...] = xn.T
+    n = centered * inverse
+    n_ref[...] = n
+    inv_ref[...] = jnp.broadcast_to(inverse, inv_ref.shape)
+    xn = (n * gain_ref[...] + bias_ref[...]).astype(BF)
+    xn_ref[...] = xn
     projected = []
     for j in range(4):
         columns[j].wait()
         projected.append(nn(xn, w_ref[j]))
-    control = jnp.exp(projected[3]).T
-    control_ref[...] = control
-    c = control.astype(BF)
+    raw_ref[...] = projected[3]
+    c = jnp.exp(projected[3]).astype(BF).T
     for j in range(3):
         t = projected[j].astype(BF).T
         for h in range(HEADS):
             heads_ref[h, j * HEAD : j * HEAD + HEAD, :] = t[h * HEAD : h * HEAD + HEAD]
-    tail = tail_row(doc_begin_row(starts_ref, length), length)
     c_tail = c * tail.astype(BF)
     for h in range(HEADS):
         rows = slice(h * HEAD, h * HEAD + HEAD)
@@ -238,22 +246,24 @@
 def project(x, gain, bias, w, starts):
     length, width = x.shape
     hbm = pl.BlockSpec(memory_space=pltpu.MemorySpace.HBM)
+    pin = lambda a: pltpu.with_memory_space_constraint(a, pltpu.HBM)
     return call(
         project_body,
         (),
         [hbm, hbm, hbm, hbm, SMEM],
-        [VM] * 5,
+        [VM] * 8,
         [
-            shape(BF, HEADS, 4 * HEAD, length), shape(F32, width, length), shape(BF, width, length),
-            shape(BF, PACK, 128), shape(BF, length, length),
+            shape(BF, HEADS, 4 * HEAD, length), shape(F32, length, width), shape(BF, length, width),
+            shape(BF, PACK, 128), shape(BF, length, length), shape(F32, 8, length),
+            shape(F32, length, width), shape(F32, length, 128),
         ],
         [
             pltpu.VMEM((length, width), BF), pltpu.VMEM((1, width), F32), pltpu.VMEM((1, width), F32),
             pltpu.VMEM((4, width, width), BF), pltpu.SemaphoreType.DMA((7,)),
         ],
         us=4.3,
-        vmem=48,
-    )(*(pltpu.with_memory_space_constraint(a, pltpu.HBM) for a in (x, gain, bias, w, starts)))
+        vmem=K1_VMEM,
+    )(*(pin(a) for a in (x, gain, bias, w, starts)))
 
 
 def parts(heads_ref, head):
@@ -327,20 +337,15 @@
     )(heads, mask)
 
 
-def enters_row(starts_ref, length):
-    return jnp.where(doc_begin_row(starts_ref, length) < 0, 1.0, 0.0)
-
-
-def mix_body(starts_ref, heads_ref, mask_ref, partner_ref, far_ref, *refs):
+def mix_body(rows_ref, heads_ref, mask_ref, partner_ref, far_ref, *refs):
     refs = list(refs)
     take = lambda n: [refs.pop(0) for _ in range(n)]
     ins = [take(2), take(2)]
     mixed_ref, mem_ref = take(2)
     outs = [take(5), take(5)]
     (totals_ref,) = refs
-    length = heads_ref.shape[2]
-    arrived(False, length, starts_ref, partner_ref, far_ref, mem_ref, totals_ref)
-    enters = enters_row(starts_ref, length)
+    arrived(False, rows_ref, partner_ref, far_ref, mem_ref, totals_ref)
+    enters = rows_ref[0:1, :]
     jobs = [(own_side, i) for own_side in (False, True) for i in range(SIDE)]
     spreads, links = [], []
     for own_side, i in jobs:
@@ -367,40 +372,43 @@
         mixed_ref[head_rows(head), :] = mixed.astype(BF)
 
 
-def mix(starts, heads, mask, partner, far, local_other, local_own, after=()):
+def mix(rows, heads, mask, partner, far, local_other, local_own, after=()):
     length, width = heads.shape[2], HEADS * HEAD
     side = [shape(F32, SIDE * HEAD, length)] * 3 + pair_shapes(length)
     mixed, mem, *rest = call(
         mix_body,
         (),
-        [SMEM] + [VM] * 8,
+        [VM] * 9,
         [VM] * 12,
         [shape(BF, width, length), shape(BF, width, 128)] + side + side,
         [pltpu.VMEM((width, 8), F32)],
         us=4.0,
         after=after,
-    )(starts, heads, mask, partner, far, *local_other, *local_own)
+    )(rows, heads, mask, partner, far, *local_other, *local_own)
     return mixed, mem, rest[:5], rest[5:]
 
 
-def prepare_body(cot_ref, down_other, down_own, other_ref, own_ref, cott_ref):
+def prepare_body(cot_ref, down_ref, down_other_ref, raw_ref, xn_ref, other_ref, own_ref, cott_ref, control_ref, xnt_ref):
     cot = cot_ref[...]
+    other_ref[...] = nn(cot, down_other_ref[...])
+    own_ref[...] = nn(cot, down_ref[...])
     cott_ref[...] = cot.T
-    other_ref[...] = nn(cot, down_other[...])
-    own_ref[...] = nn(cot, down_own[...])
-
-
-def prepare(cotangent, down_other, down_own, after=()):
+    xnt_ref[...] = xn_ref[...].T
+    control_ref[...] = jnp.exp(raw_ref[...]).T
+
+
+def prepare(cotangent, down, down_other, raw, xn, after=()):
     length, width = cotangent.shape
     return call(
         prepare_body,
         (),
-        [VM] * 3,
-        [VM] * 3,
-        [shape(F32, length, down_own.shape[1])] * 2 + [shape(BF, width, length)],
+        [VM] * 5,
+        [VM] * 5,
+        [shape(F32, length, down.shape[1])] * 2
+        + [shape(BF, width, length), shape(F32, width, length), shape(BF, width, length)],
         us=2.0,
         after=after,
-    )(cotangent, down_other, down_own)
+    )(cotangent, down, down_other, raw, xn)
 
 
 def activations(xn, d_hidden_ref, up_ref):
@@ -495,7 +503,7 @@
     )(*saved, cott, d_hidden, mixed, cotangent, w_out, gain, up, down)
 
 
-def scores_back_body(own_side, starts_ref, heads_ref, mask_ref, g_ref, mem_ref, number_ref, inverse_ref, weight_ref,
+def scores_back_body(own_side, rows_ref, heads_ref, mask_ref, g_ref, mem_ref, number_ref, inverse_ref, weight_ref,
                      *refs):
     if own_side:
         pack_in, sums_in, a_ref, spread_ref, d_total_ref, early_ref, late_ref, pack_ref, sums_ref = refs
@@ -503,8 +511,7 @@
         sums_ref[...] = sums_in[...]
     else:
         a_ref, spread_ref, d_total_ref, early_ref, late_ref, pack_ref, sums_ref = refs
-    length = heads_ref.shape[2]
-    enters = enters_row(starts_ref, length)
+    enters = rows_ref[0:1, :]
     heads = [head_of(own_side, i) for i in range(SIDE)]
     rows = [head_rows(head) for head in heads]
     held = [parts(heads_ref, head) for head in heads]
@@ -537,73 +544,77 @@
         pack_totals(pack_ref, sums_ref[...].T[0:8])
 
 
-def scores_back(own_side, starts, heads, mask, g, mem, saved, packs=(), after=()):
+def scores_back(own_side, rows, heads, mask, g, mem, saved, packs=(), after=()):
     length, width = heads.shape[2], HEADS * HEAD
     sums = [] if own_side else [shape(F32, width, 128)]
     outs = [shape(BF, SIDE * HEAD, length)] * 3 + pair_shapes(length) + [shape(BF, PACK, 128)] + sums
     return call(
         functools.partial(scores_back_body, own_side),
         (),
-        [SMEM] + [VM] * (7 + len(packs)),
+        [VM] * (8 + len(packs)),
         [VM] * len(outs),
         outs,
         [pltpu.VMEM((width, 128), F32)] if own_side else [],
         us=3.0,
         after=after,
-    )(starts, heads, mask, g, mem, *saved[:3], *packs)
-
-
-def heads_back_body(own_side, starts_ref, heads_ref, mask_ref, g_ref, mem_ref, a_ref, spread_ref, d_total_ref,
+    )(rows, heads, mask, g, mem, *saved[:3], *packs)
+
+
+def heads_back_body(own_side, begin, rows_ref, heads_ref, mask_ref, g_ref, mem_ref, a_ref, spread_ref, d_total_ref,
                     v_early, v_late, l_early, l_late, p_early, p_late, d_ref):
-    length = heads_ref.shape[2]
-    enters = enters_row(starts_ref, length)
-    heads = [head_of(own_side, i) for i in range(SIDE)]
+    enters = rows_ref[0:1, :]
+    count = d_ref.shape[0]
+    order = range(begin, begin + count)
+    heads = [head_of(own_side, i) for i in order]
     rows = [head_rows(head) for head in heads]
     held = [parts(heads_ref, head) for head in heads]
-    ats = [slice(i * HEAD, i * HEAD + HEAD) for i in range(SIDE)]
-    steps = [causal_pairs(held[i][3], a_ref[ats[i], :], mask_ref) for i in range(SIDE)]
-    from_totals = causal_back(mask_pair(mask_ref), d_total_ref[...].T).T
+    ats = [slice(i * HEAD, i * HEAD + HEAD) for i in order]
+    steps = [causal_pairs(h[3], a_ref[at, :], mask_ref) for h, at in zip(held, ats)]
+    totals = d_total_ref[begin * HEAD : (begin + count) * HEAD, :]
+    from_totals = causal_back(mask_pair(mask_ref), totals.T).T
     controls = []
-    for i in range(SIDE):
+    for i, at in zip(order, ats):
         odd = i % 2 == 1
         controls.append(
-            causal_back(load_pairs((p_early, p_late), i), padded(a_ref[ats[i], :], odd))
-            + causal_back(load_pairs((v_early, v_late), i), padded(spread_ref[ats[i], :], odd))
+            causal_back(load_pairs((p_early, p_late), i), padded(a_ref[at, :], odd))
+            + causal_back(load_pairs((v_early, v_late), i), padded(spread_ref[at, :], odd))
         )
-    for i in range(SIDE):
-        mem_k = mem_ref[rows[i], :][:, :HEAD]
-        d_ref[i, :HEAD, :] = causal_sum(held[i][1], steps[i]) + enters * tn(mem_k, a_ref[ats[i], :])
-    for i in range(SIDE):
-        d_ref[i, HEAD : 3 * HEAD, :] = (
-            causal_back(steps[i], padded(held[i][0], False))
-            + causal_back(load_pairs((l_early, l_late), i), padded(g_ref[rows[i], :], True))
+    for n in range(count):
+        mem_k = mem_ref[rows[n], :][:, :HEAD]
+        d_ref[n, :HEAD, :] = causal_sum(held[n][1], steps[n]) + enters * tn(mem_k, a_ref[ats[n], :])
+    for n, i in enumerate(order):
+        d_ref[n, HEAD : 3 * HEAD, :] = (
+            causal_back(steps[n], padded(held[n][0], False))
+            + causal_back(load_pairs((l_early, l_late), i), padded(g_ref[rows[n], :], True))
         ).T
-    for i in range(0, SIDE, 2):
-        two = (controls[i] + controls[i + 1]).T
-        for n in range(2):
-            d_ref[i + n, 3 * HEAD :, :] = two[n * HEAD : n * HEAD + HEAD] + from_totals[ats[i + n]]
-
-
-def heads_back(own_side, starts, heads, mask, g, mem, scores, links, pairs, after=()):
+    for n in range(0, count, 2):
+        two = (controls[n] + controls[n + 1]).T
+        for m in range(2):
+            d_ref[n + m, 3 * HEAD :, :] = (
+                two[m * HEAD : m * HEAD + HEAD] + from_totals[(n + m) * HEAD : (n + m) * HEAD + HEAD]
+            )
+
+
+def heads_back(own_side, begin, count, rows, heads, mask, g, mem, scores, links, pairs, after=()):
     length = heads.shape[2]
     return call(
-        functools.partial(heads_back_body, own_side),
-        (),
-        [SMEM] + [VM] * 13,
+        functools.partial(heads_back_body, own_side, begin),
+        (),
+        [VM] * 14,
         VM,
-        shape(F32, SIDE, 4 * HEAD, length),
+        shape(F32, count, 4 * HEAD, length),
         us=1.0,
         after=after,
-    )(starts, heads, mask, g, mem, *scores, *links, *pairs)
-
-
-def project_back_body(starts_ref, heads_ref, d_other, d_own, control_ref, partner_ref, far_ref, xnt_ref,
-                      proj_ref, keep_ref, send_ref, mem_ref, totals_ref):
-    length, width = xnt_ref.shape[1], xnt_ref.shape[0]
-    arrived(True, length, starts_ref, partner_ref, far_ref, mem_ref, totals_ref)
-    tail = tail_row(doc_begin_row(starts_ref, length), length)
+    )(rows, heads, mask, g, mem, *scores, *links, *pairs)
+
+
+def project_back_body(counts, rows_ref, heads_ref, control_ref, partner_ref, far_ref, xnt_ref, *refs):
+    d_refs, (proj_ref, keep_ref, send_ref, mem_ref, totals_ref) = refs[: len(counts)], refs[len(counts) :]
+    arrived(True, rows_ref, partner_ref, far_ref, mem_ref, totals_ref)
+    tail = rows_ref[1:2, :]
     tail_bf = tail.astype(BF)
-    jobs = [(d_ref, n, head_of(own_side, n)) for own_side, d_ref in ((False, d_other), (True, d_own)) for n in range(SIDE)]
+    places = [(d_ref, n) for d_ref, count in zip(d_refs, counts) for n in range(count)]
+    jobs = [(d_ref, n, head_of(i >= SIDE, i % SIDE)) for i, (d_ref, n) in enumerate(places)]
     more = []
     for d_ref, n, head in jobs:
         mem = mem_ref[head_rows(head), :]
@@ -628,29 +639,24 @@
                 send_ref[:, m * SIDE * HEAD : (m + 1) * SIDE * HEAD] = grad
 
 
-def project_back(starts, heads, d_other, d_own, control, partner, far, xnt, after=()):
+def project_back(rows, heads, ds, control, partner, far, xnt, after=()):
     width, length = xnt.shape
     return call(
-        project_back_body,
-        (),
-        [SMEM] + [VM] * 7,
+        functools.partial(project_back_body, [d.shape[0] for d in ds]),
+        (),
+        [VM] * (6 + len(ds)),
         [VM] * 3,
         [shape(BF, 4, width, length)] + [shape(BF, width, 4 * SIDE * HEAD)] * 2,
         [pltpu.VMEM((width, 128), BF), pltpu.VMEM((width, 8), F32)],
         us=5.0,
         after=after,
-    )(starts, heads, d_other, d_own, control, partner, far, xnt)
-
-
-def norm_back_body(proj_ref, w_ref, x_ref, gain_ref, d_hidden1_ref, norms2_ref, grad_x_ref, norms_ref):
-    length, width = x_ref.shape
+    )(rows, heads, control, partner, far, xnt, *ds)
+
+
+def norm_back_body(proj_ref, w_ref, n_ref, inv_ref, gain_ref, d_hidden1_ref, norms2_ref, grad_x_ref, norms_ref):
+    length, width = n_ref.shape
     dx = nn(w_ref[...], proj_ref[...].reshape(4 * width, length))
-    x = x_ref[...].astype(F32)
-    mean = jnp.mean(x, axis=-1, keepdims=True)
-    centered = x - mean
-    inverse = lax.rsqrt(jnp.mean(centered * centered, axis=-1, keepdims=True) + EPSILON)
-    n = centered * inverse
-    d = dx.T
+    n, d = n_ref[...], dx.T
     sums = [jnp.sum(d * n, axis=0, keepdims=True), jnp.sum(d, axis=0, keepdims=True)]
     rows8 = jnp.concatenate(sums + [norms2_ref[0:6, :]], axis=0)
     norms_ref[...] = jnp.concatenate([rows8, jnp.zeros((120, length), F32)], axis=0).T.astype(BF)
@@ -659,20 +665,20 @@
         d_n
         - jnp.mean(d_n, axis=-1, keepdims=True)
         - n * jnp.mean(d_n * n, axis=-1, keepdims=True)
-    ) * inverse
-
-
-def norm_back(proj, w, x, gain, d_hidden1, norms2, after=()):
-    length, width = x.shape
+    ) * inv_ref[:, 0:1]
+
+
+def norm_back(proj, w, n, inv, gain, d_hidden1, norms2, after=()):
+    length, width = n.shape
     return call(
         norm_back_body,
         (),
-        [VM] * 6,
+        [VM] * 7,
         [VM] * 2,
         [shape(F32, length, width), shape(BF, width, 128)],
-        us=0.1,
+        us=1e3,
         after=after,
-    )(proj, w, x, gain, d_hidden1, norms2)
+    )(proj, w, n, inv, gain, d_hidden1, norms2)
 
 
 def bit_axis(bit):
@@ -730,7 +736,7 @@
                 out[t] = total.astype(out.dtype)
 
 
-def stage(groups, after=(), dtype=BF):
+def stage(groups, after=(), dtype=BF, us=1.0):
     plan, operands, out_shape = [], [], []
     for arrays, split in groups:
         for pieces in arrays:
@@ -739,7 +745,7 @@
         plan.append(([[(first, count) for _, first, count in pieces] for pieces in arrays], split))
         out_shape += [shape(dtype, array.shape[0] >> len(split), array.shape[1], width)] * (1 << len(split))
     outs = list(
-        call(functools.partial(stage_body, plan), (), [VM] * len(operands), [VM] * len(out_shape), out_shape, after=after)(
+        call(functools.partial(stage_body, plan), (), [VM] * len(operands), [VM] * len(out_shape), out_shape, us=us, after=after)(
             *operands
         )
     )
@@ -754,57 +760,58 @@
     return [[b for n, b in enumerate(bits) if (p >> n) & 1] for p in range(1, 1 << len(bits))]
 
 
-def finish_body(a_ref, b_ref, up_ref, down_ref, out_ref):
-    total = a_ref[0].astype(F32) + b_ref[0].astype(F32)
-    half, part = up_ref.shape[1], out_ref.shape[1] // 2
-    up_ref[...] = total[:, :half]
-    down_ref[...] = total[:, half + part : 2 * half + part]
-    out_ref[:, :part] = total[:, half : half + part].astype(BF)
-    out_ref[:, part:] = total[:, 2 * half + part :].astype(BF)
-
-
-def finish(a, b, half, part, after=()):
-    rows = a.shape[1]
-    return call(
-        finish_body,
-        (),
-        [VM] * 2,
-        [VM] * 3,
-        [jax.ShapeDtypeStruct((rows, half), F32)] * 2 + [jax.ShapeDtypeStruct((rows, 2 * part), BF)],
-        after=after,
-    )(a, b)
-
-
-def join_body(own_ref, other_ref, out_own, out_other, grad_in_ref, grad_out_ref, *norm_refs):
+def last_body(late_count, columns, *refs):
+    *ins, out_ref = refs
+    sums = [
+        sum(ref[0].astype(F32) for ref in ins[:late_count]),
+        *(sum(ref[0][:, at].astype(F32) for ref in ins[late_count:]) for at in columns),
+    ]
+    out_ref[...] = jnp.concatenate(sums, axis=1).astype(BF)
+
+
+def last(late, early, columns):
+    rows = late[0].shape[1]
+    width = late[0].shape[2] + sum(at.stop - at.start for at in columns)
+    return call(
+        functools.partial(last_body, len(late), columns),
+        (),
+        [VM] * (len(late) + len(early)),
+        VM,
+        shape(BF, rows, width),
+    )(*late, *early)
+
+
+def join_body(up_at, down_at, own_ref, other_ref, a_ref, b_ref,
+              grad_in_ref, grad_out_ref, grad_up_ref, grad_down_ref, *norm_refs):
     second = lax.axis_index("ffn") == 1
-    own, other = own_ref[0].astype(F32), other_ref[0].astype(F32)
+    own, other = own_ref[...].astype(F32), other_ref[...].astype(F32)
     for f in range(2):
         keep_own = second if f else jnp.logical_not(second)
-        half = jnp.where(keep_own, own[:, :1024], other[:, :1024])
+        half = jnp.where(keep_own, own, other)
         for m in range(4):
             grad_in_ref[:, m * 512 + f * 256 : m * 512 + f * 256 + 256] = half[:, m * 256 : m * 256 + 256]
-        grad_out_ref[:, f * 256 : f * 256 + 256] = jnp.where(
-            keep_own, out_own[...], out_other[...]
-        ).astype(F32)
-    norms = (own[:, 1024:] + other[:, 1024:]).T
+        grad_out_ref[:, f * 256 : f * 256 + 256] = half[:, 1152:]
+    for at, ref in ((up_at, grad_up_ref), (down_at, grad_down_ref)):
+        ref[...] = a_ref[0][:, at].astype(F32) + b_ref[0][:, at].astype(F32)
+    norms = (own[:, 1024:1152] + other[:, 1024:1152]).T
     for n, ref in enumerate(norm_refs):
         ref[...] = norms[n]
 
 
-def join(own, other, out_own, out_other):
-    rows = own.shape[1]
-    return call(
-        join_body,
+def join(own, other, early, up_at, down_at):
+    rows = own.shape[0]
+    half = up_at.stop - up_at.start
+    return call(
+        functools.partial(join_body, up_at, down_at),
         (),
         [VM] * 4,
-        [VM] * 6,
-        [jax.ShapeDtypeStruct((rows, n), F32) for n in (2048, 512)] + [jax.ShapeDtypeStruct((rows,), F32)] * 4,
-    )(own, other, out_own, out_other)
+        [VM] * 8,
+        [shape(F32, rows, n) for n in (2048, 512, half, half)] + [shape(F32, rows)] * 4,
+    )(own, other, *early)
 
 
 def on_device(tokens, doc_starts, norm1_gain, norm1_bias, in_weight, out_weight,
               norm2_gain, norm2_bias, up_own, down_own, output_cotangent):
-    up_other, down_other = swap(up_own, "ffn", 1), swap(down_own, "ffn", 1)
     x, cotangent, starts = tokens[0], output_cotangent[0], doc_starts
     length, width = x.shape
     owners = lax.axis_size("dp") * lax.axis_size("seq")
@@ -812,15 +819,18 @@
     row = lambda a: a.reshape(1, width)
     blocked = lambda a: a.reshape(owners, width // owners, a.shape[1])
 
-    heads, control, xnt, own, mask = project(x, row(norm1_gain), row(norm1_bias), in_weight, starts)
+    heads, raw, xn, own, mask, rows, n1, inv1 = project(
+        x, row(norm1_gain), row(norm1_bias), in_weight, starts)
+    up_other, down_other = swap(up_own, "ffn", 1), swap(down_own, "ffn", 1)
     partner = swap(own, "ffn", 1)
     number_o, total_o, *pairs_other = local_sums(False, heads, mask)
-    both = combine(False, length, starts, own, partner, after=[number_o])
+    both = combine(False, rows, own, partner, after=[number_o])
     far = swap(both, "seq", 1)
     number, total, *pairs_own = local_sums(True, heads, mask, after=[both])
-    d_hidden_other, d_hidden_own, cott = prepare(cotangent, down_other, down_own, after=[number])
+    d_hidden_other, d_hidden_own, cott, control, xnt = prepare(
+        cotangent, down_own, down_other, raw, xn, after=[number])
     mixed, memory, saved_other, saved_own = mix(
-        starts, heads, mask, partner, far, (number_o, total_o), (number, total), after=[cott])
+        rows, heads, mask, partner, far, (number_o, total_o), (number, total), after=[cott])
     gup_send, gdown_send, *saved = feed_other(
         x, mixed, cott, d_hidden_other, out_weight, row(norm2_gain), row(norm2_bias), up_other, down_other)
     gup_got, gdown_got = swap(gup_send, "ffn", 1), swap(gdown_send, "ffn", 1)
@@ -858,21 +868,24 @@
         sent = [s for _, s in outs]
         return [[all_of(kept), all_of(r)] for (kept, _), r in zip(outs, got)], sent
 
-    back = (starts, heads, mask, g, memory)
+    back = (rows, heads, mask, g, memory)
     *scores_other, pack, sums = scores_back(False, *back, saved_other)
     groups, sent = advance(groups, 0, [pack])
     *scores_own, d_own = scores_back(True, *back, saved_own, packs=(pack, sums), after=sent)
     d_partner = swap(d_own, "ffn", 1)
-    d_both = combine(True, length, starts, d_own, d_partner)
+    other_side, own_side = (scores_other, saved_other[3:], pairs_other), (scores_own, saved_own[3:], pairs_own)
+    ds = []
+    if SPLIT:
+        ds.append(heads_back(False, 0, SPLIT, *back, *other_side, after=[d_own]))
+    d_both = combine(True, rows, d_own, d_partner, after=ds)
     d_far = swap(d_both, "seq", 1)
-    d_other = heads_back(False, *back, scores_other, saved_other[3:], pairs_other, after=[d_both])
-    d_mine = heads_back(True, *back, scores_own, saved_own[3:], pairs_own, after=[d_other])
-    groups, sent = advance(groups, 1, [d_mine])
-    proj, in_keep, in_send = project_back(
-        starts, heads, d_other, d_mine, control, d_partner, d_far, xnt, after=sent)
+    ds.append(heads_back(False, SPLIT, SIDE - SPLIT, *back, *other_side, after=[d_both]))
+    ds.append(heads_back(True, 0, SIDE, *back, *own_side, after=ds[-1:]))
+    proj, in_keep, in_send = project_back(rows, heads, ds, control, d_partner, d_far, xnt)
     in_got = swap(in_send, "ffn", 1)
+    groups, sent = advance(groups, 1, [in_send])
     grad_tokens, norms = norm_back(
-        proj, in_weight, x, row(norm1_gain), d_hidden1, norms2, after=[in_send])
+        proj, in_weight, n1, inv1, row(norm1_gain), d_hidden1, norms2, after=sent)
 
     late = [
         all_of(blocked(in_keep)) + all_of(blocked(norms)),
@@ -891,9 +904,14 @@
             groups, token = advance(groups, stages.pop(0), token)
             if rest:
                 break
-    grad_up, grad_down, out = finish(*(a[0][0] for a in groups[0]), gup_own.shape[1], out_half, after=[kept])
-    (final,), = stage([(late, [])], after=[out])
-    grad_in, grad_out, *norms = join(final, swap(final, "ffn", 1), out, swap(out, "ffn", 1))
+    early = [arrays[0][0] for arrays in groups[0]]
+    half = gup_own.shape[1]
+    down_at = half + out_half
+    outs_at = [slice(half, down_at), slice(down_at + half, down_at + half + out_half)]
+    (total,), = stage([(late, [])], us=1e3)
+    final = last([total], early, outs_at)
+    grad_in, grad_out, grad_up, grad_down, *norms = join(
+        final, swap(final, "ffn", 1), early, slice(0, half), slice(down_at, down_at + half))
     return (output[None], grad_tokens[None], grad_in, grad_out, grad_up, grad_down, *norms)
 
 

time: 90.5 us -> 79.9 us (0.88)
  Pallas kernels: 40.5 us -> 35.2 us
  waiting for transfers between devices: 23.9 us -> 19.3 us
    pallas_call x24 -> x25, Pallas kernels: 40.5 us -> 35.2 us  [start(): pl.pallas_call(run, grid=grid, in_specs=list(in_specs) + [ANY] * len(afte...]
    ppermute x12, waiting for transfers between devices: 19.7 us -> 15.6 us  [send_across(): lax.ppermute(a, ('dp', 'seq'), [(i, i ^ flip) for i in range(seqs * dps)])]
    ppermute x12 -> x11, waiting for transfers between devices: 4.18 us -> 3.67 us  [swap(): return lax.ppermute(a, axis, [(i, i ^ bit) for i in range(size)])]
    ppermute x12 -> x11, starting transfers between devices: 6.94 us -> 6.68 us  [swap(): return lax.ppermute(a, axis, [(i, i ^ bit) for i in range(size)])]
  transfers between devices with their start and end apart: 24 -> 23, of which waited for: 11 -> 11; matrix products, arithmetic and copies ran while one was open for 0% -> 0% of each run, Pallas kernels for 35% -> 37%
where the time goes in v4:
time: 79.9 us; the launch traced here: 79.8 us
  Pallas kernels  35.2 us (44%)
  starting transfers between devices  24.4 us (31%)
  waiting for transfers between devices  19.3 us (24%)
  between operations  0.92 us (1%)
    pallas_call x25, Pallas kernels, start(): pl.pallas_call(run, grid=grid, in_specs=list(in_specs) + [ANY] * len(afte...  35.2 us
    ppermute x12, starting transfers between devices, send_across(): lax.ppermute(a, ('dp', 'seq'), [(i, i ^ flip) for i in range(seqs * dps)])  17.7 us
    ppermute x12, waiting for transfers between devices, send_across(): lax.ppermute(a, ('dp', 'seq'), [(i, i ^ flip) for i in range(seqs * dps)])  15.6 us
    ppermute x11, starting transfers between devices, swap(): return lax.ppermute(a, axis, [(i, i ^ bit) for i in range(size)])  6.68 us
    ppermute x11, waiting for transfers between devices, swap(): return lax.ppermute(a, axis, [(i, i ^ bit) for i in range(size)])  3.67 us
  transfers between devices with their start and end apart: 23, of which 11 were waited for; matrix products, arithmetic and copies ran while one was open for 0% of the time, Pallas kernels for 37%

profile of v4, /device:TPU:0, one launch (start us, length us, event | category | flops | bytes accessed | tf_op | source)
XLA Modules:
  0.0 79.8 jit_solution(16989057000493985608)
XLA Ops:
  0.6 0.5 collective-permute-start.2
  1.2 4.5 %shard_map.186 = (bf16[8,256,512]{2,1,0:T(8,128)(2,1)S(1)}, f32[512,512]{1,0:T(8,128)S(1)}, bf16[512,512]{1,0:T(8,128)(2,1)S(1)}, bf16[576,128]{1,0:T(8,128)(2,1...) custom-call(bf16[512,512]{1,0:T(8,128)(2,1)} %bitcast.19, ...), custom_call_target="tpu_custom_call" | custom-call | flops 43000000 | bytes 8192 | tf_op jit(solution)/shard_map/pallas_call | solution.py:51
  5.8 0.5 collective-permute-start
  6.3 0.9 %shard_map.187 = (f32[256,512]{1,0:T(8,128)S(1)}, f32[256,512]{1,0:T(8,128)S(1)}, bf16[4,256,256]{2,1,0:T(8,128)(2,1)S(1)}, bf16[4,512,256]{2,1,0:T(8,128)(2,1)S(1)}) custom-call(bf16[8,256,512]{2,1,0:T(8,128)(2,1)S(1)} %get-tuple-element.107.refs_0_.refs_1_, bf16[512,512]{1,0:T(8,128)(2,1)S(1)} %get-tuple-element.108.refs_1_.refs_2_), custom_call_target="tpu_custom_call" | custom-call | flops 30000000 | bytes 8192 | tf_op jit(solution)/shard_map/pallas_call | solution.py:51
  7.4 2.9 %collective-permute-start.1 = (bf16[576,128]{1,0:T(8,128)(2,1)S(1)}, bf16[576,128]{1,0:T(8,128)(2,1)S(1)}, u32[]{:S(2)}, u32[]{:S(2)}) collective-permute-start(bf16[576,128]{1,0:T(8,128)(2,1)S(1)} %shard_map.188.refs_2_), channel_id=1, source_target_pairs={{0,2},{2,0},{1,3},{3,1},{4,6},{6,4},{5,7},{7,5},{8,10},{10,8},{9,1... | collective-permute-start | bytes 442376 | tf_op jit(solution)/shard_map/ppermute | solution.py:38
  10.3 0.9 %shard_map.189 = (f32[256,512]{1,0:T(8,128)S(1)}, f32[256,512]{1,0:T(8,128)S(1)}, bf16[4,256,256]{2,1,0:T(8,128)(2,1)S(1)}, bf16[4,512,256]{2,1,0:T(8,128)(2,1)S(1)}) custom-call(bf16[8,256,512]{2,1,0:T(8,128)(2,1)S(1)} %get-tuple-element.107.refs_0_.refs_1_, bf16[512,512]{1,0:T(8,128)(2,1)S(1)} %get-tuple-element.108.refs_1_.refs_2_, ...), custom_call_target="tpu_custom_call" | custom-call | flops 30000000 | bytes 8192 | tf_op jit(solution)/shard_map/pallas_call | solution.py:51
  11.3 1.3 %shard_map.190 = (f32[512,1024]{1,0:T(8,128)S(1)}, f32[512,1024]{1,0:T(8,128)S(1)}, bf16[512,512]{1,0:T(8,128)(2,1)S(1)}, f32[512,512]{1,0:T(8,128)S(1)}, bf16[512,512]{1,0:T(8,128)(2,1)S(1)}) custom-call(bf16[512,512]{1,0:T(8,128)(2,1)S(1)} %bitcast.17, bf16[512,1024]{1,0:T(8,128)(2,1)S(1)} %copy-done, ...), custom_call_target="tpu_custom_call" | custom-call | flops 20000000 | bytes 8192 | tf_op jit(solution)/shard_map/pallas_call | solution.py:51
  12.5 1.9 %collective-permute-done.1.refs_4_ = bf16[576,128]{1,0:T(8,128)(2,1)S(1)} collective-permute-done((bf16[576,128]{1,0:T(8,128)(2,1)S(1)}, bf16[576,128]{1,0:T(8,128)(2,1)S(1)}, u32[]{:S(2)}, u32[]{:S(2)}) %collective-permute-start.1) | collective-permute-done | bytes 147488 | tf_op jit(solution)/shard_map/ppermute | solution.py:38
  14.5 2.3 %shard_map.191 = (bf16[512,512]{1,0:T(8,128)(2,1)S(1)}, bf16[512,128]{1,0:T(8,128)(2,1)S(1)}, f32[256,512]{1,0:T(8,128)S(1)}, f32[256,512]{1,0:T(8,128)S(1)}, f3...) custom-call(f32[8,512]{1,0:T(8,128)S(1)} %get-tuple-element.106.refs, ...), custom_call_target="tpu_custom_call" | custom-call | flops 40000000 | bytes 8192 | tf_op jit(solution)/shard_map/pallas_call | solution.py:51
  16.8 4.3 %shard_map.192 = (bf16[512,1024]{1,0:T(8,128)(2,1)S(1)}, bf16[512,1024]{1,0:T(8,128)(2,1)S(1)}, f32[512,512]{1,0:T(8,128)S(1)}, f32[512,512]{1,0:T(8,128)S(1)}, ...) custom-call(bf16[512,512]{1,0:T(8,128)(2,1)S(1)} %bitcast.20, ...), custom_call_target="tpu_custom_call" | custom-call | flops 60000000 | bytes 8192 | tf_op jit(solution)/shard_map/pallas_call | solution.py:51
  21.1 0.5 collective-permute-start.4
  21.6 5.0 %shard_map.193 = (bf16[512,512]{1,0:T(8,128)(2,1)}, f32[512,512]{1,0:T(8,128)S(1)}, bf16[512,512]{1,0:T(8,128)(2,1)S(1)}, bf16[512,256]{1,0:T(8,128)(2,1)S(1)}, ...) custom-call(f32[512,512]{1,0:T(8,128)S(1)} %get-tuple-element.119.re, ...), custom_call_target="tpu_custom_call" | custom-call | flops 60000000 | bytes 8192 | tf_op jit(solution)/shard_map/pallas_call | solution.py:51
  26.7 1.4 %shard_map.194 = (bf16[256,512]{1,0:T(8,128)(2,1)S(1)}, bf16[256,512]{1,0:T(8,128)(2,1)S(1)}, bf16[256,512]{1,0:T(8,128)(2,1)S(1)}, bf16[4,256,256]{2,1,0:T(8,12...) custom-call(f32[8,512]{1,0:T(8,128)S(1)} %get-tuple-element.106.refs_0_, ...), custom_call_target="tpu_custom_call" | custom-call | flops 30000000 | bytes 8192 | tf_op jit(solution)/shard_map/pallas_call | solution.py:51
  28.2 0.4 shard_map.195
  28.6 1.9 %collective-permute-start.10 = (bf16[8,32,1152]{2,1,0:T(8,128)(2,1)S(1)}, bf16[8,32,1152]{2,1,0:T(8,128)(2,1)S(1)}, u32[]{:S(2)}, u32[]{:S(2)}) collective-permute-start(bf16[8,32,1152]{2,1,0:T(8,128)(2,1)S(1)} %get-tuple-element.146.refs_11_), channel_id=1, source_target_pairs={{0,8},{2,10},{4,12},{6,14},{8,0},{10,2},{12,4},{14,6},{16,24},{18,... | collective-permute-start | bytes 1769480 | tf_op jit(solution)/shard_map/ppermute | solution.py:696
  30.5 1.5 %collective-permute-start.9 = (bf16[8,32,1152]{2,1,0:T(8,128)(2,1)S(1)}, bf16[8,32,1152]{2,1,0:T(8,128)(2,1)S(1)}, u32[]{:S(2)}, u32[]{:S(2)}) collective-permute-start(bf16[8,32,1152]{2,1,0:T(8,128)(2,1)S(1)} %get-tuple-element.145.refs_10_), channel_id=1, source_target_pairs={{0,4},{2,6},{4,0},{6,2},{8,12},{10,14},{12,8},{14,10},{16,20},{18,... | collective-permute-start | bytes 1769480 | tf_op jit(solution)/shard_map/ppermute | solution.py:696
  32.0 1.4 %shard_map.196 = (bf16[256,512]{1,0:T(8,128)(2,1)S(1)}, bf16[256,512]{1,0:T(8,128)(2,1)S(1)}, bf16[256,512]{1,0:T(8,128)(2,1)S(1)}, bf16[4,256,256]{2,1,0:T(8,12...) custom-call(f32[8,512]{1,0:T(8,128)S(1)} %get-tuple-element.106.refs_0_, ...), custom_call_target="tpu_custom_call" | custom-call | flops 30000000 | bytes 8192 | tf_op jit(solution)/shard_map/pallas_call | solution.py:51
  33.5 1.6 %shard_map.197.refs_3_.refs_6_ = f32[2,256,512]{2,1,0:T(8,128)S(1)} custom-call(f32[8,512]{1,0:T(8,128)S(1)} %get-tuple-element.106.refs_0_, bf16[8,256,512]{2,1,0:T(8,128)(2,1)S(1)} %get-tuple-element.107.refs_0_.refs_1_, bf16[512,512]{1,0:T(8,128)(2,1)S(1)} %get-tuple-element.108.refs_1_.refs_2_, bf16[512,512]{1,0:T(8,128)(2,1)S(1)} %get-tuple-element.129.refs_3_, ...), custom_call_target="tpu_custom_call" | custom-call | flops 10000000 | bytes 8192 | tf_op jit(solution)/shard_map/pallas_call | solution.py:51
  35.2 1.6 %collective-permute-start.8 = (bf16[576,128]{1,0:T(8,128)(2,1)S(1)}, bf16[576,128]{1,0:T(8,128)(2,1)S(1)}, u32[]{:S(2)}, u32[]{:S(2)}) collective-permute-start(bf16[576,128]{1,0:T(8,128)(2,1)S(1)} %shard_map.198.refs_14_), channel_id=1, source_target_pairs={{0,2},{2,0},{1,3},{3,1},{4,6},{6,4},{5,7},{7,5},{8,10},{10,8},{9,1... | collective-permute-start | bytes 442376 | tf_op jit(solution)/shard_map/ppermute | solution.py:38
  36.7 1.6 %shard_map.199.refs_14_.refs_7_ = f32[2,256,512]{2,1,0:T(8,128)S(1)} custom-call(f32[8,512]{1,0:T(8,128)S(1)} %get-tuple-element.106.refs_0_, bf16[8,256,512]{2,1,0:T(8,128)(2,1)S(1)} %get-tuple-element.107.refs_0_.refs_1_, bf16[512,512]{1,0:T(8,128)(2,1)S(1)} %get-tuple-element.108.refs_1_.refs_2_, bf16[512,512]{1,0:T(8,128)(2,1)S(1)} %get-tuple-element.129.refs_3_, ...), custom_call_target="tpu_custom_call" | custom-call | flops 10000000 | bytes 8192 | tf_op jit(solution)/shard_map/pallas_call | solution.py:51
  38.3 2.8 %shard_map.200.refs_8_ = f32[4,256,512]{2,1,0:T(8,128)S(1)} custom-call(f32[8,512]{1,0:T(8,128)S(1)} %get-tuple-element.106.refs_0_, bf16[8,256,512]{2,1,0:T(8,128)(2,1)S(1)} %get-tuple-element.107.refs_0_.refs_1_, bf16[512,512]{1,0:T(8,128)(2,1)S(1)} %get-tuple-element.108.refs_1_.refs_2_, bf16[512,512]{1,0:T(8,128)(2,1)S(1)} %get-tuple-element.129.refs_3_, ...), custom_call_target="tpu_custom_call" | custom-call | flops 10000000 | bytes 8192 | tf_op jit(solution)/shard_map/pallas_call | solution.py:51
  41.1 0.3 collective-permute-done.8.refs_4_
  41.5 2.4 %shard_map.201 = (bf16[4,512,512]{2,1,0:T(8,128)(2,1)S(1)}, bf16[512,1024]{1,0:T(8,128)(2,1)S(1)}, bf16[512,1024]{1,0:T(8,128)(2,1)S(1)}) custom-call(f32[8,512]{1,0:T(8,128)S(1)} %get-tuple-element.106.refs_0_, bf16[8,256,512]{2,1,0:T(8,128)(2,1)S(1)} %get-tuple-element.107.refs_0_.refs_1_, f32[512,512]{1,0:T(8,128)S(1)} %get-tuple-element.128.refs_2_, ...), custom_call_target="tpu_custom_call" | custom-call | flops 50000000 | bytes 8192 | tf_op jit(solution)/shard_map/pallas_call | solution.py:51
  43.9 0.3 collective-permute-start.11
  44.2 0.1 collective-permute-done.10.refs_3_
  44.3 1.5 %collective-permute-done.9.refs_1_ = bf16[8,32,1152]{2,1,0:T(8,128)(2,1)S(1)} collective-permute-done((bf16[8,32,1152]{2,1,0:T(8,128)(2,1)S(1)}, bf16[8,32,1152]{2,1,0:T(8,128)(2,1)S(1)}, u32[]{:S(2)}, u32[]{:S(2)}) %collective-permute-start.9) | collective-permute-done | bytes 589856 | tf_op jit(solution)/shard_map/ppermute | solution.py:696
  45.8 0.1 shard_map.202
  45.9 0.4 collective-permute-start.18
  46.3 1.6 %collective-permute-start.19 = (bf16[4,32,1152]{2,1,0:T(8,128)(2,1)S(1)}, bf16[4,32,1152]{2,1,0:T(8,128)(2,1)S(1)}, u32[]{:S(2)}, u32[]{:S(2)}) collective-permute-start(bf16[4,32,1152]{2,1,0:T(8,128)(2,1)S(1)} %get-tuple-element.176.refs_8_), channel_id=1, source_target_pairs={{0,4},{2,6},{4,0},{6,2},{8,12},{10,14},{12,8},{14,10},{16,20},{18,... | collective-permute-start | bytes 884744 | tf_op jit(solution)/shard_map/ppermute | solution.py:696
  47.9 2.8 %shard_map.203 = (f32[512,512]{1,0:T(8,128)}, bf16[512,128]{1,0:T(8,128)(2,1)S(1)}) custom-call(bf16[4,512,512]{2,1,0:T(8,128)(2,1)S(1)} %get-tuple-element.167.refs_0_, bf16[512,2048]{1,0:T(8,128)(2,1)S(1)} %copy-done.2, f32[512,512]{1,0:T(8,128)S(1)} %get-tuple-element.168.refs_2_, f32[512,128]{1,0:T(8,128)S(1)} %get-tuple-element.169.refs_3_, ...), custom_call_target="tpu_custom_call" | custom-call | flops 10000000000 | bytes 8192 | tf_op jit(solution)/shard_map/pallas_call | solution.py:51
  50.7 0.2 shard_map.204
  50.9 1.6 %collective-permute-start.12 = (bf16[4,32,1152]{2,1,0:T(8,128)(2,1)S(1)}, bf16[4,32,1152]{2,1,0:T(8,128)(2,1)S(1)}, u32[]{:S(2)}, u32[]{:S(2)}) collective-permute-start(bf16[4,32,1152]{2,1,0:T(8,128)(2,1)S(1)} %get-tuple-element.181), channel_id=1, source_target_pairs={{0,2},{2,0},{4,6},{6,4},{8,10},{10,8},{12,14},{14,12},{16,18},{18,... | collective-permute-start | bytes 884744 | tf_op jit(solution)/shard_map/ppermute | solution.py:696
  52.5 0.5 collective-permute-start.13
  53.0 1.5 %collective-permute-start.14 = (bf16[4,32,1152]{2,1,0:T(8,128)(2,1)S(1)}, bf16[4,32,1152]{2,1,0:T(8,128)(2,1)S(1)}, u32[]{:S(2)}, u32[]{:S(2)}) collective-permute-start(bf16[4,32,1152]{2,1,0:T(8,128)(2,1)S(1)} %get-tuple-element.183), channel_id=1, source_target_pairs={{0,6},{2,4},{4,2},{6,0},{8,14},{10,12},{12,10},{14,8},{16,22},{18,... | collective-permute-start | bytes 884744 | tf_op jit(solution)/shard_map/ppermute | solution.py:696
  54.5 0.7 collective-permute-done.19.refs_3_
  55.2 0.1 shard_map.207
  55.3 2.7 %collective-permute-start.20 = (bf16[2,32,2304]{2,1,0:T(8,128)(2,1)S(1)}, bf16[2,32,2304]{2,1,0:T(8,128)(2,1)S(1)}, u32[]{:S(2)}, u32[]{:S(2)}) collective-permute-start(bf16[2,32,2304]{2,1,0:T(8,128)(2,1)S(1)} %get-tuple-element.191), channel_id=1, source_target_pairs={{0,16},{2,18},{4,20},{6,22},{8,24},{10,26},{12,28},{14,30},{16,0},... | collective-permute-start | bytes 884744 | tf_op jit(solution)/shard_map/ppermute | solution.py:696
  58.0 3.0 %collective-permute-done.12.refs_1_ = bf16[4,32,1152]{2,1,0:T(8,128)(2,1)S(1)} collective-permute-done((bf16[4,32,1152]{2,1,0:T(8,128)(2,1)S(1)}, bf16[4,32,1152]{2,1,0:T(8,128)(2,1)S(1)}, u32[]{:S(2)}, u32[]{:S(2)}) %collective-permute-start.12) | collective-permute-done | bytes 294944 | tf_op jit(solution)/shard_map/ppermute | solution.py:696
  61.0 6.1 %collective-permute-done.13.refs_2_ = bf16[4,32,1152]{2,1,0:T(8,128)(2,1)S(1)} collective-permute-done((bf16[4,32,1152]{2,1,0:T(8,128)(2,1)S(1)}, bf16[4,32,1152]{2,1,0:T(8,128)(2,1)S(1)}, u32[]{:S(2)}, u32[]{:S(2)}) %collective-permute-start.13) | collective-permute-done | bytes 294944 | tf_op jit(solution)/shard_map/ppermute | solution.py:696
  67.1 0.1 shard_map.205
  67.2 1.5 %collective-permute-start.15 = (bf16[1,32,1152]{2,1,0:T(8,128)(2,1)S(1)}, bf16[1,32,1152]{2,1,0:T(8,128)(2,1)S(1)}, u32[]{:S(2)}, u32[]{:S(2)}) collective-permute-start(bf16[1,32,1152]{2,1,0:T(8,128)(2,1)S(1)} %get-tuple-element.185), channel_id=1, source_target_pairs={{0,8},{2,10},{4,12},{6,14},{8,0},{10,2},{12,4},{14,6},{16,24},{18,... | collective-permute-start | bytes 221192 | tf_op jit(solution)/shard_map/ppermute | solution.py:696
  68.7 2.6 %collective-permute-start.16 = (bf16[1,32,1152]{2,1,0:T(8,128)(2,1)S(1)}, bf16[1,32,1152]{2,1,0:T(8,128)(2,1)S(1)}, u32[]{:S(2)}, u32[]{:S(2)}) collective-permute-start(bf16[1,32,1152]{2,1,0:T(8,128)(2,1)S(1)} %get-tuple-element.186), channel_id=1, source_target_pairs={{0,16},{2,18},{4,20},{6,22},{8,24},{10,26},{12,28},{14,30},{16,0},... | collective-permute-start | bytes 221192 | tf_op jit(solution)/shard_map/ppermute | solution.py:696
  71.4 0.3 collective-permute-start.17
  71.7 1.6 %collective-permute-start.21 = (bf16[1,32,2304]{2,1,0:T(8,128)(2,1)S(1)}, bf16[1,32,2304]{2,1,0:T(8,128)(2,1)S(1)}, u32[]{:S(2)}, u32[]{:S(2)}) collective-permute-start(bf16[1,32,2304]{2,1,0:T(8,128)(2,1)S(1)} %get-tuple-element.193), channel_id=1, source_target_pairs={{0,2},{2,0},{4,6},{6,4},{8,10},{10,8},{12,14},{14,12},{16,18},{18,... | collective-permute-start | bytes 442376 | tf_op jit(solution)/shard_map/ppermute | solution.py:696
  73.3 2.3 %collective-permute-done.16.refs_2_ = bf16[1,32,1152]{2,1,0:T(8,128)(2,1)S(1)} collective-permute-done((bf16[1,32,1152]{2,1,0:T(8,128)(2,1)S(1)}, bf16[1,32,1152]{2,1,0:T(8,128)(2,1)S(1)}, u32[]{:S(2)}, u32[]{:S(2)}) %collective-permute-start.16) | collective-permute-done | bytes 73760 | tf_op jit(solution)/shard_map/ppermute | solution.py:696
  75.6 1.9 %collective-permute-done.17.refs_3_ = bf16[1,32,1152]{2,1,0:T(8,128)(2,1)S(1)} collective-permute-done((bf16[1,32,1152]{2,1,0:T(8,128)(2,1)S(1)}, bf16[1,32,1152]{2,1,0:T(8,128)(2,1)S(1)}, u32[]{:S(2)}, u32[]{:S(2)}) %collective-permute-start.17) | collective-permute-done | bytes 73760 | tf_op jit(solution)/shard_map/ppermute | solution.py:696
  77.7 1.3 %collective-permute-done.22.refs_1_ = bf16[32,1408]{1,0:T(8,128)(2,1)S(1)} collective-permute-done((bf16[32,1408]{1,0:T(8,128)(2,1)S(1)}, bf16[32,1408]{1,0:T(8,128)(2,1)S(1)}, u32[]{:S(2)}, u32[]{:S(2)}) %collective-permute-start.22) | collective-permute-done | bytes 90144 | tf_op jit(solution)/shard_map/ppermute | solution.py:38
  78.9 0.8 %shard_map.210 = (f32[32,2048]{1,0:T(8,128)}, f32[32,512]{1,0:T(8,128)}, f32[32,1024]{1,0:T(8,128)}, f32[32,1024]{1,0:T(8,128)}, f32[32]{0:T(128)}, /*index=5*/f32[32]{0:T(128)}, f32[32]{0:T(128)}, f32[32]{0:T(128)}) custom-call(bf16[32,1408]{1,0:T(8,128)(2,1)S(1)} %shard_map.209.refs_0_, bf16[32,1408]{1,0:T(8,128)(2,1)S(1)} %collective-permute-done.22.refs_1_, ...), custom_call_target="tpu_custom_call" | custom-call | flops 10000000 | bytes 8192 | tf_op jit(solution)/shard_map/pallas_call | solution.py:51
  (42 shorter events, 0.8 us)
Async XLA Ops:
  0.6 10.6 %collective-permute-start.2 = (bf16[512,1024]{1,0:T(8,128)(2,1)}, bf16[512,1024]{1,0:T(8,128)(2,1)S(1)}, u32[]{:S(2)}, u32[]{:S(2)}) collective-permute-start(bf16[512,1024]{1,0:T(8,128)(2,1)} %refs_14_.1), channel_id=1, source_target_pairs={{0,1},{1,0},{2,3},{3,2},{4,5},{5,4},{6,7},{7,6},{8,9},{9,8},{10,11... | collective-permute-start | bytes 3145736 | tf_op jit(solution)/shard_map/ppermute | solution.py:38
  1.2 15.6 %collective-permute-start.3 = (bf16[512,1024]{1,0:T(8,128)(2,1)}, bf16[512,1024]{1,0:T(8,128)(2,1)S(1)}, u32[]{:S(2)}, u32[]{:S(2)}) collective-permute-start(bf16[512,1024]{1,0:T(8,128)(2,1)} %refs_13_.1), channel_id=1, source_target_pairs={{0,1},{1,0},{2,3},{3,2},{4,5},{5,4},{6,7},{7,6},{8,9},{9,8},{10,11... | collective-permute-start | bytes 3145736 | tf_op jit(solution)/shard_map/ppermute | solution.py:38
  5.8 1.5 %collective-permute-start = (bf16[576,128]{1,0:T(8,128)(2,1)S(1)}, bf16[576,128]{1,0:T(8,128)(2,1)S(1)}, u32[]{:S(2)}, u32[]{:S(2)}) collective-permute-start(bf16[576,128]{1,0:T(8,128)(2,1)S(1)} %get-tuple-element.109.refs_1_), channel_id=1, source_target_pairs={{0,1},{1,0},{2,3},{3,2},{4,5},{5,4},{6,7},{7,6},{8,9},{9,8},{10,11... | collective-permute-start | bytes 442376 | tf_op jit(solution)/shard_map/ppermute | solution.py:38
  7.2 4.0 %copy-start = (bf16[512,1024]{1,0:T(8,128)(2,1)S(1)}, bf16[512,1024]{1,0:T(8,128)(2,1)}, u32[]{:S(2)}) copy-start(bf16[512,1024]{1,0:T(8,128)(2,1)} %refs_14_.1) | copy-start | bytes 3145732
  7.3 4.0 %copy-start.1 = (bf16[1,512,512]{2,1,0:T(8,128)(2,1)S(1)}, bf16[1,512,512]{2,1,0:T(8,128)(2,1)}, u32[]{:S(2)}) copy-start(bf16[1,512,512]{2,1,0:T(8,128)(2,1)} %param.21) | copy-start | bytes 1572868
  7.4 7.1 %collective-permute-start.1 = (bf16[576,128]{1,0:T(8,128)(2,1)S(1)}, bf16[576,128]{1,0:T(8,128)(2,1)S(1)}, u32[]{:S(2)}, u32[]{:S(2)}) collective-permute-start(bf16[576,128]{1,0:T(8,128)(2,1)S(1)} %shard_map.188.refs_2_), channel_id=1, source_target_pairs={{0,2},{2,0},{1,3},{3,1},{4,6},{6,4},{5,7},{7,5},{8,10},{10,8},{9,1... | collective-permute-start | bytes 442376 | tf_op jit(solution)/shard_map/ppermute | solution.py:38
  14.5 2.3 %copy-start.3 = (bf16[512,512]{1,0:T(8,128)(2,1)S(1)}, bf16[512,512]{1,0:T(8,128)(2,1)}, u32[]{:S(2)}) copy-start(bf16[512,512]{1,0:T(8,128)(2,1)} %refs_11_.1) | copy-start | bytes 1572868
  14.5 2.3 %copy-start.4 = (bf16[1,512,512]{2,1,0:T(8,128)(2,1)S(1)}, bf16[1,512,512]{2,1,0:T(8,128)(2,1)}, u32[]{:S(2)}) copy-start(bf16[1,512,512]{2,1,0:T(8,128)(2,1)} %param.11) | copy-start | bytes 1572868
  14.5 2.3 %copy-start.6 = (f32[512]{0:T(512)S(1)}, f32[512]{0:T(512)}, u32[]{:S(2)}) copy-start(f32[512]{0:T(512)} %param.17) | copy-start | bytes 6148
  14.5 2.3 %copy-start.7 = (f32[512]{0:T(512)S(1)}, f32[512]{0:T(512)}, u32[]{:S(2)}) copy-start(f32[512]{0:T(512)} %param.18) | copy-start | bytes 6148
  16.8 4.9 %copy-start.5 = (bf16[512,1024]{1,0:T(8,128)(2,1)S(1)}, bf16[512,1024]{1,0:T(8,128)(2,1)}, u32[]{:S(2)}) copy-start(bf16[512,1024]{1,0:T(8,128)(2,1)} %refs_13_.1) | copy-start | bytes 3145732
  21.1 7.1 %collective-permute-start.6 = (bf16[512,1024]{1,0:T(8,128)(2,1)S(1)}, bf16[512,1024]{1,0:T(8,128)(2,1)S(1)}, u32[]{:S(2)}, u32[]{:S(2)}) collective-permute-start(bf16[512,1024]{1,0:T(8,128)(2,1)S(1)} %get-tuple-element.144), channel_id=1, source_target_pairs={{0,1},{1,0},{2,3},{3,2},{4,5},{5,4},{6,7},{7,6},{8,9},{9,8},{10,11... | collective-permute-start | bytes 3145736 | tf_op jit(solution)/shard_map/ppermute | solution.py:38
  21.1 7.1 %collective-permute-start.4 = (bf16[512,1024]{1,0:T(8,128)(2,1)S(1)}, bf16[512,1024]{1,0:T(8,128)(2,1)S(1)}, u32[]{:S(2)}, u32[]{:S(2)}) collective-permute-start(bf16[512,1024]{1,0:T(8,128)(2,1)S(1)} %get-tuple-element.141), channel_id=1, source_target_pairs={{0,1},{1,0},{2,3},{3,2},{4,5},{5,4},{6,7},{7,6},{8,9},{9,8},{10,11... | collective-permute-start | bytes 3145736 | tf_op jit(solution)/shard_map/ppermute | solution.py:38
  26.6 1.5 %collective-permute-start.5 = (bf16[512,256]{1,0:T(8,128)(2,1)S(1)}, bf16[512,256]{1,0:T(8,128)(2,1)S(1)}, u32[]{:S(2)}, u32[]{:S(2)}) collective-permute-start(bf16[512,256]{1,0:T(8,128)(2,1)S(1)} %get-tuple-element.142), channel_id=1, source_target_pairs={{0,1},{1,0},{2,3},{3,2},{4,5},{5,4},{6,7},{7,6},{8,9},{9,8},{10,11... | collective-permute-start | bytes 786440 | tf_op jit(solution)/shard_map/ppermute | solution.py:38
  28.6 15.7 %collective-permute-start.10 = (bf16[8,32,1152]{2,1,0:T(8,128)(2,1)S(1)}, bf16[8,32,1152]{2,1,0:T(8,128)(2,1)S(1)}, u32[]{:S(2)}, u32[]{:S(2)}) collective-permute-start(bf16[8,32,1152]{2,1,0:T(8,128)(2,1)S(1)} %get-tuple-element.146.refs_11_), channel_id=1, source_target_pairs={{0,8},{2,10},{4,12},{6,14},{8,0},{10,2},{12,4},{14,6},{16,24},{18,... | collective-permute-start | bytes 1769480 | tf_op jit(solution)/shard_map/ppermute | solution.py:696
  30.5 15.3 %collective-permute-start.9 = (bf16[8,32,1152]{2,1,0:T(8,128)(2,1)S(1)}, bf16[8,32,1152]{2,1,0:T(8,128)(2,1)S(1)}, u32[]{:S(2)}, u32[]{:S(2)}) collective-permute-start(bf16[8,32,1152]{2,1,0:T(8,128)(2,1)S(1)} %get-tuple-element.145.refs_10_), channel_id=1, source_target_pairs={{0,4},{2,6},{4,0},{6,2},{8,12},{10,14},{12,8},{14,10},{16,20},{18,... | collective-permute-start | bytes 1769480 | tf_op jit(solution)/shard_map/ppermute | solution.py:696
  33.4 1.7 %collective-permute-start.7 = (bf16[576,128]{1,0:T(8,128)(2,1)S(1)}, bf16[576,128]{1,0:T(8,128)(2,1)S(1)}, u32[]{:S(2)}, u32[]{:S(2)}) collective-permute-start(bf16[576,128]{1,0:T(8,128)(2,1)S(1)} %get-tuple-element.147.refs_14_.refs_1_), channel_id=1, source_target_pairs={{0,1},{1,0},{2,3},{3,2},{4,5},{5,4},{6,7},{7,6},{8,9},{9,8},{10,11... | collective-permute-start | bytes 442376 | tf_op jit(solution)/shard_map/ppermute | solution.py:38
  35.2 6.3 %collective-permute-start.8 = (bf16[576,128]{1,0:T(8,128)(2,1)S(1)}, bf16[576,128]{1,0:T(8,128)(2,1)S(1)}, u32[]{:S(2)}, u32[]{:S(2)}) collective-permute-start(bf16[576,128]{1,0:T(8,128)(2,1)S(1)} %shard_map.198.refs_14_), channel_id=1, source_target_pairs={{0,2},{2,0},{1,3},{3,1},{4,6},{6,4},{5,7},{7,5},{8,10},{10,8},{9,1... | collective-permute-start | bytes 442376 | tf_op jit(solution)/shard_map/ppermute | solution.py:38
  43.9 4.1 %copy-start.2 = (bf16[512,2048]{1,0:T(8,128)(2,1)S(1)}, bf16[512,2048]{1,0:T(8,128)(2,1)}, u32[]{:S(2)}) copy-start(bf16[512,2048]{1,0:T(8,128)(2,1)} %refs_1_.3) | copy-start | bytes 6291460
  43.9 4.0 %copy-start.8 = (f32[512]{0:T(512)S(1)}, f32[512]{0:T(512)}, u32[]{:S(2)}) copy-start(f32[512]{0:T(512)} %param.13) | copy-start | bytes 6148
  43.9 6.8 %collective-permute-start.11 = (bf16[512,1024]{1,0:T(8,128)(2,1)S(1)}, bf16[512,1024]{1,0:T(8,128)(2,1)S(1)}, u32[]{:S(2)}, u32[]{:S(2)}) collective-permute-start(bf16[512,1024]{1,0:T(8,128)(2,1)S(1)} %get-tuple-element.174.refs_4_), channel_id=1, source_target_pairs={{0,1},{1,0},{2,3},{3,2},{4,5},{5,4},{6,7},{7,6},{8,9},{9,8},{10,11... | collective-permute-start | bytes 3145736 | tf_op jit(solution)/shard_map/ppermute | solution.py:38
  45.9 8.6 %collective-permute-start.18 = (bf16[4,32,1152]{2,1,0:T(8,128)(2,1)S(1)}, bf16[4,32,1152]{2,1,0:T(8,128)(2,1)S(1)}, u32[]{:S(2)}, u32[]{:S(2)}) collective-permute-start(bf16[4,32,1152]{2,1,0:T(8,128)(2,1)S(1)} %get-tuple-element.175.refs_7_), channel_id=1, source_target_pairs={{0,8},{2,10},{4,12},{6,14},{8,0},{10,2},{12,4},{14,6},{16,24},{18,... | collective-permute-start | bytes 884744 | tf_op jit(solution)/shard_map/ppermute | solution.py:696
  46.3 8.9 %collective-permute-start.19 = (bf16[4,32,1152]{2,1,0:T(8,128)(2,1)S(1)}, bf16[4,32,1152]{2,1,0:T(8,128)(2,1)S(1)}, u32[]{:S(2)}, u32[]{:S(2)}) collective-permute-start(bf16[4,32,1152]{2,1,0:T(8,128)(2,1)S(1)} %get-tuple-element.176.refs_8_), channel_id=1, source_target_pairs={{0,4},{2,6},{4,0},{6,2},{8,12},{10,14},{12,8},{14,10},{16,20},{18,... | collective-permute-start | bytes 884744 | tf_op jit(solution)/shard_map/ppermute | solution.py:696
  50.9 10.0 %collective-permute-start.12 = (bf16[4,32,1152]{2,1,0:T(8,128)(2,1)S(1)}, bf16[4,32,1152]{2,1,0:T(8,128)(2,1)S(1)}, u32[]{:S(2)}, u32[]{:S(2)}) collective-permute-start(bf16[4,32,1152]{2,1,0:T(8,128)(2,1)S(1)} %get-tuple-element.181), channel_id=1, source_target_pairs={{0,2},{2,0},{4,6},{6,4},{8,10},{10,8},{12,14},{14,12},{16,18},{18,... | collective-permute-start | bytes 884744 | tf_op jit(solution)/shard_map/ppermute | solution.py:696
  52.5 14.6 %collective-permute-start.13 = (bf16[4,32,1152]{2,1,0:T(8,128)(2,1)S(1)}, bf16[4,32,1152]{2,1,0:T(8,128)(2,1)S(1)}, u32[]{:S(2)}, u32[]{:S(2)}) collective-permute-start(bf16[4,32,1152]{2,1,0:T(8,128)(2,1)S(1)} %get-tuple-element.182), channel_id=1, source_target_pairs={{0,4},{2,6},{4,0},{6,2},{8,12},{10,14},{12,8},{14,10},{16,20},{18,... | collective-permute-start | bytes 884744 | tf_op jit(solution)/shard_map/ppermute | solution.py:696
  53.0 14.1 %collective-permute-start.14 = (bf16[4,32,1152]{2,1,0:T(8,128)(2,1)S(1)}, bf16[4,32,1152]{2,1,0:T(8,128)(2,1)S(1)}, u32[]{:S(2)}, u32[]{:S(2)}) collective-permute-start(bf16[4,32,1152]{2,1,0:T(8,128)(2,1)S(1)} %get-tuple-element.183), channel_id=1, source_target_pairs={{0,6},{2,4},{4,2},{6,0},{8,14},{10,12},{12,10},{14,8},{16,22},{18,... | collective-permute-start | bytes 884744 | tf_op jit(solution)/shard_map/ppermute | solution.py:696
  55.3 16.4 %collective-permute-start.20 = (bf16[2,32,2304]{2,1,0:T(8,128)(2,1)S(1)}, bf16[2,32,2304]{2,1,0:T(8,128)(2,1)S(1)}, u32[]{:S(2)}, u32[]{:S(2)}) collective-permute-start(bf16[2,32,2304]{2,1,0:T(8,128)(2,1)S(1)} %get-tuple-element.191), channel_id=1, source_target_pairs={{0,16},{2,18},{4,20},{6,22},{8,24},{10,26},{12,28},{14,30},{16,0},... | collective-permute-start | bytes 884744 | tf_op jit(solution)/shard_map/ppermute | solution.py:696
  67.2 6.1 %collective-permute-start.15 = (bf16[1,32,1152]{2,1,0:T(8,128)(2,1)S(1)}, bf16[1,32,1152]{2,1,0:T(8,128)(2,1)S(1)}, u32[]{:S(2)}, u32[]{:S(2)}) collective-permute-start(bf16[1,32,1152]{2,1,0:T(8,128)(2,1)S(1)} %get-tuple-element.185), channel_id=1, source_target_pairs={{0,8},{2,10},{4,12},{6,14},{8,0},{10,2},{12,4},{14,6},{16,24},{18,... | collective-permute-start | bytes 221192 | tf_op jit(solution)/shard_map/ppermute | solution.py:696
  68.7 6.8 %collective-permute-start.16 = (bf16[1,32,1152]{2,1,0:T(8,128)(2,1)S(1)}, bf16[1,32,1152]{2,1,0:T(8,128)(2,1)S(1)}, u32[]{:S(2)}, u32[]{:S(2)}) collective-permute-start(bf16[1,32,1152]{2,1,0:T(8,128)(2,1)S(1)} %get-tuple-element.186), channel_id=1, source_target_pairs={{0,16},{2,18},{4,20},{6,22},{8,24},{10,26},{12,28},{14,30},{16,0},... | collective-permute-start | bytes 221192 | tf_op jit(solution)/shard_map/ppermute | solution.py:696
  71.4 6.2 %collective-permute-start.17 = (bf16[1,32,1152]{2,1,0:T(8,128)(2,1)S(1)}, bf16[1,32,1152]{2,1,0:T(8,128)(2,1)S(1)}, u32[]{:S(2)}, u32[]{:S(2)}) collective-permute-start(bf16[1,32,1152]{2,1,0:T(8,128)(2,1)S(1)} %get-tuple-element.187), channel_id=1, source_target_pairs={{0,24},{2,26},{4,28},{6,30},{8,16},{10,18},{12,20},{14,22},{16,8},... | collective-permute-start | bytes 221192 | tf_op jit(solution)/shard_map/ppermute | solution.py:696
  71.7 5.8 %collective-permute-start.21 = (bf16[1,32,2304]{2,1,0:T(8,128)(2,1)S(1)}, bf16[1,32,2304]{2,1,0:T(8,128)(2,1)S(1)}, u32[]{:S(2)}, u32[]{:S(2)}) collective-permute-start(bf16[1,32,2304]{2,1,0:T(8,128)(2,1)S(1)} %get-tuple-element.193), channel_id=1, source_target_pairs={{0,2},{2,0},{4,6},{6,4},{8,10},{10,8},{12,14},{14,12},{16,18},{18,... | collective-permute-start | bytes 442376 | tf_op jit(solution)/shard_map/ppermute | solution.py:696
  77.6 1.4 %collective-permute-start.22 = (bf16[32,1408]{1,0:T(8,128)(2,1)S(1)}, bf16[32,1408]{1,0:T(8,128)(2,1)S(1)}, u32[]{:S(2)}, u32[]{:S(2)}) collective-permute-start(bf16[32,1408]{1,0:T(8,128)(2,1)S(1)} %shard_map.209.refs_0_), channel_id=1, source_target_pairs={{0,1},{1,0},{2,3},{3,2},{4,5},{5,4},{6,7},{7,6},{8,9},{9,8},{10,11... | collective-permute-start | bytes 270344 | tf_op jit(solution)/shard_map/ppermute | solution.py:38

commit v5 on v4

--- a/solution.py
+++ b/solution.py
@@ -198,8 +198,8 @@
         pltpu.make_async_copy(bias_hbm, bias_ref, sems.at[2]),
     ]
     columns = [
-        pltpu.make_async_copy(w_hbm.at[:, pl.ds(j * width, width)], w_ref.at[j], sems.at[3 + j])
-        for j in range(4)
+        pltpu.make_async_copy(w_hbm.at[:, pl.ds((j + 1) * width, width)], w_ref.at[j], sems.at[3 + j])
+        for j in range(3)
     ]
     for copy in copies + columns:
         copy.start()
@@ -223,21 +223,21 @@
     xn = (n * gain_ref[...] + bias_ref[...]).astype(BF)
     xn_ref[...] = xn
     projected = []
-    for j in range(4):
+    for j in range(3):
         columns[j].wait()
         projected.append(nn(xn, w_ref[j]))
-    raw_ref[...] = projected[3]
-    c = jnp.exp(projected[3]).astype(BF).T
-    for j in range(3):
+    raw_ref[...] = projected[2]
+    c = jnp.exp(projected[2]).astype(BF).T
+    for j in range(2):
         t = projected[j].astype(BF).T
         for h in range(HEADS):
             heads_ref[h, j * HEAD : j * HEAD + HEAD, :] = t[h * HEAD : h * HEAD + HEAD]
     c_tail = c * tail.astype(BF)
     for h in range(HEADS):
         rows = slice(h * HEAD, h * HEAD + HEAD)
-        heads_ref[h, 3 * HEAD :, :] = c[rows]
-        mem_k = nt(c_tail[rows], heads_ref[h, HEAD : 2 * HEAD, :])
-        mem_vt = nt(heads_ref[h, 2 * HEAD : 3 * HEAD, :], c_tail[rows])
+        heads_ref[h, 2 * HEAD :, :] = c[rows]
+        mem_k = nt(c_tail[rows], heads_ref[h, :HEAD, :])
+        mem_vt = nt(heads_ref[h, HEAD : 2 * HEAD, :], c_tail[rows])
         pack_ref[rows, :] = jnp.concatenate([mem_k, mem_vt], axis=1).astype(BF)
     tail8 = jnp.broadcast_to(tail, (8, length)).astype(BF)
     pack_totals(pack_ref, nt(tail8, c))
@@ -253,21 +253,32 @@
         [hbm, hbm, hbm, hbm, SMEM],
         [VM] * 8,
         [
-            shape(BF, HEADS, 4 * HEAD, length), shape(F32, length, width), shape(BF, length, width),
+            shape(BF, HEADS, 3 * HEAD, length), shape(F32, length, width), shape(BF, length, width),
             shape(BF, PACK, 128), shape(BF, length, length), shape(F32, 8, length),
             shape(F32, length, width), shape(F32, length, 128),
         ],
         [
             pltpu.VMEM((length, width), BF), pltpu.VMEM((1, width), F32), pltpu.VMEM((1, width), F32),
-            pltpu.VMEM((4, width, width), BF), pltpu.SemaphoreType.DMA((7,)),
+            pltpu.VMEM((3, width, width), BF), pltpu.SemaphoreType.DMA((6,)),
         ],
         us=4.3,
         vmem=K1_VMEM,
     )(*(pin(a) for a in (x, gain, bias, w, starts)))
 
 
-def parts(heads_ref, head):
-    return [heads_ref[head, j * HEAD : j * HEAD + HEAD, :] for j in range(4)]
+def query_body(xn_ref, w_ref, q_ref):
+    t = nn(xn_ref[...], w_ref[:, : xn_ref.shape[1]]).astype(BF).T
+    for h in range(HEADS):
+        q_ref[h] = t[h * HEAD : h * HEAD + HEAD]
+
+
+def query(xn, w, after=()):
+    return call(query_body, (), [VM] * 2, VM, shape(BF, HEADS, HEAD, xn.shape[0]), us=0.5, after=after)(xn, w)
+
+
+def parts(refs, head):
+    q_ref, heads_ref = refs
+    return [q_ref[head]] + [heads_ref[head, j * HEAD : j * HEAD + HEAD, :] for j in range(3)]
 
 
 def mask_pair(mask_ref):
@@ -313,8 +324,8 @@
     return refs[0][i], refs[1][i]
 
 
-def local_body(own_side, heads_ref, mask_ref, number_ref, total_ref, *pair_refs):
-    held = [parts(heads_ref, head_of(own_side, i)) for i in range(SIDE)]
+def local_body(own_side, q_ref, heads_ref, mask_ref, number_ref, total_ref, *pair_refs):
+    held = [parts((q_ref, heads_ref), head_of(own_side, i)) for i in range(SIDE)]
     pairs = [causal_pairs(k, q, mask_ref) for q, k, v, c in held]
     for i in range(SIDE):
         store_pairs(pair_refs, i, pairs[i])
@@ -325,19 +336,19 @@
 
 
 def local_sums(own_side, heads, mask, after=()):
-    length = heads.shape[2]
+    length = heads[0].shape[2]
     return call(
         functools.partial(local_body, own_side),
         (),
-        [VM, VM],
+        [VM] * 3,
         [VM] * 4,
         [shape(F32, SIDE * HEAD, length)] * 2 + pair_shapes(length),
         us=3.0,
         after=after,
-    )(heads, mask)
-
-
-def mix_body(rows_ref, heads_ref, mask_ref, partner_ref, far_ref, *refs):
+    )(*heads, mask)
+
+
+def mix_body(rows_ref, q_ref, heads_ref, mask_ref, partner_ref, far_ref, *refs):
     refs = list(refs)
     take = lambda n: [refs.pop(0) for _ in range(n)]
     ins = [take(2), take(2)]
@@ -353,7 +364,7 @@
         number_ref, inverse_ref, weight_ref, *_ = outs[own_side]
         head, at = head_of(own_side, i), slice(i * HEAD, i * HEAD + HEAD)
         mem_k = mem_ref[head_rows(head), :][:, :HEAD]
-        number = number_in[at, :] + enters * nn(mem_k, parts(heads_ref, head)[0])
+        number = number_in[at, :] + enters * nn(mem_k, parts((q_ref, heads_ref), head)[0])
         inverse = 1.0 / (total_in[at, :] + enters * totals_ref[head_rows(head), 0:1])
         score = number * (inverse * SCALE)
         e = jnp.exp(score - jnp.max(score, axis=0, keepdims=True))
@@ -363,28 +374,28 @@
         weight_ref[at, :] = weight
         spreads.append((weight * inverse).astype(BF))
     for (own_side, i), spread in zip(jobs, spreads):
-        links.append(causal_pairs(parts(heads_ref, head_of(own_side, i))[3], spread, mask_ref))
+        links.append(causal_pairs(parts((q_ref, heads_ref), head_of(own_side, i))[3], spread, mask_ref))
         store_pairs(outs[own_side][3:], i, links[-1])
     for (own_side, i), spread, link in zip(jobs, spreads, links):
         head = head_of(own_side, i)
         mem_vt = mem_ref[head_rows(head), :][:, HEAD:]
-        mixed = causal_sum(parts(heads_ref, head)[2], link) + enters * nn(mem_vt, spread)
+        mixed = causal_sum(parts((q_ref, heads_ref), head)[2], link) + enters * nn(mem_vt, spread)
         mixed_ref[head_rows(head), :] = mixed.astype(BF)
 
 
 def mix(rows, heads, mask, partner, far, local_other, local_own, after=()):
-    length, width = heads.shape[2], HEADS * HEAD
+    length, width = heads[0].shape[2], HEADS * HEAD
     side = [shape(F32, SIDE * HEAD, length)] * 3 + pair_shapes(length)
     mixed, mem, *rest = call(
         mix_body,
         (),
-        [VM] * 9,
+        [VM] * 10,
         [VM] * 12,
         [shape(BF, width, length), shape(BF, width, 128)] + side + side,
         [pltpu.VMEM((width, 8), F32)],
         us=4.0,
         after=after,
-    )(rows, heads, mask, partner, far, *local_other, *local_own)
+    )(rows, *heads, mask, partner, far, *local_other, *local_own)
     return mixed, mem, rest[:5], rest[5:]
 
 
@@ -503,7 +514,7 @@
     )(*saved, cott, d_hidden, mixed, cotangent, w_out, gain, up, down)
 
 
-def scores_back_body(own_side, rows_ref, heads_ref, mask_ref, g_ref, mem_ref, number_ref, inverse_ref, weight_ref,
+def scores_back_body(own_side, rows_ref, q_ref, heads_ref, mask_ref, g_ref, mem_ref, number_ref, inverse_ref, weight_ref,
                      *refs):
     if own_side:
         pack_in, sums_in, a_ref, spread_ref, d_total_ref, early_ref, late_ref, pack_ref, sums_ref = refs
@@ -514,7 +525,7 @@
     enters = rows_ref[0:1, :]
     heads = [head_of(own_side, i) for i in range(SIDE)]
     rows = [head_rows(head) for head in heads]
-    held = [parts(heads_ref, head) for head in heads]
+    held = [parts((q_ref, heads_ref), head) for head in heads]
     values = [causal_pairs(held[i][2], g_ref[rows[i], :], mask_ref) for i in range(SIDE)]
     for i in range(SIDE):
         store_pairs((early_ref, late_ref), i, values[i])
@@ -545,29 +556,29 @@
 
 
 def scores_back(own_side, rows, heads, mask, g, mem, saved, packs=(), after=()):
-    length, width = heads.shape[2], HEADS * HEAD
+    length, width = heads[0].shape[2], HEADS * HEAD
     sums = [] if own_side else [shape(F32, width, 128)]
     outs = [shape(BF, SIDE * HEAD, length)] * 3 + pair_shapes(length) + [shape(BF, PACK, 128)] + sums
     return call(
         functools.partial(scores_back_body, own_side),
         (),
-        [VM] * (8 + len(packs)),
+        [VM] * (9 + len(packs)),
         [VM] * len(outs),
         outs,
         [pltpu.VMEM((width, 128), F32)] if own_side else [],
         us=3.0,
         after=after,
-    )(rows, heads, mask, g, mem, *saved[:3], *packs)
-
-
-def heads_back_body(own_side, begin, rows_ref, heads_ref, mask_ref, g_ref, mem_ref, a_ref, spread_ref, d_total_ref,
+    )(rows, *heads, mask, g, mem, *saved[:3], *packs)
+
+
+def heads_back_body(own_side, begin, rows_ref, q_ref, heads_ref, mask_ref, g_ref, mem_ref, a_ref, spread_ref, d_total_ref,
                     v_early, v_late, l_early, l_late, p_early, p_late, d_ref):
     enters = rows_ref[0:1, :]
     count = d_ref.shape[0]
     order = range(begin, begin + count)
     heads = [head_of(own_side, i) for i in order]
     rows = [head_rows(head) for head in heads]
-    held = [parts(heads_ref, head) for head in heads]
+    held = [parts((q_ref, heads_ref), head) for head in heads]
     ats = [slice(i * HEAD, i * HEAD + HEAD) for i in order]
     steps = [causal_pairs(h[3], a_ref[at, :], mask_ref) for h, at in zip(held, ats)]
     totals = d_total_ref[begin * HEAD : (begin + count) * HEAD, :]
@@ -596,19 +607,19 @@
 
 
 def heads_back(own_side, begin, count, rows, heads, mask, g, mem, scores, links, pairs, after=()):
-    length = heads.shape[2]
+    length = heads[0].shape[2]
     return call(
         functools.partial(heads_back_body, own_side, begin),
         (),
-        [VM] * 14,
+        [VM] * 15,
         VM,
         shape(F32, count, 4 * HEAD, length),
         us=1.0,
         after=after,
-    )(rows, heads, mask, g, mem, *scores, *links, *pairs)
-
-
-def project_back_body(counts, rows_ref, heads_ref, control_ref, partner_ref, far_ref, xnt_ref, *refs):
+    )(rows, *heads, mask, g, mem, *scores, *links, *pairs)
+
+
+def project_back_body(counts, rows_ref, q_ref, heads_ref, control_ref, partner_ref, far_ref, xnt_ref, *refs):
     d_refs, (proj_ref, keep_ref, send_ref, mem_ref, totals_ref) = refs[: len(counts)], refs[len(counts) :]
     arrived(True, rows_ref, partner_ref, far_ref, mem_ref, totals_ref)
     tail = rows_ref[1:2, :]
@@ -619,7 +630,7 @@
     for d_ref, n, head in jobs:
         mem = mem_ref[head_rows(head), :]
         back_k, back_vt = mem[:, :HEAD], mem[:, HEAD:]
-        q, k, v, c = parts(heads_ref, head)
+        q, k, v, c = parts((q_ref, heads_ref), head)
         c_tail = c * tail_bf
         more.append((tn(back_k, c_tail), nn(back_vt, c_tail), nn(back_k, k) + tn(back_vt, v)))
     for (d_ref, n, head), (more_k, more_v, more_c) in zip(jobs, more):
@@ -644,28 +655,35 @@
     return call(
         functools.partial(project_back_body, [d.shape[0] for d in ds]),
         (),
-        [VM] * (6 + len(ds)),
+        [VM] * (7 + len(ds)),
         [VM] * 3,
         [shape(BF, 4, width, length)] + [shape(BF, width, 4 * SIDE * HEAD)] * 2,
         [pltpu.VMEM((width, 128), BF), pltpu.VMEM((width, 8), F32)],
         us=5.0,
         after=after,
-    )(rows, heads, control, partner, far, xnt, *ds)
+    )(rows, *heads, control, partner, far, xnt, *ds)
 
 
 def norm_back_body(proj_ref, w_ref, n_ref, inv_ref, gain_ref, d_hidden1_ref, norms2_ref, grad_x_ref, norms_ref):
     length, width = n_ref.shape
-    dx = nn(w_ref[...], proj_ref[...].reshape(4 * width, length))
-    n, d = n_ref[...], dx.T
-    sums = [jnp.sum(d * n, axis=0, keepdims=True), jnp.sum(d, axis=0, keepdims=True)]
-    rows8 = jnp.concatenate(sums + [norms2_ref[0:6, :]], axis=0)
+    proj = proj_ref[...].reshape(4 * width, length)
+    halves = [slice(0, length // 2), slice(length // 2, length)]
+    ds = [
+        lax.dot_general(proj[:, at], w_ref[...], (((0,), (1,)), ((), ())), preferred_element_type=F32)
+        for at in halves
+    ]
+    sums = []
+    for at, d in zip(halves, ds):
+        n = n_ref[at, :]
+        sums.append([jnp.sum(d * n, axis=0, keepdims=True), jnp.sum(d, axis=0, keepdims=True)])
+        d_n = d * gain_ref[...]
+        grad_x_ref[at, :] = d_hidden1_ref[at, :] + (
+            d_n
+            - jnp.mean(d_n, axis=-1, keepdims=True)
+            - n * jnp.mean(d_n * n, axis=-1, keepdims=True)
+        ) * inv_ref[at, 0:1]
+    rows8 = jnp.concatenate([a + b for a, b in zip(*sums)] + [norms2_ref[0:6, :]], axis=0)
     norms_ref[...] = jnp.concatenate([rows8, jnp.zeros((120, length), F32)], axis=0).T.astype(BF)
-    d_n = d * gain_ref[...]
-    grad_x_ref[...] = d_hidden1_ref[...] + (
-        d_n
-        - jnp.mean(d_n, axis=-1, keepdims=True)
-        - n * jnp.mean(d_n * n, axis=-1, keepdims=True)
-    ) * inv_ref[:, 0:1]
 
 
 def norm_back(proj, w, n, inv, gain, d_hidden1, norms2, after=()):
@@ -819,13 +837,14 @@
     row = lambda a: a.reshape(1, width)
     blocked = lambda a: a.reshape(owners, width // owners, a.shape[1])
 
-    heads, raw, xn, own, mask, rows, n1, inv1 = project(
+    kvc, raw, xn, own, mask, rows, n1, inv1 = project(
         x, row(norm1_gain), row(norm1_bias), in_weight, starts)
     up_other, down_other = swap(up_own, "ffn", 1), swap(down_own, "ffn", 1)
     partner = swap(own, "ffn", 1)
-    number_o, total_o, *pairs_other = local_sums(False, heads, mask)
-    both = combine(False, rows, own, partner, after=[number_o])
+    heads = (query(xn, in_weight), kvc)
+    both = combine(False, rows, own, partner, after=heads[:1])
     far = swap(both, "seq", 1)
+    number_o, total_o, *pairs_other = local_sums(False, heads, mask, after=[both])
     number, total, *pairs_own = local_sums(True, heads, mask, after=[both])
     d_hidden_other, d_hidden_own, cott, control, xnt = prepare(
         cotangent, down_own, down_other, raw, xn, after=[number])
@@ -898,7 +917,10 @@
         split = [(b, rest.index(b)) for b in now]
         rest = rest[2:]
         (kept, *sent), = stage([(late, split)])
-        late = [all_of(kept)] + [all_of(send_across(s, p)) for s, p in zip(sent, patterns(now))]
+        pairs = list(zip(sent, patterns(now)))
+        if now[0]:
+            pairs = pairs[1:] + pairs[:1]
+        late = [all_of(kept)] + [all_of(send_across(s, p)) for s, p in pairs]
         token = [kept]
         while stages:
             groups, token = advance(groups, stages.pop(0), token)

time: 79.9 us -> 78.7 us (0.985)
  waiting for transfers between devices: 19.3 us -> 18.4 us
    pallas_call x25 -> x26, Pallas kernels: 35.2 us -> 35.4 us  [start(): pl.pallas_call(run, grid=grid, in_specs=list(in_specs) + [ANY] * len(afte...]
  transfers between devices with their start and end apart: 23 -> 23, of which waited for: 11 -> 14; matrix products, arithmetic and copies ran while one was open for 0% -> 0% of each run, Pallas kernels for 37% -> 38%
where the time goes in v5:
time: 78.7 us; the launch traced here: 78.5 us
  Pallas kernels  35.4 us (45%)
  starting transfers between devices  23.8 us (30%)
  waiting for transfers between devices  18.4 us (23%)
  between operations  0.9 us (1%)
    pallas_call x26, Pallas kernels, start(): pl.pallas_call(run, grid=grid, in_specs=list(in_specs) + [ANY] * len(afte...  35.4 us
    ppermute x12, starting transfers between devices, send_across(): lax.ppermute(a, ('dp', 'seq'), [(i, i ^ flip) for i in range(seqs * dps)])  17.3 us
    ppermute x12, waiting for transfers between devices, send_across(): lax.ppermute(a, ('dp', 'seq'), [(i, i ^ flip) for i in range(seqs * dps)])  15.3 us
    ppermute x11, starting transfers between devices, swap(): return lax.ppermute(a, axis, [(i, i ^ bit) for i in range(size)])  6.41 us
    ppermute x11, waiting for transfers between devices, swap(): return lax.ppermute(a, axis, [(i, i ^ bit) for i in range(size)])  3.15 us
  transfers between devices with their start and end apart: 23, of which 14 were waited for; matrix products, arithmetic and copies ran while one was open for 0% of the time, Pallas kernels for 38%

profile of v5, /device:TPU:0, one launch (start us, length us, event | category | flops | bytes accessed | tf_op | source)
XLA Modules:
  0.0 78.5 jit_solution(14336543932110046039)
XLA Ops:
  0.7 0.5 collective-permute-start.2
  1.3 4.2 %shard_map.186 = (bf16[8,192,512]{2,1,0:T(8,128)(2,1)S(1)}, f32[512,512]{1,0:T(8,128)S(1)}, bf16[512,512]{1,0:T(8,128)(2,1)S(1)}, bf16[576,128]{1,0:T(8,128)(2,1...) custom-call(bf16[512,512]{1,0:T(8,128)(2,1)} %bitcast.19, ...), custom_call_target="tpu_custom_call" | custom-call | flops 43000000 | bytes 8192 | tf_op jit(solution)/shard_map/pallas_call | solution.py:51
  5.5 0.5 collective-permute-start
  6.0 0.5 shard_map.187.refs_3_.refs_0_.refs_1_
  6.5 0.5 collective-permute-done.refs_2_.refs_4_
  7.1 2.9 %collective-permute-start.1 = (bf16[576,128]{1,0:T(8,128)(2,1)S(1)}, bf16[576,128]{1,0:T(8,128)(2,1)S(1)}, u32[]{:S(2)}, u32[]{:S(2)}) collective-permute-start(bf16[576,128]{1,0:T(8,128)(2,1)S(1)} %shard_map.188.refs_3_), channel_id=1, source_target_pairs={{0,2},{2,0},{1,3},{3,1},{4,6},{6,4},{5,7},{7,5},{8,10},{10,8},{9,1... | collective-permute-start | bytes 442376 | tf_op jit(solution)/shard_map/ppermute | solution.py:38
  10.0 0.9 %shard_map.190 = (f32[256,512]{1,0:T(8,128)S(1)}, f32[256,512]{1,0:T(8,128)S(1)}, bf16[4,256,256]{2,1,0:T(8,128)(2,1)S(1)}, bf16[4,512,256]{2,1,0:T(8,128)(2,1)S(1)}) custom-call(bf16[8,64,512]{2,1,0:T(8,128)(2,1)S(1)} %shard_map.187.refs_3_.refs_0_.refs_1_, bf16[8,192,512]{2,1,0:T(8,128)(2,1)S(1)} %get-tuple-element.108.refs_1_.refs_2_, ...), custom_call_target="tpu_custom_call" | custom-call | flops 30000000 | bytes 8192 | tf_op jit(solution)/shard_map/pallas_call | solution.py:51
  10.9 0.9 %shard_map.189 = (f32[256,512]{1,0:T(8,128)S(1)}, f32[256,512]{1,0:T(8,128)S(1)}, bf16[4,256,256]{2,1,0:T(8,128)(2,1)S(1)}, bf16[4,512,256]{2,1,0:T(8,128)(2,1)S(1)}) custom-call(bf16[8,64,512]{2,1,0:T(8,128)(2,1)S(1)} %shard_map.187.refs_3_.refs_0_.refs_1_, bf16[8,192,512]{2,1,0:T(8,128)(2,1)S(1)} %get-tuple-element.108.refs_1_.refs_2_, ...), custom_call_target="tpu_custom_call" | custom-call | flops 30000000 | bytes 8192 | tf_op jit(solution)/shard_map/pallas_call | solution.py:51
  11.9 1.3 %shard_map.191 = (f32[512,1024]{1,0:T(8,128)S(1)}, f32[512,1024]{1,0:T(8,128)S(1)}, bf16[512,512]{1,0:T(8,128)(2,1)S(1)}, f32[512,512]{1,0:T(8,128)S(1)}, bf16[512,512]{1,0:T(8,128)(2,1)S(1)}) custom-call(bf16[512,512]{1,0:T(8,128)(2,1)S(1)} %bitcast.17, bf16[512,1024]{1,0:T(8,128)(2,1)S(1)} %copy-done.1, ...), custom_call_target="tpu_custom_call" | custom-call | flops 20000000 | bytes 8192 | tf_op jit(solution)/shard_map/pallas_call | solution.py:51
  13.2 1.0 %collective-permute-done.1.refs_5_ = bf16[576,128]{1,0:T(8,128)(2,1)S(1)} collective-permute-done((bf16[576,128]{1,0:T(8,128)(2,1)S(1)}, bf16[576,128]{1,0:T(8,128)(2,1)S(1)}, u32[]{:S(2)}, u32[]{:S(2)}) %collective-permute-start.1) | collective-permute-done | bytes 147488 | tf_op jit(solution)/shard_map/ppermute | solution.py:38
  14.1 2.3 %shard_map.192 = (bf16[512,512]{1,0:T(8,128)(2,1)S(1)}, bf16[512,128]{1,0:T(8,128)(2,1)S(1)}, f32[256,512]{1,0:T(8,128)S(1)}, f32[256,512]{1,0:T(8,128)S(1)}, f3...) custom-call(f32[8,512]{1,0:T(8,128)S(1)} %get-tuple-element.106.refs, ...), custom_call_target="tpu_custom_call" | custom-call | flops 40000000 | bytes 8192 | tf_op jit(solution)/shard_map/pallas_call | solution.py:51
  16.5 4.2 %shard_map.193 = (bf16[512,1024]{1,0:T(8,128)(2,1)S(1)}, bf16[512,1024]{1,0:T(8,128)(2,1)S(1)}, f32[512,512]{1,0:T(8,128)S(1)}, f32[512,512]{1,0:T(8,128)S(1)}, ...) custom-call(bf16[512,512]{1,0:T(8,128)(2,1)S(1)} %bitcast.20, ...), custom_call_target="tpu_custom_call" | custom-call | flops 60000000 | bytes 8192 | tf_op jit(solution)/shard_map/pallas_call | solution.py:51
  20.8 0.5 collective-permute-start.4
  21.3 5.0 %shard_map.194 = (bf16[512,512]{1,0:T(8,128)(2,1)}, f32[512,512]{1,0:T(8,128)S(1)}, bf16[512,512]{1,0:T(8,128)(2,1)S(1)}, bf16[512,256]{1,0:T(8,128)(2,1)S(1)}, ...) custom-call(f32[512,512]{1,0:T(8,128)S(1)} %get-tuple-element.119.re, ...), custom_call_target="tpu_custom_call" | custom-call | flops 60000000 | bytes 8192 | tf_op jit(solution)/shard_map/pallas_call | solution.py:51
  26.4 1.4 %shard_map.195 = (bf16[256,512]{1,0:T(8,128)(2,1)S(1)}, bf16[256,512]{1,0:T(8,128)(2,1)S(1)}, bf16[256,512]{1,0:T(8,128)(2,1)S(1)}, bf16[4,256,256]{2,1,0:T(8,12...) custom-call(f32[8,512]{1,0:T(8,128)S(1)} %get-tuple-element.106.refs_0_, ...), custom_call_target="tpu_custom_call" | custom-call | flops 30000000 | bytes 8192 | tf_op jit(solution)/shard_map/pallas_call | solution.py:51
  27.8 0.4 shard_map.196
  28.2 1.9 %collective-permute-start.10 = (bf16[8,32,1152]{2,1,0:T(8,128)(2,1)S(1)}, bf16[8,32,1152]{2,1,0:T(8,128)(2,1)S(1)}, u32[]{:S(2)}, u32[]{:S(2)}) collective-permute-start(bf16[8,32,1152]{2,1,0:T(8,128)(2,1)S(1)} %get-tuple-element.146.refs_12_), channel_id=1, source_target_pairs={{0,8},{2,10},{4,12},{6,14},{8,0},{10,2},{12,4},{14,6},{16,24},{18,... | collective-permute-start | bytes 1769480 | tf_op jit(solution)/shard_map/ppermute | solution.py:714
  30.1 1.5 %collective-permute-start.9 = (bf16[8,32,1152]{2,1,0:T(8,128)(2,1)S(1)}, bf16[8,32,1152]{2,1,0:T(8,128)(2,1)S(1)}, u32[]{:S(2)}, u32[]{:S(2)}) collective-permute-start(bf16[8,32,1152]{2,1,0:T(8,128)(2,1)S(1)} %get-tuple-element.145.refs_11_), channel_id=1, source_target_pairs={{0,4},{2,6},{4,0},{6,2},{8,12},{10,14},{12,8},{14,10},{16,20},{18,... | collective-permute-start | bytes 1769480 | tf_op jit(solution)/shard_map/ppermute | solution.py:714
  31.6 1.4 %shard_map.197 = (bf16[256,512]{1,0:T(8,128)(2,1)S(1)}, bf16[256,512]{1,0:T(8,128)(2,1)S(1)}, bf16[256,512]{1,0:T(8,128)(2,1)S(1)}, bf16[4,256,256]{2,1,0:T(8,12...) custom-call(f32[8,512]{1,0:T(8,128)S(1)} %get-tuple-element.106.refs_0_, ...), custom_call_target="tpu_custom_call" | custom-call | flops 30000000 | bytes 8192 | tf_op jit(solution)/shard_map/pallas_call | solution.py:51
  33.1 1.6 %shard_map.198.refs_3_.refs_7_ = f32[2,256,512]{2,1,0:T(8,128)S(1)} custom-call(f32[8,512]{1,0:T(8,128)S(1)} %get-tuple-element.106.refs_0_, bf16[8,64,512]{2,1,0:T(8,128)(2,1)S(1)} %shard_map.187.refs_3_.refs_0_.refs_1_, bf16[8,192,512]{2,1,0:T(8,128)(2,1)S(1)} %get-tuple-element.108.refs_1_.refs_2_, ...), custom_call_target="tpu_custom_call" | custom-call | flops 10000000 | bytes 8192 | tf_op jit(solution)/shard_map/pallas_call | solution.py:51
  34.8 1.6 %collective-permute-start.8 = (bf16[576,128]{1,0:T(8,128)(2,1)S(1)}, bf16[576,128]{1,0:T(8,128)(2,1)S(1)}, u32[]{:S(2)}, u32[]{:S(2)}) collective-permute-start(bf16[576,128]{1,0:T(8,128)(2,1)S(1)} %shard_map.199.refs_15_), channel_id=1, source_target_pairs={{0,2},{2,0},{1,3},{3,1},{4,6},{6,4},{5,7},{7,5},{8,10},{10,8},{9,1... | collective-permute-start | bytes 442376 | tf_op jit(solution)/shard_map/ppermute | solution.py:38
  36.4 1.6 %shard_map.200.refs_15_.refs_8_ = f32[2,256,512]{2,1,0:T(8,128)S(1)} custom-call(f32[8,512]{1,0:T(8,128)S(1)} %get-tuple-element.106.refs_0_, bf16[8,64,512]{2,1,0:T(8,128)(2,1)S(1)} %shard_map.187.refs_3_.refs_0_.refs_1_, bf16[8,192,512]{2,1,0:T(8,128)(2,1)S(1)} %get-tuple-element.108.refs_1_.refs_2_, ...), custom_call_target="tpu_custom_call" | custom-call | flops 10000000 | bytes 8192 | tf_op jit(solution)/shard_map/pallas_call | solution.py:51
  38.0 2.8 %shard_map.201.refs_9_ = f32[4,256,512]{2,1,0:T(8,128)S(1)} custom-call(f32[8,512]{1,0:T(8,128)S(1)} %get-tuple-element.106.refs_0_, bf16[8,64,512]{2,1,0:T(8,128)(2,1)S(1)} %shard_map.187.refs_3_.refs_0_.refs_1_, bf16[8,192,512]{2,1,0:T(8,128)(2,1)S(1)} %get-tuple-element.108.refs_1_.refs_2_, bf16[512,512]{1,0:T(8,128)(2,1)S(1)} %get-tuple-element.109.refs_2_.refs_3_, ...), custom_call_target="tpu_custom_call" | custom-call | flops 10000000 | bytes 8192 | tf_op jit(solution)/shard_map/pallas_call | solution.py:51
  40.8 0.3 collective-permute-done.8.refs_5_
  41.1 2.6 %shard_map.202 = (bf16[4,512,512]{2,1,0:T(8,128)(2,1)S(1)}, bf16[512,1024]{1,0:T(8,128)(2,1)S(1)}, bf16[512,1024]{1,0:T(8,128)(2,1)S(1)}) custom-call(f32[8,512]{1,0:T(8,128)S(1)} %get-tuple-element.106.refs_0_, bf16[8,64,512]{2,1,0:T(8,128)(2,1)S(1)} %shard_map.187.refs_3_.refs_0_.refs_1_, bf16[8,192,512]{2,1,0:T(8,128)(2,1)S(1)} %get-tuple-element.108.refs_1_.refs_2_, ...), custom_call_target="tpu_custom_call" | custom-call | flops 50000000 | bytes 8192 | tf_op jit(solution)/shard_map/pallas_call | solution.py:51
  43.8 0.2 collective-permute-done.10.refs_3_
  44.0 1.5 %collective-permute-done.9.refs_1_ = bf16[8,32,1152]{2,1,0:T(8,128)(2,1)S(1)} collective-permute-done((bf16[8,32,1152]{2,1,0:T(8,128)(2,1)S(1)}, bf16[8,32,1152]{2,1,0:T(8,128)(2,1)S(1)}, u32[]{:S(2)}, u32[]{:S(2)}) %collective-permute-start.9) | collective-permute-done | bytes 589856 | tf_op jit(solution)/shard_map/ppermute | solution.py:714
  45.4 0.2 shard_map.203
  45.6 0.4 collective-permute-start.18
  46.0 1.6 %collective-permute-start.19 = (bf16[4,32,1152]{2,1,0:T(8,128)(2,1)S(1)}, bf16[4,32,1152]{2,1,0:T(8,128)(2,1)S(1)}, u32[]{:S(2)}, u32[]{:S(2)}) collective-permute-start(bf16[4,32,1152]{2,1,0:T(8,128)(2,1)S(1)} %get-tuple-element.176.refs_8_), channel_id=1, source_target_pairs={{0,4},{2,6},{4,0},{6,2},{8,12},{10,14},{12,8},{14,10},{16,20},{18,... | collective-permute-start | bytes 884744 | tf_op jit(solution)/shard_map/ppermute | solution.py:714
  47.6 2.5 %shard_map.204 = (f32[512,512]{1,0:T(8,128)}, bf16[512,128]{1,0:T(8,128)(2,1)S(1)}) custom-call(bf16[4,512,512]{2,1,0:T(8,128)(2,1)S(1)} %get-tuple-element.167.refs_0_, bf16[512,2048]{1,0:T(8,128)(2,1)S(1)} %copy-done, f32[512,512]{1,0:T(8,128)S(1)} %get-tuple-element.168.refs_2_, f32[512,128]{1,0:T(8,128)S(1)} %get-tuple-element.169.refs_3_, ...), custom_call_target="tpu_custom_call" | custom-call | flops 10000000000 | bytes 8192 | tf_op jit(solution)/shard_map/pallas_call | solution.py:51
  50.2 0.2 shard_map.205
  50.4 1.6 %collective-permute-start.12 = (bf16[4,32,1152]{2,1,0:T(8,128)(2,1)S(1)}, bf16[4,32,1152]{2,1,0:T(8,128)(2,1)S(1)}, u32[]{:S(2)}, u32[]{:S(2)}) collective-permute-start(bf16[4,32,1152]{2,1,0:T(8,128)(2,1)S(1)} %get-tuple-element.181), channel_id=1, source_target_pairs={{0,2},{2,0},{4,6},{6,4},{8,10},{10,8},{12,14},{14,12},{16,18},{18,... | collective-permute-start | bytes 884744 | tf_op jit(solution)/shard_map/ppermute | solution.py:714
  52.0 0.5 collective-permute-start.13
  52.5 1.5 %collective-permute-start.14 = (bf16[4,32,1152]{2,1,0:T(8,128)(2,1)S(1)}, bf16[4,32,1152]{2,1,0:T(8,128)(2,1)S(1)}, u32[]{:S(2)}, u32[]{:S(2)}) collective-permute-start(bf16[4,32,1152]{2,1,0:T(8,128)(2,1)S(1)} %get-tuple-element.183), channel_id=1, source_target_pairs={{0,6},{2,4},{4,2},{6,0},{8,14},{10,12},{12,10},{14,8},{16,22},{18,... | collective-permute-start | bytes 884744 | tf_op jit(solution)/shard_map/ppermute | solution.py:714
  54.0 1.1 %collective-permute-done.19.refs_3_ = bf16[4,32,1152]{2,1,0:T(8,128)(2,1)S(1)} collective-permute-done((bf16[4,32,1152]{2,1,0:T(8,128)(2,1)S(1)}, bf16[4,32,1152]{2,1,0:T(8,128)(2,1)S(1)}, u32[]{:S(2)}, u32[]{:S(2)}) %collective-permute-start.19) | collective-permute-done | bytes 294944 | tf_op jit(solution)/shard_map/ppermute | solution.py:714
  55.2 2.7 %collective-permute-start.20 = (bf16[2,32,2304]{2,1,0:T(8,128)(2,1)S(1)}, bf16[2,32,2304]{2,1,0:T(8,128)(2,1)S(1)}, u32[]{:S(2)}, u32[]{:S(2)}) collective-permute-start(bf16[2,32,2304]{2,1,0:T(8,128)(2,1)S(1)} %get-tuple-element.191), channel_id=1, source_target_pairs={{0,16},{2,18},{4,20},{6,22},{8,24},{10,26},{12,28},{14,30},{16,0},... | collective-permute-start | bytes 884744 | tf_op jit(solution)/shard_map/ppermute | solution.py:714
  57.9 2.6 %collective-permute-done.12.refs_1_ = bf16[4,32,1152]{2,1,0:T(8,128)(2,1)S(1)} collective-permute-done((bf16[4,32,1152]{2,1,0:T(8,128)(2,1)S(1)}, bf16[4,32,1152]{2,1,0:T(8,128)(2,1)S(1)}, u32[]{:S(2)}, u32[]{:S(2)}) %collective-permute-start.12) | collective-permute-done | bytes 294944 | tf_op jit(solution)/shard_map/ppermute | solution.py:714
  60.5 6.3 %collective-permute-done.13.refs_2_ = bf16[4,32,1152]{2,1,0:T(8,128)(2,1)S(1)} collective-permute-done((bf16[4,32,1152]{2,1,0:T(8,128)(2,1)S(1)}, bf16[4,32,1152]{2,1,0:T(8,128)(2,1)S(1)}, u32[]{:S(2)}, u32[]{:S(2)}) %collective-permute-start.13) | collective-permute-done | bytes 294944 | tf_op jit(solution)/shard_map/ppermute | solution.py:714
  66.9 2.7 %collective-permute-start.15 = (bf16[1,32,1152]{2,1,0:T(8,128)(2,1)S(1)}, bf16[1,32,1152]{2,1,0:T(8,128)(2,1)S(1)}, u32[]{:S(2)}, u32[]{:S(2)}) collective-permute-start(bf16[1,32,1152]{2,1,0:T(8,128)(2,1)S(1)} %get-tuple-element.185), channel_id=1, source_target_pairs={{0,16},{2,18},{4,20},{6,22},{8,24},{10,26},{12,28},{14,30},{16,0},... | collective-permute-start | bytes 221192 | tf_op jit(solution)/shard_map/ppermute | solution.py:714
  69.6 1.2 %collective-permute-start.16 = (bf16[1,32,1152]{2,1,0:T(8,128)(2,1)S(1)}, bf16[1,32,1152]{2,1,0:T(8,128)(2,1)S(1)}, u32[]{:S(2)}, u32[]{:S(2)}) collective-permute-start(bf16[1,32,1152]{2,1,0:T(8,128)(2,1)S(1)} %get-tuple-element.186), channel_id=1, source_target_pairs={{0,24},{2,26},{4,28},{6,30},{8,16},{10,18},{12,20},{14,22},{16,8},... | collective-permute-start | bytes 221192 | tf_op jit(solution)/shard_map/ppermute | solution.py:714
  70.8 0.3 collective-permute-start.17
  71.1 1.5 %collective-permute-start.21 = (bf16[1,32,2304]{2,1,0:T(8,128)(2,1)S(1)}, bf16[1,32,2304]{2,1,0:T(8,128)(2,1)S(1)}, u32[]{:S(2)}, u32[]{:S(2)}) collective-permute-start(bf16[1,32,2304]{2,1,0:T(8,128)(2,1)S(1)} %get-tuple-element.193), channel_id=1, source_target_pairs={{0,2},{2,0},{4,6},{6,4},{8,10},{10,8},{12,14},{14,12},{16,18},{18,... | collective-permute-start | bytes 442376 | tf_op jit(solution)/shard_map/ppermute | solution.py:714
  72.6 1.8 %collective-permute-done.15.refs_1_ = bf16[1,32,1152]{2,1,0:T(8,128)(2,1)S(1)} collective-permute-done((bf16[1,32,1152]{2,1,0:T(8,128)(2,1)S(1)}, bf16[1,32,1152]{2,1,0:T(8,128)(2,1)S(1)}, u32[]{:S(2)}, u32[]{:S(2)}) %collective-permute-start.15) | collective-permute-done | bytes 73760 | tf_op jit(solution)/shard_map/ppermute | solution.py:714
  74.5 1.5 %collective-permute-done.16.refs_2_ = bf16[1,32,1152]{2,1,0:T(8,128)(2,1)S(1)} collective-permute-done((bf16[1,32,1152]{2,1,0:T(8,128)(2,1)S(1)}, bf16[1,32,1152]{2,1,0:T(8,128)(2,1)S(1)}, u32[]{:S(2)}, u32[]{:S(2)}) %collective-permute-start.16) | collective-permute-done | bytes 73760 | tf_op jit(solution)/shard_map/ppermute | solution.py:714
  76.1 0.2 collective-permute-done.21.refs_2_.refs_3_
  76.4 1.3 %collective-permute-done.22.refs_1_ = bf16[32,1408]{1,0:T(8,128)(2,1)S(1)} collective-permute-done((bf16[32,1408]{1,0:T(8,128)(2,1)S(1)}, bf16[32,1408]{1,0:T(8,128)(2,1)S(1)}, u32[]{:S(2)}, u32[]{:S(2)}) %collective-permute-start.22) | collective-permute-done | bytes 90144 | tf_op jit(solution)/shard_map/ppermute | solution.py:38
  77.7 0.8 %shard_map.211 = (f32[32,2048]{1,0:T(8,128)}, f32[32,512]{1,0:T(8,128)}, f32[32,1024]{1,0:T(8,128)}, f32[32,1024]{1,0:T(8,128)}, f32[32]{0:T(128)}, /*index=5*/f32[32]{0:T(128)}, f32[32]{0:T(128)}, f32[32]{0:T(128)}) custom-call(bf16[32,1408]{1,0:T(8,128)(2,1)S(1)} %shard_map.210.refs_0_, bf16[32,1408]{1,0:T(8,128)(2,1)S(1)} %collective-permute-done.22.refs_1_, ...), custom_call_target="tpu_custom_call" | custom-call | flops 10000000 | bytes 8192 | tf_op jit(solution)/shard_map/pallas_call | solution.py:51
  (43 shorter events, 1.2 us)
Async XLA Ops:
  0.6 5.3 %copy-start = (bf16[512,2048]{1,0:T(8,128)(2,1)S(1)}, bf16[512,2048]{1,0:T(8,128)(2,1)}, u32[]{:S(2)}) copy-start(bf16[512,2048]{1,0:T(8,128)(2,1)} %refs_1_.5) | copy-start | bytes 6291460
  0.7 11.2 %collective-permute-start.2 = (bf16[512,1024]{1,0:T(8,128)(2,1)}, bf16[512,1024]{1,0:T(8,128)(2,1)S(1)}, u32[]{:S(2)}, u32[]{:S(2)}) collective-permute-start(bf16[512,1024]{1,0:T(8,128)(2,1)} %refs_14_.1), channel_id=1, source_target_pairs={{0,1},{1,0},{2,3},{3,2},{4,5},{5,4},{6,7},{7,6},{8,9},{9,8},{10,11... | collective-permute-start | bytes 3145736 | tf_op jit(solution)/shard_map/ppermute | solution.py:38
  1.2 15.2 %collective-permute-start.3 = (bf16[512,1024]{1,0:T(8,128)(2,1)}, bf16[512,1024]{1,0:T(8,128)(2,1)S(1)}, u32[]{:S(2)}, u32[]{:S(2)}) collective-permute-start(bf16[512,1024]{1,0:T(8,128)(2,1)} %refs_13_.1), channel_id=1, source_target_pairs={{0,1},{1,0},{2,3},{3,2},{4,5},{5,4},{6,7},{7,6},{8,9},{9,8},{10,11... | collective-permute-start | bytes 3145736 | tf_op jit(solution)/shard_map/ppermute | solution.py:38
  5.5 1.5 %collective-permute-start = (bf16[576,128]{1,0:T(8,128)(2,1)S(1)}, bf16[576,128]{1,0:T(8,128)(2,1)S(1)}, u32[]{:S(2)}, u32[]{:S(2)}) collective-permute-start(bf16[576,128]{1,0:T(8,128)(2,1)S(1)} %get-tuple-element.110.refs_1_), channel_id=1, source_target_pairs={{0,1},{1,0},{2,3},{3,2},{4,5},{5,4},{6,7},{7,6},{8,9},{9,8},{10,11... | collective-permute-start | bytes 442376 | tf_op jit(solution)/shard_map/ppermute | solution.py:38
  7.1 7.1 %collective-permute-start.1 = (bf16[576,128]{1,0:T(8,128)(2,1)S(1)}, bf16[576,128]{1,0:T(8,128)(2,1)S(1)}, u32[]{:S(2)}, u32[]{:S(2)}) collective-permute-start(bf16[576,128]{1,0:T(8,128)(2,1)S(1)} %shard_map.188.refs_3_), channel_id=1, source_target_pairs={{0,2},{2,0},{1,3},{3,1},{4,6},{6,4},{5,7},{7,5},{8,10},{10,8},{9,1... | collective-permute-start | bytes 442376 | tf_op jit(solution)/shard_map/ppermute | solution.py:38
  10.0 1.9 %copy-start.1 = (bf16[512,1024]{1,0:T(8,128)(2,1)S(1)}, bf16[512,1024]{1,0:T(8,128)(2,1)}, u32[]{:S(2)}) copy-start(bf16[512,1024]{1,0:T(8,128)(2,1)} %refs_14_.1) | copy-start | bytes 3145732
  10.0 1.9 %copy-start.2 = (bf16[1,512,512]{2,1,0:T(8,128)(2,1)S(1)}, bf16[1,512,512]{2,1,0:T(8,128)(2,1)}, u32[]{:S(2)}) copy-start(bf16[1,512,512]{2,1,0:T(8,128)(2,1)} %param.21) | copy-start | bytes 1572868
  14.1 2.3 %copy-start.3 = (bf16[512,512]{1,0:T(8,128)(2,1)S(1)}, bf16[512,512]{1,0:T(8,128)(2,1)}, u32[]{:S(2)}) copy-start(bf16[512,512]{1,0:T(8,128)(2,1)} %refs_11_.1) | copy-start | bytes 1572868
  14.1 2.3 %copy-start.4 = (bf16[1,512,512]{2,1,0:T(8,128)(2,1)S(1)}, bf16[1,512,512]{2,1,0:T(8,128)(2,1)}, u32[]{:S(2)}) copy-start(bf16[1,512,512]{2,1,0:T(8,128)(2,1)} %param.11) | copy-start | bytes 1572868
  14.1 2.3 %copy-start.6 = (f32[512]{0:T(512)S(1)}, f32[512]{0:T(512)}, u32[]{:S(2)}) copy-start(f32[512]{0:T(512)} %param.17) | copy-start | bytes 6148
  14.1 2.3 %copy-start.7 = (f32[512]{0:T(512)S(1)}, f32[512]{0:T(512)}, u32[]{:S(2)}) copy-start(f32[512]{0:T(512)} %param.18) | copy-start | bytes 6148
  16.4 4.8 %copy-start.5 = (bf16[512,1024]{1,0:T(8,128)(2,1)S(1)}, bf16[512,1024]{1,0:T(8,128)(2,1)}, u32[]{:S(2)}) copy-start(bf16[512,1024]{1,0:T(8,128)(2,1)} %refs_13_.1) | copy-start | bytes 3145732
  20.7 7.1 %collective-permute-start.6 = (bf16[512,1024]{1,0:T(8,128)(2,1)S(1)}, bf16[512,1024]{1,0:T(8,128)(2,1)S(1)}, u32[]{:S(2)}, u32[]{:S(2)}) collective-permute-start(bf16[512,1024]{1,0:T(8,128)(2,1)S(1)} %get-tuple-element.144), channel_id=1, source_target_pairs={{0,1},{1,0},{2,3},{3,2},{4,5},{5,4},{6,7},{7,6},{8,9},{9,8},{10,11... | collective-permute-start | bytes 3145736 | tf_op jit(solution)/shard_map/ppermute | solution.py:38
  20.8 7.0 %collective-permute-start.4 = (bf16[512,1024]{1,0:T(8,128)(2,1)S(1)}, bf16[512,1024]{1,0:T(8,128)(2,1)S(1)}, u32[]{:S(2)}, u32[]{:S(2)}) collective-permute-start(bf16[512,1024]{1,0:T(8,128)(2,1)S(1)} %get-tuple-element.141), channel_id=1, source_target_pairs={{0,1},{1,0},{2,3},{3,2},{4,5},{5,4},{6,7},{7,6},{8,9},{9,8},{10,11... | collective-permute-start | bytes 3145736 | tf_op jit(solution)/shard_map/ppermute | solution.py:38
  26.3 1.5 %collective-permute-start.5 = (bf16[512,256]{1,0:T(8,128)(2,1)S(1)}, bf16[512,256]{1,0:T(8,128)(2,1)S(1)}, u32[]{:S(2)}, u32[]{:S(2)}) collective-permute-start(bf16[512,256]{1,0:T(8,128)(2,1)S(1)} %get-tuple-element.142), channel_id=1, source_target_pairs={{0,1},{1,0},{2,3},{3,2},{4,5},{5,4},{6,7},{7,6},{8,9},{9,8},{10,11... | collective-permute-start | bytes 786440 | tf_op jit(solution)/shard_map/ppermute | solution.py:38
  28.2 15.8 %collective-permute-start.10 = (bf16[8,32,1152]{2,1,0:T(8,128)(2,1)S(1)}, bf16[8,32,1152]{2,1,0:T(8,128)(2,1)S(1)}, u32[]{:S(2)}, u32[]{:S(2)}) collective-permute-start(bf16[8,32,1152]{2,1,0:T(8,128)(2,1)S(1)} %get-tuple-element.146.refs_12_), channel_id=1, source_target_pairs={{0,8},{2,10},{4,12},{6,14},{8,0},{10,2},{12,4},{14,6},{16,24},{18,... | collective-permute-start | bytes 1769480 | tf_op jit(solution)/shard_map/ppermute | solution.py:714
  30.1 15.3 %collective-permute-start.9 = (bf16[8,32,1152]{2,1,0:T(8,128)(2,1)S(1)}, bf16[8,32,1152]{2,1,0:T(8,128)(2,1)S(1)}, u32[]{:S(2)}, u32[]{:S(2)}) collective-permute-start(bf16[8,32,1152]{2,1,0:T(8,128)(2,1)S(1)} %get-tuple-element.145.refs_11_), channel_id=1, source_target_pairs={{0,4},{2,6},{4,0},{6,2},{8,12},{10,14},{12,8},{14,10},{16,20},{18,... | collective-permute-start | bytes 1769480 | tf_op jit(solution)/shard_map/ppermute | solution.py:714
  33.1 1.7 %collective-permute-start.7 = (bf16[576,128]{1,0:T(8,128)(2,1)S(1)}, bf16[576,128]{1,0:T(8,128)(2,1)S(1)}, u32[]{:S(2)}, u32[]{:S(2)}) collective-permute-start(bf16[576,128]{1,0:T(8,128)(2,1)S(1)} %get-tuple-element.147.refs_15_.refs_1_), channel_id=1, source_target_pairs={{0,1},{1,0},{2,3},{3,2},{4,5},{5,4},{6,7},{7,6},{8,9},{9,8},{10,11... | collective-permute-start | bytes 442376 | tf_op jit(solution)/shard_map/ppermute | solution.py:38
  34.8 6.3 %collective-permute-start.8 = (bf16[576,128]{1,0:T(8,128)(2,1)S(1)}, bf16[576,128]{1,0:T(8,128)(2,1)S(1)}, u32[]{:S(2)}, u32[]{:S(2)}) collective-permute-start(bf16[576,128]{1,0:T(8,128)(2,1)S(1)} %shard_map.199.refs_15_), channel_id=1, source_target_pairs={{0,2},{2,0},{1,3},{3,1},{4,6},{6,4},{5,7},{7,5},{8,10},{10,8},{9,1... | collective-permute-start | bytes 442376 | tf_op jit(solution)/shard_map/ppermute | solution.py:38
  43.7 3.9 %copy-start.8 = (f32[512]{0:T(512)S(1)}, f32[512]{0:T(512)}, u32[]{:S(2)}) copy-start(f32[512]{0:T(512)} %param.13) | copy-start | bytes 6148
  43.7 6.4 %collective-permute-start.11 = (bf16[512,1024]{1,0:T(8,128)(2,1)S(1)}, bf16[512,1024]{1,0:T(8,128)(2,1)S(1)}, u32[]{:S(2)}, u32[]{:S(2)}) collective-permute-start(bf16[512,1024]{1,0:T(8,128)(2,1)S(1)} %get-tuple-element.174.refs_4_), channel_id=1, source_target_pairs={{0,1},{1,0},{2,3},{3,2},{4,5},{5,4},{6,7},{7,6},{8,9},{9,8},{10,11... | collective-permute-start | bytes 3145736 | tf_op jit(solution)/shard_map/ppermute | solution.py:38
  45.6 8.4 %collective-permute-start.18 = (bf16[4,32,1152]{2,1,0:T(8,128)(2,1)S(1)}, bf16[4,32,1152]{2,1,0:T(8,128)(2,1)S(1)}, u32[]{:S(2)}, u32[]{:S(2)}) collective-permute-start(bf16[4,32,1152]{2,1,0:T(8,128)(2,1)S(1)} %get-tuple-element.175.refs_7_), channel_id=1, source_target_pairs={{0,8},{2,10},{4,12},{6,14},{8,0},{10,2},{12,4},{14,6},{16,24},{18,... | collective-permute-start | bytes 884744 | tf_op jit(solution)/shard_map/ppermute | solution.py:714
  46.0 9.1 %collective-permute-start.19 = (bf16[4,32,1152]{2,1,0:T(8,128)(2,1)S(1)}, bf16[4,32,1152]{2,1,0:T(8,128)(2,1)S(1)}, u32[]{:S(2)}, u32[]{:S(2)}) collective-permute-start(bf16[4,32,1152]{2,1,0:T(8,128)(2,1)S(1)} %get-tuple-element.176.refs_8_), channel_id=1, source_target_pairs={{0,4},{2,6},{4,0},{6,2},{8,12},{10,14},{12,8},{14,10},{16,20},{18,... | collective-permute-start | bytes 884744 | tf_op jit(solution)/shard_map/ppermute | solution.py:714
  50.4 10.0 %collective-permute-start.12 = (bf16[4,32,1152]{2,1,0:T(8,128)(2,1)S(1)}, bf16[4,32,1152]{2,1,0:T(8,128)(2,1)S(1)}, u32[]{:S(2)}, u32[]{:S(2)}) collective-permute-start(bf16[4,32,1152]{2,1,0:T(8,128)(2,1)S(1)} %get-tuple-element.181), channel_id=1, source_target_pairs={{0,2},{2,0},{4,6},{6,4},{8,10},{10,8},{12,14},{14,12},{16,18},{18,... | collective-permute-start | bytes 884744 | tf_op jit(solution)/shard_map/ppermute | solution.py:714
  52.0 14.8 %collective-permute-start.13 = (bf16[4,32,1152]{2,1,0:T(8,128)(2,1)S(1)}, bf16[4,32,1152]{2,1,0:T(8,128)(2,1)S(1)}, u32[]{:S(2)}, u32[]{:S(2)}) collective-permute-start(bf16[4,32,1152]{2,1,0:T(8,128)(2,1)S(1)} %get-tuple-element.182), channel_id=1, source_target_pairs={{0,4},{2,6},{4,0},{6,2},{8,12},{10,14},{12,8},{14,10},{16,20},{18,... | collective-permute-start | bytes 884744 | tf_op jit(solution)/shard_map/ppermute | solution.py:714
  52.5 14.3 %collective-permute-start.14 = (bf16[4,32,1152]{2,1,0:T(8,128)(2,1)S(1)}, bf16[4,32,1152]{2,1,0:T(8,128)(2,1)S(1)}, u32[]{:S(2)}, u32[]{:S(2)}) collective-permute-start(bf16[4,32,1152]{2,1,0:T(8,128)(2,1)S(1)} %get-tuple-element.183), channel_id=1, source_target_pairs={{0,6},{2,4},{4,2},{6,0},{8,14},{10,12},{12,10},{14,8},{16,22},{18,... | collective-permute-start | bytes 884744 | tf_op jit(solution)/shard_map/ppermute | solution.py:714
  55.2 15.9 %collective-permute-start.20 = (bf16[2,32,2304]{2,1,0:T(8,128)(2,1)S(1)}, bf16[2,32,2304]{2,1,0:T(8,128)(2,1)S(1)}, u32[]{:S(2)}, u32[]{:S(2)}) collective-permute-start(bf16[2,32,2304]{2,1,0:T(8,128)(2,1)S(1)} %get-tuple-element.191), channel_id=1, source_target_pairs={{0,16},{2,18},{4,20},{6,22},{8,24},{10,26},{12,28},{14,30},{16,0},... | collective-permute-start | bytes 884744 | tf_op jit(solution)/shard_map/ppermute | solution.py:714
  66.9 7.5 %collective-permute-start.15 = (bf16[1,32,1152]{2,1,0:T(8,128)(2,1)S(1)}, bf16[1,32,1152]{2,1,0:T(8,128)(2,1)S(1)}, u32[]{:S(2)}, u32[]{:S(2)}) collective-permute-start(bf16[1,32,1152]{2,1,0:T(8,128)(2,1)S(1)} %get-tuple-element.185), channel_id=1, source_target_pairs={{0,16},{2,18},{4,20},{6,22},{8,24},{10,26},{12,28},{14,30},{16,0},... | collective-permute-start | bytes 221192 | tf_op jit(solution)/shard_map/ppermute | solution.py:714
  69.6 6.3 %collective-permute-start.16 = (bf16[1,32,1152]{2,1,0:T(8,128)(2,1)S(1)}, bf16[1,32,1152]{2,1,0:T(8,128)(2,1)S(1)}, u32[]{:S(2)}, u32[]{:S(2)}) collective-permute-start(bf16[1,32,1152]{2,1,0:T(8,128)(2,1)S(1)} %get-tuple-element.186), channel_id=1, source_target_pairs={{0,24},{2,26},{4,28},{6,30},{8,16},{10,18},{12,20},{14,22},{16,8},... | collective-permute-start | bytes 221192 | tf_op jit(solution)/shard_map/ppermute | solution.py:714
  70.8 5.2 %collective-permute-start.17 = (bf16[1,32,1152]{2,1,0:T(8,128)(2,1)S(1)}, bf16[1,32,1152]{2,1,0:T(8,128)(2,1)S(1)}, u32[]{:S(2)}, u32[]{:S(2)}) collective-permute-start(bf16[1,32,1152]{2,1,0:T(8,128)(2,1)S(1)} %get-tuple-element.187), channel_id=1, source_target_pairs={{0,8},{2,10},{4,12},{6,14},{8,0},{10,2},{12,4},{14,6},{16,24},{18,... | collective-permute-start | bytes 221192 | tf_op jit(solution)/shard_map/ppermute | solution.py:714
  71.1 5.2 %collective-permute-start.21 = (bf16[1,32,2304]{2,1,0:T(8,128)(2,1)S(1)}, bf16[1,32,2304]{2,1,0:T(8,128)(2,1)S(1)}, u32[]{:S(2)}, u32[]{:S(2)}) collective-permute-start(bf16[1,32,2304]{2,1,0:T(8,128)(2,1)S(1)} %get-tuple-element.193), channel_id=1, source_target_pairs={{0,2},{2,0},{4,6},{6,4},{8,10},{10,8},{12,14},{14,12},{16,18},{18,... | collective-permute-start | bytes 442376 | tf_op jit(solution)/shard_map/ppermute | solution.py:714
  76.3 1.4 %collective-permute-start.22 = (bf16[32,1408]{1,0:T(8,128)(2,1)S(1)}, bf16[32,1408]{1,0:T(8,128)(2,1)S(1)}, u32[]{:S(2)}, u32[]{:S(2)}) collective-permute-start(bf16[32,1408]{1,0:T(8,128)(2,1)S(1)} %shard_map.210.refs_0_), channel_id=1, source_target_pairs={{0,1},{1,0},{2,3},{3,2},{4,5},{5,4},{6,7},{7,6},{8,9},{9,8},{10,11... | collective-permute-start | bytes 270344 | tf_op jit(solution)/shard_map/ppermute | solution.py:38

commit v6 on v5

--- a/solution.py
+++ b/solution.py
@@ -189,7 +189,7 @@
 
 
 def project_body(x_hbm, gain_hbm, bias_hbm, w_hbm, starts_ref,
-                 heads_ref, raw_ref, xn_ref, pack_ref, mask_ref, rows_ref, n_ref, inv_ref,
+                 heads_ref, raw_ref, xn_ref, pack_ref, mask_ref, rows_ref, n_ref, inv_ref, wq_ref,
                  x_ref, gain_ref, bias_ref, w_ref, sems):
     length, width = x_ref.shape
     copies = [
@@ -201,7 +201,8 @@
         pltpu.make_async_copy(w_hbm.at[:, pl.ds((j + 1) * width, width)], w_ref.at[j], sems.at[3 + j])
         for j in range(3)
     ]
-    for copy in copies + columns:
+    later = pltpu.make_async_copy(w_hbm.at[:, pl.ds(0, width)], wq_ref, sems.at[6])
+    for copy in copies + columns + [later]:
         copy.start()
     doc_row = doc_begin_row(starts_ref, length)
     tail = tail_row(doc_row, length)
@@ -241,6 +242,7 @@
         pack_ref[rows, :] = jnp.concatenate([mem_k, mem_vt], axis=1).astype(BF)
     tail8 = jnp.broadcast_to(tail, (8, length)).astype(BF)
     pack_totals(pack_ref, nt(tail8, c))
+    later.wait()
 
 
 def project(x, gain, bias, w, starts):
@@ -251,15 +253,15 @@
         project_body,
         (),
         [hbm, hbm, hbm, hbm, SMEM],
-        [VM] * 8,
+        [VM] * 9,
         [
             shape(BF, HEADS, 3 * HEAD, length), shape(F32, length, width), shape(BF, length, width),
             shape(BF, PACK, 128), shape(BF, length, length), shape(F32, 8, length),
-            shape(F32, length, width), shape(F32, length, 128),
+            shape(F32, length, width), shape(F32, length, 128), shape(BF, width, width),
         ],
         [
             pltpu.VMEM((length, width), BF), pltpu.VMEM((1, width), F32), pltpu.VMEM((1, width), F32),
-            pltpu.VMEM((3, width, width), BF), pltpu.SemaphoreType.DMA((6,)),
+            pltpu.VMEM((3, width, width), BF), pltpu.SemaphoreType.DMA((7,)),
         ],
         us=4.3,
         vmem=K1_VMEM,
@@ -267,13 +269,13 @@
 
 
 def query_body(xn_ref, w_ref, q_ref):
-    t = nn(xn_ref[...], w_ref[:, : xn_ref.shape[1]]).astype(BF).T
+    t = nn(xn_ref[...], w_ref[...]).astype(BF).T
     for h in range(HEADS):
         q_ref[h] = t[h * HEAD : h * HEAD + HEAD]
 
 
 def query(xn, w, after=()):
-    return call(query_body, (), [VM] * 2, VM, shape(BF, HEADS, HEAD, xn.shape[0]), us=0.5, after=after)(xn, w)
+    return call(query_body, (), [VM] * 2, VM, shape(BF, HEADS, HEAD, xn.shape[0]), us=1e3, after=after)(xn, w)
 
 
 def parts(refs, head):
@@ -837,11 +839,11 @@
     row = lambda a: a.reshape(1, width)
     blocked = lambda a: a.reshape(owners, width // owners, a.shape[1])
 
-    kvc, raw, xn, own, mask, rows, n1, inv1 = project(
+    kvc, raw, xn, own, mask, rows, n1, inv1, wq = project(
         x, row(norm1_gain), row(norm1_bias), in_weight, starts)
     up_other, down_other = swap(up_own, "ffn", 1), swap(down_own, "ffn", 1)
     partner = swap(own, "ffn", 1)
-    heads = (query(xn, in_weight), kvc)
+    heads = (query(xn, wq), kvc)
     both = combine(False, rows, own, partner, after=heads[:1])
     far = swap(both, "seq", 1)
     number_o, total_o, *pairs_other = local_sums(False, heads, mask, after=[both])

time: 78.7 us -> 78.2 us (level)
  transfers between devices with their start and end apart: 23 -> 23, of which waited for: 14 -> 13; matrix products, arithmetic and copies ran while one was open for 0% -> 0% of each run, Pallas kernels for 38% -> 33%
where the time goes in v6:
time: 78.2 us; the launch traced here: 78 us
  Pallas kernels  35.3 us (45%)
  starting transfers between devices  23.6 us (30%)
  waiting for transfers between devices  18.1 us (23%)
  between operations  0.92 us (1%)
    pallas_call x26, Pallas kernels, start(): pl.pallas_call(run, grid=grid, in_specs=list(in_specs) + [ANY] * len(afte...  35.3 us
    ppermute x12, starting transfers between devices, send_across(): lax.ppermute(a, ('dp', 'seq'), [(i, i ^ flip) for i in range(seqs * dps)])  17.3 us
    ppermute x12, waiting for transfers between devices, send_across(): lax.ppermute(a, ('dp', 'seq'), [(i, i ^ flip) for i in range(seqs * dps)])  15.4 us
    ppermute x11, starting transfers between devices, swap(): return lax.ppermute(a, axis, [(i, i ^ bit) for i in range(size)])  6.31 us
    ppermute x11, waiting for transfers between devices, swap(): return lax.ppermute(a, axis, [(i, i ^ bit) for i in range(size)])  2.73 us
  transfers between devices with their start and end apart: 23, of which 13 were waited for; matrix products, arithmetic and copies ran while one was open for 0% of the time, Pallas kernels for 33%

profile of v6, /device:TPU:0, one launch (start us, length us, event | category | flops | bytes accessed | tf_op | source)
XLA Modules:
  0.0 78.0 jit_solution(13296984019927412380)
XLA Ops:
  0.7 4.2 %shard_map.186 = (bf16[8,192,512]{2,1,0:T(8,128)(2,1)S(1)}, f32[512,512]{1,0:T(8,128)S(1)}, bf16[512,512]{1,0:T(8,128)(2,1)S(1)}, bf16[576,128]{1,0:T(8,128)(2,1...) custom-call(bf16[512,512]{1,0:T(8,128)(2,1)} %bitcast.19, ...), custom_call_target="tpu_custom_call" | custom-call | flops 43000000 | bytes 8192 | tf_op jit(solution)/shard_map/pallas_call | solution.py:51
  4.9 0.5 collective-permute-start
  5.5 0.4 collective-permute-start.3
  5.9 0.5 shard_map.187.refs_3_.refs_0_.refs_1_
  6.5 2.9 %collective-permute-start.1 = (bf16[576,128]{1,0:T(8,128)(2,1)S(1)}, bf16[576,128]{1,0:T(8,128)(2,1)S(1)}, u32[]{:S(2)}, u32[]{:S(2)}) collective-permute-start(bf16[576,128]{1,0:T(8,128)(2,1)S(1)} %shard_map.188.refs_3_), channel_id=1, source_target_pairs={{0,2},{2,0},{1,3},{3,1},{4,6},{6,4},{5,7},{7,5},{8,10},{10,8},{9,1... | collective-permute-start | bytes 442376 | tf_op jit(solution)/shard_map/ppermute | solution.py:38
  9.4 0.9 %shard_map.190 = (f32[256,512]{1,0:T(8,128)S(1)}, f32[256,512]{1,0:T(8,128)S(1)}, bf16[4,256,256]{2,1,0:T(8,128)(2,1)S(1)}, bf16[4,512,256]{2,1,0:T(8,128)(2,1)S(1)}) custom-call(bf16[8,64,512]{2,1,0:T(8,128)(2,1)S(1)} %shard_map.187.refs_3_.refs_0_.refs_1_, bf16[8,192,512]{2,1,0:T(8,128)(2,1)S(1)} %get-tuple-element.110.refs_1_.refs_2_, ...), custom_call_target="tpu_custom_call" | custom-call | flops 30000000 | bytes 8192 | tf_op jit(solution)/shard_map/pallas_call | solution.py:51
  10.4 0.9 %shard_map.189 = (f32[256,512]{1,0:T(8,128)S(1)}, f32[256,512]{1,0:T(8,128)S(1)}, bf16[4,256,256]{2,1,0:T(8,128)(2,1)S(1)}, bf16[4,512,256]{2,1,0:T(8,128)(2,1)S(1)}) custom-call(bf16[8,64,512]{2,1,0:T(8,128)(2,1)S(1)} %shard_map.187.refs_3_.refs_0_.refs_1_, bf16[8,192,512]{2,1,0:T(8,128)(2,1)S(1)} %get-tuple-element.110.refs_1_.refs_2_, ...), custom_call_target="tpu_custom_call" | custom-call | flops 30000000 | bytes 8192 | tf_op jit(solution)/shard_map/pallas_call | solution.py:51
  11.3 1.3 %shard_map.191 = (f32[512,1024]{1,0:T(8,128)S(1)}, f32[512,1024]{1,0:T(8,128)S(1)}, bf16[512,512]{1,0:T(8,128)(2,1)S(1)}, f32[512,512]{1,0:T(8,128)S(1)}, bf16[512,512]{1,0:T(8,128)(2,1)S(1)}) custom-call(bf16[512,512]{1,0:T(8,128)(2,1)S(1)} %bitcast.17, bf16[512,1024]{1,0:T(8,128)(2,1)S(1)} %copy-done, ...), custom_call_target="tpu_custom_call" | custom-call | flops 20000000 | bytes 8192 | tf_op jit(solution)/shard_map/pallas_call | solution.py:51
  12.6 1.0 %collective-permute-done.1.refs_5_ = bf16[576,128]{1,0:T(8,128)(2,1)S(1)} collective-permute-done((bf16[576,128]{1,0:T(8,128)(2,1)S(1)}, bf16[576,128]{1,0:T(8,128)(2,1)S(1)}, u32[]{:S(2)}, u32[]{:S(2)}) %collective-permute-start.1) | collective-permute-done | bytes 147488 | tf_op jit(solution)/shard_map/ppermute | solution.py:38
  13.6 2.3 %shard_map.192 = (bf16[512,512]{1,0:T(8,128)(2,1)S(1)}, bf16[512,128]{1,0:T(8,128)(2,1)S(1)}, f32[256,512]{1,0:T(8,128)S(1)}, f32[256,512]{1,0:T(8,128)S(1)}, f3...) custom-call(f32[8,512]{1,0:T(8,128)S(1)} %get-tuple-element.107.refs, ...), custom_call_target="tpu_custom_call" | custom-call | flops 40000000 | bytes 8192 | tf_op jit(solution)/shard_map/pallas_call | solution.py:51
  16.0 4.3 %shard_map.193 = (bf16[512,1024]{1,0:T(8,128)(2,1)S(1)}, bf16[512,1024]{1,0:T(8,128)(2,1)S(1)}, f32[512,512]{1,0:T(8,128)S(1)}, f32[512,512]{1,0:T(8,128)S(1)}, ...) custom-call(bf16[512,512]{1,0:T(8,128)(2,1)S(1)} %bitcast.20, ...), custom_call_target="tpu_custom_call" | custom-call | flops 60000000 | bytes 8192 | tf_op jit(solution)/shard_map/pallas_call | solution.py:51
  20.3 0.5 collective-permute-start.4
  20.8 5.0 %shard_map.194 = (bf16[512,512]{1,0:T(8,128)(2,1)}, f32[512,512]{1,0:T(8,128)S(1)}, bf16[512,512]{1,0:T(8,128)(2,1)S(1)}, bf16[512,256]{1,0:T(8,128)(2,1)S(1)}, ...) custom-call(f32[512,512]{1,0:T(8,128)S(1)} %get-tuple-element.121.re, ...), custom_call_target="tpu_custom_call" | custom-call | flops 60000000 | bytes 8192 | tf_op jit(solution)/shard_map/pallas_call | solution.py:51
  25.9 1.4 %shard_map.195 = (bf16[256,512]{1,0:T(8,128)(2,1)S(1)}, bf16[256,512]{1,0:T(8,128)(2,1)S(1)}, bf16[256,512]{1,0:T(8,128)(2,1)S(1)}, bf16[4,256,256]{2,1,0:T(8,12...) custom-call(f32[8,512]{1,0:T(8,128)S(1)} %get-tuple-element.107.refs_0_, ...), custom_call_target="tpu_custom_call" | custom-call | flops 30000000 | bytes 8192 | tf_op jit(solution)/shard_map/pallas_call | solution.py:51
  27.3 0.4 shard_map.196
  27.7 2.0 %collective-permute-start.10 = (bf16[8,32,1152]{2,1,0:T(8,128)(2,1)S(1)}, bf16[8,32,1152]{2,1,0:T(8,128)(2,1)S(1)}, u32[]{:S(2)}, u32[]{:S(2)}) collective-permute-start(bf16[8,32,1152]{2,1,0:T(8,128)(2,1)S(1)} %get-tuple-element.148.refs_12_), channel_id=1, source_target_pairs={{0,8},{2,10},{4,12},{6,14},{8,0},{10,2},{12,4},{14,6},{16,24},{18,... | collective-permute-start | bytes 1769480 | tf_op jit(solution)/shard_map/ppermute | solution.py:716
  29.6 1.4 %collective-permute-start.9 = (bf16[8,32,1152]{2,1,0:T(8,128)(2,1)S(1)}, bf16[8,32,1152]{2,1,0:T(8,128)(2,1)S(1)}, u32[]{:S(2)}, u32[]{:S(2)}) collective-permute-start(bf16[8,32,1152]{2,1,0:T(8,128)(2,1)S(1)} %get-tuple-element.147.refs_11_), channel_id=1, source_target_pairs={{0,4},{2,6},{4,0},{6,2},{8,12},{10,14},{12,8},{14,10},{16,20},{18,... | collective-permute-start | bytes 1769480 | tf_op jit(solution)/shard_map/ppermute | solution.py:716
  31.1 1.4 %shard_map.197 = (bf16[256,512]{1,0:T(8,128)(2,1)S(1)}, bf16[256,512]{1,0:T(8,128)(2,1)S(1)}, bf16[256,512]{1,0:T(8,128)(2,1)S(1)}, bf16[4,256,256]{2,1,0:T(8,12...) custom-call(f32[8,512]{1,0:T(8,128)S(1)} %get-tuple-element.107.refs_0_, ...), custom_call_target="tpu_custom_call" | custom-call | flops 30000000 | bytes 8192 | tf_op jit(solution)/shard_map/pallas_call | solution.py:51
  32.6 1.6 %shard_map.198.refs_3_.refs_7_ = f32[2,256,512]{2,1,0:T(8,128)S(1)} custom-call(f32[8,512]{1,0:T(8,128)S(1)} %get-tuple-element.107.refs_0_, bf16[8,64,512]{2,1,0:T(8,128)(2,1)S(1)} %shard_map.187.refs_3_.refs_0_.refs_1_, bf16[8,192,512]{2,1,0:T(8,128)(2,1)S(1)} %get-tuple-element.110.refs_1_.refs_2_, ...), custom_call_target="tpu_custom_call" | custom-call | flops 10000000 | bytes 8192 | tf_op jit(solution)/shard_map/pallas_call | solution.py:51
  34.3 1.6 %collective-permute-start.8 = (bf16[576,128]{1,0:T(8,128)(2,1)S(1)}, bf16[576,128]{1,0:T(8,128)(2,1)S(1)}, u32[]{:S(2)}, u32[]{:S(2)}) collective-permute-start(bf16[576,128]{1,0:T(8,128)(2,1)S(1)} %shard_map.199.refs_15_), channel_id=1, source_target_pairs={{0,2},{2,0},{1,3},{3,1},{4,6},{6,4},{5,7},{7,5},{8,10},{10,8},{9,1... | collective-permute-start | bytes 442376 | tf_op jit(solution)/shard_map/ppermute | solution.py:38
  35.8 1.6 %shard_map.200.refs_15_.refs_8_ = f32[2,256,512]{2,1,0:T(8,128)S(1)} custom-call(f32[8,512]{1,0:T(8,128)S(1)} %get-tuple-element.107.refs_0_, bf16[8,64,512]{2,1,0:T(8,128)(2,1)S(1)} %shard_map.187.refs_3_.refs_0_.refs_1_, bf16[8,192,512]{2,1,0:T(8,128)(2,1)S(1)} %get-tuple-element.110.refs_1_.refs_2_, ...), custom_call_target="tpu_custom_call" | custom-call | flops 10000000 | bytes 8192 | tf_op jit(solution)/shard_map/pallas_call | solution.py:51
  37.4 2.8 %shard_map.201.refs_9_ = f32[4,256,512]{2,1,0:T(8,128)S(1)} custom-call(f32[8,512]{1,0:T(8,128)S(1)} %get-tuple-element.107.refs_0_, bf16[8,64,512]{2,1,0:T(8,128)(2,1)S(1)} %shard_map.187.refs_3_.refs_0_.refs_1_, bf16[8,192,512]{2,1,0:T(8,128)(2,1)S(1)} %get-tuple-element.110.refs_1_.refs_2_, bf16[512,512]{1,0:T(8,128)(2,1)S(1)} %get-tuple-element.111.refs_2_.refs_3_, ...), custom_call_target="tpu_custom_call" | custom-call | flops 10000000 | bytes 8192 | tf_op jit(solution)/shard_map/pallas_call | solution.py:51
  40.2 0.3 collective-permute-done.8.refs_5_
  40.6 2.6 %shard_map.202 = (bf16[4,512,512]{2,1,0:T(8,128)(2,1)S(1)}, bf16[512,1024]{1,0:T(8,128)(2,1)S(1)}, bf16[512,1024]{1,0:T(8,128)(2,1)S(1)}) custom-call(f32[8,512]{1,0:T(8,128)S(1)} %get-tuple-element.107.refs_0_, bf16[8,64,512]{2,1,0:T(8,128)(2,1)S(1)} %shard_map.187.refs_3_.refs_0_.refs_1_, bf16[8,192,512]{2,1,0:T(8,128)(2,1)S(1)} %get-tuple-element.110.refs_1_.refs_2_, ...), custom_call_target="tpu_custom_call" | custom-call | flops 50000000 | bytes 8192 | tf_op jit(solution)/shard_map/pallas_call | solution.py:51
  43.3 0.2 collective-permute-done.10.refs_3_
  43.5 1.5 %collective-permute-done.9.refs_1_ = bf16[8,32,1152]{2,1,0:T(8,128)(2,1)S(1)} collective-permute-done((bf16[8,32,1152]{2,1,0:T(8,128)(2,1)S(1)}, bf16[8,32,1152]{2,1,0:T(8,128)(2,1)S(1)}, u32[]{:S(2)}, u32[]{:S(2)}) %collective-permute-start.9) | collective-permute-done | bytes 589856 | tf_op jit(solution)/shard_map/ppermute | solution.py:716
  45.0 0.2 shard_map.203
  45.1 0.4 collective-permute-start.18
  45.5 1.6 %collective-permute-start.19 = (bf16[4,32,1152]{2,1,0:T(8,128)(2,1)S(1)}, bf16[4,32,1152]{2,1,0:T(8,128)(2,1)S(1)}, u32[]{:S(2)}, u32[]{:S(2)}) collective-permute-start(bf16[4,32,1152]{2,1,0:T(8,128)(2,1)S(1)} %get-tuple-element.178.refs_8_), channel_id=1, source_target_pairs={{0,4},{2,6},{4,0},{6,2},{8,12},{10,14},{12,8},{14,10},{16,20},{18,... | collective-permute-start | bytes 884744 | tf_op jit(solution)/shard_map/ppermute | solution.py:716
  47.2 2.5 %shard_map.204 = (f32[512,512]{1,0:T(8,128)}, bf16[512,128]{1,0:T(8,128)(2,1)S(1)}) custom-call(bf16[4,512,512]{2,1,0:T(8,128)(2,1)S(1)} %get-tuple-element.169.refs_0_, bf16[512,2048]{1,0:T(8,128)(2,1)S(1)} %copy-done.2, f32[512,512]{1,0:T(8,128)S(1)} %get-tuple-element.170.refs_2_, f32[512,128]{1,0:T(8,128)S(1)} %get-tuple-element.171.refs_3_, ...), custom_call_target="tpu_custom_call" | custom-call | flops 10000000000 | bytes 8192 | tf_op jit(solution)/shard_map/pallas_call | solution.py:51
  49.7 0.2 shard_map.205
  49.9 1.6 %collective-permute-start.12 = (bf16[4,32,1152]{2,1,0:T(8,128)(2,1)S(1)}, bf16[4,32,1152]{2,1,0:T(8,128)(2,1)S(1)}, u32[]{:S(2)}, u32[]{:S(2)}) collective-permute-start(bf16[4,32,1152]{2,1,0:T(8,128)(2,1)S(1)} %get-tuple-element.183), channel_id=1, source_target_pairs={{0,2},{2,0},{4,6},{6,4},{8,10},{10,8},{12,14},{14,12},{16,18},{18,... | collective-permute-start | bytes 884744 | tf_op jit(solution)/shard_map/ppermute | solution.py:716
  51.4 0.5 collective-permute-start.13
  51.9 1.5 %collective-permute-start.14 = (bf16[4,32,1152]{2,1,0:T(8,128)(2,1)S(1)}, bf16[4,32,1152]{2,1,0:T(8,128)(2,1)S(1)}, u32[]{:S(2)}, u32[]{:S(2)}) collective-permute-start(bf16[4,32,1152]{2,1,0:T(8,128)(2,1)S(1)} %get-tuple-element.185), channel_id=1, source_target_pairs={{0,6},{2,4},{4,2},{6,0},{8,14},{10,12},{12,10},{14,8},{16,22},{18,... | collective-permute-start | bytes 884744 | tf_op jit(solution)/shard_map/ppermute | solution.py:716
  53.4 1.2 %collective-permute-done.19.refs_3_ = bf16[4,32,1152]{2,1,0:T(8,128)(2,1)S(1)} collective-permute-done((bf16[4,32,1152]{2,1,0:T(8,128)(2,1)S(1)}, bf16[4,32,1152]{2,1,0:T(8,128)(2,1)S(1)}, u32[]{:S(2)}, u32[]{:S(2)}) %collective-permute-start.19) | collective-permute-done | bytes 294944 | tf_op jit(solution)/shard_map/ppermute | solution.py:716
  54.7 2.7 %collective-permute-start.20 = (bf16[2,32,2304]{2,1,0:T(8,128)(2,1)S(1)}, bf16[2,32,2304]{2,1,0:T(8,128)(2,1)S(1)}, u32[]{:S(2)}, u32[]{:S(2)}) collective-permute-start(bf16[2,32,2304]{2,1,0:T(8,128)(2,1)S(1)} %get-tuple-element.193), channel_id=1, source_target_pairs={{0,16},{2,18},{4,20},{6,22},{8,24},{10,26},{12,28},{14,30},{16,0},... | collective-permute-start | bytes 884744 | tf_op jit(solution)/shard_map/ppermute | solution.py:716
  57.4 2.5 %collective-permute-done.12.refs_1_ = bf16[4,32,1152]{2,1,0:T(8,128)(2,1)S(1)} collective-permute-done((bf16[4,32,1152]{2,1,0:T(8,128)(2,1)S(1)}, bf16[4,32,1152]{2,1,0:T(8,128)(2,1)S(1)}, u32[]{:S(2)}, u32[]{:S(2)}) %collective-permute-start.12) | collective-permute-done | bytes 294944 | tf_op jit(solution)/shard_map/ppermute | solution.py:716
  59.9 6.4 %collective-permute-done.13.refs_2_ = bf16[4,32,1152]{2,1,0:T(8,128)(2,1)S(1)} collective-permute-done((bf16[4,32,1152]{2,1,0:T(8,128)(2,1)S(1)}, bf16[4,32,1152]{2,1,0:T(8,128)(2,1)S(1)}, u32[]{:S(2)}, u32[]{:S(2)}) %collective-permute-start.13) | collective-permute-done | bytes 294944 | tf_op jit(solution)/shard_map/ppermute | solution.py:716
  66.5 2.6 %collective-permute-start.15 = (bf16[1,32,1152]{2,1,0:T(8,128)(2,1)S(1)}, bf16[1,32,1152]{2,1,0:T(8,128)(2,1)S(1)}, u32[]{:S(2)}, u32[]{:S(2)}) collective-permute-start(bf16[1,32,1152]{2,1,0:T(8,128)(2,1)S(1)} %get-tuple-element.187), channel_id=1, source_target_pairs={{0,16},{2,18},{4,20},{6,22},{8,24},{10,26},{12,28},{14,30},{16,0},... | collective-permute-start | bytes 221192 | tf_op jit(solution)/shard_map/ppermute | solution.py:716
  69.1 1.2 %collective-permute-start.16 = (bf16[1,32,1152]{2,1,0:T(8,128)(2,1)S(1)}, bf16[1,32,1152]{2,1,0:T(8,128)(2,1)S(1)}, u32[]{:S(2)}, u32[]{:S(2)}) collective-permute-start(bf16[1,32,1152]{2,1,0:T(8,128)(2,1)S(1)} %get-tuple-element.188), channel_id=1, source_target_pairs={{0,24},{2,26},{4,28},{6,30},{8,16},{10,18},{12,20},{14,22},{16,8},... | collective-permute-start | bytes 221192 | tf_op jit(solution)/shard_map/ppermute | solution.py:716
  70.3 0.2 collective-permute-start.17
  70.6 1.6 %collective-permute-start.21 = (bf16[1,32,2304]{2,1,0:T(8,128)(2,1)S(1)}, bf16[1,32,2304]{2,1,0:T(8,128)(2,1)S(1)}, u32[]{:S(2)}, u32[]{:S(2)}) collective-permute-start(bf16[1,32,2304]{2,1,0:T(8,128)(2,1)S(1)} %get-tuple-element.195), channel_id=1, source_target_pairs={{0,2},{2,0},{4,6},{6,4},{8,10},{10,8},{12,14},{14,12},{16,18},{18,... | collective-permute-start | bytes 442376 | tf_op jit(solution)/shard_map/ppermute | solution.py:716
  72.1 1.9 %collective-permute-done.15.refs_1_ = bf16[1,32,1152]{2,1,0:T(8,128)(2,1)S(1)} collective-permute-done((bf16[1,32,1152]{2,1,0:T(8,128)(2,1)S(1)}, bf16[1,32,1152]{2,1,0:T(8,128)(2,1)S(1)}, u32[]{:S(2)}, u32[]{:S(2)}) %collective-permute-start.15) | collective-permute-done | bytes 73760 | tf_op jit(solution)/shard_map/ppermute | solution.py:716
  74.0 1.4 %collective-permute-done.16.refs_2_ = bf16[1,32,1152]{2,1,0:T(8,128)(2,1)S(1)} collective-permute-done((bf16[1,32,1152]{2,1,0:T(8,128)(2,1)S(1)}, bf16[1,32,1152]{2,1,0:T(8,128)(2,1)S(1)}, u32[]{:S(2)}, u32[]{:S(2)}) %collective-permute-start.16) | collective-permute-done | bytes 73760 | tf_op jit(solution)/shard_map/ppermute | solution.py:716
  75.4 0.2 collective-permute-done.17.refs_3_
  75.6 0.2 collective-permute-done.21.refs_2_.refs_3_
  75.9 1.3 %collective-permute-done.22.refs_1_ = bf16[32,1408]{1,0:T(8,128)(2,1)S(1)} collective-permute-done((bf16[32,1408]{1,0:T(8,128)(2,1)S(1)}, bf16[32,1408]{1,0:T(8,128)(2,1)S(1)}, u32[]{:S(2)}, u32[]{:S(2)}) %collective-permute-start.22) | collective-permute-done | bytes 90144 | tf_op jit(solution)/shard_map/ppermute | solution.py:38
  77.2 0.8 %shard_map.211 = (f32[32,2048]{1,0:T(8,128)}, f32[32,512]{1,0:T(8,128)}, f32[32,1024]{1,0:T(8,128)}, f32[32,1024]{1,0:T(8,128)}, f32[32]{0:T(128)}, /*index=5*/f32[32]{0:T(128)}, f32[32]{0:T(128)}, f32[32]{0:T(128)}) custom-call(bf16[32,1408]{1,0:T(8,128)(2,1)S(1)} %shard_map.210.refs_0_, bf16[32,1408]{1,0:T(8,128)(2,1)S(1)} %collective-permute-done.22.refs_1_, ...), custom_call_target="tpu_custom_call" | custom-call | flops 10000000 | bytes 8192 | tf_op jit(solution)/shard_map/pallas_call | solution.py:51
  (43 shorter events, 1.1 us)
Async XLA Ops:
  0.6 4.8 %copy-start = (bf16[512,1024]{1,0:T(8,128)(2,1)S(1)}, bf16[512,1024]{1,0:T(8,128)(2,1)}, u32[]{:S(2)}) copy-start(bf16[512,1024]{1,0:T(8,128)(2,1)} %refs_14_.1) | copy-start | bytes 3145732
  0.7 4.9 %copy-start.5 = (bf16[512,1024]{1,0:T(8,128)(2,1)S(1)}, bf16[512,1024]{1,0:T(8,128)(2,1)}, u32[]{:S(2)}) copy-start(bf16[512,1024]{1,0:T(8,128)(2,1)} %refs_13_.1) | copy-start | bytes 3145732
  4.9 1.6 %collective-permute-start = (bf16[576,128]{1,0:T(8,128)(2,1)S(1)}, bf16[576,128]{1,0:T(8,128)(2,1)S(1)}, u32[]{:S(2)}, u32[]{:S(2)}) collective-permute-start(bf16[576,128]{1,0:T(8,128)(2,1)S(1)} %get-tuple-element.112.refs_1_), channel_id=1, source_target_pairs={{0,1},{1,0},{2,3},{3,2},{4,5},{5,4},{6,7},{7,6},{8,9},{9,8},{10,11... | collective-permute-start | bytes 442376 | tf_op jit(solution)/shard_map/ppermute | solution.py:38
  5.4 5.9 %collective-permute-start.2 = (bf16[512,1024]{1,0:T(8,128)(2,1)S(1)}, bf16[512,1024]{1,0:T(8,128)(2,1)S(1)}, u32[]{:S(2)}, u32[]{:S(2)}) collective-permute-start(bf16[512,1024]{1,0:T(8,128)(2,1)S(1)} %copy-done), channel_id=1, source_target_pairs={{0,1},{1,0},{2,3},{3,2},{4,5},{5,4},{6,7},{7,6},{8,9},{9,8},{10,11... | collective-permute-start | bytes 3145736 | tf_op jit(solution)/shard_map/ppermute | solution.py:38
  5.5 10.4 %collective-permute-start.3 = (bf16[512,1024]{1,0:T(8,128)(2,1)S(1)}, bf16[512,1024]{1,0:T(8,128)(2,1)S(1)}, u32[]{:S(2)}, u32[]{:S(2)}) collective-permute-start(bf16[512,1024]{1,0:T(8,128)(2,1)S(1)} %copy-done.5), channel_id=1, source_target_pairs={{0,1},{1,0},{2,3},{3,2},{4,5},{5,4},{6,7},{7,6},{8,9},{9,8},{10,11... | collective-permute-start | bytes 3145736 | tf_op jit(solution)/shard_map/ppermute | solution.py:38
  6.5 7.1 %collective-permute-start.1 = (bf16[576,128]{1,0:T(8,128)(2,1)S(1)}, bf16[576,128]{1,0:T(8,128)(2,1)S(1)}, u32[]{:S(2)}, u32[]{:S(2)}) collective-permute-start(bf16[576,128]{1,0:T(8,128)(2,1)S(1)} %shard_map.188.refs_3_), channel_id=1, source_target_pairs={{0,2},{2,0},{1,3},{3,1},{4,6},{6,4},{5,7},{7,5},{8,10},{10,8},{9,1... | collective-permute-start | bytes 442376 | tf_op jit(solution)/shard_map/ppermute | solution.py:38
  9.4 1.9 %copy-start.1 = (bf16[1,512,512]{2,1,0:T(8,128)(2,1)S(1)}, bf16[1,512,512]{2,1,0:T(8,128)(2,1)}, u32[]{:S(2)}) copy-start(bf16[1,512,512]{2,1,0:T(8,128)(2,1)} %param.21) | copy-start | bytes 1572868
  13.6 2.3 %copy-start.3 = (bf16[512,512]{1,0:T(8,128)(2,1)S(1)}, bf16[512,512]{1,0:T(8,128)(2,1)}, u32[]{:S(2)}) copy-start(bf16[512,512]{1,0:T(8,128)(2,1)} %refs_11_.1) | copy-start | bytes 1572868
  13.6 2.3 %copy-start.4 = (bf16[1,512,512]{2,1,0:T(8,128)(2,1)S(1)}, bf16[1,512,512]{2,1,0:T(8,128)(2,1)}, u32[]{:S(2)}) copy-start(bf16[1,512,512]{2,1,0:T(8,128)(2,1)} %param.11) | copy-start | bytes 1572868
  13.6 2.3 %copy-start.6 = (f32[512]{0:T(512)S(1)}, f32[512]{0:T(512)}, u32[]{:S(2)}) copy-start(f32[512]{0:T(512)} %param.17) | copy-start | bytes 6148
  13.6 2.3 %copy-start.7 = (f32[512]{0:T(512)S(1)}, f32[512]{0:T(512)}, u32[]{:S(2)}) copy-start(f32[512]{0:T(512)} %param.18) | copy-start | bytes 6148
  20.2 7.1 %collective-permute-start.6 = (bf16[512,1024]{1,0:T(8,128)(2,1)S(1)}, bf16[512,1024]{1,0:T(8,128)(2,1)S(1)}, u32[]{:S(2)}, u32[]{:S(2)}) collective-permute-start(bf16[512,1024]{1,0:T(8,128)(2,1)S(1)} %get-tuple-element.146), channel_id=1, source_target_pairs={{0,1},{1,0},{2,3},{3,2},{4,5},{5,4},{6,7},{7,6},{8,9},{9,8},{10,11... | collective-permute-start | bytes 3145736 | tf_op jit(solution)/shard_map/ppermute | solution.py:38
  20.3 7.0 %collective-permute-start.4 = (bf16[512,1024]{1,0:T(8,128)(2,1)S(1)}, bf16[512,1024]{1,0:T(8,128)(2,1)S(1)}, u32[]{:S(2)}, u32[]{:S(2)}) collective-permute-start(bf16[512,1024]{1,0:T(8,128)(2,1)S(1)} %get-tuple-element.143), channel_id=1, source_target_pairs={{0,1},{1,0},{2,3},{3,2},{4,5},{5,4},{6,7},{7,6},{8,9},{9,8},{10,11... | collective-permute-start | bytes 3145736 | tf_op jit(solution)/shard_map/ppermute | solution.py:38
  25.8 1.5 %collective-permute-start.5 = (bf16[512,256]{1,0:T(8,128)(2,1)S(1)}, bf16[512,256]{1,0:T(8,128)(2,1)S(1)}, u32[]{:S(2)}, u32[]{:S(2)}) collective-permute-start(bf16[512,256]{1,0:T(8,128)(2,1)S(1)} %get-tuple-element.144), channel_id=1, source_target_pairs={{0,1},{1,0},{2,3},{3,2},{4,5},{5,4},{6,7},{7,6},{8,9},{9,8},{10,11... | collective-permute-start | bytes 786440 | tf_op jit(solution)/shard_map/ppermute | solution.py:38
  27.7 15.8 %collective-permute-start.10 = (bf16[8,32,1152]{2,1,0:T(8,128)(2,1)S(1)}, bf16[8,32,1152]{2,1,0:T(8,128)(2,1)S(1)}, u32[]{:S(2)}, u32[]{:S(2)}) collective-permute-start(bf16[8,32,1152]{2,1,0:T(8,128)(2,1)S(1)} %get-tuple-element.148.refs_12_), channel_id=1, source_target_pairs={{0,8},{2,10},{4,12},{6,14},{8,0},{10,2},{12,4},{14,6},{16,24},{18,... | collective-permute-start | bytes 1769480 | tf_op jit(solution)/shard_map/ppermute | solution.py:716
  29.6 15.3 %collective-permute-start.9 = (bf16[8,32,1152]{2,1,0:T(8,128)(2,1)S(1)}, bf16[8,32,1152]{2,1,0:T(8,128)(2,1)S(1)}, u32[]{:S(2)}, u32[]{:S(2)}) collective-permute-start(bf16[8,32,1152]{2,1,0:T(8,128)(2,1)S(1)} %get-tuple-element.147.refs_11_), channel_id=1, source_target_pairs={{0,4},{2,6},{4,0},{6,2},{8,12},{10,14},{12,8},{14,10},{16,20},{18,... | collective-permute-start | bytes 1769480 | tf_op jit(solution)/shard_map/ppermute | solution.py:716
  32.5 1.7 %collective-permute-start.7 = (bf16[576,128]{1,0:T(8,128)(2,1)S(1)}, bf16[576,128]{1,0:T(8,128)(2,1)S(1)}, u32[]{:S(2)}, u32[]{:S(2)}) collective-permute-start(bf16[576,128]{1,0:T(8,128)(2,1)S(1)} %get-tuple-element.149.refs_15_.refs_1_), channel_id=1, source_target_pairs={{0,1},{1,0},{2,3},{3,2},{4,5},{5,4},{6,7},{7,6},{8,9},{9,8},{10,11... | collective-permute-start | bytes 442376 | tf_op jit(solution)/shard_map/ppermute | solution.py:38
  34.3 6.3 %collective-permute-start.8 = (bf16[576,128]{1,0:T(8,128)(2,1)S(1)}, bf16[576,128]{1,0:T(8,128)(2,1)S(1)}, u32[]{:S(2)}, u32[]{:S(2)}) collective-permute-start(bf16[576,128]{1,0:T(8,128)(2,1)S(1)} %shard_map.199.refs_15_), channel_id=1, source_target_pairs={{0,2},{2,0},{1,3},{3,1},{4,6},{6,4},{5,7},{7,5},{8,10},{10,8},{9,1... | collective-permute-start | bytes 442376 | tf_op jit(solution)/shard_map/ppermute | solution.py:38
  43.2 4.0 %copy-start.2 = (bf16[512,2048]{1,0:T(8,128)(2,1)S(1)}, bf16[512,2048]{1,0:T(8,128)(2,1)}, u32[]{:S(2)}) copy-start(bf16[512,2048]{1,0:T(8,128)(2,1)} %refs_1_.3) | copy-start | bytes 6291460
  43.2 4.0 %copy-start.8 = (f32[512]{0:T(512)S(1)}, f32[512]{0:T(512)}, u32[]{:S(2)}) copy-start(f32[512]{0:T(512)} %param.13) | copy-start | bytes 6148
  43.2 6.4 %collective-permute-start.11 = (bf16[512,1024]{1,0:T(8,128)(2,1)S(1)}, bf16[512,1024]{1,0:T(8,128)(2,1)S(1)}, u32[]{:S(2)}, u32[]{:S(2)}) collective-permute-start(bf16[512,1024]{1,0:T(8,128)(2,1)S(1)} %get-tuple-element.176.refs_4_), channel_id=1, source_target_pairs={{0,1},{1,0},{2,3},{3,2},{4,5},{5,4},{6,7},{7,6},{8,9},{9,8},{10,11... | collective-permute-start | bytes 3145736 | tf_op jit(solution)/shard_map/ppermute | solution.py:38
  45.1 8.3 %collective-permute-start.18 = (bf16[4,32,1152]{2,1,0:T(8,128)(2,1)S(1)}, bf16[4,32,1152]{2,1,0:T(8,128)(2,1)S(1)}, u32[]{:S(2)}, u32[]{:S(2)}) collective-permute-start(bf16[4,32,1152]{2,1,0:T(8,128)(2,1)S(1)} %get-tuple-element.177.refs_7_), channel_id=1, source_target_pairs={{0,8},{2,10},{4,12},{6,14},{8,0},{10,2},{12,4},{14,6},{16,24},{18,... | collective-permute-start | bytes 884744 | tf_op jit(solution)/shard_map/ppermute | solution.py:716
  45.5 9.1 %collective-permute-start.19 = (bf16[4,32,1152]{2,1,0:T(8,128)(2,1)S(1)}, bf16[4,32,1152]{2,1,0:T(8,128)(2,1)S(1)}, u32[]{:S(2)}, u32[]{:S(2)}) collective-permute-start(bf16[4,32,1152]{2,1,0:T(8,128)(2,1)S(1)} %get-tuple-element.178.refs_8_), channel_id=1, source_target_pairs={{0,4},{2,6},{4,0},{6,2},{8,12},{10,14},{12,8},{14,10},{16,20},{18,... | collective-permute-start | bytes 884744 | tf_op jit(solution)/shard_map/ppermute | solution.py:716
  49.9 10.0 %collective-permute-start.12 = (bf16[4,32,1152]{2,1,0:T(8,128)(2,1)S(1)}, bf16[4,32,1152]{2,1,0:T(8,128)(2,1)S(1)}, u32[]{:S(2)}, u32[]{:S(2)}) collective-permute-start(bf16[4,32,1152]{2,1,0:T(8,128)(2,1)S(1)} %get-tuple-element.183), channel_id=1, source_target_pairs={{0,2},{2,0},{4,6},{6,4},{8,10},{10,8},{12,14},{14,12},{16,18},{18,... | collective-permute-start | bytes 884744 | tf_op jit(solution)/shard_map/ppermute | solution.py:716
  51.4 14.9 %collective-permute-start.13 = (bf16[4,32,1152]{2,1,0:T(8,128)(2,1)S(1)}, bf16[4,32,1152]{2,1,0:T(8,128)(2,1)S(1)}, u32[]{:S(2)}, u32[]{:S(2)}) collective-permute-start(bf16[4,32,1152]{2,1,0:T(8,128)(2,1)S(1)} %get-tuple-element.184), channel_id=1, source_target_pairs={{0,4},{2,6},{4,0},{6,2},{8,12},{10,14},{12,8},{14,10},{16,20},{18,... | collective-permute-start | bytes 884744 | tf_op jit(solution)/shard_map/ppermute | solution.py:716
  51.9 14.4 %collective-permute-start.14 = (bf16[4,32,1152]{2,1,0:T(8,128)(2,1)S(1)}, bf16[4,32,1152]{2,1,0:T(8,128)(2,1)S(1)}, u32[]{:S(2)}, u32[]{:S(2)}) collective-permute-start(bf16[4,32,1152]{2,1,0:T(8,128)(2,1)S(1)} %get-tuple-element.185), channel_id=1, source_target_pairs={{0,6},{2,4},{4,2},{6,0},{8,14},{10,12},{12,10},{14,8},{16,22},{18,... | collective-permute-start | bytes 884744 | tf_op jit(solution)/shard_map/ppermute | solution.py:716
  54.7 15.8 %collective-permute-start.20 = (bf16[2,32,2304]{2,1,0:T(8,128)(2,1)S(1)}, bf16[2,32,2304]{2,1,0:T(8,128)(2,1)S(1)}, u32[]{:S(2)}, u32[]{:S(2)}) collective-permute-start(bf16[2,32,2304]{2,1,0:T(8,128)(2,1)S(1)} %get-tuple-element.193), channel_id=1, source_target_pairs={{0,16},{2,18},{4,20},{6,22},{8,24},{10,26},{12,28},{14,30},{16,0},... | collective-permute-start | bytes 884744 | tf_op jit(solution)/shard_map/ppermute | solution.py:716
  66.5 7.6 %collective-permute-start.15 = (bf16[1,32,1152]{2,1,0:T(8,128)(2,1)S(1)}, bf16[1,32,1152]{2,1,0:T(8,128)(2,1)S(1)}, u32[]{:S(2)}, u32[]{:S(2)}) collective-permute-start(bf16[1,32,1152]{2,1,0:T(8,128)(2,1)S(1)} %get-tuple-element.187), channel_id=1, source_target_pairs={{0,16},{2,18},{4,20},{6,22},{8,24},{10,26},{12,28},{14,30},{16,0},... | collective-permute-start | bytes 221192 | tf_op jit(solution)/shard_map/ppermute | solution.py:716
  69.1 6.3 %collective-permute-start.16 = (bf16[1,32,1152]{2,1,0:T(8,128)(2,1)S(1)}, bf16[1,32,1152]{2,1,0:T(8,128)(2,1)S(1)}, u32[]{:S(2)}, u32[]{:S(2)}) collective-permute-start(bf16[1,32,1152]{2,1,0:T(8,128)(2,1)S(1)} %get-tuple-element.188), channel_id=1, source_target_pairs={{0,24},{2,26},{4,28},{6,30},{8,16},{10,18},{12,20},{14,22},{16,8},... | collective-permute-start | bytes 221192 | tf_op jit(solution)/shard_map/ppermute | solution.py:716
  70.3 5.3 %collective-permute-start.17 = (bf16[1,32,1152]{2,1,0:T(8,128)(2,1)S(1)}, bf16[1,32,1152]{2,1,0:T(8,128)(2,1)S(1)}, u32[]{:S(2)}, u32[]{:S(2)}) collective-permute-start(bf16[1,32,1152]{2,1,0:T(8,128)(2,1)S(1)} %get-tuple-element.189), channel_id=1, source_target_pairs={{0,8},{2,10},{4,12},{6,14},{8,0},{10,2},{12,4},{14,6},{16,24},{18,... | collective-permute-start | bytes 221192 | tf_op jit(solution)/shard_map/ppermute | solution.py:716
  70.6 5.2 %collective-permute-start.21 = (bf16[1,32,2304]{2,1,0:T(8,128)(2,1)S(1)}, bf16[1,32,2304]{2,1,0:T(8,128)(2,1)S(1)}, u32[]{:S(2)}, u32[]{:S(2)}) collective-permute-start(bf16[1,32,2304]{2,1,0:T(8,128)(2,1)S(1)} %get-tuple-element.195), channel_id=1, source_target_pairs={{0,2},{2,0},{4,6},{6,4},{8,10},{10,8},{12,14},{14,12},{16,18},{18,... | collective-permute-start | bytes 442376 | tf_op jit(solution)/shard_map/ppermute | solution.py:716
  75.8 1.4 %collective-permute-start.22 = (bf16[32,1408]{1,0:T(8,128)(2,1)S(1)}, bf16[32,1408]{1,0:T(8,128)(2,1)S(1)}, u32[]{:S(2)}, u32[]{:S(2)}) collective-permute-start(bf16[32,1408]{1,0:T(8,128)(2,1)S(1)} %shard_map.210.refs_0_), channel_id=1, source_target_pairs={{0,1},{1,0},{2,3},{3,2},{4,5},{5,4},{6,7},{7,6},{8,9},{9,8},{10,11... | collective-permute-start | bytes 270344 | tf_op jit(solution)/shard_map/ppermute | solution.py:38

commit v7 on v6

--- a/solution.py
+++ b/solution.py
@@ -868,7 +868,7 @@
         [[*all_of(a), (o, 0, out_half)] for a, o in zip(ups, outs)],
         [[*all_of(a), (o, out_half, out_half)] for a, o in zip(downs, outs)],
     ]
-    orders = [[1, 2], [2, 1]]
+    orders = [[2, 1], [1, 2]]
     left = [list(range(bits)) for _ in groups]
 
     def advance(groups, n, after):

time: 78.2 us -> 78 us (level)
  no operation moved by 1% of the time
where the time goes in v7:
time: 78 us; the launch traced here: 77.8 us
  Pallas kernels  35.3 us (45%)
  starting transfers between devices  24 us (31%)
  waiting for transfers between devices  17.6 us (23%)
  between operations  0.92 us (1%)
    pallas_call x26, Pallas kernels, start(): pl.pallas_call(run, grid=grid, in_specs=list(in_specs) + [ANY] * len(afte...  35.3 us
    ppermute x12, starting transfers between devices, send_across(): lax.ppermute(a, ('dp', 'seq'), [(i, i ^ flip) for i in range(seqs * dps)])  17.7 us
    ppermute x12, waiting for transfers between devices, send_across(): lax.ppermute(a, ('dp', 'seq'), [(i, i ^ flip) for i in range(seqs * dps)])  14.8 us
    ppermute x11, starting transfers between devices, swap(): return lax.ppermute(a, axis, [(i, i ^ bit) for i in range(size)])  6.31 us
    ppermute x11, waiting for transfers between devices, swap(): return lax.ppermute(a, axis, [(i, i ^ bit) for i in range(size)])  2.73 us
  transfers between devices with their start and end apart: 23, of which 13 were waited for; matrix products, arithmetic and copies ran while one was open for 0% of the time, Pallas kernels for 33%

profile of v7, /device:TPU:0, one launch (start us, length us, event | category | flops | bytes accessed | tf_op | source)
XLA Modules:
  0.0 77.8 jit_solution(2580649271741036987)
XLA Ops:
  0.7 4.2 %shard_map.186 = (bf16[8,192,512]{2,1,0:T(8,128)(2,1)S(1)}, f32[512,512]{1,0:T(8,128)S(1)}, bf16[512,512]{1,0:T(8,128)(2,1)S(1)}, bf16[576,128]{1,0:T(8,128)(2,1...) custom-call(bf16[512,512]{1,0:T(8,128)(2,1)} %bitcast.19, ...), custom_call_target="tpu_custom_call" | custom-call | flops 43000000 | bytes 8192 | tf_op jit(solution)/shard_map/pallas_call | solution.py:51
  4.9 0.5 collective-permute-start
  5.5 0.4 collective-permute-start.3
  5.9 0.5 shard_map.187.refs_3_.refs_0_.refs_1_
  6.5 2.9 %collective-permute-start.1 = (bf16[576,128]{1,0:T(8,128)(2,1)S(1)}, bf16[576,128]{1,0:T(8,128)(2,1)S(1)}, u32[]{:S(2)}, u32[]{:S(2)}) collective-permute-start(bf16[576,128]{1,0:T(8,128)(2,1)S(1)} %shard_map.188.refs_3_), channel_id=1, source_target_pairs={{0,2},{2,0},{1,3},{3,1},{4,6},{6,4},{5,7},{7,5},{8,10},{10,8},{9,1... | collective-permute-start | bytes 442376 | tf_op jit(solution)/shard_map/ppermute | solution.py:38
  9.4 0.9 %shard_map.190 = (f32[256,512]{1,0:T(8,128)S(1)}, f32[256,512]{1,0:T(8,128)S(1)}, bf16[4,256,256]{2,1,0:T(8,128)(2,1)S(1)}, bf16[4,512,256]{2,1,0:T(8,128)(2,1)S(1)}) custom-call(bf16[8,64,512]{2,1,0:T(8,128)(2,1)S(1)} %shard_map.187.refs_3_.refs_0_.refs_1_, bf16[8,192,512]{2,1,0:T(8,128)(2,1)S(1)} %get-tuple-element.110.refs_1_.refs_2_, ...), custom_call_target="tpu_custom_call" | custom-call | flops 30000000 | bytes 8192 | tf_op jit(solution)/shard_map/pallas_call | solution.py:51
  10.4 0.9 %shard_map.189 = (f32[256,512]{1,0:T(8,128)S(1)}, f32[256,512]{1,0:T(8,128)S(1)}, bf16[4,256,256]{2,1,0:T(8,128)(2,1)S(1)}, bf16[4,512,256]{2,1,0:T(8,128)(2,1)S(1)}) custom-call(bf16[8,64,512]{2,1,0:T(8,128)(2,1)S(1)} %shard_map.187.refs_3_.refs_0_.refs_1_, bf16[8,192,512]{2,1,0:T(8,128)(2,1)S(1)} %get-tuple-element.110.refs_1_.refs_2_, ...), custom_call_target="tpu_custom_call" | custom-call | flops 30000000 | bytes 8192 | tf_op jit(solution)/shard_map/pallas_call | solution.py:51
  11.3 1.3 %shard_map.191 = (f32[512,1024]{1,0:T(8,128)S(1)}, f32[512,1024]{1,0:T(8,128)S(1)}, bf16[512,512]{1,0:T(8,128)(2,1)S(1)}, f32[512,512]{1,0:T(8,128)S(1)}, bf16[512,512]{1,0:T(8,128)(2,1)S(1)}) custom-call(bf16[512,512]{1,0:T(8,128)(2,1)S(1)} %bitcast.17, bf16[512,1024]{1,0:T(8,128)(2,1)S(1)} %copy-done, ...), custom_call_target="tpu_custom_call" | custom-call | flops 20000000 | bytes 8192 | tf_op jit(solution)/shard_map/pallas_call | solution.py:51
  12.6 1.0 %collective-permute-done.1.refs_5_ = bf16[576,128]{1,0:T(8,128)(2,1)S(1)} collective-permute-done((bf16[576,128]{1,0:T(8,128)(2,1)S(1)}, bf16[576,128]{1,0:T(8,128)(2,1)S(1)}, u32[]{:S(2)}, u32[]{:S(2)}) %collective-permute-start.1) | collective-permute-done | bytes 147488 | tf_op jit(solution)/shard_map/ppermute | solution.py:38
  13.6 2.3 %shard_map.192 = (bf16[512,512]{1,0:T(8,128)(2,1)S(1)}, bf16[512,128]{1,0:T(8,128)(2,1)S(1)}, f32[256,512]{1,0:T(8,128)S(1)}, f32[256,512]{1,0:T(8,128)S(1)}, f3...) custom-call(f32[8,512]{1,0:T(8,128)S(1)} %get-tuple-element.107.refs, ...), custom_call_target="tpu_custom_call" | custom-call | flops 40000000 | bytes 8192 | tf_op jit(solution)/shard_map/pallas_call | solution.py:51
  16.0 4.3 %shard_map.193 = (bf16[512,1024]{1,0:T(8,128)(2,1)S(1)}, bf16[512,1024]{1,0:T(8,128)(2,1)S(1)}, f32[512,512]{1,0:T(8,128)S(1)}, f32[512,512]{1,0:T(8,128)S(1)}, ...) custom-call(bf16[512,512]{1,0:T(8,128)(2,1)S(1)} %bitcast.20, ...), custom_call_target="tpu_custom_call" | custom-call | flops 60000000 | bytes 8192 | tf_op jit(solution)/shard_map/pallas_call | solution.py:51
  20.3 0.5 collective-permute-start.4
  20.8 5.0 %shard_map.194 = (bf16[512,512]{1,0:T(8,128)(2,1)}, f32[512,512]{1,0:T(8,128)S(1)}, bf16[512,512]{1,0:T(8,128)(2,1)S(1)}, bf16[512,256]{1,0:T(8,128)(2,1)S(1)}, ...) custom-call(f32[512,512]{1,0:T(8,128)S(1)} %get-tuple-element.121.re, ...), custom_call_target="tpu_custom_call" | custom-call | flops 60000000 | bytes 8192 | tf_op jit(solution)/shard_map/pallas_call | solution.py:51
  25.9 1.4 %shard_map.195 = (bf16[256,512]{1,0:T(8,128)(2,1)S(1)}, bf16[256,512]{1,0:T(8,128)(2,1)S(1)}, bf16[256,512]{1,0:T(8,128)(2,1)S(1)}, bf16[4,256,256]{2,1,0:T(8,12...) custom-call(f32[8,512]{1,0:T(8,128)S(1)} %get-tuple-element.107.refs_0_, ...), custom_call_target="tpu_custom_call" | custom-call | flops 30000000 | bytes 8192 | tf_op jit(solution)/shard_map/pallas_call | solution.py:51
  27.3 0.4 shard_map.196
  27.7 1.8 %collective-permute-start.10 = (bf16[8,32,1152]{2,1,0:T(8,128)(2,1)S(1)}, bf16[8,32,1152]{2,1,0:T(8,128)(2,1)S(1)}, u32[]{:S(2)}, u32[]{:S(2)}) collective-permute-start(bf16[8,32,1152]{2,1,0:T(8,128)(2,1)S(1)} %get-tuple-element.148.refs_12_), channel_id=1, source_target_pairs={{0,4},{2,6},{4,0},{6,2},{8,12},{10,14},{12,8},{14,10},{16,20},{18,... | collective-permute-start | bytes 1769480 | tf_op jit(solution)/shard_map/ppermute | solution.py:716
  29.5 1.6 %collective-permute-start.9 = (bf16[8,32,1152]{2,1,0:T(8,128)(2,1)S(1)}, bf16[8,32,1152]{2,1,0:T(8,128)(2,1)S(1)}, u32[]{:S(2)}, u32[]{:S(2)}) collective-permute-start(bf16[8,32,1152]{2,1,0:T(8,128)(2,1)S(1)} %get-tuple-element.147.refs_11_), channel_id=1, source_target_pairs={{0,8},{2,10},{4,12},{6,14},{8,0},{10,2},{12,4},{14,6},{16,24},{18,... | collective-permute-start | bytes 1769480 | tf_op jit(solution)/shard_map/ppermute | solution.py:716
  31.1 1.4 %shard_map.197 = (bf16[256,512]{1,0:T(8,128)(2,1)S(1)}, bf16[256,512]{1,0:T(8,128)(2,1)S(1)}, bf16[256,512]{1,0:T(8,128)(2,1)S(1)}, bf16[4,256,256]{2,1,0:T(8,12...) custom-call(f32[8,512]{1,0:T(8,128)S(1)} %get-tuple-element.107.refs_0_, ...), custom_call_target="tpu_custom_call" | custom-call | flops 30000000 | bytes 8192 | tf_op jit(solution)/shard_map/pallas_call | solution.py:51
  32.6 1.6 %shard_map.198.refs_3_.refs_7_ = f32[2,256,512]{2,1,0:T(8,128)S(1)} custom-call(f32[8,512]{1,0:T(8,128)S(1)} %get-tuple-element.107.refs_0_, bf16[8,64,512]{2,1,0:T(8,128)(2,1)S(1)} %shard_map.187.refs_3_.refs_0_.refs_1_, bf16[8,192,512]{2,1,0:T(8,128)(2,1)S(1)} %get-tuple-element.110.refs_1_.refs_2_, ...), custom_call_target="tpu_custom_call" | custom-call | flops 10000000 | bytes 8192 | tf_op jit(solution)/shard_map/pallas_call | solution.py:51
  34.3 1.6 %collective-permute-start.8 = (bf16[576,128]{1,0:T(8,128)(2,1)S(1)}, bf16[576,128]{1,0:T(8,128)(2,1)S(1)}, u32[]{:S(2)}, u32[]{:S(2)}) collective-permute-start(bf16[576,128]{1,0:T(8,128)(2,1)S(1)} %shard_map.199.refs_15_), channel_id=1, source_target_pairs={{0,2},{2,0},{1,3},{3,1},{4,6},{6,4},{5,7},{7,5},{8,10},{10,8},{9,1... | collective-permute-start | bytes 442376 | tf_op jit(solution)/shard_map/ppermute | solution.py:38
  35.8 1.6 %shard_map.200.refs_15_.refs_8_ = f32[2,256,512]{2,1,0:T(8,128)S(1)} custom-call(f32[8,512]{1,0:T(8,128)S(1)} %get-tuple-element.107.refs_0_, bf16[8,64,512]{2,1,0:T(8,128)(2,1)S(1)} %shard_map.187.refs_3_.refs_0_.refs_1_, bf16[8,192,512]{2,1,0:T(8,128)(2,1)S(1)} %get-tuple-element.110.refs_1_.refs_2_, ...), custom_call_target="tpu_custom_call" | custom-call | flops 10000000 | bytes 8192 | tf_op jit(solution)/shard_map/pallas_call | solution.py:51
  37.4 2.8 %shard_map.201.refs_9_ = f32[4,256,512]{2,1,0:T(8,128)S(1)} custom-call(f32[8,512]{1,0:T(8,128)S(1)} %get-tuple-element.107.refs_0_, bf16[8,64,512]{2,1,0:T(8,128)(2,1)S(1)} %shard_map.187.refs_3_.refs_0_.refs_1_, bf16[8,192,512]{2,1,0:T(8,128)(2,1)S(1)} %get-tuple-element.110.refs_1_.refs_2_, bf16[512,512]{1,0:T(8,128)(2,1)S(1)} %get-tuple-element.111.refs_2_.refs_3_, ...), custom_call_target="tpu_custom_call" | custom-call | flops 10000000 | bytes 8192 | tf_op jit(solution)/shard_map/pallas_call | solution.py:51
  40.2 0.3 collective-permute-done.8.refs_5_
  40.6 2.6 %shard_map.202 = (bf16[4,512,512]{2,1,0:T(8,128)(2,1)S(1)}, bf16[512,1024]{1,0:T(8,128)(2,1)S(1)}, bf16[512,1024]{1,0:T(8,128)(2,1)S(1)}) custom-call(f32[8,512]{1,0:T(8,128)S(1)} %get-tuple-element.107.refs_0_, bf16[8,64,512]{2,1,0:T(8,128)(2,1)S(1)} %shard_map.187.refs_3_.refs_0_.refs_1_, bf16[8,192,512]{2,1,0:T(8,128)(2,1)S(1)} %get-tuple-element.110.refs_1_.refs_2_, ...), custom_call_target="tpu_custom_call" | custom-call | flops 50000000 | bytes 8192 | tf_op jit(solution)/shard_map/pallas_call | solution.py:51
  43.4 1.5 %collective-permute-done.9.refs_1_ = bf16[8,32,1152]{2,1,0:T(8,128)(2,1)S(1)} collective-permute-done((bf16[8,32,1152]{2,1,0:T(8,128)(2,1)S(1)}, bf16[8,32,1152]{2,1,0:T(8,128)(2,1)S(1)}, u32[]{:S(2)}, u32[]{:S(2)}) %collective-permute-start.9) | collective-permute-done | bytes 589856 | tf_op jit(solution)/shard_map/ppermute | solution.py:716
  44.9 0.2 shard_map.203
  45.1 0.5 collective-permute-start.18
  45.5 1.7 %collective-permute-start.19 = (bf16[4,32,1152]{2,1,0:T(8,128)(2,1)S(1)}, bf16[4,32,1152]{2,1,0:T(8,128)(2,1)S(1)}, u32[]{:S(2)}, u32[]{:S(2)}) collective-permute-start(bf16[4,32,1152]{2,1,0:T(8,128)(2,1)S(1)} %get-tuple-element.178.refs_8_), channel_id=1, source_target_pairs={{0,8},{2,10},{4,12},{6,14},{8,0},{10,2},{12,4},{14,6},{16,24},{18,... | collective-permute-start | bytes 884744 | tf_op jit(solution)/shard_map/ppermute | solution.py:716
  47.3 2.5 %shard_map.204 = (f32[512,512]{1,0:T(8,128)}, bf16[512,128]{1,0:T(8,128)(2,1)S(1)}) custom-call(bf16[4,512,512]{2,1,0:T(8,128)(2,1)S(1)} %get-tuple-element.169.refs_0_, bf16[512,2048]{1,0:T(8,128)(2,1)S(1)} %copy-done.2, f32[512,512]{1,0:T(8,128)S(1)} %get-tuple-element.170.refs_2_, f32[512,128]{1,0:T(8,128)S(1)} %get-tuple-element.171.refs_3_, ...), custom_call_target="tpu_custom_call" | custom-call | flops 10000000000 | bytes 8192 | tf_op jit(solution)/shard_map/pallas_call | solution.py:51
  49.8 0.2 shard_map.205
  50.0 1.5 %collective-permute-start.12 = (bf16[4,32,1152]{2,1,0:T(8,128)(2,1)S(1)}, bf16[4,32,1152]{2,1,0:T(8,128)(2,1)S(1)}, u32[]{:S(2)}, u32[]{:S(2)}) collective-permute-start(bf16[4,32,1152]{2,1,0:T(8,128)(2,1)S(1)} %get-tuple-element.183), channel_id=1, source_target_pairs={{0,2},{2,0},{4,6},{6,4},{8,10},{10,8},{12,14},{14,12},{16,18},{18,... | collective-permute-start | bytes 884744 | tf_op jit(solution)/shard_map/ppermute | solution.py:716
  51.5 1.5 %collective-permute-start.13 = (bf16[4,32,1152]{2,1,0:T(8,128)(2,1)S(1)}, bf16[4,32,1152]{2,1,0:T(8,128)(2,1)S(1)}, u32[]{:S(2)}, u32[]{:S(2)}) collective-permute-start(bf16[4,32,1152]{2,1,0:T(8,128)(2,1)S(1)} %get-tuple-element.184), channel_id=1, source_target_pairs={{0,4},{2,6},{4,0},{6,2},{8,12},{10,14},{12,8},{14,10},{16,20},{18,... | collective-permute-start | bytes 884744 | tf_op jit(solution)/shard_map/ppermute | solution.py:716
  53.0 0.5 collective-permute-start.14
  53.5 0.5 collective-permute-done.18.refs_2_
  54.1 2.7 %collective-permute-start.20 = (bf16[2,32,2304]{2,1,0:T(8,128)(2,1)S(1)}, bf16[2,32,2304]{2,1,0:T(8,128)(2,1)S(1)}, u32[]{:S(2)}, u32[]{:S(2)}) collective-permute-start(bf16[2,32,2304]{2,1,0:T(8,128)(2,1)S(1)} %get-tuple-element.193), channel_id=1, source_target_pairs={{0,16},{2,18},{4,20},{6,22},{8,24},{10,26},{12,28},{14,30},{16,0},... | collective-permute-start | bytes 884744 | tf_op jit(solution)/shard_map/ppermute | solution.py:716
  56.8 3.1 %collective-permute-done.12.refs_1_ = bf16[4,32,1152]{2,1,0:T(8,128)(2,1)S(1)} collective-permute-done((bf16[4,32,1152]{2,1,0:T(8,128)(2,1)S(1)}, bf16[4,32,1152]{2,1,0:T(8,128)(2,1)S(1)}, u32[]{:S(2)}, u32[]{:S(2)}) %collective-permute-start.12) | collective-permute-done | bytes 294944 | tf_op jit(solution)/shard_map/ppermute | solution.py:716
  60.0 6.0 %collective-permute-done.13.refs_2_ = bf16[4,32,1152]{2,1,0:T(8,128)(2,1)S(1)} collective-permute-done((bf16[4,32,1152]{2,1,0:T(8,128)(2,1)S(1)}, bf16[4,32,1152]{2,1,0:T(8,128)(2,1)S(1)}, u32[]{:S(2)}, u32[]{:S(2)}) %collective-permute-start.13) | collective-permute-done | bytes 294944 | tf_op jit(solution)/shard_map/ppermute | solution.py:716
  66.0 0.1 shard_map.206
  66.1 2.7 %collective-permute-start.15 = (bf16[1,32,1152]{2,1,0:T(8,128)(2,1)S(1)}, bf16[1,32,1152]{2,1,0:T(8,128)(2,1)S(1)}, u32[]{:S(2)}, u32[]{:S(2)}) collective-permute-start(bf16[1,32,1152]{2,1,0:T(8,128)(2,1)S(1)} %get-tuple-element.187), channel_id=1, source_target_pairs={{0,16},{2,18},{4,20},{6,22},{8,24},{10,26},{12,28},{14,30},{16,0},... | collective-permute-start | bytes 221192 | tf_op jit(solution)/shard_map/ppermute | solution.py:716
  68.8 1.3 %collective-permute-start.16 = (bf16[1,32,1152]{2,1,0:T(8,128)(2,1)S(1)}, bf16[1,32,1152]{2,1,0:T(8,128)(2,1)S(1)}, u32[]{:S(2)}, u32[]{:S(2)}) collective-permute-start(bf16[1,32,1152]{2,1,0:T(8,128)(2,1)S(1)} %get-tuple-element.188), channel_id=1, source_target_pairs={{0,24},{2,26},{4,28},{6,30},{8,16},{10,18},{12,20},{14,22},{16,8},... | collective-permute-start | bytes 221192 | tf_op jit(solution)/shard_map/ppermute | solution.py:716
  70.2 0.2 collective-permute-start.17
  70.4 1.6 %collective-permute-start.21 = (bf16[1,32,2304]{2,1,0:T(8,128)(2,1)S(1)}, bf16[1,32,2304]{2,1,0:T(8,128)(2,1)S(1)}, u32[]{:S(2)}, u32[]{:S(2)}) collective-permute-start(bf16[1,32,2304]{2,1,0:T(8,128)(2,1)S(1)} %get-tuple-element.195), channel_id=1, source_target_pairs={{0,2},{2,0},{4,6},{6,4},{8,10},{10,8},{12,14},{14,12},{16,18},{18,... | collective-permute-start | bytes 442376 | tf_op jit(solution)/shard_map/ppermute | solution.py:716
  72.0 0.9 %collective-permute-done.15.refs_1_ = bf16[1,32,1152]{2,1,0:T(8,128)(2,1)S(1)} collective-permute-done((bf16[1,32,1152]{2,1,0:T(8,128)(2,1)S(1)}, bf16[1,32,1152]{2,1,0:T(8,128)(2,1)S(1)}, u32[]{:S(2)}, u32[]{:S(2)}) %collective-permute-start.15) | collective-permute-done | bytes 73760 | tf_op jit(solution)/shard_map/ppermute | solution.py:716
  72.9 2.2 %collective-permute-done.16.refs_2_ = bf16[1,32,1152]{2,1,0:T(8,128)(2,1)S(1)} collective-permute-done((bf16[1,32,1152]{2,1,0:T(8,128)(2,1)S(1)}, bf16[1,32,1152]{2,1,0:T(8,128)(2,1)S(1)}, u32[]{:S(2)}, u32[]{:S(2)}) %collective-permute-start.16) | collective-permute-done | bytes 73760 | tf_op jit(solution)/shard_map/ppermute | solution.py:716
  75.1 0.2 collective-permute-done.17.refs_3_
  75.3 0.3 collective-permute-done.21.refs_2_.refs_3_
  75.7 1.3 %collective-permute-done.22.refs_1_ = bf16[32,1408]{1,0:T(8,128)(2,1)S(1)} collective-permute-done((bf16[32,1408]{1,0:T(8,128)(2,1)S(1)}, bf16[32,1408]{1,0:T(8,128)(2,1)S(1)}, u32[]{:S(2)}, u32[]{:S(2)}) %collective-permute-start.22) | collective-permute-done | bytes 90144 | tf_op jit(solution)/shard_map/ppermute | solution.py:38
  77.0 0.8 %shard_map.211 = (f32[32,2048]{1,0:T(8,128)}, f32[32,512]{1,0:T(8,128)}, f32[32,1024]{1,0:T(8,128)}, f32[32,1024]{1,0:T(8,128)}, f32[32]{0:T(128)}, /*index=5*/f32[32]{0:T(128)}, f32[32]{0:T(128)}, f32[32]{0:T(128)}) custom-call(bf16[32,1408]{1,0:T(8,128)(2,1)S(1)} %shard_map.210.refs_0_, bf16[32,1408]{1,0:T(8,128)(2,1)S(1)} %collective-permute-done.22.refs_1_, ...), custom_call_target="tpu_custom_call" | custom-call | flops 10000000 | bytes 8192 | tf_op jit(solution)/shard_map/pallas_call | solution.py:51
  (43 shorter events, 1.1 us)
Async XLA Ops:
  0.6 4.8 %copy-start = (bf16[512,1024]{1,0:T(8,128)(2,1)S(1)}, bf16[512,1024]{1,0:T(8,128)(2,1)}, u32[]{:S(2)}) copy-start(bf16[512,1024]{1,0:T(8,128)(2,1)} %refs_14_.1) | copy-start | bytes 3145732
  0.7 4.9 %copy-start.5 = (bf16[512,1024]{1,0:T(8,128)(2,1)S(1)}, bf16[512,1024]{1,0:T(8,128)(2,1)}, u32[]{:S(2)}) copy-start(bf16[512,1024]{1,0:T(8,128)(2,1)} %refs_13_.1) | copy-start | bytes 3145732
  4.9 1.6 %collective-permute-start = (bf16[576,128]{1,0:T(8,128)(2,1)S(1)}, bf16[576,128]{1,0:T(8,128)(2,1)S(1)}, u32[]{:S(2)}, u32[]{:S(2)}) collective-permute-start(bf16[576,128]{1,0:T(8,128)(2,1)S(1)} %get-tuple-element.112.refs_1_), channel_id=1, source_target_pairs={{0,1},{1,0},{2,3},{3,2},{4,5},{5,4},{6,7},{7,6},{8,9},{9,8},{10,11... | collective-permute-start | bytes 442376 | tf_op jit(solution)/shard_map/ppermute | solution.py:38
  5.4 5.9 %collective-permute-start.2 = (bf16[512,1024]{1,0:T(8,128)(2,1)S(1)}, bf16[512,1024]{1,0:T(8,128)(2,1)S(1)}, u32[]{:S(2)}, u32[]{:S(2)}) collective-permute-start(bf16[512,1024]{1,0:T(8,128)(2,1)S(1)} %copy-done), channel_id=1, source_target_pairs={{0,1},{1,0},{2,3},{3,2},{4,5},{5,4},{6,7},{7,6},{8,9},{9,8},{10,11... | collective-permute-start | bytes 3145736 | tf_op jit(solution)/shard_map/ppermute | solution.py:38
  5.5 10.4 %collective-permute-start.3 = (bf16[512,1024]{1,0:T(8,128)(2,1)S(1)}, bf16[512,1024]{1,0:T(8,128)(2,1)S(1)}, u32[]{:S(2)}, u32[]{:S(2)}) collective-permute-start(bf16[512,1024]{1,0:T(8,128)(2,1)S(1)} %copy-done.5), channel_id=1, source_target_pairs={{0,1},{1,0},{2,3},{3,2},{4,5},{5,4},{6,7},{7,6},{8,9},{9,8},{10,11... | collective-permute-start | bytes 3145736 | tf_op jit(solution)/shard_map/ppermute | solution.py:38
  6.5 7.1 %collective-permute-start.1 = (bf16[576,128]{1,0:T(8,128)(2,1)S(1)}, bf16[576,128]{1,0:T(8,128)(2,1)S(1)}, u32[]{:S(2)}, u32[]{:S(2)}) collective-permute-start(bf16[576,128]{1,0:T(8,128)(2,1)S(1)} %shard_map.188.refs_3_), channel_id=1, source_target_pairs={{0,2},{2,0},{1,3},{3,1},{4,6},{6,4},{5,7},{7,5},{8,10},{10,8},{9,1... | collective-permute-start | bytes 442376 | tf_op jit(solution)/shard_map/ppermute | solution.py:38
  9.4 1.9 %copy-start.1 = (bf16[1,512,512]{2,1,0:T(8,128)(2,1)S(1)}, bf16[1,512,512]{2,1,0:T(8,128)(2,1)}, u32[]{:S(2)}) copy-start(bf16[1,512,512]{2,1,0:T(8,128)(2,1)} %param.21) | copy-start | bytes 1572868
  13.6 2.3 %copy-start.3 = (bf16[512,512]{1,0:T(8,128)(2,1)S(1)}, bf16[512,512]{1,0:T(8,128)(2,1)}, u32[]{:S(2)}) copy-start(bf16[512,512]{1,0:T(8,128)(2,1)} %refs_11_.1) | copy-start | bytes 1572868
  13.6 2.3 %copy-start.4 = (bf16[1,512,512]{2,1,0:T(8,128)(2,1)S(1)}, bf16[1,512,512]{2,1,0:T(8,128)(2,1)}, u32[]{:S(2)}) copy-start(bf16[1,512,512]{2,1,0:T(8,128)(2,1)} %param.11) | copy-start | bytes 1572868
  13.6 2.3 %copy-start.6 = (f32[512]{0:T(512)S(1)}, f32[512]{0:T(512)}, u32[]{:S(2)}) copy-start(f32[512]{0:T(512)} %param.17) | copy-start | bytes 6148
  13.6 2.3 %copy-start.7 = (f32[512]{0:T(512)S(1)}, f32[512]{0:T(512)}, u32[]{:S(2)}) copy-start(f32[512]{0:T(512)} %param.18) | copy-start | bytes 6148
  20.2 7.1 %collective-permute-start.6 = (bf16[512,1024]{1,0:T(8,128)(2,1)S(1)}, bf16[512,1024]{1,0:T(8,128)(2,1)S(1)}, u32[]{:S(2)}, u32[]{:S(2)}) collective-permute-start(bf16[512,1024]{1,0:T(8,128)(2,1)S(1)} %get-tuple-element.146), channel_id=1, source_target_pairs={{0,1},{1,0},{2,3},{3,2},{4,5},{5,4},{6,7},{7,6},{8,9},{9,8},{10,11... | collective-permute-start | bytes 3145736 | tf_op jit(solution)/shard_map/ppermute | solution.py:38
  20.3 7.0 %collective-permute-start.4 = (bf16[512,1024]{1,0:T(8,128)(2,1)S(1)}, bf16[512,1024]{1,0:T(8,128)(2,1)S(1)}, u32[]{:S(2)}, u32[]{:S(2)}) collective-permute-start(bf16[512,1024]{1,0:T(8,128)(2,1)S(1)} %get-tuple-element.143), channel_id=1, source_target_pairs={{0,1},{1,0},{2,3},{3,2},{4,5},{5,4},{6,7},{7,6},{8,9},{9,8},{10,11... | collective-permute-start | bytes 3145736 | tf_op jit(solution)/shard_map/ppermute | solution.py:38
  25.8 1.5 %collective-permute-start.5 = (bf16[512,256]{1,0:T(8,128)(2,1)S(1)}, bf16[512,256]{1,0:T(8,128)(2,1)S(1)}, u32[]{:S(2)}, u32[]{:S(2)}) collective-permute-start(bf16[512,256]{1,0:T(8,128)(2,1)S(1)} %get-tuple-element.144), channel_id=1, source_target_pairs={{0,1},{1,0},{2,3},{3,2},{4,5},{5,4},{6,7},{7,6},{8,9},{9,8},{10,11... | collective-permute-start | bytes 786440 | tf_op jit(solution)/shard_map/ppermute | solution.py:38
  27.7 15.7 %collective-permute-start.10 = (bf16[8,32,1152]{2,1,0:T(8,128)(2,1)S(1)}, bf16[8,32,1152]{2,1,0:T(8,128)(2,1)S(1)}, u32[]{:S(2)}, u32[]{:S(2)}) collective-permute-start(bf16[8,32,1152]{2,1,0:T(8,128)(2,1)S(1)} %get-tuple-element.148.refs_12_), channel_id=1, source_target_pairs={{0,4},{2,6},{4,0},{6,2},{8,12},{10,14},{12,8},{14,10},{16,20},{18,... | collective-permute-start | bytes 1769480 | tf_op jit(solution)/shard_map/ppermute | solution.py:716
  29.5 15.4 %collective-permute-start.9 = (bf16[8,32,1152]{2,1,0:T(8,128)(2,1)S(1)}, bf16[8,32,1152]{2,1,0:T(8,128)(2,1)S(1)}, u32[]{:S(2)}, u32[]{:S(2)}) collective-permute-start(bf16[8,32,1152]{2,1,0:T(8,128)(2,1)S(1)} %get-tuple-element.147.refs_11_), channel_id=1, source_target_pairs={{0,8},{2,10},{4,12},{6,14},{8,0},{10,2},{12,4},{14,6},{16,24},{18,... | collective-permute-start | bytes 1769480 | tf_op jit(solution)/shard_map/ppermute | solution.py:716
  32.5 1.7 %collective-permute-start.7 = (bf16[576,128]{1,0:T(8,128)(2,1)S(1)}, bf16[576,128]{1,0:T(8,128)(2,1)S(1)}, u32[]{:S(2)}, u32[]{:S(2)}) collective-permute-start(bf16[576,128]{1,0:T(8,128)(2,1)S(1)} %get-tuple-element.149.refs_15_.refs_1_), channel_id=1, source_target_pairs={{0,1},{1,0},{2,3},{3,2},{4,5},{5,4},{6,7},{7,6},{8,9},{9,8},{10,11... | collective-permute-start | bytes 442376 | tf_op jit(solution)/shard_map/ppermute | solution.py:38
  34.3 6.3 %collective-permute-start.8 = (bf16[576,128]{1,0:T(8,128)(2,1)S(1)}, bf16[576,128]{1,0:T(8,128)(2,1)S(1)}, u32[]{:S(2)}, u32[]{:S(2)}) collective-permute-start(bf16[576,128]{1,0:T(8,128)(2,1)S(1)} %shard_map.199.refs_15_), channel_id=1, source_target_pairs={{0,2},{2,0},{1,3},{3,1},{4,6},{6,4},{5,7},{7,5},{8,10},{10,8},{9,1... | collective-permute-start | bytes 442376 | tf_op jit(solution)/shard_map/ppermute | solution.py:38
  43.2 4.1 %copy-start.2 = (bf16[512,2048]{1,0:T(8,128)(2,1)S(1)}, bf16[512,2048]{1,0:T(8,128)(2,1)}, u32[]{:S(2)}) copy-start(bf16[512,2048]{1,0:T(8,128)(2,1)} %refs_1_.3) | copy-start | bytes 6291460
  43.2 4.1 %copy-start.8 = (f32[512]{0:T(512)S(1)}, f32[512]{0:T(512)}, u32[]{:S(2)}) copy-start(f32[512]{0:T(512)} %param.13) | copy-start | bytes 6148
  43.2 6.5 %collective-permute-start.11 = (bf16[512,1024]{1,0:T(8,128)(2,1)S(1)}, bf16[512,1024]{1,0:T(8,128)(2,1)S(1)}, u32[]{:S(2)}, u32[]{:S(2)}) collective-permute-start(bf16[512,1024]{1,0:T(8,128)(2,1)S(1)} %get-tuple-element.176.refs_4_), channel_id=1, source_target_pairs={{0,1},{1,0},{2,3},{3,2},{4,5},{5,4},{6,7},{7,6},{8,9},{9,8},{10,11... | collective-permute-start | bytes 3145736 | tf_op jit(solution)/shard_map/ppermute | solution.py:38
  45.1 8.9 %collective-permute-start.18 = (bf16[4,32,1152]{2,1,0:T(8,128)(2,1)S(1)}, bf16[4,32,1152]{2,1,0:T(8,128)(2,1)S(1)}, u32[]{:S(2)}, u32[]{:S(2)}) collective-permute-start(bf16[4,32,1152]{2,1,0:T(8,128)(2,1)S(1)} %get-tuple-element.177.refs_7_), channel_id=1, source_target_pairs={{0,4},{2,6},{4,0},{6,2},{8,12},{10,14},{12,8},{14,10},{16,20},{18,... | collective-permute-start | bytes 884744 | tf_op jit(solution)/shard_map/ppermute | solution.py:716
  45.5 8.5 %collective-permute-start.19 = (bf16[4,32,1152]{2,1,0:T(8,128)(2,1)S(1)}, bf16[4,32,1152]{2,1,0:T(8,128)(2,1)S(1)}, u32[]{:S(2)}, u32[]{:S(2)}) collective-permute-start(bf16[4,32,1152]{2,1,0:T(8,128)(2,1)S(1)} %get-tuple-element.178.refs_8_), channel_id=1, source_target_pairs={{0,8},{2,10},{4,12},{6,14},{8,0},{10,2},{12,4},{14,6},{16,24},{18,... | collective-permute-start | bytes 884744 | tf_op jit(solution)/shard_map/ppermute | solution.py:716
  50.0 10.0 %collective-permute-start.12 = (bf16[4,32,1152]{2,1,0:T(8,128)(2,1)S(1)}, bf16[4,32,1152]{2,1,0:T(8,128)(2,1)S(1)}, u32[]{:S(2)}, u32[]{:S(2)}) collective-permute-start(bf16[4,32,1152]{2,1,0:T(8,128)(2,1)S(1)} %get-tuple-element.183), channel_id=1, source_target_pairs={{0,2},{2,0},{4,6},{6,4},{8,10},{10,8},{12,14},{14,12},{16,18},{18,... | collective-permute-start | bytes 884744 | tf_op jit(solution)/shard_map/ppermute | solution.py:716
  51.5 14.5 %collective-permute-start.13 = (bf16[4,32,1152]{2,1,0:T(8,128)(2,1)S(1)}, bf16[4,32,1152]{2,1,0:T(8,128)(2,1)S(1)}, u32[]{:S(2)}, u32[]{:S(2)}) collective-permute-start(bf16[4,32,1152]{2,1,0:T(8,128)(2,1)S(1)} %get-tuple-element.184), channel_id=1, source_target_pairs={{0,4},{2,6},{4,0},{6,2},{8,12},{10,14},{12,8},{14,10},{16,20},{18,... | collective-permute-start | bytes 884744 | tf_op jit(solution)/shard_map/ppermute | solution.py:716
  53.0 13.0 %collective-permute-start.14 = (bf16[4,32,1152]{2,1,0:T(8,128)(2,1)S(1)}, bf16[4,32,1152]{2,1,0:T(8,128)(2,1)S(1)}, u32[]{:S(2)}, u32[]{:S(2)}) collective-permute-start(bf16[4,32,1152]{2,1,0:T(8,128)(2,1)S(1)} %get-tuple-element.185), channel_id=1, source_target_pairs={{0,6},{2,4},{4,2},{6,0},{8,14},{10,12},{12,10},{14,8},{16,22},{18,... | collective-permute-start | bytes 884744 | tf_op jit(solution)/shard_map/ppermute | solution.py:716
  54.1 16.3 %collective-permute-start.20 = (bf16[2,32,2304]{2,1,0:T(8,128)(2,1)S(1)}, bf16[2,32,2304]{2,1,0:T(8,128)(2,1)S(1)}, u32[]{:S(2)}, u32[]{:S(2)}) collective-permute-start(bf16[2,32,2304]{2,1,0:T(8,128)(2,1)S(1)} %get-tuple-element.193), channel_id=1, source_target_pairs={{0,16},{2,18},{4,20},{6,22},{8,24},{10,26},{12,28},{14,30},{16,0},... | collective-permute-start | bytes 884744 | tf_op jit(solution)/shard_map/ppermute | solution.py:716
  66.1 6.7 %collective-permute-start.15 = (bf16[1,32,1152]{2,1,0:T(8,128)(2,1)S(1)}, bf16[1,32,1152]{2,1,0:T(8,128)(2,1)S(1)}, u32[]{:S(2)}, u32[]{:S(2)}) collective-permute-start(bf16[1,32,1152]{2,1,0:T(8,128)(2,1)S(1)} %get-tuple-element.187), channel_id=1, source_target_pairs={{0,16},{2,18},{4,20},{6,22},{8,24},{10,26},{12,28},{14,30},{16,0},... | collective-permute-start | bytes 221192 | tf_op jit(solution)/shard_map/ppermute | solution.py:716
  68.8 6.3 %collective-permute-start.16 = (bf16[1,32,1152]{2,1,0:T(8,128)(2,1)S(1)}, bf16[1,32,1152]{2,1,0:T(8,128)(2,1)S(1)}, u32[]{:S(2)}, u32[]{:S(2)}) collective-permute-start(bf16[1,32,1152]{2,1,0:T(8,128)(2,1)S(1)} %get-tuple-element.188), channel_id=1, source_target_pairs={{0,24},{2,26},{4,28},{6,30},{8,16},{10,18},{12,20},{14,22},{16,8},... | collective-permute-start | bytes 221192 | tf_op jit(solution)/shard_map/ppermute | solution.py:716
  70.2 5.1 %collective-permute-start.17 = (bf16[1,32,1152]{2,1,0:T(8,128)(2,1)S(1)}, bf16[1,32,1152]{2,1,0:T(8,128)(2,1)S(1)}, u32[]{:S(2)}, u32[]{:S(2)}) collective-permute-start(bf16[1,32,1152]{2,1,0:T(8,128)(2,1)S(1)} %get-tuple-element.189), channel_id=1, source_target_pairs={{0,8},{2,10},{4,12},{6,14},{8,0},{10,2},{12,4},{14,6},{16,24},{18,... | collective-permute-start | bytes 221192 | tf_op jit(solution)/shard_map/ppermute | solution.py:716
  70.4 5.2 %collective-permute-start.21 = (bf16[1,32,2304]{2,1,0:T(8,128)(2,1)S(1)}, bf16[1,32,2304]{2,1,0:T(8,128)(2,1)S(1)}, u32[]{:S(2)}, u32[]{:S(2)}) collective-permute-start(bf16[1,32,2304]{2,1,0:T(8,128)(2,1)S(1)} %get-tuple-element.195), channel_id=1, source_target_pairs={{0,2},{2,0},{4,6},{6,4},{8,10},{10,8},{12,14},{14,12},{16,18},{18,... | collective-permute-start | bytes 442376 | tf_op jit(solution)/shard_map/ppermute | solution.py:716
  75.7 1.4 %collective-permute-start.22 = (bf16[32,1408]{1,0:T(8,128)(2,1)S(1)}, bf16[32,1408]{1,0:T(8,128)(2,1)S(1)}, u32[]{:S(2)}, u32[]{:S(2)}) collective-permute-start(bf16[32,1408]{1,0:T(8,128)(2,1)S(1)} %shard_map.210.refs_0_), channel_id=1, source_target_pairs={{0,1},{1,0},{2,3},{3,2},{4,5},{5,4},{6,7},{7,6},{8,9},{9,8},{10,11... | collective-permute-start | bytes 270344 | tf_op jit(solution)/shard_map/ppermute | solution.py:38
